TPU v7x, 32 devices: a whole 2x2x4 slice. The times are simulated.
32 devices in a mesh: dp: 4 (over x, core), expert: 8 (over z, y).
Axes of the slice: x: 2, y: 2, z: 4, core: 2. Of those that a mesh axis runs over, the one named last changes fastest.
Arguments:
- tokens: bfloat16 [768, 4096], P(('dp', 'expert')), may hold values from -6 to 6
- expert_ids: int32 [768, 8], P(('dp', 'expert')), may hold values from 0 to 15, all different within a row; in each aligned block of 24 rows (0 to 23, 24 to 47, ...) at most 24 rows name the same one
- route_weight: float32 [768, 8], P(('dp', 'expert')), may hold values from 0.05 to 0.5
- slot_of: int32 [16, 2], replicated, may hold values from 0 to 31, as said below
- swap_flag: int32 [32], P(('dp', 'expert')), may hold values from 0 to 1, as said below
- w_gate: bfloat16 [32, 4096, 512], P(('dp', 'expert')), may hold values from -0.09375 to 0.09375
- w_up: bfloat16 [32, 4096, 512], P(('dp', 'expert')), may hold values from -0.09375 to 0.09375
- w_down: bfloat16 [32, 512, 4096], P(('dp', 'expert')), may hold values from -0.1875 to 0.1875
Outputs:
- moe_out: bfloat16 [768, 4096], P(('dp', 'expert'))
Inputs may be any that keep to these rules, and one draw needn't show every extreme that they name: `expert_ids`: in each aligned block of 24 rows (the rows of one device) no expert is chosen by more than 24 rows, and some expert is chosen by exactly 24 rows in some block. `slot_of`: every slot number appears exactly once. `swap_flag`: slot s = d * 8 + x pairs with the slot of dp index d XOR 1 and the same x; both slots of a pair carry the same flag.
All inputs are finite; a program needn't handle non-finite values.
Results may differ from a plain program's by a relative error of at most 0.0058.
Values may be sent and summed in bfloat16 or wider, within the bound.
No kernel may reach another device: no remote copies, remote signals or barrier semaphores. Data moves between devices by JAX's collectives and lax.ppermute only.
A program may use at most 128 MiB of HBM per device.

v0:
```python
import jax
import jax.numpy as jnp
from jax import lax
from jax.sharding import PartitionSpec as P


def partner(value, axis, distance):
    mask = 2**distance
    pairs = [(source, source ^ mask) for source in range(lax.axis_size(axis))]
    return lax.ppermute(value, axis, pairs)


def on_device(tokens, expert_ids, route_weight, slot_of, swap_flag, w_gate, w_up, w_down):
    dp_count = lax.axis_size("dp")
    ex_count = lax.axis_size("expert")
    slot_count = dp_count * ex_count
    tok_rows, model_width = tokens.shape
    top_count = expert_ids.shape[1]
    experts = slot_of.shape[0]
    capacity = 2 * tok_rows * top_count // experts
    moved_shards = partner((w_gate, w_up, w_down), "dp", 0)
    taking = swap_flag[0] == 1
    gate_w = jnp.where(taking, moved_shards[0][0], w_gate[0])
    up_w = jnp.where(taking, moved_shards[1][0], w_up[0])
    down_w = jnp.where(taking, moved_shards[2][0], w_down[0])
    pair_count = tok_rows * top_count
    flat_ids = expert_ids.reshape(pair_count)
    onehot = (flat_ids[:, None] == jnp.arange(experts, dtype=jnp.int32)).astype(jnp.int32)
    order_rank = jnp.sum((jnp.cumsum(onehot, axis=0) - onehot) * onehot, axis=1)
    dest_slot = jnp.sum(onehot[:, :, None] * slot_of[None, :, :], axis=1)
    position = dest_slot * capacity + order_rank[:, None]
    pair_ids = jnp.broadcast_to(jnp.arange(pair_count, dtype=jnp.int32)[:, None], (pair_count, 2))
    owner = (
        jnp.full((slot_count * capacity,), -1, jnp.int32)
        .at[position.reshape(-1)]
        .set(pair_ids.reshape(-1))
    )
    token_row = jnp.maximum(owner, 0) // top_count
    outbox = jnp.where((owner >= 0)[:, None], tokens[token_row], jnp.zeros((), tokens.dtype))
    outbox = outbox.reshape(dp_count, ex_count, capacity, model_width)
    inbox_rows = lax.all_to_all(
        lax.all_to_all(outbox, "dp", split_axis=0, concat_axis=0, tiled=True),
        "expert",
        split_axis=1,
        concat_axis=1,
        tiled=True,
    )
    arrived = inbox_rows.reshape(slot_count * capacity, model_width)
    gate_sum = jnp.dot(arrived, gate_w, preferred_element_type=jnp.float32)
    up_sum = jnp.dot(arrived, up_w, preferred_element_type=jnp.float32)
    hidden = (jax.nn.silu(gate_sum) * up_sum).astype(jnp.bfloat16)
    partial_out = jnp.dot(hidden, down_w, preferred_element_type=jnp.float32).astype(jnp.bfloat16)
    partial_out = partial_out.reshape(dp_count, ex_count, capacity, model_width)
    returned = lax.all_to_all(
        lax.all_to_all(partial_out, "dp", split_axis=0, concat_axis=0, tiled=True),
        "expert",
        split_axis=1,
        concat_axis=1,
        tiled=True,
    )
    returned = returned.reshape(slot_count * capacity, model_width)
    picked = returned[position].astype(jnp.float32)
    scaled = jnp.sum(picked, axis=1) * route_weight.reshape(pair_count)[:, None]
    return jnp.sum(scaled.reshape(tok_rows, top_count, model_width), axis=1).astype(jnp.bfloat16)


def solution(mesh):
    return jax.shard_map(
        on_device,
        mesh=mesh,
        in_specs=(
            P(("dp", "expert"), None),
            P(("dp", "expert"), None),
            P(("dp", "expert"), None),
            P(),
            P(("dp", "expert")),
            P(("dp", "expert"), None, None),
            P(("dp", "expert"), None, None),
            P(("dp", "expert"), None, None),
        ),
        out_specs=P(("dp", "expert"), None),
        check_vma=False,
    )
```

profile of v0, /device:TPU:0, one launch (start us, length us, event | category | flops | bytes accessed | tf_op | source)
XLA Modules:
  0.0 512.9 jit_solution(4211380868453267929)
XLA Ops:
  0.0 0.0 copy-start
  0.0 0.8 copy.47
  0.8 0.1 eq.32
  0.9 0.6 reduce-window.6
  1.5 0.2 slice_reduce_fusion
  1.7 0.1 bitcast_bitcast_fusion
  1.9 0.8 multiply_reduce_fusion
  2.6 0.1 copy.50
  2.8 0.1 add.69
  2.9 0.1 reshape.175
  3.1 2.9 scatter_custom_fusion
  6.1 0.1 broadcast_in_dim.35
  6.2 0.0 copy-done
  6.2 5.7 %gather_fusion = bf16[768,4096]{1,0:T(8,128)(2,1)} fusion(bf16[24,4096]{1,0:T(8,128)(2,1)S(1)} %copy-done, s32[1024]{0:T(1024)S(1)} %pad_clamp_fusion.1), kind=kCustom, calls=%fused_computation | custom fusion | bytes 12585984 | tf_op jit(solution)/shard_map/gather | solution.py:39
  11.9 3.3 broadcast_select_fusion
  15.2 74.7 %all_to_all.20 = bf16[4,8,24,4096]{3,2,1,0:T(8,128)(2,1)S(1)} all-to-all(bf16[4,8,24,4096]{3,2,1,0:T(8,128)(2,1)S(1)} %broadcast_select_fusion), channel_id=1, replica_groups=mesh['dp'=4,'expert'=8] {'dp'}, dimensions={0} | all-to-all | bytes 12582912 | tf_op jit(solution)/shard_map/all_to_all | solution.py:42
  89.8 3.1 copy.51
  92.9 5.9 %all-to-all-start.1 = ((bf16[4,8,24,4096]{3,2,0,1:T(8,128)(2,1)}), bf16[4,8,24,4096]{3,2,0,1:T(8,128)(2,1)}, u32[]{:S(2)}, u32[]{:S(2)}) async-start(bf16[4,8,24,4096]{3,2,0,1:T(8,128)(2,1)} %copy.51), calls=%async_computation.1 | async-start | bytes 12582912 | tf_op jit(solution)/shard_map/all_to_all | solution.py:41
  98.8 0.0 collective-permute-start.1
  98.8 0.5 collective-permute-start
  99.3 0.1 collective-permute-start.2
  100.1 136.6 %all-to-all-done.1 = bf16[4,8,24,4096]{3,2,0,1:T(8,128)(2,1)} async-done(((bf16[4,8,24,4096]{3,2,0,1:T(8,128)(2,1)}), bf16[4,8,24,4096]{3,2,0,1:T(8,128)(2,1)}, u32[]{:S(2)}, u32[]{:S(2)}) %all-to-all-start.1) | async-done | bytes 6291488 | tf_op jit(solution)/shard_map/all_to_all | solution.py:41
  236.7 0.0 copy-start.3
  236.7 3.4 copy.52
  240.1 0.0 collective-permute-done.1
  240.1 0.6 copy-done.3
  240.7 0.0 copy-start.4
  240.7 5.8 %fusion.1 = f32[768,512]{1,0:T(8,128)S(1)} fusion(bf16[768,4096]{1,0:T(8,128)(2,1)S(1)} %bitcast.40, bf16[1,4096,512]{2,1,0:T(8,128)(2,1)} %collective-permute-done.1, bf16[1,4096,512]{2,1,0:T(8,128)(2,1)S(1)} %copy-done.3, pred[]{:T(512)} %bitcast.3), kind=kOutput, calls=%fused_computation.6 | convolution fusion | flops 3223322624 | bytes 16252929 | tf_op jit(solution)/shard_map/dot_general | solution.py:50
  246.5 0.0 collective-permute-done
  246.5 0.0 copy-done.4
  246.5 5.7 %fusion.3 = f32[768,512]{1,0:T(8,128)S(1)} fusion(bf16[768,4096]{1,0:T(8,128)(2,1)S(1)} %bitcast.41, bf16[1,4096,512]{2,1,0:T(8,128)(2,1)} %collective-permute-done, bf16[1,4096,512]{2,1,0:T(8,128)(2,1)S(1)} %copy-done.4, pred[]{:T(512)} %bitcast.3), kind=kOutput, calls=%fused_computation.8 | convolution fusion | flops 3223322624 | bytes 16252929 | tf_op jit(solution)/shard_map/dot_general | solution.py:49
  252.2 0.0 collective-permute-done.2
  252.2 6.0 %convolution_convert_fusion = bf16[768,4096]{1,0:T(8,128)(2,1)S(1)} fusion(bf16[1,512,4096]{2,1,0:T(8,128)(2,1)} %collective-permute-done.2, bf16[1,512,4096]{2,1,0:T(8,128)(2,1)} %param.15, pred[]{:T(512)} %bitcast.3, f32[768,512]{1,0:T(8,128)S(1)} %fusion.1, f32[768,512]{1,0:T(8,128)S(1)} %fusion.3), kind=kOutput, calls=%fused_computation.3 | convolution fusion | flops 3228827648 | bytes 17825792 | tf_op jit(solution)/shard_map/dot_general | solution.py:52
  258.2 73.3 %all_to_all.21 = bf16[4,8,24,4096]{3,2,1,0:T(8,128)(2,1)S(1)} all-to-all(bf16[4,8,24,4096]{3,2,1,0:T(8,128)(2,1)S(1)} %bitcast.42), channel_id=1, replica_groups=mesh['dp'=4,'expert'=8] {'dp'}, dimensions={0} | all-to-all | bytes 12582912 | tf_op jit(solution)/shard_map/all_to_all | solution.py:55
  331.5 3.1 copy.53
  334.6 0.0 copy-start.2
  334.6 5.1 all-to-all-start.3
  339.7 0.1 copy.55
  339.8 0.1 reshape.165
  339.9 0.0 copy-done.2
  339.9 0.1 copy.56
  340.0 137.4 %all-to-all-done.3 = bf16[4,8,24,4096]{3,2,0,1:T(8,128)(2,1)} async-done(((bf16[4,8,24,4096]{3,2,0,1:T(8,128)(2,1)}), bf16[4,8,24,4096]{3,2,0,1:T(8,128)(2,1)}, u32[]{:S(2)}, u32[]{:S(2)}) %all-to-all-start.3) | async-done | bytes 6291488 | tf_op jit(solution)/shard_map/all_to_all | solution.py:54
  477.5 6.2 %copy.54 = bf16[4,8,24,4096]{3,2,1,0:T(8,128)(2,1)} copy(bf16[4,8,24,4096]{3,2,0,1:T(8,128)(2,1)} %all-to-all-done.3) | data formatting | bytes 12582912 | tf_op jit(solution)/shard_map/all_to_all | solution.py:54
  483.7 11.1 %gather_fusion.1 = bf16[384,4096]{1,0:T(8,128)(2,1)S(1)} fusion(bf16[768,4096]{1,0:T(8,128)(2,1)} %bitcast.38, s32[1024]{0:T(1024)S(1)} %pad_clamp_fusion), kind=kCustom, calls=%fused_computation.1 | custom fusion | bytes 6292992 | tf_op jit(solution)/shard_map/gather | solution.py:62
  494.8 0.0 copy-start.1
  494.8 5.7 %reshape.181 = f32[192,2,4096]{2,1,0:T(2,128)} reshape(bf16[384,4096]{1,0:T(8,128)(2,1)S(1)} %gather_fusion.1) | data formatting | bytes 9437184 | tf_op jit(solution)/shard_map/convert_element_type | solution.py:62
  500.5 10.7 %reduce_sum.40 = f32[192,4096]{1,0:T(8,128)S(1)} reduce(f32[192,2,4096]{2,1,0:T(2,128)} %reshape.181, f32[]{:T(128)} %constant.44.clone.1), dimensions={1}, to_apply=%region_5.6 | reduce | flops 786432 | bytes 9437188 | tf_op jit(solution)/shard_map/reduce_sum | solution.py:63
  511.2 1.7 fusion.11
  512.9 0.0 copy-done.1
  (14 shorter events, 0.2 us)
Async XLA Ops:
  0.0 6.2 %copy-start = (bf16[24,4096]{1,0:T(8,128)(2,1)S(1)}, bf16[24,4096]{1,0:T(8,128)(2,1)}, u32[]{:S(2)}) copy-start(bf16[24,4096]{1,0:T(8,128)(2,1)} %param.8) | copy-start | bytes 589828
  92.9 143.8 %all-to-all-start.1 = ((bf16[4,8,24,4096]{3,2,0,1:T(8,128)(2,1)}), bf16[4,8,24,4096]{3,2,0,1:T(8,128)(2,1)}, u32[]{:S(2)}, u32[]{:S(2)}) async-start(bf16[4,8,24,4096]{3,2,0,1:T(8,128)(2,1)} %copy.51), calls=%async_computation.1 | async-start | bytes 12582912 | tf_op jit(solution)/shard_map/all_to_all | solution.py:41
  98.8 141.2 %collective-permute-start.1 = (bf16[1,4096,512]{2,1,0:T(8,128)(2,1)}, bf16[1,4096,512]{2,1,0:T(8,128)(2,1)}, u32[]{:S(2)}, u32[]{:S(2)}) collective-permute-start(bf16[1,4096,512]{2,1,0:T(8,128)(2,1)} %param.14), channel_id=1, source_target_pairs={{0,8},{8,0},{16,24},{24,16},{1,9},{9,1},{17,25},{25,17},{2,10},{10... | collective-permute-start | bytes 12582920 | tf_op jit(solution)/shard_map/ppermute | solution.py:10
  98.8 147.7 %collective-permute-start = (bf16[1,4096,512]{2,1,0:T(8,128)(2,1)}, bf16[1,4096,512]{2,1,0:T(8,128)(2,1)}, u32[]{:S(2)}, u32[]{:S(2)}) collective-permute-start(bf16[1,4096,512]{2,1,0:T(8,128)(2,1)} %param.13), channel_id=1, source_target_pairs={{0,8},{8,0},{16,24},{24,16},{1,9},{9,1},{17,25},{25,17},{2,10},{10... | collective-permute-start | bytes 12582920 | tf_op jit(solution)/shard_map/ppermute | solution.py:10
  99.3 152.9 %collective-permute-start.2 = (bf16[1,512,4096]{2,1,0:T(8,128)(2,1)}, bf16[1,512,4096]{2,1,0:T(8,128)(2,1)}, u32[]{:S(2)}, u32[]{:S(2)}) collective-permute-start(bf16[1,512,4096]{2,1,0:T(8,128)(2,1)} %param.15), channel_id=1, source_target_pairs={{0,8},{8,0},{16,24},{24,16},{1,9},{9,1},{17,25},{25,17},{2,10},{10... | collective-permute-start | bytes 12582920 | tf_op jit(solution)/shard_map/ppermute | solution.py:10
  236.7 4.0 copy-start.3
  240.7 5.8 %copy-start.4 = (bf16[1,4096,512]{2,1,0:T(8,128)(2,1)S(1)}, bf16[1,4096,512]{2,1,0:T(8,128)(2,1)}, u32[]{:S(2)}) copy-start(bf16[1,4096,512]{2,1,0:T(8,128)(2,1)} %param.13) | copy-start | bytes 12582916
  334.6 5.4 %copy-start.2 = (f32[24,8]{0,1:T(8,128)S(1)}, f32[24,8]{0,1:T(8,128)}, u32[]{:S(2)}) copy-start(f32[24,8]{0,1:T(8,128)} %param.10) | copy-start | bytes 2308
  334.6 142.9 %all-to-all-start.3 = ((bf16[4,8,24,4096]{3,2,0,1:T(8,128)(2,1)}), bf16[4,8,24,4096]{3,2,0,1:T(8,128)(2,1)}, u32[]{:S(2)}, u32[]{:S(2)}) async-start(bf16[4,8,24,4096]{3,2,0,1:T(8,128)(2,1)} %copy.53), calls=%async_computation.3 | async-start | bytes 12582912 | tf_op jit(solution)/shard_map/all_to_all | solution.py:54
  494.8 18.1 %copy-start.1 = (bf16[24,4096]{1,0:T(8,128)(2,1)S(1)}, bf16[24,4096]{1,0:T(8,128)(2,1)}, u32[]{:S(2)}) copy-start(bf16[24,4096]{1,0:T(8,128)(2,1)} %param.8) | copy-start | bytes 589828
where the time goes:
time: 513 us
  waiting for transfers between devices  274 us (53%)
  blocking collectives  148 us (29%)
  local copies, waits for them, and re-layouts  43.7 us (9%)
  matrix products  17.4 us (3%)
  other arithmetic  17.2 us (3%)
  starting transfers between devices  11.6 us (2%)
    all_to_all x1, waiting for transfers between devices, on_device(): lax.all_to_all(lax.all_to_all(partial_out, 'dp', split_axis=0, concat_axi...  137 us
    all_to_all x1, waiting for transfers between devices, on_device(): lax.all_to_all(lax.all_to_all(outbox, 'dp', split_axis=0, concat_axis=0,...  137 us
    all_to_all x1, blocking collectives, on_device(): lax.all_to_all(outbox, 'dp', split_axis=0, concat_axis=0, tiled=True)  74.7 us
    all_to_all x1, blocking collectives, on_device(): lax.all_to_all(partial_out, 'dp', split_axis=0, concat_axis=0, tiled=True)  73.3 us
    gather x1, local copies, waits for them, and re-layouts, on_device(): picked = returned[position].astype(jnp.float32)  11.1 us
    reduce_sum x1, other arithmetic, on_device(): scaled = jnp.sum(picked, axis=1) * route_weight.reshape(pair_count)[:, None]  10.7 us
  transfers between devices with their start and end apart: 5, of which 2 were waited for; matrix products, arithmetic and copies ran while one was open for 3% of the time, Pallas kernels for 0%

commit v1 on v0

--- a/solution.py
+++ b/solution.py
@@ -2,6 +2,8 @@
 import jax.numpy as jnp
 from jax import lax
 from jax.sharding import PartitionSpec as P
+
+AXES = ("dp", "expert")
 
 
 def partner(value, axis, distance):
@@ -10,7 +12,17 @@
     return lax.ppermute(value, axis, pairs)
 
 
-def on_device(tokens, expert_ids, route_weight, slot_of, swap_flag, w_gate, w_up, w_down):
+def exchange(value):
+    return lax.all_to_all(
+        lax.all_to_all(value, "dp", split_axis=0, concat_axis=0, tiled=True),
+        "expert",
+        split_axis=1,
+        concat_axis=1,
+        tiled=True,
+    )
+
+
+def sparse(tokens, expert_ids, route_weight, slot_of, swap_flag, w_gate, w_up, w_down):
     dp_count = lax.axis_size("dp")
     ex_count = lax.axis_size("expert")
     slot_count = dp_count * ex_count
@@ -38,30 +50,45 @@
     token_row = jnp.maximum(owner, 0) // top_count
     outbox = jnp.where((owner >= 0)[:, None], tokens[token_row], jnp.zeros((), tokens.dtype))
     outbox = outbox.reshape(dp_count, ex_count, capacity, model_width)
-    inbox_rows = lax.all_to_all(
-        lax.all_to_all(outbox, "dp", split_axis=0, concat_axis=0, tiled=True),
-        "expert",
-        split_axis=1,
-        concat_axis=1,
-        tiled=True,
-    )
-    arrived = inbox_rows.reshape(slot_count * capacity, model_width)
+    arrived = exchange(outbox).reshape(slot_count * capacity, model_width)
     gate_sum = jnp.dot(arrived, gate_w, preferred_element_type=jnp.float32)
     up_sum = jnp.dot(arrived, up_w, preferred_element_type=jnp.float32)
     hidden = (jax.nn.silu(gate_sum) * up_sum).astype(jnp.bfloat16)
     partial_out = jnp.dot(hidden, down_w, preferred_element_type=jnp.float32).astype(jnp.bfloat16)
     partial_out = partial_out.reshape(dp_count, ex_count, capacity, model_width)
-    returned = lax.all_to_all(
-        lax.all_to_all(partial_out, "dp", split_axis=0, concat_axis=0, tiled=True),
-        "expert",
-        split_axis=1,
-        concat_axis=1,
-        tiled=True,
-    )
-    returned = returned.reshape(slot_count * capacity, model_width)
+    returned = exchange(partial_out).reshape(slot_count * capacity, model_width)
     picked = returned[position].astype(jnp.float32)
     scaled = jnp.sum(picked, axis=1) * route_weight.reshape(pair_count)[:, None]
     return jnp.sum(scaled.reshape(tok_rows, top_count, model_width), axis=1).astype(jnp.bfloat16)
+
+
+def served_expert(slot_of, swap_flag):
+    d = lax.axis_index("dp")
+    x = lax.axis_index("expert")
+    serving = jnp.where(swap_flag[0] == 1, d ^ 1, d) * lax.axis_size("expert") + x
+    numbers = jnp.arange(slot_of.shape[0], dtype=jnp.int32)[:, None]
+    return jnp.sum(jnp.where(slot_of == serving, numbers, 0))
+
+
+def dense(tokens, expert_ids, route_weight, slot_of, swap_flag, w_gate, w_up, w_down):
+    mine = served_expert(slot_of, swap_flag)
+    all_ids = lax.all_gather(expert_ids, AXES, tiled=True)
+    all_weights = lax.all_gather(route_weight, AXES, tiled=True)
+    scale = jnp.sum(jnp.where(all_ids == mine, all_weights, 0.0), axis=1)
+    arrived = lax.all_gather(tokens, AXES, tiled=True)
+    gate_sum = jnp.dot(arrived, w_gate[0], preferred_element_type=jnp.float32)
+    up_sum = jnp.dot(arrived, w_up[0], preferred_element_type=jnp.float32)
+    hidden = (jax.nn.silu(gate_sum) * up_sum).astype(jnp.bfloat16)
+    partial_out = jnp.dot(hidden, w_down[0], preferred_element_type=jnp.float32)
+    partial_out = (partial_out * scale[:, None]).astype(jnp.bfloat16)
+    return lax.psum_scatter(partial_out, AXES, scatter_dimension=0, tiled=True)
+
+
+def on_device(tokens, expert_ids, *rest):
+    slot_of = rest[1]
+    capacity = 2 * tokens.shape[0] * expert_ids.shape[1] // slot_of.shape[0]
+    serve = dense if capacity >= tokens.shape[0] else sparse
+    return serve(tokens, expert_ids, *rest)
 
 
 def solution(mesh):
@@ -69,15 +96,15 @@
         on_device,
         mesh=mesh,
         in_specs=(
-            P(("dp", "expert"), None),
-            P(("dp", "expert"), None),
-            P(("dp", "expert"), None),
+            P(AXES, None),
+            P(AXES, None),
+            P(AXES, None),
             P(),
-            P(("dp", "expert")),
-            P(("dp", "expert"), None, None),
-            P(("dp", "expert"), None, None),
-            P(("dp", "expert"), None, None),
+            P(AXES),
+            P(AXES, None, None),
+            P(AXES, None, None),
+            P(AXES, None, None),
         ),
-        out_specs=P(("dp", "expert"), None),
+        out_specs=P(AXES, None),
         check_vma=False,
     )

time: 513 us -> 286 us (0.56)
  waiting for transfers between devices: 274 us -> 114 us
  local copies, waits for them, and re-layouts: 43.7 us -> 0.08 us
  other arithmetic: 17.2 us -> 2.01 us
  between operations: 0.9 us -> 14.1 us
  blocking collectives: 148 us -> 136 us
  starting transfers between devices: 11.6 us -> 0.04 us
    all_to_all x2 -> x0, waiting for transfers between devices: 274 us -> none  [the longest x1 137 us: on_device(): lax.all_to_all(lax.all_to_all(partial_out, 'dp', split_axis=0, concat_axi...]
    all_to_all x2 -> x0, blocking collectives: 148 us -> none  [the longest x1 74.7 us: on_device(): lax.all_to_all(outbox, 'dp', split_axis=0, concat_axis=0, tiled=True)]
    all_gather x0 -> x2, blocking collectives: none -> 136 us  [the longest x1 71.4 us: dense(): all_ids = lax.all_gather(expert_ids, AXES, tiled=True)]
    reduce_scatter x0 -> x1, waiting for transfers between devices: none -> 113 us  [dense(): return lax.psum_scatter(partial_out, AXES, scatter_dimension=0, tiled=True)]
    gather x2 -> x0, local copies, waits for them, and re-layouts: 16.8 us -> none  [the longest x1 11.1 us: on_device(): picked = returned[position].astype(jnp.float32)]
    all_to_all x4 -> x0, local copies, waits for them, and re-layouts: 15.8 us -> none  [the longest x1 6.24 us: on_device(): lax.all_to_all(lax.all_to_all(partial_out, 'dp', split_axis=0, concat_axi...]
    reduce_sum x4 -> x2, other arithmetic: 13.2 us -> 2.01 us  [the longest x1 1.32 us: served_expert(): return jnp.sum(jnp.where(slot_of == serving, numbers, 0))]
    all_to_all x2 -> x0, starting transfers between devices: 11 us -> none  [the longest x1 5.93 us: on_device(): lax.all_to_all(lax.all_to_all(outbox, 'dp', split_axis=0, concat_axis=0,...]
  transfers between devices with their start and end apart: 5 -> 2, of which waited for: 2 -> 1; matrix products, arithmetic and copies ran while one was open for 3% -> 1% of each run, Pallas kernels for 0% -> 0%
where the time goes in v1:
time: 286 us
  blocking collectives  136 us (48%)
  waiting for transfers between devices  114 us (40%)
  matrix products  19.9 us (7%)
  between operations  14.1 us (5%)
    reduce_scatter x1, waiting for transfers between devices, dense(): return lax.psum_scatter(partial_out, AXES, scatter_dimension=0, tiled=True)  113 us
    all_gather x1, blocking collectives, dense(): all_ids = lax.all_gather(expert_ids, AXES, tiled=True)  71.4 us
    all_gather x1, blocking collectives, dense(): all_weights = lax.all_gather(route_weight, AXES, tiled=True)  64.3 us
    dot_general x1, matrix products, dense(): partial_out = jnp.dot(hidden, w_down[0], preferred_element_type=jnp.float32)  13.1 us
    dot_general x1, matrix products, dense(): gate_sum = jnp.dot(arrived, w_gate[0], preferred_element_type=jnp.float32)  6.75 us
  transfers between devices with their start and end apart: 2, of which 1 were waited for; matrix products, arithmetic and copies ran while one was open for 1% of the time, Pallas kernels for 0%

profile of v1, /device:TPU:0, one launch (start us, length us, event | category | flops | bytes accessed | tf_op | source)
XLA Modules:
  0.0 285.5 jit_solution(5560201783781206621)
XLA Ops:
  6.5 0.0 all-gather.4.cloned.1.call-start
  6.5 0.7 all-gather.4.cloned.1.call-update
  7.3 0.0 reduce-scatter.2.cloned.1.call-start
  8.0 71.4 %all-gather = s32[32,24,8]{1,2,0:T(8,128)S(1)} all-gather(s32[1,24,8]{1,2,0:T(8,128)} %bitcast.18), channel_id=1, replica_groups=mesh['dp'=4,'expert'=8] {'dp','expert'}, dimensions={0}, use_global_device_ids=true | all-gather | bytes 25344 | tf_op jit(solution)/shard_map/all_gather | solution.py:75
  79.4 64.3 %all-gather.1 = f32[32,24,8]{1,2,0:T(8,128)S(1)} all-gather(f32[1,24,8]{1,2,0:T(8,128)} %bitcast.19), channel_id=1, replica_groups=mesh['dp'=4,'expert'=8] {'dp','expert'}, dimensions={0}, use_global_device_ids=true | all-gather | bytes 25344 | tf_op jit(solution)/shard_map/all_gather | solution.py:76
  143.7 1.3 fusion.10
  145.0 0.7 select_reduce_fusion
  145.7 0.1 reshape.11
  145.8 0.0 all-gather.4.cloned.1.call-done
  145.8 6.7 %fusion.3 = f32[768,512]{1,0:T(8,128)S(1)} fusion(bf16[768,4096]{1,0:T(8,128)(2,1)} %all-gather.4.cloned.1.call-done, bf16[1,4096,512]{2,1,0:T(8,128)(2,1)} %param.13), kind=kOutput, calls=%fused_computation.4 | convolution fusion | flops 3221225472 | bytes 12058624 | tf_op jit(solution)/shard_map/dot_general | solution.py:79
  152.6 13.1 %multiply_convert_fusion = bf16[768,4096]{1,0:T(8,128)(2,1)} fusion(f32[768]{0:T(1024)S(1)} %reshape.11, bf16[1,512,4096]{2,1,0:T(8,128)(2,1)} %param.15, f32[768,512]{1,0:T(8,128)S(1)} %fusion.3, bf16[768,4096]{1,0:T(8,128)(2,1)} %all-gather.4.cloned.1.call-done, bf16[1,4096,512]{2,1,0:T(8,128)(2,1)} %param.14), kind=kOutput, calls=%fused_computation | convolution fusion | flops 6451101696 | bytes 22547456 | tf_op jit(solution)/shard_map/dot_general | solution.py:82
  165.7 0.0 reduce-scatter.2.cloned.1.call-update
  165.7 113.0 %reduce-scatter.2.cloned.1.call-done = bf16[24,4096]{1,0:T(8,128)(2,1)} async-done(((bf16[768,4096]{1,0:T(8,128)(2,1)}), bf16[24,4096]{1,0:T(8,128)(2,1)}) %reduce-scatter.2.cloned.1.call-update) | async-done | bytes 196624 | tf_op jit(solution)/shard_map/reduce_scatter | solution.py:84
Async XLA Ops:
  6.5 139.3 %all-gather.4.cloned.1.call-start = ((), (), s32[]{:S(2)}) async-start(), calls=%async_computation.1 | async-start | bytes 6488064 | tf_op jit(solution)/shard_map/all_gather | solution.py:78
  7.3 271.4 %reduce-scatter.2.cloned.1.call-start = ((), (), s32[]{:S(2)}) async-start(), calls=%async_computation.2 | async-start | bytes 6488064 | tf_op jit(solution)/shard_map/reduce_scatter | solution.py:84
Sparse Core Ops, SparseCore 0:
  10.3 72.6 all-gather.3
  165.8 112.7 reduce-scatter.1

commit v2 on v1

--- a/solution.py
+++ b/solution.py
@@ -4,6 +4,7 @@
 from jax.sharding import PartitionSpec as P
 
 AXES = ("dp", "expert")
+LANES = 128
 
 
 def partner(value, axis, distance):
@@ -70,18 +71,98 @@
     return jnp.sum(jnp.where(slot_of == serving, numbers, 0))
 
 
+def permute(value, move):
+    ex_count = lax.axis_size("expert")
+    pairs = []
+    for source in range(lax.axis_size("dp") * ex_count):
+        d, e = divmod(source, ex_count)
+        d, e = move(d, e)
+        pairs.append((source, d * ex_count + e))
+    return lax.ppermute(value, AXES, pairs)
+
+
+def to_sibling(d, e):
+    return d ^ 1, e
+
+
+def over_first(d, e):
+    return (d ^ 2, e) if d % 2 else (d, e ^ 1)
+
+
+def over_second(d, e):
+    return (d, e ^ 1) if d % 2 else (d ^ 2, e)
+
+
+def along_line(distance):
+    ex_count = lax.axis_size("expert")
+    return lambda d, e: (d, (e + 2 * distance) % ex_count)
+
+
+def packed(tokens, expert_ids, route_weight):
+    top_count = expert_ids.shape[1]
+    parts = []
+    rest = route_weight
+    for _ in range(3):
+        part = lax.reduce_precision(rest, exponent_bits=8, mantissa_bits=7)
+        parts.append(part.astype(jnp.bfloat16))
+        rest = rest - part
+    ids = expert_ids.astype(jnp.bfloat16)
+    extra = jnp.concatenate([ids] + parts, axis=1)
+    extra = jnp.pad(extra, ((0, 0), (0, LANES - 4 * top_count)))
+    return jnp.concatenate([tokens, extra], axis=1)
+
+
+def scale_of(extra, mine, top_count):
+    ids = extra[:, :top_count].astype(jnp.float32)
+    values = extra[:, top_count : 4 * top_count].astype(jnp.float32)
+    weights = values[:, :top_count] + values[:, top_count : 2 * top_count] + values[:, 2 * top_count :]
+    return jnp.sum(jnp.where(ids == mine.astype(jnp.float32), weights, 0.0), axis=1, keepdims=True)
+
+
+def serve_rows(rows, mine, top_count, w_gate, w_up, w_down):
+    width = w_gate.shape[0]
+    arrived = rows[:, :width]
+    gate_sum = jnp.dot(arrived, w_gate, preferred_element_type=jnp.float32)
+    up_sum = jnp.dot(arrived, w_up, preferred_element_type=jnp.float32)
+    hidden = (jax.nn.silu(gate_sum) * up_sum).astype(jnp.bfloat16)
+    partial_out = jnp.dot(hidden, w_down, preferred_element_type=jnp.float32)
+    return (partial_out * scale_of(rows[:, width:], mine, top_count)).astype(jnp.bfloat16)
+
+
+def total(*terms):
+    return sum(term.astype(jnp.float32) for term in terms).astype(jnp.bfloat16)
+
+
 def dense(tokens, expert_ids, route_weight, slot_of, swap_flag, w_gate, w_up, w_down):
+    tok_rows, width = tokens.shape
+    top_count = expert_ids.shape[1]
+    line_count = lax.axis_size("expert") // 2
     mine = served_expert(slot_of, swap_flag)
-    all_ids = lax.all_gather(expert_ids, AXES, tiled=True)
-    all_weights = lax.all_gather(route_weight, AXES, tiled=True)
-    scale = jnp.sum(jnp.where(all_ids == mine, all_weights, 0.0), axis=1)
-    arrived = lax.all_gather(tokens, AXES, tiled=True)
-    gate_sum = jnp.dot(arrived, w_gate[0], preferred_element_type=jnp.float32)
-    up_sum = jnp.dot(arrived, w_up[0], preferred_element_type=jnp.float32)
-    hidden = (jax.nn.silu(gate_sum) * up_sum).astype(jnp.bfloat16)
-    partial_out = jnp.dot(hidden, w_down[0], preferred_element_type=jnp.float32)
-    partial_out = (partial_out * scale[:, None]).astype(jnp.bfloat16)
-    return lax.psum_scatter(partial_out, AXES, scatter_dimension=0, tiled=True)
+    own = packed(tokens, expert_ids, route_weight)
+    line = jnp.concatenate([own] + [permute(own, along_line(k)) for k in range(1, line_count)])
+    first = permute(line, over_first)
+    sib_line = permute(line, to_sibling)
+    early = jnp.concatenate([line, first])
+    late = permute(early, over_second)
+    sib_first = permute(first, to_sibling)
+    sib_late = permute(late, to_sibling)
+
+    args = (mine, top_count, w_gate[0], w_up[0], w_down[0])
+    half = early.shape[0]
+    out_early = serve_rows(jnp.concatenate([early, sib_line, sib_first]), *args)
+    out_late = serve_rows(jnp.concatenate([late, sib_late]), *args)
+    got_early = permute(out_early[half:], to_sibling)
+    got_late = permute(out_late[half:], to_sibling)
+    late_sum = total(out_late[:half], got_late)
+    got = permute(late_sum, over_second)
+    early_sum = total(out_early[:half], got_early, got)
+    half = line.shape[0]
+    got = permute(early_sum[half:], over_first)
+    line_sum = total(early_sum[:half], got)
+    terms = [line_sum[:tok_rows]]
+    for k in range(1, line_count):
+        terms.append(permute(line_sum[k * tok_rows : (k + 1) * tok_rows], along_line(-k)))
+    return total(*terms)
 
 
 def on_device(tokens, expert_ids, *rest):

time: 286 us -> 156 us (0.55)
  blocking collectives: 136 us -> 0 us
  waiting for transfers between devices: 114 us -> 80.9 us
  starting transfers between devices: 0.04 us -> 23.4 us
  local copies, waits for them, and re-layouts: 0.08 us -> 13.6 us
  between operations: 14.1 us -> 1.49 us
  other arithmetic: 2.01 us -> 10.9 us
  matrix products: 19.9 us -> 24.8 us
    all_gather x2 -> x0, blocking collectives: 136 us -> none  [the longest x1 71.4 us: dense(): all_ids = lax.all_gather(expert_ids, AXES, tiled=True)]
    reduce_scatter x1 -> x0, waiting for transfers between devices: 113 us -> none  [dense(): return lax.psum_scatter(partial_out, AXES, scatter_dimension=0, tiled=True)]
    ppermute x0 -> x15, waiting for transfers between devices: none -> 80.9 us  [permute(): return lax.ppermute(value, AXES, pairs)]
    ppermute x0 -> x15, starting transfers between devices: none -> 23.4 us  [permute(): return lax.ppermute(value, AXES, pairs)]
    unnamed x0 -> x19, local copies, waits for them, and re-layouts: none -> 9.59 us
    convert_element_type x0 -> x8, other arithmetic: none -> 6.17 us  [the longest x4 3.72 us: total(): sum((term.astype(jnp.float32) for term in terms)).astype(jnp.bfloat16)]
    dot_general x2 -> x4, matrix products: 19.9 us -> 24.8 us  [the longest x2 16.3 us: serve_rows(): partial_out = jnp.dot(hidden, w_down, preferred_element_type=jnp.float32)]
  transfers between devices with their start and end apart: 2 -> 15, of which waited for: 1 -> 8; matrix products, arithmetic and copies ran while one was open for 1% -> 16% of each run, Pallas kernels for 0% -> 0%
where the time goes in v2:
time: 156 us; the launch traced here: 155 us
  waiting for transfers between devices  80.9 us (52%)
  matrix products  24.8 us (16%)
  starting transfers between devices  23.4 us (15%)
  local copies, waits for them, and re-layouts  13.6 us (9%)
  other arithmetic  10.9 us (7%)
    ppermute x15, waiting for transfers between devices, permute(): return lax.ppermute(value, AXES, pairs)  80.9 us
    ppermute x15, starting transfers between devices, permute(): return lax.ppermute(value, AXES, pairs)  23.4 us
    dot_general x2, matrix products, serve_rows(): partial_out = jnp.dot(hidden, w_down, preferred_element_type=jnp.float32)  16.3 us
    unnamed x19, local copies, waits for them, and re-layouts  9.59 us
    dot_general x2, matrix products, serve_rows(): up_sum = jnp.dot(arrived, w_up, preferred_element_type=jnp.float32)  8.49 us
    convert_element_type x4, other arithmetic, total(): sum((term.astype(jnp.float32) for term in terms)).astype(jnp.bfloat16)  3.72 us
  transfers between devices with their start and end apart: 15, of which 8 were waited for; matrix products, arithmetic and copies ran while one was open for 16% of the time, Pallas kernels for 0%

profile of v2, /device:TPU:0, one launch (start us, length us, event | category | flops | bytes accessed | tf_op | source)
XLA Modules:
  0.0 155.1 jit_solution(10913452661128790999)
XLA Ops:
  0.0 0.7 convert_element_type.87
  0.7 0.7 reduce-precision_convert_fusion.1
  1.4 0.1 copy.10
  1.5 0.0 copy-start.4
  1.5 1.6 %constant_dynamic-update-slice_fusion.6 = (bf16[384,4224]{1,0:T(8,128)(2,1)S(1)}, bf16[192,4224]{1,0:T(8,128)(2,1)}, bf16[24,4224]{1,0:T(8,128)(2,1)S(1)}) fusion(bf16[24,128]{1,0:T(8,128)(2,1)S(1)} %pad.4.clone, bf16[24,4096]{1,0:T(8,128)(2,1)} %param.8), kind=kLoop, calls=%fused_computation.44 | loop fusion | flops 405502 | bytes 811008
  3.1 4.0 %collective-permute-start.1 = (bf16[24,4224]{1,0:T(8,128)(2,1)S(1)}, bf16[24,4224]{1,0:T(8,128)(2,1)S(1)}, u32[]{:S(2)}, u32[]{:S(2)}) collective-permute-start(bf16[24,4224]{1,0:T(8,128)(2,1)S(1)} %get-tuple-element.18), channel_id=1, source_target_pairs={{0,4},{1,5},{2,6},{3,7},{4,0},{5,1},{6,2},{7,3},{8,12},{9,13},{10,... | collective-permute-start | bytes 608264 | tf_op jit(solution)/shard_map/ppermute | solution.py:81
  7.2 1.6 %collective-permute-start = (bf16[24,4224]{1,0:T(8,128)(2,1)S(1)}, bf16[24,4224]{1,0:T(8,128)(2,1)S(1)}, u32[]{:S(2)}, u32[]{:S(2)}) collective-permute-start(bf16[24,4224]{1,0:T(8,128)(2,1)S(1)} %get-tuple-element.18), channel_id=1, source_target_pairs={{0,2},{1,3},{2,4},{3,5},{4,6},{5,7},{6,0},{7,1},{8,10},{9,11},{10,... | collective-permute-start | bytes 608264 | tf_op jit(solution)/shard_map/ppermute | solution.py:81
  8.8 2.2 %collective-permute-start.2 = (bf16[24,4224]{1,0:T(8,128)(2,1)S(1)}, bf16[24,4224]{1,0:T(8,128)(2,1)S(1)}, u32[]{:S(2)}, u32[]{:S(2)}) collective-permute-start(bf16[24,4224]{1,0:T(8,128)(2,1)S(1)} %get-tuple-element.18), channel_id=1, source_target_pairs={{0,6},{1,7},{2,0},{3,1},{4,2},{5,3},{6,4},{7,5},{8,14},{9,15},{10,... | collective-permute-start | bytes 608264 | tf_op jit(solution)/shard_map/ppermute | solution.py:81
  11.0 10.8 %collective-permute-done.1 = bf16[24,4224]{1,0:T(8,128)(2,1)S(1)} collective-permute-done((bf16[24,4224]{1,0:T(8,128)(2,1)S(1)}, bf16[24,4224]{1,0:T(8,128)(2,1)S(1)}, u32[]{:S(2)}, u32[]{:S(2)}) %collective-permute-start.1) | collective-permute-done | bytes 202784 | tf_op jit(solution)/shard_map/ppermute | solution.py:81
  21.8 0.0 collective-permute-done
  21.8 0.7 collective-permute-done.2
  22.5 1.0 pad_maximum_fusion
  23.5 1.6 %collective-permute-start.3 = (bf16[96,4224]{1,0:T(8,128)(2,1)S(1)}, bf16[96,4224]{1,0:T(8,128)(2,1)S(1)}, u32[]{:S(2)}, u32[]{:S(2)}) collective-permute-start(bf16[96,4224]{1,0:T(8,128)(2,1)S(1)} %pad_maximum_fusion), channel_id=1, source_target_pairs={{0,1},{1,0},{2,3},{3,2},{4,5},{5,4},{6,7},{7,6},{8,24},{9,25},{10,... | collective-permute-start | bytes 2433032 | tf_op jit(solution)/shard_map/ppermute | solution.py:81
  25.1 0.7 constant_dynamic-update-slice_fusion.5
  25.8 0.7 constant_dynamic-update-slice_fusion.4
  26.6 0.7 constant_dynamic-update-slice_fusion.3
  27.3 8.5 %collective-permute-done.3 = bf16[96,4224]{1,0:T(8,128)(2,1)S(1)} collective-permute-done((bf16[96,4224]{1,0:T(8,128)(2,1)S(1)}, bf16[96,4224]{1,0:T(8,128)(2,1)S(1)}, u32[]{:S(2)}, u32[]{:S(2)}) %collective-permute-start.3) | collective-permute-done | bytes 811040 | tf_op jit(solution)/shard_map/ppermute | solution.py:81
  35.8 1.0 constant_dynamic-update-slice_fusion.2
  36.8 1.5 collective-permute-start.7
  38.4 0.0 collective-permute-start.4
  38.4 0.5 collective-permute-start.5
  39.5 0.6 fusion.38
  40.8 17.1 %collective-permute-done.7 = bf16[192,4224]{1,0:T(8,128)(2,1)S(1)} collective-permute-done((bf16[192,4224]{1,0:T(8,128)(2,1)}, bf16[192,4224]{1,0:T(8,128)(2,1)S(1)}, u32[]{:S(2)}, u32[]{:S(2)}) %collective-permute-start.7) | collective-permute-done | bytes 1622048 | tf_op jit(solution)/shard_map/ppermute | solution.py:81
  58.0 0.0 collective-permute-start.8
  58.0 0.0 collective-permute-done.4
  58.0 2.1 %constant_dynamic-update-slice_fusion.1 = bf16[384,4224]{1,0:T(8,128)(2,1)} fusion(bf16[384,4224]{1,0:T(8,128)(2,1)} %copy-done.3, bf16[96,4224]{1,0:T(8,128)(2,1)} %collective-permute-done.4), kind=kLoop, calls=%fused_computation.39 | loop fusion | bytes 1622016
  60.1 0.0 collective-permute-done.5
  60.1 2.1 %constant_dynamic-update-slice_fusion = bf16[384,4224]{1,0:T(8,128)(2,1)} fusion(bf16[384,4224]{1,0:T(8,128)(2,1)} %constant_dynamic-update-slice_fusion.1, bf16[96,4224]{1,0:T(8,128)(2,1)} %collective-permute-done.5), kind=kLoop, calls=%fused_computation.38 | loop fusion | bytes 1622016 | tf_op jit(solution)/shard_map/concatenate | solution.py:152
  62.2 1.0 slice_convert_fusion.1
  63.2 1.2 fusion.35
  64.3 0.1 constant_dynamic-update-slice_fusion.13
  64.5 0.0 collective-permute-done.8
  64.5 0.2 constant_dynamic-update-slice_fusion.12
  64.7 0.1 slice_convert_fusion
  64.8 0.3 fusion.33
  65.1 1.3 copy-done.2
  66.4 1.3 copy-done.5
  67.7 2.7 %fusion.2 = f32[384,512]{1,0:T(8,128)} fusion(bf16[1,4096,512]{2,1,0:T(8,128)(2,1)S(1)} %copy-done.5, bf16[384,4224]{1,0:T(8,128)(2,1)S(1)} %constant_dynamic-update-slice_fusion.12), kind=kOutput, calls=%fused_computation.4 | convolution fusion | flops 1610612736 | bytes 8126464 | tf_op jit(solution)/shard_map/dot_general | solution.py:126
  70.4 8.2 %multiply_convert_fusion = bf16[384,4096]{1,0:T(8,128)(2,1)S(1)} fusion(bf16[1,512,4096]{2,1,0:T(8,128)(2,1)} %param.15, f32[384]{0:T(512)S(1)} %fusion.33, f32[384,512]{1,0:T(8,128)} %fusion.2, bf16[1,4096,512]{2,1,0:T(8,128)(2,1)} %param.13, bf16[384,4224]{1,0:T(8,128)(2,1)} %copy-done.2), kind=kOutput, calls=%fused_computation | convolution fusion | flops 3225550848 | bytes 15468032 | tf_op jit(solution)/shard_map/dot_general | solution.py:128
  78.6 1.5 slice.109
  80.1 0.5 collective-permute-start.9
  80.6 0.3 copy-done
  80.9 5.8 %fusion.4 = f32[384,512]{1,0:T(8,128)} fusion(bf16[1,4096,512]{2,1,0:T(8,128)(2,1)} %param.14, bf16[384,4224]{1,0:T(8,128)(2,1)} %constant_dynamic-update-slice_fusion), kind=kOutput, calls=%fused_computation.6 | convolution fusion | flops 1610612736 | bytes 8126464 | tf_op jit(solution)/shard_map/dot_general | solution.py:126
  86.7 8.2 %multiply_convert_fusion.1 = bf16[384,4096]{1,0:T(8,128)(2,1)S(1)} fusion(bf16[1,512,4096]{2,1,0:T(8,128)(2,1)} %param.15, f32[384]{0:T(512)S(1)} %fusion.35, f32[384,512]{1,0:T(8,128)} %fusion.4, bf16[1,4096,512]{2,1,0:T(8,128)(2,1)} %param.13, bf16[384,4224]{1,0:T(8,128)(2,1)} %constant_dynamic-update-slice_fusion), kind=kOutput, calls=%fused_computation.1 | convolution fusion | flops 3225550848 | bytes 15468032 | tf_op jit(solution)/shard_map/dot_general | solution.py:128
  94.9 0.1 slice.101
  95.0 0.6 collective-permute-start.6
  95.5 0.0 collective-permute-done.9
  95.6 1.2 copy-done.1
  96.7 2.0 %add_convert_fusion.1 = bf16[192,4096]{1,0:T(8,128)(2,1)S(1)} fusion(bf16[192,4096]{1,0:T(8,128)(2,1)} %collective-permute-done.9, bf16[384,4096]{1,0:T(8,128)(2,1)S(1)} %copy-done.1), kind=kLoop, calls=%fused_computation.13 | loop fusion | flops 3145728 | bytes 4718592 | tf_op jit(solution)/shard_map/convert_element_type | solution.py:133
  98.7 1.6 %collective-permute-start.10 = (bf16[192,4096]{1,0:T(8,128)(2,1)S(1)}, bf16[192,4096]{1,0:T(8,128)(2,1)S(1)}, u32[]{:S(2)}, u32[]{:S(2)}) collective-permute-start(bf16[192,4096]{1,0:T(8,128)(2,1)S(1)} %add_convert_fusion.1), channel_id=1, source_target_pairs={{0,16},{1,17},{2,18},{3,19},{4,20},{5,21},{6,22},{7,23},{8,9},{9,8... | collective-permute-start | bytes 4718600 | tf_op jit(solution)/shard_map/ppermute | solution.py:81
  100.3 0.0 collective-permute-done.6
  100.3 18.9 %collective-permute-done.10 = bf16[192,4096]{1,0:T(8,128)(2,1)S(1)} collective-permute-done((bf16[192,4096]{1,0:T(8,128)(2,1)S(1)}, bf16[192,4096]{1,0:T(8,128)(2,1)S(1)}, u32[]{:S(2)}, u32[]{:S(2)}) %collective-permute-start.10) | collective-permute-done | bytes 1572896 | tf_op jit(solution)/shard_map/ppermute | solution.py:81
  119.2 0.8 add_convert_fusion
  120.0 0.1 slice.111
  120.0 1.6 %collective-permute-start.11 = (bf16[96,4096]{1,0:T(8,128)(2,1)S(1)}, bf16[96,4096]{1,0:T(8,128)(2,1)S(1)}, u32[]{:S(2)}, u32[]{:S(2)}) collective-permute-start(bf16[96,4096]{1,0:T(8,128)(2,1)S(1)} %slice.111), channel_id=1, source_target_pairs={{0,1},{1,0},{2,3},{3,2},{4,5},{5,4},{6,7},{7,6},{8,24},{9,25},{10,... | collective-permute-start | bytes 2359304 | tf_op jit(solution)/shard_map/ppermute | solution.py:81
  121.7 10.4 %collective-permute-done.11 = bf16[96,4096]{1,0:T(8,128)(2,1)S(1)} collective-permute-done((bf16[96,4096]{1,0:T(8,128)(2,1)S(1)}, bf16[96,4096]{1,0:T(8,128)(2,1)S(1)}, u32[]{:S(2)}, u32[]{:S(2)}) %collective-permute-start.11) | collective-permute-done | bytes 786464 | tf_op jit(solution)/shard_map/ppermute | solution.py:81
  132.1 0.2 add_convert_fusion.2
  132.4 2.1 %collective-permute-start.12 = (bf16[24,4096]{1,0:T(8,128)(2,1)S(1)}, bf16[24,4096]{1,0:T(8,128)(2,1)S(1)}, u32[]{:S(2)}, u32[]{:S(2)}) collective-permute-start(bf16[24,4096]{1,0:T(8,128)(2,1)S(1)} %get-tuple-element.7), channel_id=1, source_target_pairs={{0,6},{1,7},{2,0},{3,1},{4,2},{5,3},{6,4},{7,5},{8,14},{9,15},{10,... | collective-permute-start | bytes 589832 | tf_op jit(solution)/shard_map/ppermute | solution.py:81
  134.5 1.5 collective-permute-start.14
  136.0 3.9 %collective-permute-start.13 = (bf16[24,4096]{1,0:T(8,128)(2,1)S(1)}, bf16[24,4096]{1,0:T(8,128)(2,1)S(1)}, u32[]{:S(2)}, u32[]{:S(2)}) collective-permute-start(bf16[24,4096]{1,0:T(8,128)(2,1)S(1)} %get-tuple-element.9), channel_id=1, source_target_pairs={{0,4},{1,5},{2,6},{3,7},{4,0},{5,1},{6,2},{7,3},{8,12},{9,13},{10,... | collective-permute-start | bytes 589832 | tf_op jit(solution)/shard_map/ppermute | solution.py:81
  139.8 0.0 collective-permute-done.12
  139.9 9.3 %collective-permute-done.14 = bf16[24,4096]{1,0:T(8,128)(2,1)S(1)} collective-permute-done((bf16[24,4096]{1,0:T(8,128)(2,1)S(1)}, bf16[24,4096]{1,0:T(8,128)(2,1)S(1)}, u32[]{:S(2)}, u32[]{:S(2)}) %collective-permute-start.14) | collective-permute-done | bytes 196640 | tf_op jit(solution)/shard_map/ppermute | solution.py:81
  149.2 5.1 %collective-permute-done.13 = bf16[24,4096]{1,0:T(8,128)(2,1)S(1)} collective-permute-done((bf16[24,4096]{1,0:T(8,128)(2,1)S(1)}, bf16[24,4096]{1,0:T(8,128)(2,1)S(1)}, u32[]{:S(2)}, u32[]{:S(2)}) %collective-permute-start.13) | collective-permute-done | bytes 196640 | tf_op jit(solution)/shard_map/ppermute | solution.py:81
  154.3 0.8 add_convert_fusion.3
  (10 shorter events, 0.1 us)
Async XLA Ops:
  1.5 38.0 %copy-start.4 = (s32[16,2]{0,1:T(2,128)S(1)}, s32[16,2]{0,1:T(2,128)}, u32[]{:S(2)}) copy-start(s32[16,2]{0,1:T(2,128)} %param.11) | copy-start | bytes 388
  3.1 18.6 %collective-permute-start.1 = (bf16[24,4224]{1,0:T(8,128)(2,1)S(1)}, bf16[24,4224]{1,0:T(8,128)(2,1)S(1)}, u32[]{:S(2)}, u32[]{:S(2)}) collective-permute-start(bf16[24,4224]{1,0:T(8,128)(2,1)S(1)} %get-tuple-element.18), channel_id=1, source_target_pairs={{0,4},{1,5},{2,6},{3,7},{4,0},{5,1},{6,2},{7,3},{8,12},{9,13},{10,... | collective-permute-start | bytes 608264 | tf_op jit(solution)/shard_map/ppermute | solution.py:81
  7.2 14.6 %collective-permute-start = (bf16[24,4224]{1,0:T(8,128)(2,1)S(1)}, bf16[24,4224]{1,0:T(8,128)(2,1)S(1)}, u32[]{:S(2)}, u32[]{:S(2)}) collective-permute-start(bf16[24,4224]{1,0:T(8,128)(2,1)S(1)} %get-tuple-element.18), channel_id=1, source_target_pairs={{0,2},{1,3},{2,4},{3,5},{4,6},{5,7},{6,0},{7,1},{8,10},{9,11},{10,... | collective-permute-start | bytes 608264 | tf_op jit(solution)/shard_map/ppermute | solution.py:81
  8.8 13.7 %collective-permute-start.2 = (bf16[24,4224]{1,0:T(8,128)(2,1)S(1)}, bf16[24,4224]{1,0:T(8,128)(2,1)S(1)}, u32[]{:S(2)}, u32[]{:S(2)}) collective-permute-start(bf16[24,4224]{1,0:T(8,128)(2,1)S(1)} %get-tuple-element.18), channel_id=1, source_target_pairs={{0,6},{1,7},{2,0},{3,1},{4,2},{5,3},{6,4},{7,5},{8,14},{9,15},{10,... | collective-permute-start | bytes 608264 | tf_op jit(solution)/shard_map/ppermute | solution.py:81
  23.5 12.3 %collective-permute-start.3 = (bf16[96,4224]{1,0:T(8,128)(2,1)S(1)}, bf16[96,4224]{1,0:T(8,128)(2,1)S(1)}, u32[]{:S(2)}, u32[]{:S(2)}) collective-permute-start(bf16[96,4224]{1,0:T(8,128)(2,1)S(1)} %pad_maximum_fusion), channel_id=1, source_target_pairs={{0,1},{1,0},{2,3},{3,2},{4,5},{5,4},{6,7},{7,6},{8,24},{9,25},{10,... | collective-permute-start | bytes 2433032 | tf_op jit(solution)/shard_map/ppermute | solution.py:81
  36.8 2.1 %copy-start.3 = (bf16[384,4224]{1,0:T(8,128)(2,1)}, bf16[384,4224]{1,0:T(8,128)(2,1)S(1)}, u32[]{:S(2)}) copy-start(bf16[384,4224]{1,0:T(8,128)(2,1)S(1)} %get-tuple-element.5) | copy-start | bytes 9732100
  36.8 21.2 %collective-permute-start.7 = (bf16[192,4224]{1,0:T(8,128)(2,1)}, bf16[192,4224]{1,0:T(8,128)(2,1)S(1)}, u32[]{:S(2)}, u32[]{:S(2)}) collective-permute-start(bf16[192,4224]{1,0:T(8,128)(2,1)} %get-tuple-element.6), channel_id=1, source_target_pairs={{0,16},{1,17},{2,18},{3,19},{4,20},{5,21},{6,22},{7,23},{8,9},{9,8... | collective-permute-start | bytes 4866056 | tf_op jit(solution)/shard_map/ppermute | solution.py:81
  38.4 19.6 %collective-permute-start.4 = (bf16[96,4224]{1,0:T(8,128)(2,1)S(1)}, bf16[96,4224]{1,0:T(8,128)(2,1)}, u32[]{:S(2)}, u32[]{:S(2)}) collective-permute-start(bf16[96,4224]{1,0:T(8,128)(2,1)S(1)} %pad_maximum_fusion), channel_id=1, source_target_pairs={{0,8},{1,9},{2,10},{3,11},{4,12},{5,13},{6,14},{7,15},{8,0},{9,1},... | collective-permute-start | bytes 2433032 | tf_op jit(solution)/shard_map/ppermute | solution.py:81
  38.4 21.7 %collective-permute-start.5 = (bf16[96,4224]{1,0:T(8,128)(2,1)S(1)}, bf16[96,4224]{1,0:T(8,128)(2,1)}, u32[]{:S(2)}, u32[]{:S(2)}) collective-permute-start(bf16[96,4224]{1,0:T(8,128)(2,1)S(1)} %collective-permute-done.3), channel_id=1, source_target_pairs={{0,8},{1,9},{2,10},{3,11},{4,12},{5,13},{6,14},{7,15},{8,0},{9,1},... | collective-permute-start | bytes 2433032 | tf_op jit(solution)/shard_map/ppermute | solution.py:81
  58.0 6.5 %collective-permute-start.8 = (bf16[192,4224]{1,0:T(8,128)(2,1)S(1)}, bf16[192,4224]{1,0:T(8,128)(2,1)S(1)}, u32[]{:S(2)}, u32[]{:S(2)}) collective-permute-start(bf16[192,4224]{1,0:T(8,128)(2,1)S(1)} %collective-permute-done.7), channel_id=1, source_target_pairs={{0,8},{1,9},{2,10},{3,11},{4,12},{5,13},{6,14},{7,15},{8,0},{9,1},... | collective-permute-start | bytes 4866056 | tf_op jit(solution)/shard_map/ppermute | solution.py:81
  64.3 3.4 %copy-start.5 = (bf16[1,4096,512]{2,1,0:T(8,128)(2,1)S(1)}, bf16[1,4096,512]{2,1,0:T(8,128)(2,1)}, u32[]{:S(2)}) copy-start(bf16[1,4096,512]{2,1,0:T(8,128)(2,1)} %param.14) | copy-start | bytes 12582916
  64.7 1.7 %copy-start.2 = (bf16[384,4224]{1,0:T(8,128)(2,1)}, bf16[384,4224]{1,0:T(8,128)(2,1)S(1)}, u32[]{:S(2)}) copy-start(bf16[384,4224]{1,0:T(8,128)(2,1)S(1)} %constant_dynamic-update-slice_fusion.12) | copy-start | bytes 9732100
  78.6 2.3 %copy-start = (bf16[384,4096]{1,0:T(8,128)(2,1)}, bf16[384,4096]{1,0:T(8,128)(2,1)S(1)}, u32[]{:S(2)}) copy-start(bf16[384,4096]{1,0:T(8,128)(2,1)S(1)} %multiply_convert_fusion) | copy-start | bytes 9437188
  80.1 15.5 %collective-permute-start.9 = (bf16[192,4096]{1,0:T(8,128)(2,1)}, bf16[192,4096]{1,0:T(8,128)(2,1)}, u32[]{:S(2)}, u32[]{:S(2)}) collective-permute-start(bf16[192,4096]{1,0:T(8,128)(2,1)} %slice.109), channel_id=1, source_target_pairs={{0,8},{1,9},{2,10},{3,11},{4,12},{5,13},{6,14},{7,15},{8,0},{9,1},... | collective-permute-start | bytes 4718600 | tf_op jit(solution)/shard_map/ppermute | solution.py:81
  94.9 1.9 %copy-start.1 = (bf16[384,4096]{1,0:T(8,128)(2,1)S(1)}, bf16[384,4096]{1,0:T(8,128)(2,1)}, u32[]{:S(2)}) copy-start(bf16[384,4096]{1,0:T(8,128)(2,1)} %copy-done) | copy-start | bytes 9437188
  95.0 5.4 %collective-permute-start.6 = (bf16[192,4096]{1,0:T(8,128)(2,1)S(1)}, bf16[192,4096]{1,0:T(8,128)(2,1)S(1)}, u32[]{:S(2)}, u32[]{:S(2)}) collective-permute-start(bf16[192,4096]{1,0:T(8,128)(2,1)S(1)} %slice.101), channel_id=1, source_target_pairs={{0,8},{1,9},{2,10},{3,11},{4,12},{5,13},{6,14},{7,15},{8,0},{9,1},... | collective-permute-start | bytes 4718600 | tf_op jit(solution)/shard_map/ppermute | solution.py:81
  98.7 20.5 %collective-permute-start.10 = (bf16[192,4096]{1,0:T(8,128)(2,1)S(1)}, bf16[192,4096]{1,0:T(8,128)(2,1)S(1)}, u32[]{:S(2)}, u32[]{:S(2)}) collective-permute-start(bf16[192,4096]{1,0:T(8,128)(2,1)S(1)} %add_convert_fusion.1), channel_id=1, source_target_pairs={{0,16},{1,17},{2,18},{3,19},{4,20},{5,21},{6,22},{7,23},{8,9},{9,8... | collective-permute-start | bytes 4718600 | tf_op jit(solution)/shard_map/ppermute | solution.py:81
  120.0 12.1 %collective-permute-start.11 = (bf16[96,4096]{1,0:T(8,128)(2,1)S(1)}, bf16[96,4096]{1,0:T(8,128)(2,1)S(1)}, u32[]{:S(2)}, u32[]{:S(2)}) collective-permute-start(bf16[96,4096]{1,0:T(8,128)(2,1)S(1)} %slice.111), channel_id=1, source_target_pairs={{0,1},{1,0},{2,3},{3,2},{4,5},{5,4},{6,7},{7,6},{8,24},{9,25},{10,... | collective-permute-start | bytes 2359304 | tf_op jit(solution)/shard_map/ppermute | solution.py:81
  132.4 7.5 %collective-permute-start.12 = (bf16[24,4096]{1,0:T(8,128)(2,1)S(1)}, bf16[24,4096]{1,0:T(8,128)(2,1)S(1)}, u32[]{:S(2)}, u32[]{:S(2)}) collective-permute-start(bf16[24,4096]{1,0:T(8,128)(2,1)S(1)} %get-tuple-element.7), channel_id=1, source_target_pairs={{0,6},{1,7},{2,0},{3,1},{4,2},{5,3},{6,4},{7,5},{8,14},{9,15},{10,... | collective-permute-start | bytes 589832 | tf_op jit(solution)/shard_map/ppermute | solution.py:81
  134.5 14.7 %collective-permute-start.14 = (bf16[24,4096]{1,0:T(8,128)(2,1)S(1)}, bf16[24,4096]{1,0:T(8,128)(2,1)S(1)}, u32[]{:S(2)}, u32[]{:S(2)}) collective-permute-start(bf16[24,4096]{1,0:T(8,128)(2,1)S(1)} %get-tuple-element.8), channel_id=1, source_target_pairs={{0,2},{1,3},{2,4},{3,5},{4,6},{5,7},{6,0},{7,1},{8,10},{9,11},{10,... | collective-permute-start | bytes 589832 | tf_op jit(solution)/shard_map/ppermute | solution.py:81
  136.0 18.3 %collective-permute-start.13 = (bf16[24,4096]{1,0:T(8,128)(2,1)S(1)}, bf16[24,4096]{1,0:T(8,128)(2,1)S(1)}, u32[]{:S(2)}, u32[]{:S(2)}) collective-permute-start(bf16[24,4096]{1,0:T(8,128)(2,1)S(1)} %get-tuple-element.9), channel_id=1, source_target_pairs={{0,4},{1,5},{2,6},{3,7},{4,0},{5,1},{6,2},{7,3},{8,12},{9,13},{10,... | collective-permute-start | bytes 589832 | tf_op jit(solution)/shard_map/ppermute | solution.py:81

commit v3 on v2

--- a/solution.py
+++ b/solution.py
@@ -71,16 +71,6 @@
     return jnp.sum(jnp.where(slot_of == serving, numbers, 0))
 
 
-def permute(value, move):
-    ex_count = lax.axis_size("expert")
-    pairs = []
-    for source in range(lax.axis_size("dp") * ex_count):
-        d, e = divmod(source, ex_count)
-        d, e = move(d, e)
-        pairs.append((source, d * ex_count + e))
-    return lax.ppermute(value, AXES, pairs)
-
-
 def to_sibling(d, e):
     return d ^ 1, e
 
@@ -129,40 +119,32 @@
     return (partial_out * scale_of(rows[:, width:], mine, top_count)).astype(jnp.bfloat16)
 
 
-def total(*terms):
-    return sum(term.astype(jnp.float32) for term in terms).astype(jnp.bfloat16)
+def groups_of(*moves):
+    ex_count = lax.axis_size("expert")
+    found = set()
+    for source in range(lax.axis_size("dp") * ex_count):
+        d, e = divmod(source, ex_count)
+        found.add(tuple(sorted({source} | {a * ex_count + b for a, b in (move(d, e) for move in moves)})))
+    return [list(group) for group in sorted(found)]
 
 
 def dense(tokens, expert_ids, route_weight, slot_of, swap_flag, w_gate, w_up, w_down):
-    tok_rows, width = tokens.shape
     top_count = expert_ids.shape[1]
     line_count = lax.axis_size("expert") // 2
     mine = served_expert(slot_of, swap_flag)
-    own = packed(tokens, expert_ids, route_weight)
-    line = jnp.concatenate([own] + [permute(own, along_line(k)) for k in range(1, line_count)])
-    first = permute(line, over_first)
-    sib_line = permute(line, to_sibling)
-    early = jnp.concatenate([line, first])
-    late = permute(early, over_second)
-    sib_first = permute(first, to_sibling)
-    sib_late = permute(late, to_sibling)
-
-    args = (mine, top_count, w_gate[0], w_up[0], w_down[0])
-    half = early.shape[0]
-    out_early = serve_rows(jnp.concatenate([early, sib_line, sib_first]), *args)
-    out_late = serve_rows(jnp.concatenate([late, sib_late]), *args)
-    got_early = permute(out_early[half:], to_sibling)
-    got_late = permute(out_late[half:], to_sibling)
-    late_sum = total(out_late[:half], got_late)
-    got = permute(late_sum, over_second)
-    early_sum = total(out_early[:half], got_early, got)
-    half = line.shape[0]
-    got = permute(early_sum[half:], over_first)
-    line_sum = total(early_sum[:half], got)
-    terms = [line_sum[:tok_rows]]
-    for k in range(1, line_count):
-        terms.append(permute(line_sum[k * tok_rows : (k + 1) * tok_rows], along_line(-k)))
-    return total(*terms)
+    rows = packed(tokens, expert_ids, route_weight)
+    stages = [
+        groups_of(*[along_line(k) for k in range(1, line_count)]),
+        groups_of(over_first),
+        groups_of(over_second),
+        groups_of(to_sibling),
+    ]
+    for groups in stages:
+        rows = lax.all_gather(rows, AXES, axis_index_groups=groups, tiled=True)
+    out = serve_rows(rows, mine, top_count, w_gate[0], w_up[0], w_down[0])
+    for groups in stages[::-1]:
+        out = lax.psum_scatter(out, AXES, scatter_dimension=0, axis_index_groups=groups, tiled=True)
+    return out
 
 
 def on_device(tokens, expert_ids, *rest):

time: 156 us -> 221 us (1.42)
  waiting for transfers between devices: 80.9 us -> 158 us
  starting transfers between devices: 23.4 us -> 0.24 us
  blocking collectives: 0 us -> 22 us
  local copies, waits for them, and re-layouts: 13.6 us -> 0.09 us
  between operations: 1.49 us -> 14.8 us
  other arithmetic: 10.9 us -> 5.36 us
  matrix products: 24.8 us -> 19.9 us
    reduce_scatter x0 -> x4, waiting for transfers between devices: none -> 91.8 us  [dense(): lax.psum_scatter(out, AXES, scatter_dimension=0, axis_index_groups=groups...]
    ppermute x15 -> x0, waiting for transfers between devices: 80.9 us -> none  [permute(): return lax.ppermute(value, AXES, pairs)]
    all_gather x0 -> x3, waiting for transfers between devices: none -> 66.4 us  [dense(): rows = lax.all_gather(rows, AXES, axis_index_groups=groups, tiled=True)]
    ppermute x15 -> x0, starting transfers between devices: 23.4 us -> none  [permute(): return lax.ppermute(value, AXES, pairs)]
    all_gather x0 -> x1, blocking collectives: none -> 22 us  [dense(): rows = lax.all_gather(rows, AXES, axis_index_groups=groups, tiled=True)]
    unnamed x19 -> x3, local copies, waits for them, and re-layouts: 9.59 us -> 0.09 us
    convert_element_type x4 -> x0, other arithmetic: 3.72 us -> none  [total(): sum((term.astype(jnp.float32) for term in terms)).astype(jnp.bfloat16)]
    dot_general x2 -> x1, matrix products: 16.3 us -> 13.1 us  [serve_rows(): partial_out = jnp.dot(hidden, w_down, preferred_element_type=jnp.float32)]
  transfers between devices with their start and end apart: 15 -> 7, of which waited for: 8 -> 7; matrix products, arithmetic and copies ran while one was open for 16% -> 0% of each run, Pallas kernels for 0% -> 0%
where the time goes in v3:
time: 221 us
  waiting for transfers between devices  158 us (71%)
  blocking collectives  22 us (10%)
  matrix products  19.9 us (9%)
  between operations  14.8 us (7%)
  other arithmetic  5.36 us (2%)
    reduce_scatter x4, waiting for transfers between devices, dense(): lax.psum_scatter(out, AXES, scatter_dimension=0, axis_index_groups=groups...  91.8 us
    all_gather x3, waiting for transfers between devices, dense(): rows = lax.all_gather(rows, AXES, axis_index_groups=groups, tiled=True)  66.4 us
    all_gather x1, blocking collectives, dense(): rows = lax.all_gather(rows, AXES, axis_index_groups=groups, tiled=True)  22 us
    dot_general x1, matrix products, serve_rows(): partial_out = jnp.dot(hidden, w_down, preferred_element_type=jnp.float32)  13.1 us
    dot_general x1, matrix products, serve_rows(): gate_sum = jnp.dot(arrived, w_gate, preferred_element_type=jnp.float32)  6.75 us
  transfers between devices with their start and end apart: 7, of which 7 were waited for; matrix products, arithmetic and copies ran while one was open for 0% of the time, Pallas kernels for 0%

profile of v3, /device:TPU:0, one launch (start us, length us, event | category | flops | bytes accessed | tf_op | source)
XLA Modules:
  0.0 220.7 jit_solution(9485077286433102303)
XLA Ops:
  6.5 0.0 copy-start
  6.5 0.0 all-gather.4.cloned.1.call-start
  6.5 0.7 convert_element_type.29
  7.2 0.7 reduce-precision_convert_fusion.1
  7.9 0.1 copy.10
  8.0 0.9 fusion.19
  9.0 22.0 %all_gather.12 = bf16[96,4224]{1,0:T(8,128)(2,1)} all-gather(bf16[24,4224]{1,0:T(8,128)(2,1)S(1)} %fusion.19), channel_id=1, replica_groups={{0,2,4,6},{1,3,5,7},{8,10,12,14},{9,11,13,15},{16,18,20,22},{17,19,21,2..., dimensions={0}, use_global_device_ids=true | all-gather | bytes 1013760 | tf_op jit(solution)/shard_map/all_gather | solution.py:143
  31.0 0.0 all-gather.4.cloned.1.call-update
  31.0 0.0 all-gather.6.cloned.1.call-start
  31.0 19.2 %all-gather.4.cloned.1.call-done = bf16[192,4224]{1,0:T(8,128)(2,1)} async-done(((bf16[96,4224]{1,0:T(8,128)(2,1)}), bf16[192,4224]{1,0:T(8,128)(2,1)}) %all-gather.4.cloned.1.call-update) | async-done | bytes 1622032 | tf_op jit(solution)/shard_map/all_gather | solution.py:143
  50.2 0.0 all-gather.6.cloned.1.call-update
  50.3 0.0 all-gather.8.cloned.1.call-start
  50.3 30.6 %all-gather.6.cloned.1.call-done = bf16[384,4224]{1,0:T(8,128)(2,1)} async-done(((bf16[192,4224]{1,0:T(8,128)(2,1)}), bf16[384,4224]{1,0:T(8,128)(2,1)}) %all-gather.6.cloned.1.call-update) | async-done | bytes 3244048 | tf_op jit(solution)/shard_map/all_gather | solution.py:143
  80.9 0.0 all-gather.8.cloned.1.call-update
  80.9 0.0 reduce-scatter.5.cloned.1.call-start
  81.6 0.0 copy-done
  81.6 0.6 fusion.22
  82.9 16.6 %all-gather.8.cloned.1.call-done = bf16[768,4224]{1,0:T(8,128)(2,1)} async-done(((bf16[384,4224]{1,0:T(8,128)(2,1)}), bf16[768,4224]{1,0:T(8,128)(2,1)}) %all-gather.8.cloned.1.call-update) | async-done | bytes 6488080 | tf_op jit(solution)/shard_map/all_gather | solution.py:143
  99.5 1.0 slice_convert_fusion
  100.6 6.7 %fusion.2 = f32[768,512]{1,0:T(8,128)S(1)} fusion(bf16[768,4224]{1,0:T(8,128)(2,1)} %all-gather.8.cloned.1.call-done, bf16[1,4096,512]{2,1,0:T(8,128)(2,1)} %param.13), kind=kOutput, calls=%fused_computation.3 | convolution fusion | flops 3221225472 | bytes 12058624 | tf_op jit(solution)/shard_map/dot_general | solution.py:115
  107.3 1.3 fusion.18
  108.7 13.1 %multiply_convert_fusion = bf16[768,4096]{1,0:T(8,128)(2,1)} fusion(f32[768]{0:T(1024)S(1)} %fusion.18, bf16[1,512,4096]{2,1,0:T(8,128)(2,1)} %param.15, f32[768,512]{1,0:T(8,128)S(1)} %fusion.2, bf16[1,4096,512]{2,1,0:T(8,128)(2,1)} %param.14, bf16[768,4224]{1,0:T(8,128)(2,1)} %all-gather.8.cloned.1.call-done), kind=kOutput, calls=%fused_computation | convolution fusion | flops 6451101696 | bytes 22547456 | tf_op jit(solution)/shard_map/dot_general | solution.py:118
  121.8 0.0 reduce-scatter.5.cloned.1.call-update
  121.8 0.0 reduce-scatter.7.cloned.1.call-start
  121.9 15.8 %reduce-scatter.5.cloned.1.call-done = bf16[384,4096]{1,0:T(8,128)(2,1)} async-done(((bf16[768,4096]{1,0:T(8,128)(2,1)}), bf16[384,4096]{1,0:T(8,128)(2,1)}) %reduce-scatter.5.cloned.1.call-update) | async-done | bytes 3145744 | tf_op jit(solution)/shard_map/reduce_scatter | solution.py:146
  137.6 0.0 reduce-scatter.7.cloned.1.call-update
  137.7 0.0 reduce-scatter.9.cloned.1.call-start
  137.7 30.2 %reduce-scatter.7.cloned.1.call-done = bf16[192,4096]{1,0:T(8,128)(2,1)} async-done(((bf16[384,4096]{1,0:T(8,128)(2,1)}), bf16[192,4096]{1,0:T(8,128)(2,1)}) %reduce-scatter.7.cloned.1.call-update) | async-done | bytes 1572880 | tf_op jit(solution)/shard_map/reduce_scatter | solution.py:146
  167.9 0.0 reduce-scatter.9.cloned.1.call-update
  167.9 0.0 reduce-scatter.11.cloned.1.call-start
  168.0 20.1 %reduce-scatter.9.cloned.1.call-done = bf16[96,4096]{1,0:T(8,128)(2,1)} async-done(((bf16[192,4096]{1,0:T(8,128)(2,1)}), bf16[96,4096]{1,0:T(8,128)(2,1)}) %reduce-scatter.9.cloned.1.call-update) | async-done | bytes 786448 | tf_op jit(solution)/shard_map/reduce_scatter | solution.py:146
  188.1 0.0 reduce-scatter.11.cloned.1.call-update
  188.1 25.7 %reduce-scatter.11.cloned.1.call-done = bf16[24,4096]{1,0:T(8,128)(2,1)} async-done(((bf16[96,4096]{1,0:T(8,128)(2,1)}), bf16[24,4096]{1,0:T(8,128)(2,1)}) %reduce-scatter.11.cloned.1.call-update) | async-done | bytes 196624 | tf_op jit(solution)/shard_map/reduce_scatter | solution.py:146
  (1 shorter events, 0.0 us)
Async XLA Ops:
  6.5 75.1 %copy-start = (s32[16,2]{0,1:T(2,128)S(1)}, s32[16,2]{0,1:T(2,128)}, u32[]{:S(2)}) copy-start(s32[16,2]{0,1:T(2,128)} %param.11) | copy-start | bytes 388
  6.5 43.7 %all-gather.4.cloned.1.call-start = ((), (), s32[]{:S(2)}) async-start(), calls=%async_computation.4 | async-start | bytes 2433024 | tf_op jit(solution)/shard_map/all_gather | solution.py:143
  31.0 49.9 %all-gather.6.cloned.1.call-start = ((), (), s32[]{:S(2)}) async-start(), calls=%async_computation.5 | async-start | bytes 4866048 | tf_op jit(solution)/shard_map/all_gather | solution.py:143
  50.3 49.3 %all-gather.8.cloned.1.call-start = ((), (), s32[]{:S(2)}) async-start(), calls=%async_computation.6 | async-start | bytes 9732096 | tf_op jit(solution)/shard_map/all_gather | solution.py:143
  80.9 56.7 %reduce-scatter.5.cloned.1.call-start = ((), (), s32[]{:S(2)}) async-start(), calls=%async_computation.7 | async-start | bytes 9437184 | tf_op jit(solution)/shard_map/reduce_scatter | solution.py:146
  121.8 46.1 %reduce-scatter.7.cloned.1.call-start = ((), (), s32[]{:S(2)}) async-start(), calls=%async_computation.8 | async-start | bytes 4718592 | tf_op jit(solution)/shard_map/reduce_scatter | solution.py:146
  137.7 50.5 %reduce-scatter.9.cloned.1.call-start = ((), (), s32[]{:S(2)}) async-start(), calls=%async_computation.9 | async-start | bytes 2359296 | tf_op jit(solution)/shard_map/reduce_scatter | solution.py:146
  167.9 45.9 %reduce-scatter.11.cloned.1.call-start = ((), (), s32[]{:S(2)}) async-start(), calls=%async_computation.10 | async-start | bytes 983040 | tf_op jit(solution)/shard_map/reduce_scatter | solution.py:146
Sparse Core Ops, SparseCore 0:
  31.1 19.0 all-gather.3
  51.8 29.0 all-gather.5
  82.4 17.0 all-gather.7
  122.0 15.6 reduce-scatter.4
  139.8 28.0 reduce-scatter.6
  170.0 18.0 reduce-scatter.8
  190.5 23.2 reduce-scatter.10

commit v4 on v1

--- a/solution.py
+++ b/solution.py
@@ -1,9 +1,16 @@
+import functools
+
 import jax
 import jax.numpy as jnp
 from jax import lax
+from jax.experimental import pallas as pl
+from jax.experimental.pallas import tpu as pltpu
 from jax.sharding import PartitionSpec as P
 
 AXES = ("dp", "expert")
+LANES = 128
+PARTS = 4
+ROWS_AT_ONCE = 8
 
 
 def partner(value, axis, distance):
@@ -70,24 +77,160 @@
     return jnp.sum(jnp.where(slot_of == serving, numbers, 0))
 
 
+def permute(value, move):
+    ex_count = lax.axis_size("expert")
+    pairs = []
+    for source in range(lax.axis_size("dp") * ex_count):
+        d, e = move(*divmod(source, ex_count))
+        pairs.append((source, d * ex_count + e))
+    return lax.ppermute(value, AXES, pairs)
+
+
+def to_sibling(d, e):
+    return d ^ 1, e
+
+
+def over_first(d, e):
+    return (d ^ 2, e) if d % 2 else (d, e ^ 1)
+
+
+def over_second(d, e):
+    return (d, e ^ 1) if d % 2 else (d ^ 2, e)
+
+
+def along_line(distance):
+    return lambda d, e: (d, e ^ (2 * distance))
+
+
+def choices(expert_ids, route_weight):
+    parts = [expert_ids.astype(jnp.bfloat16)]
+    rest = route_weight
+    for _ in range(3):
+        part = lax.reduce_precision(rest, exponent_bits=8, mantissa_bits=7)
+        parts.append(part.astype(jnp.bfloat16))
+        rest = rest - part
+    extra = jnp.concatenate(parts, axis=1)
+    return jnp.pad(extra, ((0, 0), (0, -extra.shape[1] % LANES)))
+
+
+def scale_of(extra, mine, top_count):
+    extra = extra.astype(jnp.float32)
+    ids, hi, mid, lo = (extra[:, k * top_count : (k + 1) * top_count] for k in range(4))
+    return jnp.sum(jnp.where(ids == mine, hi + mid + lo, 0.0), axis=1, keepdims=True)
+
+
+def serve_kernel(
+    top_count, mine, own, sib, w_gate, w_up, w_down, out_own, out_sib, x, gate, up, down, y, in_sem, out_sem
+):
+    rows, packed_width = own.shape
+    width, hidden_width = w_gate.shape
+    depth = width // PARTS
+    loads = [
+        pltpu.make_async_copy(own, x.at[:rows], in_sem.at[0]),
+        pltpu.make_async_copy(sib, x.at[rows:], in_sem.at[1]),
+    ]
+    for k in range(PARTS):
+        part = pl.ds(k * depth, depth)
+        loads.append(pltpu.make_async_copy(w_gate.at[part], gate.at[part], in_sem.at[2 + 2 * k]))
+        loads.append(pltpu.make_async_copy(w_up.at[part], up.at[part], in_sem.at[3 + 2 * k]))
+    load_down = pltpu.make_async_copy(w_down, down, in_sem.at[2 + 2 * PARTS])
+    for load in loads:
+        load.start()
+    load_down.start()
+    loads[0].wait()
+    loads[1].wait()
+    gate_sum = jnp.zeros((2 * rows, hidden_width), jnp.float32)
+    up_sum = jnp.zeros((2 * rows, hidden_width), jnp.float32)
+    for k in range(PARTS):
+        part = pl.ds(k * depth, depth)
+        loads[2 + 2 * k].wait()
+        gate_sum += jnp.dot(x[:, part], gate[part], preferred_element_type=jnp.float32)
+        loads[3 + 2 * k].wait()
+        up_sum += jnp.dot(x[:, part], up[part], preferred_element_type=jnp.float32)
+    hidden = (gate_sum / (1.0 + jnp.exp(-gate_sum)) * up_sum).astype(jnp.bfloat16)
+    scale = scale_of(x[:, width:], mine[0].astype(jnp.float32), top_count)
+    load_down.wait()
+    stores = []
+    for k in range(PARTS):
+        part = pl.ds(k * depth, depth)
+        served = jnp.dot(hidden, down[:, part], preferred_element_type=jnp.float32)
+        y[:, part] = (served * scale).astype(jnp.bfloat16)
+        stores.append(pltpu.make_async_copy(y.at[rows:, part], out_sib.at[:, part], out_sem.at[2 * k]))
+        stores.append(pltpu.make_async_copy(y.at[:rows, part], out_own.at[:, part], out_sem.at[2 * k + 1]))
+        stores[-2].start()
+        stores[-1].start()
+    for store in stores:
+        store.wait()
+
+
+def serve_rows(own, sib, mine, top_count, w_gate, w_up, w_down):
+    rows, packed_width = own.shape
+    width, hidden_width = w_gate.shape
+    anywhere = pl.BlockSpec(memory_space=pl.ANY)
+    out = jax.ShapeDtypeStruct((rows, width), jnp.bfloat16)
+    moved = 2 * (4 * rows * width + 3 * width * hidden_width)
+    return pl.pallas_call(
+        functools.partial(serve_kernel, top_count),
+        out_shape=(out, out),
+        in_specs=[pl.BlockSpec(memory_space=pltpu.SMEM)] + [anywhere] * 5,
+        out_specs=(anywhere, anywhere),
+        scratch_shapes=[
+            pltpu.VMEM((2 * rows, packed_width), jnp.bfloat16),
+            pltpu.VMEM((width, hidden_width), jnp.bfloat16),
+            pltpu.VMEM((width, hidden_width), jnp.bfloat16),
+            pltpu.VMEM((hidden_width, width), jnp.bfloat16),
+            pltpu.VMEM((2 * rows, width), jnp.bfloat16),
+            pltpu.SemaphoreType.DMA((3 + 2 * PARTS,)),
+            pltpu.SemaphoreType.DMA((2 * PARTS,)),
+        ],
+        compiler_params=pltpu.CompilerParams(vmem_limit_bytes=40 * 2**20),
+        cost_estimate=pl.CostEstimate(
+            flops=12 * rows * width * hidden_width, bytes_accessed=moved, transcendentals=2 * rows * hidden_width
+        ),
+        name="serve_rows",
+    )(mine.reshape(1), own, sib, w_gate, w_up, w_down)
+
+
+def total(*terms):
+    return sum(term.astype(jnp.float32) for term in terms).astype(jnp.bfloat16)
+
+
+def gather_and_serve(own, moves, serve):
+    rows = own.shape[0]
+    held = own
+    for move in moves:
+        held = jnp.concatenate([held, permute(held, move)])
+    out, out_sib = serve(held, permute(held, to_sibling))
+    terms = [out, permute(out_sib, to_sibling)]
+    for move in moves[::-1]:
+        half = terms[-1].shape[0] // 2
+        sent = total(*[term[half : 2 * half] for term in terms])
+        terms.append(permute(sent, move))
+    return total(*[term[:rows] for term in terms])
+
+
 def dense(tokens, expert_ids, route_weight, slot_of, swap_flag, w_gate, w_up, w_down):
+    tok_rows = tokens.shape[0]
+    top_count = expert_ids.shape[1]
     mine = served_expert(slot_of, swap_flag)
-    all_ids = lax.all_gather(expert_ids, AXES, tiled=True)
-    all_weights = lax.all_gather(route_weight, AXES, tiled=True)
-    scale = jnp.sum(jnp.where(all_ids == mine, all_weights, 0.0), axis=1)
-    arrived = lax.all_gather(tokens, AXES, tiled=True)
-    gate_sum = jnp.dot(arrived, w_gate[0], preferred_element_type=jnp.float32)
-    up_sum = jnp.dot(arrived, w_up[0], preferred_element_type=jnp.float32)
-    hidden = (jax.nn.silu(gate_sum) * up_sum).astype(jnp.bfloat16)
-    partial_out = jnp.dot(hidden, w_down[0], preferred_element_type=jnp.float32)
-    partial_out = (partial_out * scale[:, None]).astype(jnp.bfloat16)
-    return lax.psum_scatter(partial_out, AXES, scatter_dimension=0, tiled=True)
+    line_bits = (lax.axis_size("expert") // 2).bit_length() - 1
+    moves = [along_line(2**bit) for bit in range(line_bits)][::-1] + [over_first, over_second]
+    step = ROWS_AT_ONCE if tok_rows % ROWS_AT_ONCE == 0 else tok_rows
+    extra = choices(expert_ids, route_weight)
+    outs = []
+    for at in range(0, tok_rows, step):
+        own = jnp.concatenate([tokens[at : at + step], extra[at : at + step]], axis=1)
+        serve = lambda held, sib: serve_rows(held, sib, mine, top_count, w_gate[0], w_up[0], w_down[0])
+        outs.append(gather_and_serve(own, moves, serve))
+    return jnp.concatenate(outs)
 
 
 def on_device(tokens, expert_ids, *rest):
     slot_of = rest[1]
+    ex_count = lax.axis_size("expert")
     capacity = 2 * tokens.shape[0] * expert_ids.shape[1] // slot_of.shape[0]
-    serve = dense if capacity >= tokens.shape[0] else sparse
+    paired = lax.axis_size("dp") == 4 and ex_count >= 2 and ex_count & (ex_count - 1) == 0
+    serve = dense if capacity >= tokens.shape[0] and paired else sparse
     return serve(tokens, expert_ids, *rest)
 
 

time: 286 us -> 120 us (0.42)
  blocking collectives: 136 us -> 0 us
  waiting for transfers between devices: 114 us -> 42.1 us
  starting transfers between devices: 0.04 us -> 41.1 us
  matrix products: 19.9 us -> 0 us
  Pallas kernels: 0 us -> 19.6 us
  between operations: 14.1 us -> 0.88 us
  other arithmetic: 2.01 us -> 11.5 us
  local copies, waits for them, and re-layouts: 0.08 us -> 3.93 us
    all_gather x2 -> x0, blocking collectives: 136 us -> none  [the longest x1 71.4 us: dense(): all_ids = lax.all_gather(expert_ids, AXES, tiled=True)]
    reduce_scatter x1 -> x0, waiting for transfers between devices: 113 us -> none  [dense(): return lax.psum_scatter(partial_out, AXES, scatter_dimension=0, tiled=True)]
    ppermute x0 -> x30, waiting for transfers between devices: none -> 42.1 us  [permute(): return lax.ppermute(value, AXES, pairs)]
    ppermute x0 -> x30, starting transfers between devices: none -> 41.1 us  [permute(): return lax.ppermute(value, AXES, pairs)]
    dot_general x2 -> x0, matrix products: 19.9 us -> none  [the longest x1 13.1 us: dense(): partial_out = jnp.dot(hidden, w_down[0], preferred_element_type=jnp.float32)]
    pallas_call x0 -> x3, Pallas kernels: none -> 19.6 us  [serve_rows(): pl.pallas_call(functools.partial(serve_kernel, top_count), out_shape=(out...]
    concatenate x0 -> x14, other arithmetic: none -> 8.27 us  [the longest x9 5.58 us: gather_and_serve(): held = jnp.concatenate([held, permute(held, move)])]
  transfers between devices with their start and end apart: 2 -> 30, of which waited for: 1 -> 16; matrix products, arithmetic and copies ran while one was open for 1% -> 9% of each run, Pallas kernels for 0% -> 16%
where the time goes in v4:
time: 120 us; the launch traced here: 119 us
  waiting for transfers between devices  42.1 us (35%)
  starting transfers between devices  41.1 us (34%)
  Pallas kernels  19.6 us (16%)
  other arithmetic  11.5 us (10%)
  local copies, waits for them, and re-layouts  3.93 us (3%)
    ppermute x30, waiting for transfers between devices, permute(): return lax.ppermute(value, AXES, pairs)  42.1 us
    ppermute x30, starting transfers between devices, permute(): return lax.ppermute(value, AXES, pairs)  41.1 us
    pallas_call x3, Pallas kernels, serve_rows(): pl.pallas_call(functools.partial(serve_kernel, top_count), out_shape=(out...  19.6 us
    concatenate x9, other arithmetic, gather_and_serve(): held = jnp.concatenate([held, permute(held, move)])  5.58 us
    unnamed x16, local copies, waits for them, and re-layouts  2.7 us
  transfers between devices with their start and end apart: 30, of which 16 were waited for; matrix products, arithmetic and copies ran while one was open for 9% of the time, Pallas kernels for 16%

profile of v4, /device:TPU:0, one launch (start us, length us, event | category | flops | bytes accessed | tf_op | source)
XLA Modules:
  0.0 119.0 jit_solution(14640223006032386159)
XLA Ops:
  0.0 0.7 reduce_precision.9
  0.7 0.8 copy.13
  1.4 0.7 convert_element_type.239
  2.4 0.9 fusion.10
  3.3 0.6 pad_maximum_fusion.10
  4.0 4.0 %collective-permute-start = (bf16[8,4224]{1,0:T(8,128)(2,1)}, bf16[8,4224]{1,0:T(8,128)(2,1)}, u32[]{:S(2)}, u32[]{:S(2)}) collective-permute-start(bf16[8,4224]{1,0:T(8,128)(2,1)} %get-tuple-element.20), channel_id=1, source_target_pairs={{0,4},{1,5},{2,6},{3,7},{4,0},{5,1},{6,2},{7,3},{8,12},{9,13},{10,... | collective-permute-start | bytes 202760 | tf_op jit(solution)/shard_map/ppermute | solution.py:86
  8.0 0.6 pad_maximum_fusion.12
  8.7 0.6 pad_maximum_fusion.11
  9.3 2.9 %collective-permute-start.10 = (bf16[8,4224]{1,0:T(8,128)(2,1)}, bf16[8,4224]{1,0:T(8,128)(2,1)S(1)}, u32[]{:S(2)}, u32[]{:S(2)}) collective-permute-start(bf16[8,4224]{1,0:T(8,128)(2,1)} %get-tuple-element.22), channel_id=1, source_target_pairs={{0,4},{1,5},{2,6},{3,7},{4,0},{5,1},{6,2},{7,3},{8,12},{9,13},{10,... | collective-permute-start | bytes 202760 | tf_op jit(solution)/shard_map/ppermute | solution.py:86
  12.9 0.9 pad_maximum_fusion.7
  13.8 2.0 %collective-permute-start.1 = (bf16[16,4224]{1,0:T(8,128)(2,1)S(1)}, bf16[16,4224]{1,0:T(8,128)(2,1)S(1)}, u32[]{:S(2)}, u32[]{:S(2)}) collective-permute-start(bf16[16,4224]{1,0:T(8,128)(2,1)S(1)} %pad_maximum_fusion.7), channel_id=1, source_target_pairs={{0,2},{1,3},{2,0},{3,1},{4,6},{5,7},{6,4},{7,5},{8,10},{9,11},{10,... | collective-permute-start | bytes 405512 | tf_op jit(solution)/shard_map/ppermute | solution.py:86
  15.8 1.4 %collective-permute-done.20 = bf16[8,4224]{1,0:T(8,128)(2,1)} collective-permute-done((bf16[8,4224]{1,0:T(8,128)(2,1)}, bf16[8,4224]{1,0:T(8,128)(2,1)}, u32[]{:S(2)}, u32[]{:S(2)}) %collective-permute-start.20) | collective-permute-done | bytes 67616 | tf_op jit(solution)/shard_map/ppermute | solution.py:86
  17.2 0.9 pad_maximum_fusion.9
  18.2 2.1 %collective-permute-start.11 = (bf16[16,4224]{1,0:T(8,128)(2,1)S(1)}, bf16[16,4224]{1,0:T(8,128)(2,1)S(1)}, u32[]{:S(2)}, u32[]{:S(2)}) collective-permute-start(bf16[16,4224]{1,0:T(8,128)(2,1)S(1)} %pad_maximum_fusion.8), channel_id=1, source_target_pairs={{0,2},{1,3},{2,0},{3,1},{4,6},{5,7},{6,4},{7,5},{8,10},{9,11},{10,... | collective-permute-start | bytes 405512 | tf_op jit(solution)/shard_map/ppermute | solution.py:86
  20.2 0.9 constant_dynamic-update-slice_fusion.3
  21.1 0.9 constant_dynamic-update-slice_fusion.13
  22.0 0.9 pad_maximum_fusion.3
  22.9 1.8 %collective-permute-start.2 = (bf16[32,4224]{1,0:T(8,128)(2,1)S(1)}, bf16[32,4224]{1,0:T(8,128)(2,1)S(1)}, u32[]{:S(2)}, u32[]{:S(2)}) collective-permute-start(bf16[32,4224]{1,0:T(8,128)(2,1)S(1)} %pad_maximum_fusion.3), channel_id=1, source_target_pairs={{0,1},{1,0},{2,3},{3,2},{4,5},{5,4},{6,7},{7,6},{8,24},{9,25},{10,... | collective-permute-start | bytes 811016 | tf_op jit(solution)/shard_map/ppermute | solution.py:86
  24.8 0.9 pad_maximum_fusion.5
  25.7 1.7 %collective-permute-start.22 = (bf16[32,4224]{1,0:T(8,128)(2,1)S(1)}, bf16[32,4224]{1,0:T(8,128)(2,1)S(1)}, u32[]{:S(2)}, u32[]{:S(2)}) collective-permute-start(bf16[32,4224]{1,0:T(8,128)(2,1)S(1)} %pad_maximum_fusion.5), channel_id=1, source_target_pairs={{0,1},{1,0},{2,3},{3,2},{4,5},{5,4},{6,7},{7,6},{8,24},{9,25},{10,... | collective-permute-start | bytes 811016 | tf_op jit(solution)/shard_map/ppermute | solution.py:86
  27.4 0.8 collective-permute-start.12
  28.3 1.2 collective-permute-done.2
  29.5 1.0 pad_maximum_fusion
  30.5 1.7 %collective-permute-start.3 = (bf16[64,4224]{1,0:T(8,128)(2,1)S(1)}, bf16[64,4224]{1,0:T(8,128)(2,1)S(1)}, u32[]{:S(2)}, u32[]{:S(2)}) collective-permute-start(bf16[64,4224]{1,0:T(8,128)(2,1)S(1)} %pad_maximum_fusion), channel_id=1, source_target_pairs={{0,16},{1,17},{2,18},{3,19},{4,20},{5,21},{6,22},{7,23},{8,9},{9,8... | collective-permute-start | bytes 1622024 | tf_op jit(solution)/shard_map/ppermute | solution.py:86
  32.2 1.4 %collective-permute-done.22 = bf16[32,4224]{1,0:T(8,128)(2,1)S(1)} collective-permute-done((bf16[32,4224]{1,0:T(8,128)(2,1)S(1)}, bf16[32,4224]{1,0:T(8,128)(2,1)S(1)}, u32[]{:S(2)}, u32[]{:S(2)}) %collective-permute-start.22) | collective-permute-done | bytes 270368 | tf_op jit(solution)/shard_map/ppermute | solution.py:86
  33.6 0.9 pad_maximum_fusion.2
  34.5 2.1 %collective-permute-start.23 = (bf16[64,4224]{1,0:T(8,128)(2,1)S(1)}, bf16[64,4224]{1,0:T(8,128)(2,1)S(1)}, u32[]{:S(2)}, u32[]{:S(2)}) collective-permute-start(bf16[64,4224]{1,0:T(8,128)(2,1)S(1)} %pad_maximum_fusion.2), channel_id=1, source_target_pairs={{0,16},{1,17},{2,18},{3,19},{4,20},{5,21},{6,22},{7,23},{8,9},{9,8... | collective-permute-start | bytes 1622024 | tf_op jit(solution)/shard_map/ppermute | solution.py:86
  36.6 2.8 %collective-permute-done.12 = bf16[32,4224]{1,0:T(8,128)(2,1)S(1)} collective-permute-done((bf16[32,4224]{1,0:T(8,128)(2,1)S(1)}, bf16[32,4224]{1,0:T(8,128)(2,1)S(1)}, u32[]{:S(2)}, u32[]{:S(2)}) %collective-permute-start.12) | collective-permute-done | bytes 270368 | tf_op jit(solution)/shard_map/ppermute | solution.py:86
  39.4 2.1 %collective-permute-start.13 = (bf16[64,4224]{1,0:T(8,128)(2,1)S(1)}, bf16[64,4224]{1,0:T(8,128)(2,1)S(1)}, u32[]{:S(2)}, u32[]{:S(2)}) collective-permute-start(bf16[64,4224]{1,0:T(8,128)(2,1)S(1)} %pad_maximum_fusion.1), channel_id=1, source_target_pairs={{0,16},{1,17},{2,18},{3,19},{4,20},{5,21},{6,22},{7,23},{8,9},{9,8... | collective-permute-start | bytes 1622024 | tf_op jit(solution)/shard_map/ppermute | solution.py:86
  41.7 3.9 %collective-permute-done.23 = bf16[64,4224]{1,0:T(8,128)(2,1)S(1)} collective-permute-done((bf16[64,4224]{1,0:T(8,128)(2,1)S(1)}, bf16[64,4224]{1,0:T(8,128)(2,1)S(1)}, u32[]{:S(2)}, u32[]{:S(2)}) %collective-permute-start.23) | collective-permute-done | bytes 540704 | tf_op jit(solution)/shard_map/ppermute | solution.py:86
  45.7 1.3 %collective-permute-start.24 = (bf16[128,4224]{1,0:T(8,128)(2,1)S(1)}, bf16[128,4224]{1,0:T(8,128)(2,1)S(1)}, u32[]{:S(2)}, u32[]{:S(2)}) collective-permute-start(bf16[128,4224]{1,0:T(8,128)(2,1)S(1)} %constant_dynamic-update-slice_fusion.10.own), channel_id=1, source_target_pairs={{0,8},{1,9},{2,10},{3,11},{4,12},{5,13},{6,14},{7,15},{8,0},{9,1},... | collective-permute-start | bytes 3244040 | tf_op jit(solution)/shard_map/ppermute | solution.py:86
  47.1 4.4 %collective-permute-done.13 = bf16[64,4224]{1,0:T(8,128)(2,1)S(1)} collective-permute-done((bf16[64,4224]{1,0:T(8,128)(2,1)S(1)}, bf16[64,4224]{1,0:T(8,128)(2,1)S(1)}, u32[]{:S(2)}, u32[]{:S(2)}) %collective-permute-start.13) | collective-permute-done | bytes 540704 | tf_op jit(solution)/shard_map/ppermute | solution.py:86
  51.5 1.1 collective-permute-start.14
  52.6 0.6 fusion.9
  53.2 6.5 %serve_rows.3 = (bf16[128,4096]{1,0:T(8,128)(2,1)S(1)}, bf16[128,4096]{1,0:T(8,128)(2,1)S(1)}) custom-call(s32[1]{0:T(128)} %bitcast.1.mine, bf16[128,4224]{1,0:T(8,128)(2,1)S(1)} %constant_dynamic-update-slice_fusion.own, bf16[128,4224]{1,0:T(8,128)(2,1)S(1)} %collective-permute-done.4.sib, bf16[4096,512]{1,0:T(8,128)(2,1)S(1)} %bitcast.5, ...), custom_call_target="tpu_custom_call" | custom-call | flops 3221225472 | bytes 16777216 | tf_op jit(solution)/shard_map/serve_rows/pallas_call | solution.py:172
  59.8 6.5 %serve_rows.5 = (bf16[128,4096]{1,0:T(8,128)(2,1)S(1)}, bf16[128,4096]{1,0:T(8,128)(2,1)S(1)}) custom-call(s32[1]{0:T(128)} %bitcast.1.mine, bf16[128,4224]{1,0:T(8,128)(2,1)S(1)} %constant_dynamic-update-slice_fusion.10.own, bf16[128,4224]{1,0:T(8,128)(2,1)S(1)} %collective-permute-done.24.sib, bf16[4096,512]{1,0:T(8,128)(2,1)S(1)} %bitcast.6, ...), custom_call_target="tpu_custom_call" | custom-call | flops 3221225472 | bytes 16777216 | tf_op jit(solution)/shard_map/serve_rows/pallas_call | solution.py:172
  66.2 0.6 collective-permute-start.25
  66.8 6.6 %serve_rows.4 = (bf16[128,4096]{1,0:T(8,128)(2,1)S(1)}, bf16[128,4096]{1,0:T(8,128)(2,1)S(1)}) custom-call(s32[1]{0:T(128)} %bitcast.1.mine, bf16[128,4224]{1,0:T(8,128)(2,1)S(1)} %constant_dynamic-update-slice_fusion.5.own, bf16[128,4224]{1,0:T(8,128)(2,1)S(1)} %collective-permute-done.14.sib, bf16[4096,512]{1,0:T(8,128)(2,1)S(1)} %bitcast.7, ...), custom_call_target="tpu_custom_call" | custom-call | flops 3221225472 | bytes 16777216 | tf_op jit(solution)/shard_map/serve_rows/pallas_call | solution.py:172
  73.5 0.1 add_convert_fusion.2
  73.7 1.8 %collective-permute-start.6 = (bf16[64,4096]{1,0:T(8,128)(2,1)S(1)}, bf16[64,4096]{1,0:T(8,128)(2,1)S(1)}, u32[]{:S(2)}, u32[]{:S(2)}) collective-permute-start(bf16[64,4096]{1,0:T(8,128)(2,1)S(1)} %add_convert_fusion.2), channel_id=1, source_target_pairs={{0,16},{1,17},{2,18},{3,19},{4,20},{5,21},{6,22},{7,23},{8,9},{9,8... | collective-permute-start | bytes 1572872 | tf_op jit(solution)/shard_map/ppermute | solution.py:86
  75.5 0.1 add_convert_fusion
  75.6 0.4 collective-permute-start.26
  76.0 0.2 collective-permute-done.15
  76.2 0.1 add_convert_fusion.1
  76.3 1.8 %collective-permute-start.16 = (bf16[64,4096]{1,0:T(8,128)(2,1)S(1)}, bf16[64,4096]{1,0:T(8,128)(2,1)S(1)}, u32[]{:S(2)}, u32[]{:S(2)}) collective-permute-start(bf16[64,4096]{1,0:T(8,128)(2,1)S(1)} %add_convert_fusion.1), channel_id=1, source_target_pairs={{0,16},{1,17},{2,18},{3,19},{4,20},{5,21},{6,22},{7,23},{8,9},{9,8... | collective-permute-start | bytes 1572872 | tf_op jit(solution)/shard_map/ppermute | solution.py:86
  78.1 4.8 %collective-permute-done.6 = bf16[64,4096]{1,0:T(8,128)(2,1)S(1)} collective-permute-done((bf16[64,4096]{1,0:T(8,128)(2,1)S(1)}, bf16[64,4096]{1,0:T(8,128)(2,1)S(1)}, u32[]{:S(2)}, u32[]{:S(2)}) %collective-permute-start.6) | collective-permute-done | bytes 524320 | tf_op jit(solution)/shard_map/ppermute | solution.py:86
  82.9 0.1 add_convert_fusion.5
  83.0 1.8 %collective-permute-start.7 = (bf16[32,4096]{1,0:T(8,128)(2,1)S(1)}, bf16[32,4096]{1,0:T(8,128)(2,1)S(1)}, u32[]{:S(2)}, u32[]{:S(2)}) collective-permute-start(bf16[32,4096]{1,0:T(8,128)(2,1)S(1)} %add_convert_fusion.5), channel_id=1, source_target_pairs={{0,1},{1,0},{2,3},{3,2},{4,5},{5,4},{6,7},{7,6},{8,24},{9,25},{10,... | collective-permute-start | bytes 786440 | tf_op jit(solution)/shard_map/ppermute | solution.py:86
  84.8 6.5 %collective-permute-done.26 = bf16[64,4096]{1,0:T(8,128)(2,1)S(1)} collective-permute-done((bf16[64,4096]{1,0:T(8,128)(2,1)S(1)}, bf16[64,4096]{1,0:T(8,128)(2,1)S(1)}, u32[]{:S(2)}, u32[]{:S(2)}) %collective-permute-start.26) | collective-permute-done | bytes 524320 | tf_op jit(solution)/shard_map/ppermute | solution.py:86
  91.3 0.1 add_convert_fusion.3
  91.4 1.8 %collective-permute-start.27 = (bf16[32,4096]{1,0:T(8,128)(2,1)S(1)}, bf16[32,4096]{1,0:T(8,128)(2,1)S(1)}, u32[]{:S(2)}, u32[]{:S(2)}) collective-permute-start(bf16[32,4096]{1,0:T(8,128)(2,1)S(1)} %add_convert_fusion.3), channel_id=1, source_target_pairs={{0,1},{1,0},{2,3},{3,2},{4,5},{5,4},{6,7},{7,6},{8,24},{9,25},{10,... | collective-permute-start | bytes 786440 | tf_op jit(solution)/shard_map/ppermute | solution.py:86
  93.3 6.5 %collective-permute-done.16 = bf16[64,4096]{1,0:T(8,128)(2,1)S(1)} collective-permute-done((bf16[64,4096]{1,0:T(8,128)(2,1)S(1)}, bf16[64,4096]{1,0:T(8,128)(2,1)S(1)}, u32[]{:S(2)}, u32[]{:S(2)}) %collective-permute-start.16) | collective-permute-done | bytes 524320 | tf_op jit(solution)/shard_map/ppermute | solution.py:86
  99.9 1.8 %collective-permute-start.17 = (bf16[32,4096]{1,0:T(8,128)(2,1)S(1)}, bf16[32,4096]{1,0:T(8,128)(2,1)S(1)}, u32[]{:S(2)}, u32[]{:S(2)}) collective-permute-start(bf16[32,4096]{1,0:T(8,128)(2,1)S(1)} %add_convert_fusion.4), channel_id=1, source_target_pairs={{0,1},{1,0},{2,3},{3,2},{4,5},{5,4},{6,7},{7,6},{8,24},{9,25},{10,... | collective-permute-start | bytes 786440 | tf_op jit(solution)/shard_map/ppermute | solution.py:86
  101.9 2.1 %collective-permute-start.28 = (bf16[16,4096]{1,0:T(8,128)(2,1)S(1)}, bf16[16,4096]{1,0:T(8,128)(2,1)S(1)}, u32[]{:S(2)}, u32[]{:S(2)}) collective-permute-start(bf16[16,4096]{1,0:T(8,128)(2,1)S(1)} %add_convert_fusion.6), channel_id=1, source_target_pairs={{0,2},{1,3},{2,0},{3,1},{4,6},{5,7},{6,4},{7,5},{8,10},{9,11},{10,... | collective-permute-start | bytes 393224 | tf_op jit(solution)/shard_map/ppermute | solution.py:86
  104.0 2.3 %collective-permute-done.17 = bf16[32,4096]{1,0:T(8,128)(2,1)S(1)} collective-permute-done((bf16[32,4096]{1,0:T(8,128)(2,1)S(1)}, bf16[32,4096]{1,0:T(8,128)(2,1)S(1)}, u32[]{:S(2)}, u32[]{:S(2)}) %collective-permute-start.17) | collective-permute-done | bytes 262176 | tf_op jit(solution)/shard_map/ppermute | solution.py:86
  106.5 0.8 collective-permute-done.8
  107.3 2.6 %collective-permute-start.9 = (bf16[8,4096]{1,0:T(8,128)(2,1)S(1)}, bf16[8,4096]{1,0:T(8,128)(2,1)S(1)}, u32[]{:S(2)}, u32[]{:S(2)}) collective-permute-start(bf16[8,4096]{1,0:T(8,128)(2,1)S(1)} %add_convert_fusion.14), channel_id=1, source_target_pairs={{0,4},{1,5},{2,6},{3,7},{4,0},{5,1},{6,2},{7,3},{8,12},{9,13},{10,... | collective-permute-start | bytes 196616 | tf_op jit(solution)/shard_map/ppermute | solution.py:86
  109.9 1.1 collective-permute-done.28
  111.0 1.0 collective-permute-start.29
  112.1 0.9 collective-permute-done.18
  113.1 1.3 %collective-permute-start.19 = (bf16[8,4096]{1,0:T(8,128)(2,1)S(1)}, bf16[8,4096]{1,0:T(8,128)(2,1)S(1)}, u32[]{:S(2)}, u32[]{:S(2)}) collective-permute-start(bf16[8,4096]{1,0:T(8,128)(2,1)S(1)} %add_convert_fusion.12), channel_id=1, source_target_pairs={{0,4},{1,5},{2,6},{3,7},{4,0},{5,1},{6,2},{7,3},{8,12},{9,13},{10,... | collective-permute-start | bytes 196616 | tf_op jit(solution)/shard_map/ppermute | solution.py:86
  114.4 2.7 %collective-permute-done.29 = bf16[8,4096]{1,0:T(8,128)(2,1)S(1)} collective-permute-done((bf16[8,4096]{1,0:T(8,128)(2,1)S(1)}, bf16[8,4096]{1,0:T(8,128)(2,1)S(1)}, u32[]{:S(2)}, u32[]{:S(2)}) %collective-permute-start.29) | collective-permute-done | bytes 65568 | tf_op jit(solution)/shard_map/ppermute | solution.py:86
  117.1 1.2 collective-permute-done.19
  118.4 0.7 pad_maximum_fusion.6
  (55 shorter events, 1.8 us)
Async XLA Ops:
  4.0 8.9 %collective-permute-start = (bf16[8,4224]{1,0:T(8,128)(2,1)}, bf16[8,4224]{1,0:T(8,128)(2,1)}, u32[]{:S(2)}, u32[]{:S(2)}) collective-permute-start(bf16[8,4224]{1,0:T(8,128)(2,1)} %get-tuple-element.20), channel_id=1, source_target_pairs={{0,4},{1,5},{2,6},{3,7},{4,0},{5,1},{6,2},{7,3},{8,12},{9,13},{10,... | collective-permute-start | bytes 202760 | tf_op jit(solution)/shard_map/ppermute | solution.py:86
  8.6 8.5 %collective-permute-start.20 = (bf16[8,4224]{1,0:T(8,128)(2,1)}, bf16[8,4224]{1,0:T(8,128)(2,1)}, u32[]{:S(2)}, u32[]{:S(2)}) collective-permute-start(bf16[8,4224]{1,0:T(8,128)(2,1)} %get-tuple-element.24), channel_id=1, source_target_pairs={{0,4},{1,5},{2,6},{3,7},{4,0},{5,1},{6,2},{7,3},{8,12},{9,13},{10,... | collective-permute-start | bytes 202760 | tf_op jit(solution)/shard_map/ppermute | solution.py:86
  9.3 8.9 %collective-permute-start.10 = (bf16[8,4224]{1,0:T(8,128)(2,1)}, bf16[8,4224]{1,0:T(8,128)(2,1)S(1)}, u32[]{:S(2)}, u32[]{:S(2)}) collective-permute-start(bf16[8,4224]{1,0:T(8,128)(2,1)} %get-tuple-element.22), channel_id=1, source_target_pairs={{0,4},{1,5},{2,6},{3,7},{4,0},{5,1},{6,2},{7,3},{8,12},{9,13},{10,... | collective-permute-start | bytes 202760 | tf_op jit(solution)/shard_map/ppermute | solution.py:86
  13.8 8.3 %collective-permute-start.1 = (bf16[16,4224]{1,0:T(8,128)(2,1)S(1)}, bf16[16,4224]{1,0:T(8,128)(2,1)S(1)}, u32[]{:S(2)}, u32[]{:S(2)}) collective-permute-start(bf16[16,4224]{1,0:T(8,128)(2,1)S(1)} %pad_maximum_fusion.7), channel_id=1, source_target_pairs={{0,2},{1,3},{2,0},{3,1},{4,6},{5,7},{6,4},{7,5},{8,10},{9,11},{10,... | collective-permute-start | bytes 405512 | tf_op jit(solution)/shard_map/ppermute | solution.py:86
  18.1 6.7 %collective-permute-start.21 = (bf16[16,4224]{1,0:T(8,128)(2,1)S(1)}, bf16[16,4224]{1,0:T(8,128)(2,1)S(1)}, u32[]{:S(2)}, u32[]{:S(2)}) collective-permute-start(bf16[16,4224]{1,0:T(8,128)(2,1)S(1)} %pad_maximum_fusion.9), channel_id=1, source_target_pairs={{0,2},{1,3},{2,0},{3,1},{4,6},{5,7},{6,4},{7,5},{8,10},{9,11},{10,... | collective-permute-start | bytes 405512 | tf_op jit(solution)/shard_map/ppermute | solution.py:86
  18.2 9.2 %collective-permute-start.11 = (bf16[16,4224]{1,0:T(8,128)(2,1)S(1)}, bf16[16,4224]{1,0:T(8,128)(2,1)S(1)}, u32[]{:S(2)}, u32[]{:S(2)}) collective-permute-start(bf16[16,4224]{1,0:T(8,128)(2,1)S(1)} %pad_maximum_fusion.8), channel_id=1, source_target_pairs={{0,2},{1,3},{2,0},{3,1},{4,6},{5,7},{6,4},{7,5},{8,10},{9,11},{10,... | collective-permute-start | bytes 405512 | tf_op jit(solution)/shard_map/ppermute | solution.py:86
  22.9 6.5 %collective-permute-start.2 = (bf16[32,4224]{1,0:T(8,128)(2,1)S(1)}, bf16[32,4224]{1,0:T(8,128)(2,1)S(1)}, u32[]{:S(2)}, u32[]{:S(2)}) collective-permute-start(bf16[32,4224]{1,0:T(8,128)(2,1)S(1)} %pad_maximum_fusion.3), channel_id=1, source_target_pairs={{0,1},{1,0},{2,3},{3,2},{4,5},{5,4},{6,7},{7,6},{8,24},{9,25},{10,... | collective-permute-start | bytes 811016 | tf_op jit(solution)/shard_map/ppermute | solution.py:86
  25.7 7.9 %collective-permute-start.22 = (bf16[32,4224]{1,0:T(8,128)(2,1)S(1)}, bf16[32,4224]{1,0:T(8,128)(2,1)S(1)}, u32[]{:S(2)}, u32[]{:S(2)}) collective-permute-start(bf16[32,4224]{1,0:T(8,128)(2,1)S(1)} %pad_maximum_fusion.5), channel_id=1, source_target_pairs={{0,1},{1,0},{2,3},{3,2},{4,5},{5,4},{6,7},{7,6},{8,24},{9,25},{10,... | collective-permute-start | bytes 811016 | tf_op jit(solution)/shard_map/ppermute | solution.py:86
  27.4 12.0 %collective-permute-start.12 = (bf16[32,4224]{1,0:T(8,128)(2,1)S(1)}, bf16[32,4224]{1,0:T(8,128)(2,1)S(1)}, u32[]{:S(2)}, u32[]{:S(2)}) collective-permute-start(bf16[32,4224]{1,0:T(8,128)(2,1)S(1)} %pad_maximum_fusion.4), channel_id=1, source_target_pairs={{0,1},{1,0},{2,3},{3,2},{4,5},{5,4},{6,7},{7,6},{8,24},{9,25},{10,... | collective-permute-start | bytes 811016 | tf_op jit(solution)/shard_map/ppermute | solution.py:86
  28.3 24.9 %copy-start.1 = (bf16[1,4096,512]{2,1,0:T(8,128)(2,1)S(1)}, bf16[1,4096,512]{2,1,0:T(8,128)(2,1)}, u32[]{:S(2)}) copy-start(bf16[1,4096,512]{2,1,0:T(8,128)(2,1)} %param.14) | copy-start | bytes 12582916
  30.5 11.1 %collective-permute-start.3 = (bf16[64,4224]{1,0:T(8,128)(2,1)S(1)}, bf16[64,4224]{1,0:T(8,128)(2,1)S(1)}, u32[]{:S(2)}, u32[]{:S(2)}) collective-permute-start(bf16[64,4224]{1,0:T(8,128)(2,1)S(1)} %pad_maximum_fusion), channel_id=1, source_target_pairs={{0,16},{1,17},{2,18},{3,19},{4,20},{5,21},{6,22},{7,23},{8,9},{9,8... | collective-permute-start | bytes 1622024 | tf_op jit(solution)/shard_map/ppermute | solution.py:86
  34.5 11.1 %collective-permute-start.23 = (bf16[64,4224]{1,0:T(8,128)(2,1)S(1)}, bf16[64,4224]{1,0:T(8,128)(2,1)S(1)}, u32[]{:S(2)}, u32[]{:S(2)}) collective-permute-start(bf16[64,4224]{1,0:T(8,128)(2,1)S(1)} %pad_maximum_fusion.2), channel_id=1, source_target_pairs={{0,16},{1,17},{2,18},{3,19},{4,20},{5,21},{6,22},{7,23},{8,9},{9,8... | collective-permute-start | bytes 1622024 | tf_op jit(solution)/shard_map/ppermute | solution.py:86
  39.4 12.0 %collective-permute-start.13 = (bf16[64,4224]{1,0:T(8,128)(2,1)S(1)}, bf16[64,4224]{1,0:T(8,128)(2,1)S(1)}, u32[]{:S(2)}, u32[]{:S(2)}) collective-permute-start(bf16[64,4224]{1,0:T(8,128)(2,1)S(1)} %pad_maximum_fusion.1), channel_id=1, source_target_pairs={{0,16},{1,17},{2,18},{3,19},{4,20},{5,21},{6,22},{7,23},{8,9},{9,8... | collective-permute-start | bytes 1622024 | tf_op jit(solution)/shard_map/ppermute | solution.py:86
  41.5 11.1 %copy-start.2 = (s32[16,2]{0,1:T(2,128)S(1)}, s32[16,2]{0,1:T(2,128)}, u32[]{:S(2)}) copy-start(s32[16,2]{0,1:T(2,128)} %param.11) | copy-start | bytes 388
  41.5 11.7 %copy-start = (bf16[1,4096,512]{2,1,0:T(8,128)(2,1)S(1)}, bf16[1,4096,512]{2,1,0:T(8,128)(2,1)}, u32[]{:S(2)}) copy-start(bf16[1,4096,512]{2,1,0:T(8,128)(2,1)} %param.13) | copy-start | bytes 12582916
  41.7 11.6 %collective-permute-start.4 = (bf16[128,4224]{1,0:T(8,128)(2,1)S(1)}, bf16[128,4224]{1,0:T(8,128)(2,1)S(1)}, u32[]{:S(2)}, u32[]{:S(2)}) collective-permute-start(bf16[128,4224]{1,0:T(8,128)(2,1)S(1)} %constant_dynamic-update-slice_fusion.own), channel_id=1, source_target_pairs={{0,8},{1,9},{2,10},{3,11},{4,12},{5,13},{6,14},{7,15},{8,0},{9,1},... | collective-permute-start | bytes 3244040 | tf_op jit(solution)/shard_map/ppermute | solution.py:86
  45.7 14.0 %collective-permute-start.24 = (bf16[128,4224]{1,0:T(8,128)(2,1)S(1)}, bf16[128,4224]{1,0:T(8,128)(2,1)S(1)}, u32[]{:S(2)}, u32[]{:S(2)}) collective-permute-start(bf16[128,4224]{1,0:T(8,128)(2,1)S(1)} %constant_dynamic-update-slice_fusion.10.own), channel_id=1, source_target_pairs={{0,8},{1,9},{2,10},{3,11},{4,12},{5,13},{6,14},{7,15},{8,0},{9,1},... | collective-permute-start | bytes 3244040 | tf_op jit(solution)/shard_map/ppermute | solution.py:86
  51.5 15.3 %collective-permute-start.14 = (bf16[128,4224]{1,0:T(8,128)(2,1)S(1)}, bf16[128,4224]{1,0:T(8,128)(2,1)S(1)}, u32[]{:S(2)}, u32[]{:S(2)}) collective-permute-start(bf16[128,4224]{1,0:T(8,128)(2,1)S(1)} %constant_dynamic-update-slice_fusion.5.own), channel_id=1, source_target_pairs={{0,8},{1,9},{2,10},{3,11},{4,12},{5,13},{6,14},{7,15},{8,0},{9,1},... | collective-permute-start | bytes 3244040 | tf_op jit(solution)/shard_map/ppermute | solution.py:86
  59.7 13.8 %collective-permute-start.5 = (bf16[128,4096]{1,0:T(8,128)(2,1)S(1)}, bf16[128,4096]{1,0:T(8,128)(2,1)S(1)}, u32[]{:S(2)}, u32[]{:S(2)}) collective-permute-start(bf16[128,4096]{1,0:T(8,128)(2,1)S(1)} %get-tuple-element.12), channel_id=1, source_target_pairs={{0,8},{1,9},{2,10},{3,11},{4,12},{5,13},{6,14},{7,15},{8,0},{9,1},... | collective-permute-start | bytes 3145736 | tf_op jit(solution)/shard_map/ppermute | solution.py:86
  66.2 9.2 %collective-permute-start.25 = (bf16[128,4096]{1,0:T(8,128)(2,1)S(1)}, bf16[128,4096]{1,0:T(8,128)(2,1)S(1)}, u32[]{:S(2)}, u32[]{:S(2)}) collective-permute-start(bf16[128,4096]{1,0:T(8,128)(2,1)S(1)} %get-tuple-element.16), channel_id=1, source_target_pairs={{0,8},{1,9},{2,10},{3,11},{4,12},{5,13},{6,14},{7,15},{8,0},{9,1},... | collective-permute-start | bytes 3145736 | tf_op jit(solution)/shard_map/ppermute | solution.py:86
  73.4 2.7 %collective-permute-start.15 = (bf16[128,4096]{1,0:T(8,128)(2,1)S(1)}, bf16[128,4096]{1,0:T(8,128)(2,1)S(1)}, u32[]{:S(2)}, u32[]{:S(2)}) collective-permute-start(bf16[128,4096]{1,0:T(8,128)(2,1)S(1)} %get-tuple-element.14), channel_id=1, source_target_pairs={{0,8},{1,9},{2,10},{3,11},{4,12},{5,13},{6,14},{7,15},{8,0},{9,1},... | collective-permute-start | bytes 3145736 | tf_op jit(solution)/shard_map/ppermute | solution.py:86
  73.7 9.2 %collective-permute-start.6 = (bf16[64,4096]{1,0:T(8,128)(2,1)S(1)}, bf16[64,4096]{1,0:T(8,128)(2,1)S(1)}, u32[]{:S(2)}, u32[]{:S(2)}) collective-permute-start(bf16[64,4096]{1,0:T(8,128)(2,1)S(1)} %add_convert_fusion.2), channel_id=1, source_target_pairs={{0,16},{1,17},{2,18},{3,19},{4,20},{5,21},{6,22},{7,23},{8,9},{9,8... | collective-permute-start | bytes 1572872 | tf_op jit(solution)/shard_map/ppermute | solution.py:86
  75.6 15.8 %collective-permute-start.26 = (bf16[64,4096]{1,0:T(8,128)(2,1)S(1)}, bf16[64,4096]{1,0:T(8,128)(2,1)S(1)}, u32[]{:S(2)}, u32[]{:S(2)}) collective-permute-start(bf16[64,4096]{1,0:T(8,128)(2,1)S(1)} %add_convert_fusion), channel_id=1, source_target_pairs={{0,16},{1,17},{2,18},{3,19},{4,20},{5,21},{6,22},{7,23},{8,9},{9,8... | collective-permute-start | bytes 1572872 | tf_op jit(solution)/shard_map/ppermute | solution.py:86
  76.3 23.5 %collective-permute-start.16 = (bf16[64,4096]{1,0:T(8,128)(2,1)S(1)}, bf16[64,4096]{1,0:T(8,128)(2,1)S(1)}, u32[]{:S(2)}, u32[]{:S(2)}) collective-permute-start(bf16[64,4096]{1,0:T(8,128)(2,1)S(1)} %add_convert_fusion.1), channel_id=1, source_target_pairs={{0,16},{1,17},{2,18},{3,19},{4,20},{5,21},{6,22},{7,23},{8,9},{9,8... | collective-permute-start | bytes 1572872 | tf_op jit(solution)/shard_map/ppermute | solution.py:86
  83.0 18.7 %collective-permute-start.7 = (bf16[32,4096]{1,0:T(8,128)(2,1)S(1)}, bf16[32,4096]{1,0:T(8,128)(2,1)S(1)}, u32[]{:S(2)}, u32[]{:S(2)}) collective-permute-start(bf16[32,4096]{1,0:T(8,128)(2,1)S(1)} %add_convert_fusion.5), channel_id=1, source_target_pairs={{0,1},{1,0},{2,3},{3,2},{4,5},{5,4},{6,7},{7,6},{8,24},{9,25},{10,... | collective-permute-start | bytes 786440 | tf_op jit(solution)/shard_map/ppermute | solution.py:86
  91.4 10.4 %collective-permute-start.27 = (bf16[32,4096]{1,0:T(8,128)(2,1)S(1)}, bf16[32,4096]{1,0:T(8,128)(2,1)S(1)}, u32[]{:S(2)}, u32[]{:S(2)}) collective-permute-start(bf16[32,4096]{1,0:T(8,128)(2,1)S(1)} %add_convert_fusion.3), channel_id=1, source_target_pairs={{0,1},{1,0},{2,3},{3,2},{4,5},{5,4},{6,7},{7,6},{8,24},{9,25},{10,... | collective-permute-start | bytes 786440 | tf_op jit(solution)/shard_map/ppermute | solution.py:86
  99.9 6.4 %collective-permute-start.17 = (bf16[32,4096]{1,0:T(8,128)(2,1)S(1)}, bf16[32,4096]{1,0:T(8,128)(2,1)S(1)}, u32[]{:S(2)}, u32[]{:S(2)}) collective-permute-start(bf16[32,4096]{1,0:T(8,128)(2,1)S(1)} %add_convert_fusion.4), channel_id=1, source_target_pairs={{0,1},{1,0},{2,3},{3,2},{4,5},{5,4},{6,7},{7,6},{8,24},{9,25},{10,... | collective-permute-start | bytes 786440 | tf_op jit(solution)/shard_map/ppermute | solution.py:86
  101.8 5.5 %collective-permute-start.8 = (bf16[16,4096]{1,0:T(8,128)(2,1)S(1)}, bf16[16,4096]{1,0:T(8,128)(2,1)S(1)}, u32[]{:S(2)}, u32[]{:S(2)}) collective-permute-start(bf16[16,4096]{1,0:T(8,128)(2,1)S(1)} %add_convert_fusion.8), channel_id=1, source_target_pairs={{0,2},{1,3},{2,0},{3,1},{4,6},{5,7},{6,4},{7,5},{8,10},{9,11},{10,... | collective-permute-start | bytes 393224 | tf_op jit(solution)/shard_map/ppermute | solution.py:86
  101.9 9.1 %collective-permute-start.28 = (bf16[16,4096]{1,0:T(8,128)(2,1)S(1)}, bf16[16,4096]{1,0:T(8,128)(2,1)S(1)}, u32[]{:S(2)}, u32[]{:S(2)}) collective-permute-start(bf16[16,4096]{1,0:T(8,128)(2,1)S(1)} %add_convert_fusion.6), channel_id=1, source_target_pairs={{0,2},{1,3},{2,0},{3,1},{4,6},{5,7},{6,4},{7,5},{8,10},{9,11},{10,... | collective-permute-start | bytes 393224 | tf_op jit(solution)/shard_map/ppermute | solution.py:86
  106.4 6.6 %collective-permute-start.18 = (bf16[16,4096]{1,0:T(8,128)(2,1)S(1)}, bf16[16,4096]{1,0:T(8,128)(2,1)S(1)}, u32[]{:S(2)}, u32[]{:S(2)}) collective-permute-start(bf16[16,4096]{1,0:T(8,128)(2,1)S(1)} %add_convert_fusion.7), channel_id=1, source_target_pairs={{0,2},{1,3},{2,0},{3,1},{4,6},{5,7},{6,4},{7,5},{8,10},{9,11},{10,... | collective-permute-start | bytes 393224 | tf_op jit(solution)/shard_map/ppermute | solution.py:86
  107.3 7.1 %collective-permute-start.9 = (bf16[8,4096]{1,0:T(8,128)(2,1)S(1)}, bf16[8,4096]{1,0:T(8,128)(2,1)S(1)}, u32[]{:S(2)}, u32[]{:S(2)}) collective-permute-start(bf16[8,4096]{1,0:T(8,128)(2,1)S(1)} %add_convert_fusion.14), channel_id=1, source_target_pairs={{0,4},{1,5},{2,6},{3,7},{4,0},{5,1},{6,2},{7,3},{8,12},{9,13},{10,... | collective-permute-start | bytes 196616 | tf_op jit(solution)/shard_map/ppermute | solution.py:86
  111.0 6.0 %collective-permute-start.29 = (bf16[8,4096]{1,0:T(8,128)(2,1)S(1)}, bf16[8,4096]{1,0:T(8,128)(2,1)S(1)}, u32[]{:S(2)}, u32[]{:S(2)}) collective-permute-start(bf16[8,4096]{1,0:T(8,128)(2,1)S(1)} %add_convert_fusion.10), channel_id=1, source_target_pairs={{0,4},{1,5},{2,6},{3,7},{4,0},{5,1},{6,2},{7,3},{8,12},{9,13},{10,... | collective-permute-start | bytes 196616 | tf_op jit(solution)/shard_map/ppermute | solution.py:86
  113.1 5.2 %collective-permute-start.19 = (bf16[8,4096]{1,0:T(8,128)(2,1)S(1)}, bf16[8,4096]{1,0:T(8,128)(2,1)S(1)}, u32[]{:S(2)}, u32[]{:S(2)}) collective-permute-start(bf16[8,4096]{1,0:T(8,128)(2,1)S(1)} %add_convert_fusion.12), channel_id=1, source_target_pairs={{0,4},{1,5},{2,6},{3,7},{4,0},{5,1},{6,2},{7,3},{8,12},{9,13},{10,... | collective-permute-start | bytes 196616 | tf_op jit(solution)/shard_map/ppermute | solution.py:86

commit v5 on v4

--- a/solution.py
+++ b/solution.py
@@ -195,18 +195,23 @@
     return sum(term.astype(jnp.float32) for term in terms).astype(jnp.bfloat16)
 
 
-def gather_and_serve(own, moves, serve):
+def gather_and_serve(own, moves, serve, after):
     rows = own.shape[0]
     held = own
+    marks = []
+    if after is not None:
+        held, _ = lax.optimization_barrier((held, after))
     for move in moves:
-        held = jnp.concatenate([held, permute(held, move)])
+        got = permute(held, move)
+        marks.append(got)
+        held = jnp.concatenate([held, got])
     out, out_sib = serve(held, permute(held, to_sibling))
     terms = [out, permute(out_sib, to_sibling)]
     for move in moves[::-1]:
         half = terms[-1].shape[0] // 2
         sent = total(*[term[half : 2 * half] for term in terms])
         terms.append(permute(sent, move))
-    return total(*[term[:rows] for term in terms])
+    return total(*[term[:rows] for term in terms]), marks[2]
 
 
 def dense(tokens, expert_ids, route_weight, slot_of, swap_flag, w_gate, w_up, w_down):
@@ -218,10 +223,12 @@
     step = ROWS_AT_ONCE if tok_rows % ROWS_AT_ONCE == 0 else tok_rows
     extra = choices(expert_ids, route_weight)
     outs = []
+    after = None
     for at in range(0, tok_rows, step):
         own = jnp.concatenate([tokens[at : at + step], extra[at : at + step]], axis=1)
         serve = lambda held, sib: serve_rows(held, sib, mine, top_count, w_gate[0], w_up[0], w_down[0])
-        outs.append(gather_and_serve(own, moves, serve))
+        out, after = gather_and_serve(own, moves, serve, after)
+        outs.append(out)
     return jnp.concatenate(outs)
 
 

time: 120 us -> 131 us (1.092)
  waiting for transfers between devices: 42.1 us -> 61.2 us
  other arithmetic: 11.5 us -> 4.9 us
  local copies, waits for them, and re-layouts: 3.93 us -> 2.17 us
  starting transfers between devices: 41.1 us -> 42.5 us
    ppermute x30, waiting for transfers between devices: 42.1 us -> 61.2 us  [permute(): return lax.ppermute(value, AXES, pairs)]
    concatenate x9, other arithmetic: 5.58 us -> 0.23 us  [gather_and_serve(): held = jnp.concatenate([held, got])]
    concatenate x3 -> x2, other arithmetic: 1.92 us -> 0.02 us  [dense(): own = jnp.concatenate([tokens[at:at + step], extra[at:at + step]], axis=1)]
    unnamed x16, local copies, waits for them, and re-layouts: 2.7 us -> 0.94 us
    ppermute x30, starting transfers between devices: 41.1 us -> 42.5 us  [permute(): return lax.ppermute(value, AXES, pairs)]
  transfers between devices with their start and end apart: 30 -> 30, of which waited for: 16 -> 18; matrix products, arithmetic and copies ran while one was open for 9% -> 2% of each run, Pallas kernels for 16% -> 15%
where the time goes in v5:
time: 131 us
  waiting for transfers between devices  61.2 us (47%)
  starting transfers between devices  42.5 us (32%)
  Pallas kernels  19.4 us (15%)
  other arithmetic  4.9 us (4%)
  local copies, waits for them, and re-layouts  2.17 us (2%)
    ppermute x30, waiting for transfers between devices, permute(): return lax.ppermute(value, AXES, pairs)  61.2 us
    ppermute x30, starting transfers between devices, permute(): return lax.ppermute(value, AXES, pairs)  42.5 us
    pallas_call x3, Pallas kernels, serve_rows(): pl.pallas_call(functools.partial(serve_kernel, top_count), out_shape=(out...  19.4 us
  transfers between devices with their start and end apart: 30, of which 18 were waited for; matrix products, arithmetic and copies ran while one was open for 2% of the time, Pallas kernels for 15%

profile of v5, /device:TPU:0, one launch (start us, length us, event | category | flops | bytes accessed | tf_op | source)
XLA Modules:
  0.0 131.1 jit_solution(12571915864278352381)
XLA Ops:
  0.0 0.7 reduce_precision.9
  0.7 0.8 copy.13
  1.4 0.1 copy.12
  1.5 0.7 convert_element_type.239
  2.2 0.1 copy.15
  2.3 0.1 fusion.8
  2.4 0.9 fusion.10
  3.3 4.1 %collective-permute-start = (bf16[8,4224]{1,0:T(8,128)(2,1)S(1)}, bf16[8,4224]{1,0:T(8,128)(2,1)S(1)}, u32[]{:S(2)}, u32[]{:S(2)}) collective-permute-start(bf16[8,4224]{1,0:T(8,128)(2,1)S(1)} %get-tuple-element.25), channel_id=1, source_target_pairs={{0,4},{1,5},{2,6},{3,7},{4,0},{5,1},{6,2},{7,3},{8,12},{9,13},{10,... | collective-permute-start | bytes 202760 | tf_op jit(solution)/shard_map/ppermute | solution.py:86
  8.1 1.3 %fusion.9 = s32[]{:T(128)} fusion(s32[16,2]{0,1:T(2,128)} %param.11, s32[]{:T(128)S(6)} %add.140), kind=kLoop, calls=%fused_computation.56 | loop fusion | flops 95 | bytes 136 | tf_op jit(solution)/shard_map/reduce_sum | solution.py:77
  9.5 1.7 %collective-permute-done = bf16[8,4224]{1,0:T(8,128)(2,1)S(1)} collective-permute-done((bf16[8,4224]{1,0:T(8,128)(2,1)S(1)}, bf16[8,4224]{1,0:T(8,128)(2,1)S(1)}, u32[]{:S(2)}, u32[]{:S(2)}) %collective-permute-start) | collective-permute-done | bytes 67616 | tf_op jit(solution)/shard_map/ppermute | solution.py:86
  11.2 0.7 collective-permute-start.1
  11.8 4.4 %collective-permute-done.1 = bf16[16,4224]{1,0:T(8,128)(2,1)S(1)} collective-permute-done((bf16[16,4224]{1,0:T(8,128)(2,1)S(1)}, bf16[16,4224]{1,0:T(8,128)(2,1)S(1)}, u32[]{:S(2)}, u32[]{:S(2)}) %collective-permute-start.1) | collective-permute-done | bytes 135200 | tf_op jit(solution)/shard_map/ppermute | solution.py:86
  16.3 1.8 %collective-permute-start.2 = (bf16[32,4224]{1,0:T(8,128)(2,1)S(1)}, bf16[32,4224]{1,0:T(8,128)(2,1)S(1)}, u32[]{:S(2)}, u32[]{:S(2)}) collective-permute-start(bf16[32,4224]{1,0:T(8,128)(2,1)S(1)} %pad_maximum_fusion.3), channel_id=1, source_target_pairs={{0,1},{1,0},{2,3},{3,2},{4,5},{5,4},{6,7},{7,6},{8,24},{9,25},{10,... | collective-permute-start | bytes 811016 | tf_op jit(solution)/shard_map/ppermute | solution.py:86
  18.1 4.7 %collective-permute-done.2 = bf16[32,4224]{1,0:T(8,128)(2,1)S(1)} collective-permute-done((bf16[32,4224]{1,0:T(8,128)(2,1)S(1)}, bf16[32,4224]{1,0:T(8,128)(2,1)S(1)}, u32[]{:S(2)}, u32[]{:S(2)}) %collective-permute-start.2) | collective-permute-done | bytes 270368 | tf_op jit(solution)/shard_map/ppermute | solution.py:86
  22.8 2.4 %collective-permute-start.10 = (bf16[8,4224]{1,0:T(8,128)(2,1)S(1)}, bf16[8,4224]{1,0:T(8,128)(2,1)S(1)}, u32[]{:S(2)}, u32[]{:S(2)}) collective-permute-start(bf16[8,4224]{1,0:T(8,128)(2,1)S(1)} %pad_maximum_fusion.11), channel_id=1, source_target_pairs={{0,4},{1,5},{2,6},{3,7},{4,0},{5,1},{6,2},{7,3},{8,12},{9,13},{10,... | collective-permute-start | bytes 202760 | tf_op jit(solution)/shard_map/ppermute | solution.py:86
  25.2 1.6 %collective-permute-start.3 = (bf16[64,4224]{1,0:T(8,128)(2,1)S(1)}, bf16[64,4224]{1,0:T(8,128)(2,1)S(1)}, u32[]{:S(2)}, u32[]{:S(2)}) collective-permute-start(bf16[64,4224]{1,0:T(8,128)(2,1)S(1)} %pad_maximum_fusion), channel_id=1, source_target_pairs={{0,16},{1,17},{2,18},{3,19},{4,20},{5,21},{6,22},{7,23},{8,9},{9,8... | collective-permute-start | bytes 1622024 | tf_op jit(solution)/shard_map/ppermute | solution.py:86
  26.8 1.2 collective-permute-done.10
  28.1 1.3 collective-permute-start.11
  29.4 3.8 %collective-permute-done.11 = bf16[16,4224]{1,0:T(8,128)(2,1)S(1)} collective-permute-done((bf16[16,4224]{1,0:T(8,128)(2,1)S(1)}, bf16[16,4224]{1,0:T(8,128)(2,1)S(1)}, u32[]{:S(2)}, u32[]{:S(2)}) %collective-permute-start.11) | collective-permute-done | bytes 135200 | tf_op jit(solution)/shard_map/ppermute | solution.py:86
  33.2 2.6 %collective-permute-start.12 = (bf16[32,4224]{1,0:T(8,128)(2,1)S(1)}, bf16[32,4224]{1,0:T(8,128)(2,1)S(1)}, u32[]{:S(2)}, u32[]{:S(2)}) collective-permute-start(bf16[32,4224]{1,0:T(8,128)(2,1)S(1)} %pad_maximum_fusion.4), channel_id=1, source_target_pairs={{0,1},{1,0},{2,3},{3,2},{4,5},{5,4},{6,7},{7,6},{8,24},{9,25},{10,... | collective-permute-start | bytes 811016 | tf_op jit(solution)/shard_map/ppermute | solution.py:86
  35.7 4.5 %collective-permute-done.12 = bf16[32,4224]{1,0:T(8,128)(2,1)S(1)} collective-permute-done((bf16[32,4224]{1,0:T(8,128)(2,1)S(1)}, bf16[32,4224]{1,0:T(8,128)(2,1)S(1)}, u32[]{:S(2)}, u32[]{:S(2)}) %collective-permute-start.12) | collective-permute-done | bytes 270368 | tf_op jit(solution)/shard_map/ppermute | solution.py:86
  40.3 2.5 %collective-permute-start.13 = (bf16[64,4224]{1,0:T(8,128)(2,1)S(1)}, bf16[64,4224]{1,0:T(8,128)(2,1)S(1)}, u32[]{:S(2)}, u32[]{:S(2)}) collective-permute-start(bf16[64,4224]{1,0:T(8,128)(2,1)S(1)} %pad_maximum_fusion.1), channel_id=1, source_target_pairs={{0,16},{1,17},{2,18},{3,19},{4,20},{5,21},{6,22},{7,23},{8,9},{9,8... | collective-permute-start | bytes 1622024 | tf_op jit(solution)/shard_map/ppermute | solution.py:86
  42.8 2.7 %collective-permute-start.20 = (bf16[8,4224]{1,0:T(8,128)(2,1)S(1)}, bf16[8,4224]{1,0:T(8,128)(2,1)S(1)}, u32[]{:S(2)}, u32[]{:S(2)}) collective-permute-start(bf16[8,4224]{1,0:T(8,128)(2,1)S(1)} %pad_maximum_fusion.12), channel_id=1, source_target_pairs={{0,4},{1,5},{2,6},{3,7},{4,0},{5,1},{6,2},{7,3},{8,12},{9,13},{10,... | collective-permute-start | bytes 202760 | tf_op jit(solution)/shard_map/ppermute | solution.py:86
  45.6 0.1 collective-permute-start.4
  45.6 2.3 %collective-permute-done.20 = bf16[8,4224]{1,0:T(8,128)(2,1)S(1)} collective-permute-done((bf16[8,4224]{1,0:T(8,128)(2,1)S(1)}, bf16[8,4224]{1,0:T(8,128)(2,1)S(1)}, u32[]{:S(2)}, u32[]{:S(2)}) %collective-permute-start.20) | collective-permute-done | bytes 67616 | tf_op jit(solution)/shard_map/ppermute | solution.py:86
  48.0 2.9 %collective-permute-start.21 = (bf16[16,4224]{1,0:T(8,128)(2,1)S(1)}, bf16[16,4224]{1,0:T(8,128)(2,1)S(1)}, u32[]{:S(2)}, u32[]{:S(2)}) collective-permute-start(bf16[16,4224]{1,0:T(8,128)(2,1)S(1)} %pad_maximum_fusion.9), channel_id=1, source_target_pairs={{0,2},{1,3},{2,0},{3,1},{4,6},{5,7},{6,4},{7,5},{8,10},{9,11},{10,... | collective-permute-start | bytes 405512 | tf_op jit(solution)/shard_map/ppermute | solution.py:86
  50.8 3.0 %collective-permute-done.21 = bf16[16,4224]{1,0:T(8,128)(2,1)S(1)} collective-permute-done((bf16[16,4224]{1,0:T(8,128)(2,1)S(1)}, bf16[16,4224]{1,0:T(8,128)(2,1)S(1)}, u32[]{:S(2)}, u32[]{:S(2)}) %collective-permute-start.21) | collective-permute-done | bytes 135200 | tf_op jit(solution)/shard_map/ppermute | solution.py:86
  53.9 1.6 %collective-permute-start.22 = (bf16[32,4224]{1,0:T(8,128)(2,1)S(1)}, bf16[32,4224]{1,0:T(8,128)(2,1)S(1)}, u32[]{:S(2)}, u32[]{:S(2)}) collective-permute-start(bf16[32,4224]{1,0:T(8,128)(2,1)S(1)} %pad_maximum_fusion.5), channel_id=1, source_target_pairs={{0,1},{1,0},{2,3},{3,2},{4,5},{5,4},{6,7},{7,6},{8,24},{9,25},{10,... | collective-permute-start | bytes 811016 | tf_op jit(solution)/shard_map/ppermute | solution.py:86
  55.5 6.4 %collective-permute-done.22 = bf16[32,4224]{1,0:T(8,128)(2,1)S(1)} collective-permute-done((bf16[32,4224]{1,0:T(8,128)(2,1)S(1)}, bf16[32,4224]{1,0:T(8,128)(2,1)S(1)}, u32[]{:S(2)}, u32[]{:S(2)}) %collective-permute-start.22) | collective-permute-done | bytes 270368 | tf_op jit(solution)/shard_map/ppermute | solution.py:86
  61.9 0.3 collective-permute-start.23
  62.2 6.5 %serve_rows.3 = (bf16[128,4096]{1,0:T(8,128)(2,1)S(1)}, bf16[128,4096]{1,0:T(8,128)(2,1)S(1)}) custom-call(s32[1]{0:T(128)} %bitcast.1.mine, bf16[128,4224]{1,0:T(8,128)(2,1)S(1)} %constant_dynamic-update-slice_fusion.own, bf16[128,4224]{1,0:T(8,128)(2,1)S(1)} %collective-permute-done.4.sib, bf16[4096,512]{1,0:T(8,128)(2,1)S(1)} %bitcast.5, ...), custom_call_target="tpu_custom_call" | custom-call | flops 3221225472 | bytes 16777216 | tf_op jit(solution)/shard_map/serve_rows/pallas_call | solution.py:172
  68.7 0.1 collective-permute-start.5
  68.8 0.6 collective-permute-start.14
  69.4 2.0 %collective-permute-done.5 = bf16[128,4096]{1,0:T(8,128)(2,1)S(1)} collective-permute-done((bf16[128,4096]{1,0:T(8,128)(2,1)S(1)}, bf16[128,4096]{1,0:T(8,128)(2,1)S(1)}, u32[]{:S(2)}, u32[]{:S(2)}) %collective-permute-start.5) | collective-permute-done | bytes 1048608 | tf_op jit(solution)/shard_map/ppermute | solution.py:86
  71.4 0.1 add_convert_fusion.2
  71.5 1.9 %collective-permute-start.6 = (bf16[64,4096]{1,0:T(8,128)(2,1)S(1)}, bf16[64,4096]{1,0:T(8,128)(2,1)S(1)}, u32[]{:S(2)}, u32[]{:S(2)}) collective-permute-start(bf16[64,4096]{1,0:T(8,128)(2,1)S(1)} %add_convert_fusion.2), channel_id=1, source_target_pairs={{0,16},{1,17},{2,18},{3,19},{4,20},{5,21},{6,22},{7,23},{8,9},{9,8... | collective-permute-start | bytes 1572872 | tf_op jit(solution)/shard_map/ppermute | solution.py:86
  73.4 0.1 collective-permute-start.24
  73.5 6.5 %serve_rows.4 = (bf16[128,4096]{1,0:T(8,128)(2,1)S(1)}, bf16[128,4096]{1,0:T(8,128)(2,1)S(1)}) custom-call(s32[1]{0:T(128)} %bitcast.1.mine, bf16[128,4224]{1,0:T(8,128)(2,1)S(1)} %constant_dynamic-update-slice_fusion.5.own, bf16[128,4224]{1,0:T(8,128)(2,1)S(1)} %collective-permute-done.14.sib, bf16[4096,512]{1,0:T(8,128)(2,1)S(1)} %bitcast.6, ...), custom_call_target="tpu_custom_call" | custom-call | flops 3221225472 | bytes 16777216 | tf_op jit(solution)/shard_map/serve_rows/pallas_call | solution.py:172
  80.0 0.6 collective-permute-start.15
  80.5 0.2 collective-permute-done.6
  80.8 0.1 add_convert_fusion.5
  80.9 1.6 %collective-permute-start.7 = (bf16[32,4096]{1,0:T(8,128)(2,1)S(1)}, bf16[32,4096]{1,0:T(8,128)(2,1)S(1)}, u32[]{:S(2)}, u32[]{:S(2)}) collective-permute-start(bf16[32,4096]{1,0:T(8,128)(2,1)S(1)} %add_convert_fusion.5), channel_id=1, source_target_pairs={{0,1},{1,0},{2,3},{3,2},{4,5},{5,4},{6,7},{7,6},{8,24},{9,25},{10,... | collective-permute-start | bytes 786440 | tf_op jit(solution)/shard_map/ppermute | solution.py:86
  82.5 6.5 %serve_rows.5 = (bf16[128,4096]{1,0:T(8,128)(2,1)S(1)}, bf16[128,4096]{1,0:T(8,128)(2,1)S(1)}) custom-call(s32[1]{0:T(128)} %bitcast.1.mine, bf16[128,4224]{1,0:T(8,128)(2,1)S(1)} %constant_dynamic-update-slice_fusion.10.own, bf16[128,4224]{1,0:T(8,128)(2,1)S(1)} %collective-permute-done.24.sib, bf16[4096,512]{1,0:T(8,128)(2,1)S(1)} %bitcast.7, ...), custom_call_target="tpu_custom_call" | custom-call | flops 3221225472 | bytes 16777216 | tf_op jit(solution)/shard_map/serve_rows/pallas_call | solution.py:172
  89.1 2.7 %collective-permute-start.8 = (bf16[16,4096]{1,0:T(8,128)(2,1)S(1)}, bf16[16,4096]{1,0:T(8,128)(2,1)S(1)}, u32[]{:S(2)}, u32[]{:S(2)}) collective-permute-start(bf16[16,4096]{1,0:T(8,128)(2,1)S(1)} %add_convert_fusion.8), channel_id=1, source_target_pairs={{0,2},{1,3},{2,0},{3,1},{4,6},{5,7},{6,4},{7,5},{8,10},{9,11},{10,... | collective-permute-start | bytes 393224 | tf_op jit(solution)/shard_map/ppermute | solution.py:86
  91.8 0.1 add_convert_fusion.1
  91.9 1.5 %collective-permute-start.16 = (bf16[64,4096]{1,0:T(8,128)(2,1)S(1)}, bf16[64,4096]{1,0:T(8,128)(2,1)S(1)}, u32[]{:S(2)}, u32[]{:S(2)}) collective-permute-start(bf16[64,4096]{1,0:T(8,128)(2,1)S(1)} %add_convert_fusion.1), channel_id=1, source_target_pairs={{0,16},{1,17},{2,18},{3,19},{4,20},{5,21},{6,22},{7,23},{8,9},{9,8... | collective-permute-start | bytes 1572872 | tf_op jit(solution)/shard_map/ppermute | solution.py:86
  93.5 2.5 %collective-permute-done.8 = bf16[16,4096]{1,0:T(8,128)(2,1)S(1)} collective-permute-done((bf16[16,4096]{1,0:T(8,128)(2,1)S(1)}, bf16[16,4096]{1,0:T(8,128)(2,1)S(1)}, u32[]{:S(2)}, u32[]{:S(2)}) %collective-permute-start.8) | collective-permute-done | bytes 131104 | tf_op jit(solution)/shard_map/ppermute | solution.py:86
  96.0 3.4 %collective-permute-start.9 = (bf16[8,4096]{1,0:T(8,128)(2,1)S(1)}, bf16[8,4096]{1,0:T(8,128)(2,1)S(1)}, u32[]{:S(2)}, u32[]{:S(2)}) collective-permute-start(bf16[8,4096]{1,0:T(8,128)(2,1)S(1)} %add_convert_fusion.14), channel_id=1, source_target_pairs={{0,4},{1,5},{2,6},{3,7},{4,0},{5,1},{6,2},{7,3},{8,12},{9,13},{10,... | collective-permute-start | bytes 196616 | tf_op jit(solution)/shard_map/ppermute | solution.py:86
  99.4 0.1 add_convert_fusion
  99.5 1.8 %collective-permute-start.26 = (bf16[64,4096]{1,0:T(8,128)(2,1)S(1)}, bf16[64,4096]{1,0:T(8,128)(2,1)S(1)}, u32[]{:S(2)}, u32[]{:S(2)}) collective-permute-start(bf16[64,4096]{1,0:T(8,128)(2,1)S(1)} %add_convert_fusion), channel_id=1, source_target_pairs={{0,16},{1,17},{2,18},{3,19},{4,20},{5,21},{6,22},{7,23},{8,9},{9,8... | collective-permute-start | bytes 1572872 | tf_op jit(solution)/shard_map/ppermute | solution.py:86
  101.3 1.8 %collective-permute-done.9 = bf16[8,4096]{1,0:T(8,128)(2,1)S(1)} collective-permute-done((bf16[8,4096]{1,0:T(8,128)(2,1)S(1)}, bf16[8,4096]{1,0:T(8,128)(2,1)S(1)}, u32[]{:S(2)}, u32[]{:S(2)}) %collective-permute-start.9) | collective-permute-done | bytes 65568 | tf_op jit(solution)/shard_map/ppermute | solution.py:86
  103.1 0.1 add_convert_fusion.4
  103.2 0.6 collective-permute-start.17
  103.8 8.5 %collective-permute-done.26 = bf16[64,4096]{1,0:T(8,128)(2,1)S(1)} collective-permute-done((bf16[64,4096]{1,0:T(8,128)(2,1)S(1)}, bf16[64,4096]{1,0:T(8,128)(2,1)S(1)}, u32[]{:S(2)}, u32[]{:S(2)}) %collective-permute-start.26) | collective-permute-done | bytes 524320 | tf_op jit(solution)/shard_map/ppermute | solution.py:86
  112.3 0.1 add_convert_fusion.3
  112.4 0.6 collective-permute-start.27
  113.1 1.1 collective-permute-start.18
  114.2 4.7 %collective-permute-done.27 = bf16[32,4096]{1,0:T(8,128)(2,1)S(1)} collective-permute-done((bf16[32,4096]{1,0:T(8,128)(2,1)S(1)}, bf16[32,4096]{1,0:T(8,128)(2,1)S(1)}, u32[]{:S(2)}, u32[]{:S(2)}) %collective-permute-start.27) | collective-permute-done | bytes 262176 | tf_op jit(solution)/shard_map/ppermute | solution.py:86
  118.9 1.1 collective-permute-start.28
  120.1 4.6 %collective-permute-done.28 = bf16[16,4096]{1,0:T(8,128)(2,1)S(1)} collective-permute-done((bf16[16,4096]{1,0:T(8,128)(2,1)S(1)}, bf16[16,4096]{1,0:T(8,128)(2,1)S(1)}, u32[]{:S(2)}, u32[]{:S(2)}) %collective-permute-start.28) | collective-permute-done | bytes 131104 | tf_op jit(solution)/shard_map/ppermute | solution.py:86
  124.7 0.6 collective-permute-start.29
  125.3 0.8 collective-permute-done.19
  126.1 4.2 %collective-permute-done.29 = bf16[8,4096]{1,0:T(8,128)(2,1)S(1)} collective-permute-done((bf16[8,4096]{1,0:T(8,128)(2,1)S(1)}, bf16[8,4096]{1,0:T(8,128)(2,1)S(1)}, u32[]{:S(2)}, u32[]{:S(2)}) %collective-permute-start.29) | collective-permute-done | bytes 65568 | tf_op jit(solution)/shard_map/ppermute | solution.py:86
  130.4 0.7 pad_maximum_fusion.6
  (55 shorter events, 1.3 us)
Async XLA Ops:
  3.3 7.8 %collective-permute-start = (bf16[8,4224]{1,0:T(8,128)(2,1)S(1)}, bf16[8,4224]{1,0:T(8,128)(2,1)S(1)}, u32[]{:S(2)}, u32[]{:S(2)}) collective-permute-start(bf16[8,4224]{1,0:T(8,128)(2,1)S(1)} %get-tuple-element.25), channel_id=1, source_target_pairs={{0,4},{1,5},{2,6},{3,7},{4,0},{5,1},{6,2},{7,3},{8,12},{9,13},{10,... | collective-permute-start | bytes 202760 | tf_op jit(solution)/shard_map/ppermute | solution.py:86
  11.2 5.1 %collective-permute-start.1 = (bf16[16,4224]{1,0:T(8,128)(2,1)S(1)}, bf16[16,4224]{1,0:T(8,128)(2,1)S(1)}, u32[]{:S(2)}, u32[]{:S(2)}) collective-permute-start(bf16[16,4224]{1,0:T(8,128)(2,1)S(1)} %pad_maximum_fusion.7), channel_id=1, source_target_pairs={{0,2},{1,3},{2,0},{3,1},{4,6},{5,7},{6,4},{7,5},{8,10},{9,11},{10,... | collective-permute-start | bytes 405512 | tf_op jit(solution)/shard_map/ppermute | solution.py:86
  16.3 45.9 %copy-start.1 = (bf16[1,4096,512]{2,1,0:T(8,128)(2,1)S(1)}, bf16[1,4096,512]{2,1,0:T(8,128)(2,1)}, u32[]{:S(2)}) copy-start(bf16[1,4096,512]{2,1,0:T(8,128)(2,1)} %param.14) | copy-start | bytes 12582916
  16.3 6.5 %collective-permute-start.2 = (bf16[32,4224]{1,0:T(8,128)(2,1)S(1)}, bf16[32,4224]{1,0:T(8,128)(2,1)S(1)}, u32[]{:S(2)}, u32[]{:S(2)}) collective-permute-start(bf16[32,4224]{1,0:T(8,128)(2,1)S(1)} %pad_maximum_fusion.3), channel_id=1, source_target_pairs={{0,1},{1,0},{2,3},{3,2},{4,5},{5,4},{6,7},{7,6},{8,24},{9,25},{10,... | collective-permute-start | bytes 811016 | tf_op jit(solution)/shard_map/ppermute | solution.py:86
  22.8 5.2 %collective-permute-start.10 = (bf16[8,4224]{1,0:T(8,128)(2,1)S(1)}, bf16[8,4224]{1,0:T(8,128)(2,1)S(1)}, u32[]{:S(2)}, u32[]{:S(2)}) collective-permute-start(bf16[8,4224]{1,0:T(8,128)(2,1)S(1)} %pad_maximum_fusion.11), channel_id=1, source_target_pairs={{0,4},{1,5},{2,6},{3,7},{4,0},{5,1},{6,2},{7,3},{8,12},{9,13},{10,... | collective-permute-start | bytes 202760 | tf_op jit(solution)/shard_map/ppermute | solution.py:86
  25.2 20.2 %collective-permute-start.3 = (bf16[64,4224]{1,0:T(8,128)(2,1)S(1)}, bf16[64,4224]{1,0:T(8,128)(2,1)S(1)}, u32[]{:S(2)}, u32[]{:S(2)}) collective-permute-start(bf16[64,4224]{1,0:T(8,128)(2,1)S(1)} %pad_maximum_fusion), channel_id=1, source_target_pairs={{0,16},{1,17},{2,18},{3,19},{4,20},{5,21},{6,22},{7,23},{8,9},{9,8... | collective-permute-start | bytes 1622024 | tf_op jit(solution)/shard_map/ppermute | solution.py:86
  28.1 5.1 %collective-permute-start.11 = (bf16[16,4224]{1,0:T(8,128)(2,1)S(1)}, bf16[16,4224]{1,0:T(8,128)(2,1)S(1)}, u32[]{:S(2)}, u32[]{:S(2)}) collective-permute-start(bf16[16,4224]{1,0:T(8,128)(2,1)S(1)} %pad_maximum_fusion.8), channel_id=1, source_target_pairs={{0,2},{1,3},{2,0},{3,1},{4,6},{5,7},{6,4},{7,5},{8,10},{9,11},{10,... | collective-permute-start | bytes 405512 | tf_op jit(solution)/shard_map/ppermute | solution.py:86
  33.2 7.0 %collective-permute-start.12 = (bf16[32,4224]{1,0:T(8,128)(2,1)S(1)}, bf16[32,4224]{1,0:T(8,128)(2,1)S(1)}, u32[]{:S(2)}, u32[]{:S(2)}) collective-permute-start(bf16[32,4224]{1,0:T(8,128)(2,1)S(1)} %pad_maximum_fusion.4), channel_id=1, source_target_pairs={{0,1},{1,0},{2,3},{3,2},{4,5},{5,4},{6,7},{7,6},{8,24},{9,25},{10,... | collective-permute-start | bytes 811016 | tf_op jit(solution)/shard_map/ppermute | solution.py:86
  40.2 22.0 %copy-start = (bf16[1,4096,512]{2,1,0:T(8,128)(2,1)S(1)}, bf16[1,4096,512]{2,1,0:T(8,128)(2,1)}, u32[]{:S(2)}) copy-start(bf16[1,4096,512]{2,1,0:T(8,128)(2,1)} %param.13) | copy-start | bytes 12582916
  40.3 28.5 %collective-permute-start.13 = (bf16[64,4224]{1,0:T(8,128)(2,1)S(1)}, bf16[64,4224]{1,0:T(8,128)(2,1)S(1)}, u32[]{:S(2)}, u32[]{:S(2)}) collective-permute-start(bf16[64,4224]{1,0:T(8,128)(2,1)S(1)} %pad_maximum_fusion.1), channel_id=1, source_target_pairs={{0,16},{1,17},{2,18},{3,19},{4,20},{5,21},{6,22},{7,23},{8,9},{9,8... | collective-permute-start | bytes 1622024 | tf_op jit(solution)/shard_map/ppermute | solution.py:86
  42.8 5.2 %collective-permute-start.20 = (bf16[8,4224]{1,0:T(8,128)(2,1)S(1)}, bf16[8,4224]{1,0:T(8,128)(2,1)S(1)}, u32[]{:S(2)}, u32[]{:S(2)}) collective-permute-start(bf16[8,4224]{1,0:T(8,128)(2,1)S(1)} %pad_maximum_fusion.12), channel_id=1, source_target_pairs={{0,4},{1,5},{2,6},{3,7},{4,0},{5,1},{6,2},{7,3},{8,12},{9,13},{10,... | collective-permute-start | bytes 202760 | tf_op jit(solution)/shard_map/ppermute | solution.py:86
  45.6 16.6 %collective-permute-start.4 = (bf16[128,4224]{1,0:T(8,128)(2,1)S(1)}, bf16[128,4224]{1,0:T(8,128)(2,1)S(1)}, u32[]{:S(2)}, u32[]{:S(2)}) collective-permute-start(bf16[128,4224]{1,0:T(8,128)(2,1)S(1)} %constant_dynamic-update-slice_fusion.own), channel_id=1, source_target_pairs={{0,8},{1,9},{2,10},{3,11},{4,12},{5,13},{6,14},{7,15},{8,0},{9,1},... | collective-permute-start | bytes 3244040 | tf_op jit(solution)/shard_map/ppermute | solution.py:86
  48.0 5.9 %collective-permute-start.21 = (bf16[16,4224]{1,0:T(8,128)(2,1)S(1)}, bf16[16,4224]{1,0:T(8,128)(2,1)S(1)}, u32[]{:S(2)}, u32[]{:S(2)}) collective-permute-start(bf16[16,4224]{1,0:T(8,128)(2,1)S(1)} %pad_maximum_fusion.9), channel_id=1, source_target_pairs={{0,2},{1,3},{2,0},{3,1},{4,6},{5,7},{6,4},{7,5},{8,10},{9,11},{10,... | collective-permute-start | bytes 405512 | tf_op jit(solution)/shard_map/ppermute | solution.py:86
  53.9 8.0 %collective-permute-start.22 = (bf16[32,4224]{1,0:T(8,128)(2,1)S(1)}, bf16[32,4224]{1,0:T(8,128)(2,1)S(1)}, u32[]{:S(2)}, u32[]{:S(2)}) collective-permute-start(bf16[32,4224]{1,0:T(8,128)(2,1)S(1)} %pad_maximum_fusion.5), channel_id=1, source_target_pairs={{0,1},{1,0},{2,3},{3,2},{4,5},{5,4},{6,7},{7,6},{8,24},{9,25},{10,... | collective-permute-start | bytes 811016 | tf_op jit(solution)/shard_map/ppermute | solution.py:86
  61.9 11.5 %collective-permute-start.23 = (bf16[64,4224]{1,0:T(8,128)(2,1)S(1)}, bf16[64,4224]{1,0:T(8,128)(2,1)S(1)}, u32[]{:S(2)}, u32[]{:S(2)}) collective-permute-start(bf16[64,4224]{1,0:T(8,128)(2,1)S(1)} %pad_maximum_fusion.2), channel_id=1, source_target_pairs={{0,16},{1,17},{2,18},{3,19},{4,20},{5,21},{6,22},{7,23},{8,9},{9,8... | collective-permute-start | bytes 1622024 | tf_op jit(solution)/shard_map/ppermute | solution.py:86
  68.7 2.7 %collective-permute-start.5 = (bf16[128,4096]{1,0:T(8,128)(2,1)S(1)}, bf16[128,4096]{1,0:T(8,128)(2,1)S(1)}, u32[]{:S(2)}, u32[]{:S(2)}) collective-permute-start(bf16[128,4096]{1,0:T(8,128)(2,1)S(1)} %get-tuple-element.14), channel_id=1, source_target_pairs={{0,8},{1,9},{2,10},{3,11},{4,12},{5,13},{6,14},{7,15},{8,0},{9,1},... | collective-permute-start | bytes 3145736 | tf_op jit(solution)/shard_map/ppermute | solution.py:86
  68.8 4.7 %collective-permute-start.14 = (bf16[128,4224]{1,0:T(8,128)(2,1)S(1)}, bf16[128,4224]{1,0:T(8,128)(2,1)S(1)}, u32[]{:S(2)}, u32[]{:S(2)}) collective-permute-start(bf16[128,4224]{1,0:T(8,128)(2,1)S(1)} %constant_dynamic-update-slice_fusion.5.own), channel_id=1, source_target_pairs={{0,8},{1,9},{2,10},{3,11},{4,12},{5,13},{6,14},{7,15},{8,0},{9,1},... | collective-permute-start | bytes 3244040 | tf_op jit(solution)/shard_map/ppermute | solution.py:86
  71.5 9.2 %collective-permute-start.6 = (bf16[64,4096]{1,0:T(8,128)(2,1)S(1)}, bf16[64,4096]{1,0:T(8,128)(2,1)S(1)}, u32[]{:S(2)}, u32[]{:S(2)}) collective-permute-start(bf16[64,4096]{1,0:T(8,128)(2,1)S(1)} %add_convert_fusion.2), channel_id=1, source_target_pairs={{0,16},{1,17},{2,18},{3,19},{4,20},{5,21},{6,22},{7,23},{8,9},{9,8... | collective-permute-start | bytes 1572872 | tf_op jit(solution)/shard_map/ppermute | solution.py:86
  73.4 9.0 %collective-permute-start.24 = (bf16[128,4224]{1,0:T(8,128)(2,1)S(1)}, bf16[128,4224]{1,0:T(8,128)(2,1)S(1)}, u32[]{:S(2)}, u32[]{:S(2)}) collective-permute-start(bf16[128,4224]{1,0:T(8,128)(2,1)S(1)} %constant_dynamic-update-slice_fusion.10.own), channel_id=1, source_target_pairs={{0,8},{1,9},{2,10},{3,11},{4,12},{5,13},{6,14},{7,15},{8,0},{9,1},... | collective-permute-start | bytes 3244040 | tf_op jit(solution)/shard_map/ppermute | solution.py:86
  80.0 11.8 %collective-permute-start.15 = (bf16[128,4096]{1,0:T(8,128)(2,1)S(1)}, bf16[128,4096]{1,0:T(8,128)(2,1)S(1)}, u32[]{:S(2)}, u32[]{:S(2)}) collective-permute-start(bf16[128,4096]{1,0:T(8,128)(2,1)S(1)} %get-tuple-element.17), channel_id=1, source_target_pairs={{0,8},{1,9},{2,10},{3,11},{4,12},{5,13},{6,14},{7,15},{8,0},{9,1},... | collective-permute-start | bytes 3145736 | tf_op jit(solution)/shard_map/ppermute | solution.py:86
  80.9 8.1 %collective-permute-start.7 = (bf16[32,4096]{1,0:T(8,128)(2,1)S(1)}, bf16[32,4096]{1,0:T(8,128)(2,1)S(1)}, u32[]{:S(2)}, u32[]{:S(2)}) collective-permute-start(bf16[32,4096]{1,0:T(8,128)(2,1)S(1)} %add_convert_fusion.5), channel_id=1, source_target_pairs={{0,1},{1,0},{2,3},{3,2},{4,5},{5,4},{6,7},{7,6},{8,24},{9,25},{10,... | collective-permute-start | bytes 786440 | tf_op jit(solution)/shard_map/ppermute | solution.py:86
  88.9 10.4 %collective-permute-start.25 = (bf16[128,4096]{1,0:T(8,128)(2,1)S(1)}, bf16[128,4096]{1,0:T(8,128)(2,1)S(1)}, u32[]{:S(2)}, u32[]{:S(2)}) collective-permute-start(bf16[128,4096]{1,0:T(8,128)(2,1)S(1)} %get-tuple-element.20), channel_id=1, source_target_pairs={{0,8},{1,9},{2,10},{3,11},{4,12},{5,13},{6,14},{7,15},{8,0},{9,1},... | collective-permute-start | bytes 3145736 | tf_op jit(solution)/shard_map/ppermute | solution.py:86
  89.1 6.9 %collective-permute-start.8 = (bf16[16,4096]{1,0:T(8,128)(2,1)S(1)}, bf16[16,4096]{1,0:T(8,128)(2,1)S(1)}, u32[]{:S(2)}, u32[]{:S(2)}) collective-permute-start(bf16[16,4096]{1,0:T(8,128)(2,1)S(1)} %add_convert_fusion.8), channel_id=1, source_target_pairs={{0,2},{1,3},{2,0},{3,1},{4,6},{5,7},{6,4},{7,5},{8,10},{9,11},{10,... | collective-permute-start | bytes 393224 | tf_op jit(solution)/shard_map/ppermute | solution.py:86
  91.9 11.1 %collective-permute-start.16 = (bf16[64,4096]{1,0:T(8,128)(2,1)S(1)}, bf16[64,4096]{1,0:T(8,128)(2,1)S(1)}, u32[]{:S(2)}, u32[]{:S(2)}) collective-permute-start(bf16[64,4096]{1,0:T(8,128)(2,1)S(1)} %add_convert_fusion.1), channel_id=1, source_target_pairs={{0,16},{1,17},{2,18},{3,19},{4,20},{5,21},{6,22},{7,23},{8,9},{9,8... | collective-permute-start | bytes 1572872 | tf_op jit(solution)/shard_map/ppermute | solution.py:86
  96.0 7.0 %collective-permute-start.9 = (bf16[8,4096]{1,0:T(8,128)(2,1)S(1)}, bf16[8,4096]{1,0:T(8,128)(2,1)S(1)}, u32[]{:S(2)}, u32[]{:S(2)}) collective-permute-start(bf16[8,4096]{1,0:T(8,128)(2,1)S(1)} %add_convert_fusion.14), channel_id=1, source_target_pairs={{0,4},{1,5},{2,6},{3,7},{4,0},{5,1},{6,2},{7,3},{8,12},{9,13},{10,... | collective-permute-start | bytes 196616 | tf_op jit(solution)/shard_map/ppermute | solution.py:86
  99.5 12.8 %collective-permute-start.26 = (bf16[64,4096]{1,0:T(8,128)(2,1)S(1)}, bf16[64,4096]{1,0:T(8,128)(2,1)S(1)}, u32[]{:S(2)}, u32[]{:S(2)}) collective-permute-start(bf16[64,4096]{1,0:T(8,128)(2,1)S(1)} %add_convert_fusion), channel_id=1, source_target_pairs={{0,16},{1,17},{2,18},{3,19},{4,20},{5,21},{6,22},{7,23},{8,9},{9,8... | collective-permute-start | bytes 1572872 | tf_op jit(solution)/shard_map/ppermute | solution.py:86
  103.2 9.8 %collective-permute-start.17 = (bf16[32,4096]{1,0:T(8,128)(2,1)S(1)}, bf16[32,4096]{1,0:T(8,128)(2,1)S(1)}, u32[]{:S(2)}, u32[]{:S(2)}) collective-permute-start(bf16[32,4096]{1,0:T(8,128)(2,1)S(1)} %add_convert_fusion.4), channel_id=1, source_target_pairs={{0,1},{1,0},{2,3},{3,2},{4,5},{5,4},{6,7},{7,6},{8,24},{9,25},{10,... | collective-permute-start | bytes 786440 | tf_op jit(solution)/shard_map/ppermute | solution.py:86
  112.4 6.4 %collective-permute-start.27 = (bf16[32,4096]{1,0:T(8,128)(2,1)S(1)}, bf16[32,4096]{1,0:T(8,128)(2,1)S(1)}, u32[]{:S(2)}, u32[]{:S(2)}) collective-permute-start(bf16[32,4096]{1,0:T(8,128)(2,1)S(1)} %add_convert_fusion.3), channel_id=1, source_target_pairs={{0,1},{1,0},{2,3},{3,2},{4,5},{5,4},{6,7},{7,6},{8,24},{9,25},{10,... | collective-permute-start | bytes 786440 | tf_op jit(solution)/shard_map/ppermute | solution.py:86
  113.1 6.9 %collective-permute-start.18 = (bf16[16,4096]{1,0:T(8,128)(2,1)S(1)}, bf16[16,4096]{1,0:T(8,128)(2,1)S(1)}, u32[]{:S(2)}, u32[]{:S(2)}) collective-permute-start(bf16[16,4096]{1,0:T(8,128)(2,1)S(1)} %add_convert_fusion.7), channel_id=1, source_target_pairs={{0,2},{1,3},{2,0},{3,1},{4,6},{5,7},{6,4},{7,5},{8,10},{9,11},{10,... | collective-permute-start | bytes 393224 | tf_op jit(solution)/shard_map/ppermute | solution.py:86
  118.9 5.8 %collective-permute-start.28 = (bf16[16,4096]{1,0:T(8,128)(2,1)S(1)}, bf16[16,4096]{1,0:T(8,128)(2,1)S(1)}, u32[]{:S(2)}, u32[]{:S(2)}) collective-permute-start(bf16[16,4096]{1,0:T(8,128)(2,1)S(1)} %add_convert_fusion.6), channel_id=1, source_target_pairs={{0,2},{1,3},{2,0},{3,1},{4,6},{5,7},{6,4},{7,5},{8,10},{9,11},{10,... | collective-permute-start | bytes 393224 | tf_op jit(solution)/shard_map/ppermute | solution.py:86
  120.0 6.1 %collective-permute-start.19 = (bf16[8,4096]{1,0:T(8,128)(2,1)S(1)}, bf16[8,4096]{1,0:T(8,128)(2,1)S(1)}, u32[]{:S(2)}, u32[]{:S(2)}) collective-permute-start(bf16[8,4096]{1,0:T(8,128)(2,1)S(1)} %add_convert_fusion.12), channel_id=1, source_target_pairs={{0,4},{1,5},{2,6},{3,7},{4,0},{5,1},{6,2},{7,3},{8,12},{9,13},{10,... | collective-permute-start | bytes 196616 | tf_op jit(solution)/shard_map/ppermute | solution.py:86
  124.7 5.6 %collective-permute-start.29 = (bf16[8,4096]{1,0:T(8,128)(2,1)S(1)}, bf16[8,4096]{1,0:T(8,128)(2,1)S(1)}, u32[]{:S(2)}, u32[]{:S(2)}) collective-permute-start(bf16[8,4096]{1,0:T(8,128)(2,1)S(1)} %add_convert_fusion.10), channel_id=1, source_target_pairs={{0,4},{1,5},{2,6},{3,7},{4,0},{5,1},{6,2},{7,3},{8,12},{9,13},{10,... | collective-permute-start | bytes 196616 | tf_op jit(solution)/shard_map/ppermute | solution.py:86

commit v6 on v4

--- a/solution.py
+++ b/solution.py
@@ -11,6 +11,7 @@
 LANES = 128
 PARTS = 4
 ROWS_AT_ONCE = 8
+ORDER = [0, 1, 0, 1, 0, 2, 1, 0, 2, 1, 0, 2, 0, 1, 2, 0, 1, 1, 2, 0, 1, 2, 2, 0, 2, 0, 1, 2, 0, 1, 2, 1, 2, 0, 1, 2]
 
 
 def partner(value, axis, distance):
@@ -195,18 +196,44 @@
     return sum(term.astype(jnp.float32) for term in terms).astype(jnp.bfloat16)
 
 
-def gather_and_serve(own, moves, serve):
+def chunk_steps(own, moves, serve):
     rows = own.shape[0]
-    held = own
+    (held,) = yield (own,)
     for move in moves:
-        held = jnp.concatenate([held, permute(held, move)])
-    out, out_sib = serve(held, permute(held, to_sibling))
-    terms = [out, permute(out_sib, to_sibling)]
+        (got,) = yield (permute(held, move),)
+        held = jnp.concatenate([held, got])
+    (sib,) = yield (permute(held, to_sibling),)
+    out, out_sib = yield serve(held, sib)
+    terms = [out]
+    (got,) = yield (permute(out_sib, to_sibling),)
     for move in moves[::-1]:
-        half = terms[-1].shape[0] // 2
+        terms.append(got)
+        half = got.shape[0] // 2
         sent = total(*[term[half : 2 * half] for term in terms])
-        terms.append(permute(sent, move))
+        (got,) = yield (permute(sent, move),)
+    terms.append(got)
     return total(*[term[:rows] for term in terms])
+
+
+def in_order(chunks, order):
+    waits = [next(chunk) for chunk in chunks]
+    results = [None] * len(chunks)
+    before = ()
+    for number in order:
+        count = len(waits[number])
+        ready = lax.optimization_barrier(waits[number] + before)[:count]
+        before = waits[number]
+        try:
+            waits[number] = chunks[number].send(ready)
+        except StopIteration as end:
+            results[number] = end.value
+    return results
+
+
+def step_order(chunk_count, step_count):
+    if chunk_count == 3 and step_count == len(ORDER) // 3:
+        return ORDER
+    return [number for _ in range(step_count) for number in range(chunk_count)]
 
 
 def dense(tokens, expert_ids, route_weight, slot_of, swap_flag, w_gate, w_up, w_down):
@@ -217,12 +244,12 @@
     moves = [along_line(2**bit) for bit in range(line_bits)][::-1] + [over_first, over_second]
     step = ROWS_AT_ONCE if tok_rows % ROWS_AT_ONCE == 0 else tok_rows
     extra = choices(expert_ids, route_weight)
-    outs = []
+    chunks = []
     for at in range(0, tok_rows, step):
         own = jnp.concatenate([tokens[at : at + step], extra[at : at + step]], axis=1)
         serve = lambda held, sib: serve_rows(held, sib, mine, top_count, w_gate[0], w_up[0], w_down[0])
-        outs.append(gather_and_serve(own, moves, serve))
-    return jnp.concatenate(outs)
+        chunks.append(chunk_steps(own, moves, serve))
+    return jnp.concatenate(in_order(chunks, step_order(len(chunks), 2 * len(moves) + 4)))
 
 
 def on_device(tokens, expert_ids, *rest):

time: 120 us -> 118 us (0.983)
  other arithmetic: 11.5 us -> 4.23 us
  starting transfers between devices: 41.1 us -> 46.9 us
    ppermute x30, starting transfers between devices: 41.1 us -> 46.9 us  [permute(): return lax.ppermute(value, AXES, pairs)]
    concatenate x10, other arithmetic: 6.27 us -> 0.94 us  [the longest x1 0.69 us: dense(): jnp.concatenate(in_order(chunks, step_order(len(chunks), 2 * len(moves) +...]
    concatenate x3, other arithmetic: 1.92 us -> 0.02 us  [dense(): own = jnp.concatenate([tokens[at:at + step], extra[at:at + step]], axis=1)]
    unnamed x16 -> x21, local copies, waits for them, and re-layouts: 2.7 us -> 3.14 us
  transfers between devices with their start and end apart: 30 -> 30, of which waited for: 16 -> 17; matrix products, arithmetic and copies ran while one was open for 9% -> 2% of each run, Pallas kernels for 16% -> 5%
where the time goes in v6:
time: 118 us
  starting transfers between devices  46.9 us (40%)
  waiting for transfers between devices  42.3 us (36%)
  Pallas kernels  19.4 us (16%)
  local copies, waits for them, and re-layouts  4.37 us (4%)
  other arithmetic  4.23 us (4%)
    ppermute x30, starting transfers between devices, permute(): return lax.ppermute(value, AXES, pairs)  46.9 us
    ppermute x30, waiting for transfers between devices, permute(): return lax.ppermute(value, AXES, pairs)  42.3 us
    pallas_call x3, Pallas kernels, serve_rows(): pl.pallas_call(functools.partial(serve_kernel, top_count), out_shape=(out...  19.4 us
    unnamed x21, local copies, waits for them, and re-layouts  3.14 us
  transfers between devices with their start and end apart: 30, of which 17 were waited for; matrix products, arithmetic and copies ran while one was open for 2% of the time, Pallas kernels for 5%

profile of v6, /device:TPU:0, one launch (start us, length us, event | category | flops | bytes accessed | tf_op | source)
XLA Modules:
  0.0 118.0 jit_solution(916051997480646798)
XLA Ops:
  0.0 0.7 reduce_precision.9
  0.7 0.8 copy.13
  1.5 0.1 copy.12
  1.5 0.7 convert_element_type.239
  2.2 0.1 copy.15
  2.3 0.1 fusion.8
  2.4 0.9 fusion.10
  3.4 4.1 %collective-permute-start = (bf16[8,4224]{1,0:T(8,128)(2,1)S(1)}, bf16[8,4224]{1,0:T(8,128)(2,1)S(1)}, u32[]{:S(2)}, u32[]{:S(2)}) collective-permute-start(bf16[8,4224]{1,0:T(8,128)(2,1)S(1)} %pad_maximum_fusion.10), channel_id=1, source_target_pairs={{0,4},{1,5},{2,6},{3,7},{4,0},{5,1},{6,2},{7,3},{8,12},{9,13},{10,... | collective-permute-start | bytes 202760 | tf_op jit(solution)/shard_map/ppermute | solution.py:87
  7.5 0.1 collective-permute-start.2
  8.3 0.6 fusion.9
  8.9 2.3 %collective-permute-done = bf16[8,4224]{1,0:T(8,128)(2,1)S(1)} collective-permute-done((bf16[8,4224]{1,0:T(8,128)(2,1)S(1)}, bf16[8,4224]{1,0:T(8,128)(2,1)S(1)}, u32[]{:S(2)}, u32[]{:S(2)}) %collective-permute-start) | collective-permute-done | bytes 67616 | tf_op jit(solution)/shard_map/ppermute | solution.py:87
  11.2 2.2 %collective-permute-start.1 = (bf16[16,4224]{1,0:T(8,128)(2,1)S(1)}, bf16[16,4224]{1,0:T(8,128)(2,1)S(1)}, u32[]{:S(2)}, u32[]{:S(2)}) collective-permute-start(bf16[16,4224]{1,0:T(8,128)(2,1)S(1)} %pad_maximum_fusion.7), channel_id=1, source_target_pairs={{0,2},{1,3},{2,0},{3,1},{4,6},{5,7},{6,4},{7,5},{8,10},{9,11},{10,... | collective-permute-start | bytes 405512 | tf_op jit(solution)/shard_map/ppermute | solution.py:87
  13.4 0.7 collective-permute-done.2
  14.1 0.7 collective-permute-start.4
  14.8 3.0 %collective-permute-done.1 = bf16[16,4224]{1,0:T(8,128)(2,1)S(1)} collective-permute-done((bf16[16,4224]{1,0:T(8,128)(2,1)S(1)}, bf16[16,4224]{1,0:T(8,128)(2,1)S(1)}, u32[]{:S(2)}, u32[]{:S(2)}) %collective-permute-start.1) | collective-permute-done | bytes 135200 | tf_op jit(solution)/shard_map/ppermute | solution.py:87
  17.8 2.0 %collective-permute-start.3 = (bf16[32,4224]{1,0:T(8,128)(2,1)S(1)}, bf16[32,4224]{1,0:T(8,128)(2,1)S(1)}, u32[]{:S(2)}, u32[]{:S(2)}) collective-permute-start(bf16[32,4224]{1,0:T(8,128)(2,1)S(1)} %pad_maximum_fusion.3), channel_id=1, source_target_pairs={{0,1},{1,0},{2,3},{3,2},{4,5},{5,4},{6,7},{7,6},{8,24},{9,25},{10,... | collective-permute-start | bytes 811016 | tf_op jit(solution)/shard_map/ppermute | solution.py:87
  19.9 0.1 collective-permute-done.4
  20.0 2.0 %collective-permute-start.6 = (bf16[32,4224]{1,0:T(8,128)(2,1)S(1)}, bf16[32,4224]{1,0:T(8,128)(2,1)S(1)}, u32[]{:S(2)}, u32[]{:S(2)}) collective-permute-start(bf16[32,4224]{1,0:T(8,128)(2,1)S(1)} %pad_maximum_fusion.4), channel_id=1, source_target_pairs={{0,1},{1,0},{2,3},{3,2},{4,5},{5,4},{6,7},{7,6},{8,24},{9,25},{10,... | collective-permute-start | bytes 811016 | tf_op jit(solution)/shard_map/ppermute | solution.py:87
  22.0 3.0 %collective-permute-start.8 = (bf16[8,4224]{1,0:T(8,128)(2,1)S(1)}, bf16[8,4224]{1,0:T(8,128)(2,1)S(1)}, u32[]{:S(2)}, u32[]{:S(2)}) collective-permute-start(bf16[8,4224]{1,0:T(8,128)(2,1)S(1)} %pad_maximum_fusion.12), channel_id=1, source_target_pairs={{0,4},{1,5},{2,6},{3,7},{4,0},{5,1},{6,2},{7,3},{8,12},{9,13},{10,... | collective-permute-start | bytes 202760 | tf_op jit(solution)/shard_map/ppermute | solution.py:87
  25.1 1.6 %collective-permute-start.5 = (bf16[64,4224]{1,0:T(8,128)(2,1)S(1)}, bf16[64,4224]{1,0:T(8,128)(2,1)S(1)}, u32[]{:S(2)}, u32[]{:S(2)}) collective-permute-start(bf16[64,4224]{1,0:T(8,128)(2,1)S(1)} %pad_maximum_fusion), channel_id=1, source_target_pairs={{0,16},{1,17},{2,18},{3,19},{4,20},{5,21},{6,22},{7,23},{8,9},{9,8... | collective-permute-start | bytes 1622024 | tf_op jit(solution)/shard_map/ppermute | solution.py:87
  26.6 0.6 collective-permute-done.8
  27.2 1.8 %collective-permute-start.9 = (bf16[16,4224]{1,0:T(8,128)(2,1)S(1)}, bf16[16,4224]{1,0:T(8,128)(2,1)S(1)}, u32[]{:S(2)}, u32[]{:S(2)}) collective-permute-start(bf16[16,4224]{1,0:T(8,128)(2,1)S(1)} %pad_maximum_fusion.9), channel_id=1, source_target_pairs={{0,2},{1,3},{2,0},{3,1},{4,6},{5,7},{6,4},{7,5},{8,10},{9,11},{10,... | collective-permute-start | bytes 405512 | tf_op jit(solution)/shard_map/ppermute | solution.py:87
  29.1 2.2 %collective-permute-start.12 = (bf16[64,4224]{1,0:T(8,128)(2,1)S(1)}, bf16[64,4224]{1,0:T(8,128)(2,1)S(1)}, u32[]{:S(2)}, u32[]{:S(2)}) collective-permute-start(bf16[64,4224]{1,0:T(8,128)(2,1)S(1)} %pad_maximum_fusion.1), channel_id=1, source_target_pairs={{0,16},{1,17},{2,18},{3,19},{4,20},{5,21},{6,22},{7,23},{8,9},{9,8... | collective-permute-start | bytes 1622024 | tf_op jit(solution)/shard_map/ppermute | solution.py:87
  31.4 3.1 %collective-permute-done.5 = bf16[64,4224]{1,0:T(8,128)(2,1)S(1)} collective-permute-done((bf16[64,4224]{1,0:T(8,128)(2,1)S(1)}, bf16[64,4224]{1,0:T(8,128)(2,1)S(1)}, u32[]{:S(2)}, u32[]{:S(2)}) %collective-permute-start.5) | collective-permute-done | bytes 540704 | tf_op jit(solution)/shard_map/ppermute | solution.py:87
  34.7 1.4 %collective-permute-start.10 = (bf16[32,4224]{1,0:T(8,128)(2,1)S(1)}, bf16[32,4224]{1,0:T(8,128)(2,1)S(1)}, u32[]{:S(2)}, u32[]{:S(2)}) collective-permute-start(bf16[32,4224]{1,0:T(8,128)(2,1)S(1)} %pad_maximum_fusion.5), channel_id=1, source_target_pairs={{0,1},{1,0},{2,3},{3,2},{4,5},{5,4},{6,7},{7,6},{8,24},{9,25},{10,... | collective-permute-start | bytes 811016 | tf_op jit(solution)/shard_map/ppermute | solution.py:87
  36.1 6.6 %collective-permute-done.12 = bf16[64,4224]{1,0:T(8,128)(2,1)S(1)} collective-permute-done((bf16[64,4224]{1,0:T(8,128)(2,1)S(1)}, bf16[64,4224]{1,0:T(8,128)(2,1)S(1)}, u32[]{:S(2)}, u32[]{:S(2)}) %collective-permute-start.12) | collective-permute-done | bytes 540704 | tf_op jit(solution)/shard_map/ppermute | solution.py:87
  42.7 2.2 %copy-done.1 = bf16[1,4096,512]{2,1,0:T(8,128)(2,1)S(1)} copy-done((bf16[1,4096,512]{2,1,0:T(8,128)(2,1)S(1)}, bf16[1,4096,512]{2,1,0:T(8,128)(2,1)}, u32[]{:S(2)}) %copy-start.1) | copy-done | bytes 4194328
  44.9 6.5 %serve_rows.3 = (bf16[128,4096]{1,0:T(8,128)(2,1)S(1)}, bf16[128,4096]{1,0:T(8,128)(2,1)S(1)}) custom-call(s32[1]{0:T(128)} %bitcast.1.mine, bf16[128,4224]{1,0:T(8,128)(2,1)S(1)} %constant_dynamic-update-slice_fusion.own, bf16[128,4224]{1,0:T(8,128)(2,1)S(1)} %collective-permute-done.7.sib, bf16[4096,512]{1,0:T(8,128)(2,1)S(1)} %bitcast.5, ...), custom_call_target="tpu_custom_call" | custom-call | flops 3221225472 | bytes 16777216 | tf_op jit(solution)/shard_map/serve_rows/pallas_call | solution.py:173
  51.4 0.4 collective-permute-start.11
  51.8 0.3 collective-permute-start.15
  52.1 1.6 %collective-permute-start.13 = (bf16[64,4224]{1,0:T(8,128)(2,1)S(1)}, bf16[64,4224]{1,0:T(8,128)(2,1)S(1)}, u32[]{:S(2)}, u32[]{:S(2)}) collective-permute-start(bf16[64,4224]{1,0:T(8,128)(2,1)S(1)} %pad_maximum_fusion.2), channel_id=1, source_target_pairs={{0,16},{1,17},{2,18},{3,19},{4,20},{5,21},{6,22},{7,23},{8,9},{9,8... | collective-permute-start | bytes 1622024 | tf_op jit(solution)/shard_map/ppermute | solution.py:87
  53.7 7.8 %collective-permute-done.13 = bf16[64,4224]{1,0:T(8,128)(2,1)S(1)} collective-permute-done((bf16[64,4224]{1,0:T(8,128)(2,1)S(1)}, bf16[64,4224]{1,0:T(8,128)(2,1)S(1)}, u32[]{:S(2)}, u32[]{:S(2)}) %collective-permute-start.13) | collective-permute-done | bytes 540704 | tf_op jit(solution)/shard_map/ppermute | solution.py:87
  61.5 6.5 %serve_rows.4 = (bf16[128,4096]{1,0:T(8,128)(2,1)S(1)}, bf16[128,4096]{1,0:T(8,128)(2,1)S(1)}) custom-call(s32[1]{0:T(128)} %bitcast.1.mine, bf16[128,4224]{1,0:T(8,128)(2,1)S(1)} %constant_dynamic-update-slice_fusion.5.own, bf16[128,4224]{1,0:T(8,128)(2,1)S(1)} %collective-permute-done.15.sib, bf16[4096,512]{1,0:T(8,128)(2,1)S(1)} %bitcast.6, ...), custom_call_target="tpu_custom_call" | custom-call | flops 3221225472 | bytes 16777216 | tf_op jit(solution)/shard_map/serve_rows/pallas_call | solution.py:173
  68.2 0.5 collective-permute-start.16
  68.7 0.1 add_convert_fusion.2
  68.8 1.6 %collective-permute-start.14 = (bf16[64,4096]{1,0:T(8,128)(2,1)S(1)}, bf16[64,4096]{1,0:T(8,128)(2,1)S(1)}, u32[]{:S(2)}, u32[]{:S(2)}) collective-permute-start(bf16[64,4096]{1,0:T(8,128)(2,1)S(1)} %add_convert_fusion.2), channel_id=1, source_target_pairs={{0,16},{1,17},{2,18},{3,19},{4,20},{5,21},{6,22},{7,23},{8,9},{9,8... | collective-permute-start | bytes 1572872 | tf_op jit(solution)/shard_map/ppermute | solution.py:87
  70.4 0.3 collective-permute-done.17
  70.7 0.1 add_convert_fusion
  70.9 1.6 %collective-permute-start.23 = (bf16[64,4096]{1,0:T(8,128)(2,1)S(1)}, bf16[64,4096]{1,0:T(8,128)(2,1)S(1)}, u32[]{:S(2)}, u32[]{:S(2)}) collective-permute-start(bf16[64,4096]{1,0:T(8,128)(2,1)S(1)} %add_convert_fusion), channel_id=1, source_target_pairs={{0,16},{1,17},{2,18},{3,19},{4,20},{5,21},{6,22},{7,23},{8,9},{9,8... | collective-permute-start | bytes 1572872 | tf_op jit(solution)/shard_map/ppermute | solution.py:87
  72.4 6.5 %serve_rows.5 = (bf16[128,4096]{1,0:T(8,128)(2,1)S(1)}, bf16[128,4096]{1,0:T(8,128)(2,1)S(1)}) custom-call(s32[1]{0:T(128)} %bitcast.1.mine, bf16[128,4224]{1,0:T(8,128)(2,1)S(1)} %constant_dynamic-update-slice_fusion.10.own, bf16[128,4224]{1,0:T(8,128)(2,1)S(1)} %collective-permute-done.16.sib, bf16[4096,512]{1,0:T(8,128)(2,1)S(1)} %bitcast.7, ...), custom_call_target="tpu_custom_call" | custom-call | flops 3221225472 | bytes 16777216 | tf_op jit(solution)/shard_map/serve_rows/pallas_call | solution.py:173
  78.9 0.1 add_convert_fusion.5
  79.0 1.4 %collective-permute-start.18 = (bf16[32,4096]{1,0:T(8,128)(2,1)S(1)}, bf16[32,4096]{1,0:T(8,128)(2,1)S(1)}, u32[]{:S(2)}, u32[]{:S(2)}) collective-permute-start(bf16[32,4096]{1,0:T(8,128)(2,1)S(1)} %add_convert_fusion.5), channel_id=1, source_target_pairs={{0,1},{1,0},{2,3},{3,2},{4,5},{5,4},{6,7},{7,6},{8,24},{9,25},{10,... | collective-permute-start | bytes 786440 | tf_op jit(solution)/shard_map/ppermute | solution.py:87
  80.4 5.2 %collective-permute-done.18 = bf16[32,4096]{1,0:T(8,128)(2,1)S(1)} collective-permute-done((bf16[32,4096]{1,0:T(8,128)(2,1)S(1)}, bf16[32,4096]{1,0:T(8,128)(2,1)S(1)}, u32[]{:S(2)}, u32[]{:S(2)}) %collective-permute-start.18) | collective-permute-done | bytes 262176 | tf_op jit(solution)/shard_map/ppermute | solution.py:87
  85.6 0.1 collective-permute-done.23
  85.7 0.1 add_convert_fusion.3
  85.8 1.4 %collective-permute-start.25 = (bf16[32,4096]{1,0:T(8,128)(2,1)S(1)}, bf16[32,4096]{1,0:T(8,128)(2,1)S(1)}, u32[]{:S(2)}, u32[]{:S(2)}) collective-permute-start(bf16[32,4096]{1,0:T(8,128)(2,1)S(1)} %add_convert_fusion.3), channel_id=1, source_target_pairs={{0,1},{1,0},{2,3},{3,2},{4,5},{5,4},{6,7},{7,6},{8,24},{9,25},{10,... | collective-permute-start | bytes 786440 | tf_op jit(solution)/shard_map/ppermute | solution.py:87
  87.2 1.7 %collective-permute-start.20 = (bf16[16,4096]{1,0:T(8,128)(2,1)S(1)}, bf16[16,4096]{1,0:T(8,128)(2,1)S(1)}, u32[]{:S(2)}, u32[]{:S(2)}) collective-permute-start(bf16[16,4096]{1,0:T(8,128)(2,1)S(1)} %add_convert_fusion.8), channel_id=1, source_target_pairs={{0,2},{1,3},{2,0},{3,1},{4,6},{5,7},{6,4},{7,5},{8,10},{9,11},{10,... | collective-permute-start | bytes 393224 | tf_op jit(solution)/shard_map/ppermute | solution.py:87
  88.9 0.1 add_convert_fusion.1
  89.0 1.6 %collective-permute-start.21 = (bf16[64,4096]{1,0:T(8,128)(2,1)S(1)}, bf16[64,4096]{1,0:T(8,128)(2,1)S(1)}, u32[]{:S(2)}, u32[]{:S(2)}) collective-permute-start(bf16[64,4096]{1,0:T(8,128)(2,1)S(1)} %add_convert_fusion.1), channel_id=1, source_target_pairs={{0,16},{1,17},{2,18},{3,19},{4,20},{5,21},{6,22},{7,23},{8,9},{9,8... | collective-permute-start | bytes 1572872 | tf_op jit(solution)/shard_map/ppermute | solution.py:87
  90.6 1.7 %collective-permute-done.25 = bf16[32,4096]{1,0:T(8,128)(2,1)S(1)} collective-permute-done((bf16[32,4096]{1,0:T(8,128)(2,1)S(1)}, bf16[32,4096]{1,0:T(8,128)(2,1)S(1)}, u32[]{:S(2)}, u32[]{:S(2)}) %collective-permute-start.25) | collective-permute-done | bytes 262176 | tf_op jit(solution)/shard_map/ppermute | solution.py:87
  92.2 1.0 collective-permute-done.20
  93.3 2.3 %collective-permute-start.27 = (bf16[16,4096]{1,0:T(8,128)(2,1)S(1)}, bf16[16,4096]{1,0:T(8,128)(2,1)S(1)}, u32[]{:S(2)}, u32[]{:S(2)}) collective-permute-start(bf16[16,4096]{1,0:T(8,128)(2,1)S(1)} %add_convert_fusion.6), channel_id=1, source_target_pairs={{0,2},{1,3},{2,0},{3,1},{4,6},{5,7},{6,4},{7,5},{8,10},{9,11},{10,... | collective-permute-start | bytes 393224 | tf_op jit(solution)/shard_map/ppermute | solution.py:87
  95.6 2.7 %collective-permute-done.21 = bf16[64,4096]{1,0:T(8,128)(2,1)S(1)} collective-permute-done((bf16[64,4096]{1,0:T(8,128)(2,1)S(1)}, bf16[64,4096]{1,0:T(8,128)(2,1)S(1)}, u32[]{:S(2)}, u32[]{:S(2)}) %collective-permute-start.21) | collective-permute-done | bytes 524320 | tf_op jit(solution)/shard_map/ppermute | solution.py:87
  98.3 0.1 add_convert_fusion.4
  98.4 0.9 collective-permute-start.24
  99.3 3.4 %collective-permute-start.22 = (bf16[8,4096]{1,0:T(8,128)(2,1)S(1)}, bf16[8,4096]{1,0:T(8,128)(2,1)S(1)}, u32[]{:S(2)}, u32[]{:S(2)}) collective-permute-start(bf16[8,4096]{1,0:T(8,128)(2,1)S(1)} %add_convert_fusion.14), channel_id=1, source_target_pairs={{0,4},{1,5},{2,6},{3,7},{4,0},{5,1},{6,2},{7,3},{8,12},{9,13},{10,... | collective-permute-start | bytes 196616 | tf_op jit(solution)/shard_map/ppermute | solution.py:87
  102.7 2.1 %collective-permute-done.24 = bf16[32,4096]{1,0:T(8,128)(2,1)S(1)} collective-permute-done((bf16[32,4096]{1,0:T(8,128)(2,1)S(1)}, bf16[32,4096]{1,0:T(8,128)(2,1)S(1)}, u32[]{:S(2)}, u32[]{:S(2)}) %collective-permute-start.24) | collective-permute-done | bytes 262176 | tf_op jit(solution)/shard_map/ppermute | solution.py:87
  104.9 1.1 collective-permute-start.26
  106.0 3.4 %collective-permute-start.28 = (bf16[8,4096]{1,0:T(8,128)(2,1)S(1)}, bf16[8,4096]{1,0:T(8,128)(2,1)S(1)}, u32[]{:S(2)}, u32[]{:S(2)}) collective-permute-start(bf16[8,4096]{1,0:T(8,128)(2,1)S(1)} %add_convert_fusion.12), channel_id=1, source_target_pairs={{0,4},{1,5},{2,6},{3,7},{4,0},{5,1},{6,2},{7,3},{8,12},{9,13},{10,... | collective-permute-start | bytes 196616 | tf_op jit(solution)/shard_map/ppermute | solution.py:87
  109.4 2.5 %collective-permute-done.28 = bf16[8,4096]{1,0:T(8,128)(2,1)S(1)} collective-permute-done((bf16[8,4096]{1,0:T(8,128)(2,1)S(1)}, bf16[8,4096]{1,0:T(8,128)(2,1)S(1)}, u32[]{:S(2)}, u32[]{:S(2)}) %collective-permute-start.28) | collective-permute-done | bytes 65568 | tf_op jit(solution)/shard_map/ppermute | solution.py:87
  112.0 2.8 %collective-permute-start.29 = (bf16[8,4096]{1,0:T(8,128)(2,1)S(1)}, bf16[8,4096]{1,0:T(8,128)(2,1)S(1)}, u32[]{:S(2)}, u32[]{:S(2)}) collective-permute-start(bf16[8,4096]{1,0:T(8,128)(2,1)S(1)} %add_convert_fusion.10), channel_id=1, source_target_pairs={{0,4},{1,5},{2,6},{3,7},{4,0},{5,1},{6,2},{7,3},{8,12},{9,13},{10,... | collective-permute-start | bytes 196616 | tf_op jit(solution)/shard_map/ppermute | solution.py:87
  114.8 2.4 %collective-permute-done.29 = bf16[8,4096]{1,0:T(8,128)(2,1)S(1)} collective-permute-done((bf16[8,4096]{1,0:T(8,128)(2,1)S(1)}, bf16[8,4096]{1,0:T(8,128)(2,1)S(1)}, u32[]{:S(2)}, u32[]{:S(2)}) %collective-permute-start.29) | collective-permute-done | bytes 65568 | tf_op jit(solution)/shard_map/ppermute | solution.py:87
  117.2 0.1 add_convert_fusion.9
  117.3 0.7 pad_maximum_fusion.6
  (59 shorter events, 1.2 us)
Async XLA Ops:
  0.0 8.2 %copy-start.3 = (s32[16,2]{0,1:T(2,128)S(1)}, s32[16,2]{0,1:T(2,128)}, u32[]{:S(2)}) copy-start(s32[16,2]{0,1:T(2,128)} %param.11) | copy-start | bytes 388
  3.4 7.9 %collective-permute-start = (bf16[8,4224]{1,0:T(8,128)(2,1)S(1)}, bf16[8,4224]{1,0:T(8,128)(2,1)S(1)}, u32[]{:S(2)}, u32[]{:S(2)}) collective-permute-start(bf16[8,4224]{1,0:T(8,128)(2,1)S(1)} %pad_maximum_fusion.10), channel_id=1, source_target_pairs={{0,4},{1,5},{2,6},{3,7},{4,0},{5,1},{6,2},{7,3},{8,12},{9,13},{10,... | collective-permute-start | bytes 202760 | tf_op jit(solution)/shard_map/ppermute | solution.py:87
  7.5 6.6 %collective-permute-start.2 = (bf16[8,4224]{1,0:T(8,128)(2,1)S(1)}, bf16[8,4224]{1,0:T(8,128)(2,1)S(1)}, u32[]{:S(2)}, u32[]{:S(2)}) collective-permute-start(bf16[8,4224]{1,0:T(8,128)(2,1)S(1)} %pad_maximum_fusion.11), channel_id=1, source_target_pairs={{0,4},{1,5},{2,6},{3,7},{4,0},{5,1},{6,2},{7,3},{8,12},{9,13},{10,... | collective-permute-start | bytes 202760 | tf_op jit(solution)/shard_map/ppermute | solution.py:87
  11.2 6.6 %collective-permute-start.1 = (bf16[16,4224]{1,0:T(8,128)(2,1)S(1)}, bf16[16,4224]{1,0:T(8,128)(2,1)S(1)}, u32[]{:S(2)}, u32[]{:S(2)}) collective-permute-start(bf16[16,4224]{1,0:T(8,128)(2,1)S(1)} %pad_maximum_fusion.7), channel_id=1, source_target_pairs={{0,2},{1,3},{2,0},{3,1},{4,6},{5,7},{6,4},{7,5},{8,10},{9,11},{10,... | collective-permute-start | bytes 405512 | tf_op jit(solution)/shard_map/ppermute | solution.py:87
  14.1 5.9 %collective-permute-start.4 = (bf16[16,4224]{1,0:T(8,128)(2,1)S(1)}, bf16[16,4224]{1,0:T(8,128)(2,1)S(1)}, u32[]{:S(2)}, u32[]{:S(2)}) collective-permute-start(bf16[16,4224]{1,0:T(8,128)(2,1)S(1)} %pad_maximum_fusion.8), channel_id=1, source_target_pairs={{0,2},{1,3},{2,0},{3,1},{4,6},{5,7},{6,4},{7,5},{8,10},{9,11},{10,... | collective-permute-start | bytes 405512 | tf_op jit(solution)/shard_map/ppermute | solution.py:87
  17.8 7.2 %collective-permute-start.3 = (bf16[32,4224]{1,0:T(8,128)(2,1)S(1)}, bf16[32,4224]{1,0:T(8,128)(2,1)S(1)}, u32[]{:S(2)}, u32[]{:S(2)}) collective-permute-start(bf16[32,4224]{1,0:T(8,128)(2,1)S(1)} %pad_maximum_fusion.3), channel_id=1, source_target_pairs={{0,1},{1,0},{2,3},{3,2},{4,5},{5,4},{6,7},{7,6},{8,24},{9,25},{10,... | collective-permute-start | bytes 811016 | tf_op jit(solution)/shard_map/ppermute | solution.py:87
  20.0 9.1 %collective-permute-start.6 = (bf16[32,4224]{1,0:T(8,128)(2,1)S(1)}, bf16[32,4224]{1,0:T(8,128)(2,1)S(1)}, u32[]{:S(2)}, u32[]{:S(2)}) collective-permute-start(bf16[32,4224]{1,0:T(8,128)(2,1)S(1)} %pad_maximum_fusion.4), channel_id=1, source_target_pairs={{0,1},{1,0},{2,3},{3,2},{4,5},{5,4},{6,7},{7,6},{8,24},{9,25},{10,... | collective-permute-start | bytes 811016 | tf_op jit(solution)/shard_map/ppermute | solution.py:87
  22.0 5.2 %collective-permute-start.8 = (bf16[8,4224]{1,0:T(8,128)(2,1)S(1)}, bf16[8,4224]{1,0:T(8,128)(2,1)S(1)}, u32[]{:S(2)}, u32[]{:S(2)}) collective-permute-start(bf16[8,4224]{1,0:T(8,128)(2,1)S(1)} %pad_maximum_fusion.12), channel_id=1, source_target_pairs={{0,4},{1,5},{2,6},{3,7},{4,0},{5,1},{6,2},{7,3},{8,12},{9,13},{10,... | collective-permute-start | bytes 202760 | tf_op jit(solution)/shard_map/ppermute | solution.py:87
  25.0 17.7 %copy-start = (bf16[1,4096,512]{2,1,0:T(8,128)(2,1)S(1)}, bf16[1,4096,512]{2,1,0:T(8,128)(2,1)}, u32[]{:S(2)}) copy-start(bf16[1,4096,512]{2,1,0:T(8,128)(2,1)} %param.13) | copy-start | bytes 12582916
  25.1 9.4 %collective-permute-start.5 = (bf16[64,4224]{1,0:T(8,128)(2,1)S(1)}, bf16[64,4224]{1,0:T(8,128)(2,1)S(1)}, u32[]{:S(2)}, u32[]{:S(2)}) collective-permute-start(bf16[64,4224]{1,0:T(8,128)(2,1)S(1)} %pad_maximum_fusion), channel_id=1, source_target_pairs={{0,16},{1,17},{2,18},{3,19},{4,20},{5,21},{6,22},{7,23},{8,9},{9,8... | collective-permute-start | bytes 1622024 | tf_op jit(solution)/shard_map/ppermute | solution.py:87
  27.2 7.4 %collective-permute-start.9 = (bf16[16,4224]{1,0:T(8,128)(2,1)S(1)}, bf16[16,4224]{1,0:T(8,128)(2,1)S(1)}, u32[]{:S(2)}, u32[]{:S(2)}) collective-permute-start(bf16[16,4224]{1,0:T(8,128)(2,1)S(1)} %pad_maximum_fusion.9), channel_id=1, source_target_pairs={{0,2},{1,3},{2,0},{3,1},{4,6},{5,7},{6,4},{7,5},{8,10},{9,11},{10,... | collective-permute-start | bytes 405512 | tf_op jit(solution)/shard_map/ppermute | solution.py:87
  29.1 13.6 %collective-permute-start.12 = (bf16[64,4224]{1,0:T(8,128)(2,1)S(1)}, bf16[64,4224]{1,0:T(8,128)(2,1)S(1)}, u32[]{:S(2)}, u32[]{:S(2)}) collective-permute-start(bf16[64,4224]{1,0:T(8,128)(2,1)S(1)} %pad_maximum_fusion.1), channel_id=1, source_target_pairs={{0,16},{1,17},{2,18},{3,19},{4,20},{5,21},{6,22},{7,23},{8,9},{9,8... | collective-permute-start | bytes 1622024 | tf_op jit(solution)/shard_map/ppermute | solution.py:87
  34.6 8.2 %collective-permute-start.7 = (bf16[128,4224]{1,0:T(8,128)(2,1)S(1)}, bf16[128,4224]{1,0:T(8,128)(2,1)S(1)}, u32[]{:S(2)}, u32[]{:S(2)}) collective-permute-start(bf16[128,4224]{1,0:T(8,128)(2,1)S(1)} %constant_dynamic-update-slice_fusion.own), channel_id=1, source_target_pairs={{0,8},{1,9},{2,10},{3,11},{4,12},{5,13},{6,14},{7,15},{8,0},{9,1},... | collective-permute-start | bytes 3244040 | tf_op jit(solution)/shard_map/ppermute | solution.py:87
  34.7 8.0 %collective-permute-start.10 = (bf16[32,4224]{1,0:T(8,128)(2,1)S(1)}, bf16[32,4224]{1,0:T(8,128)(2,1)S(1)}, u32[]{:S(2)}, u32[]{:S(2)}) collective-permute-start(bf16[32,4224]{1,0:T(8,128)(2,1)S(1)} %pad_maximum_fusion.5), channel_id=1, source_target_pairs={{0,1},{1,0},{2,3},{3,2},{4,5},{5,4},{6,7},{7,6},{8,24},{9,25},{10,... | collective-permute-start | bytes 811016 | tf_op jit(solution)/shard_map/ppermute | solution.py:87
  42.7 2.2 %copy-start.1 = (bf16[1,4096,512]{2,1,0:T(8,128)(2,1)S(1)}, bf16[1,4096,512]{2,1,0:T(8,128)(2,1)}, u32[]{:S(2)}) copy-start(bf16[1,4096,512]{2,1,0:T(8,128)(2,1)} %param.14) | copy-start | bytes 12582916
  51.4 10.2 %collective-permute-start.11 = (bf16[128,4096]{1,0:T(8,128)(2,1)S(1)}, bf16[128,4096]{1,0:T(8,128)(2,1)S(1)}, u32[]{:S(2)}, u32[]{:S(2)}) collective-permute-start(bf16[128,4096]{1,0:T(8,128)(2,1)S(1)} %get-tuple-element.63), channel_id=1, source_target_pairs={{0,8},{1,9},{2,10},{3,11},{4,12},{5,13},{6,14},{7,15},{8,0},{9,1},... | collective-permute-start | bytes 3145736 | tf_op jit(solution)/shard_map/ppermute | solution.py:87
  51.8 9.7 %collective-permute-start.15 = (bf16[128,4224]{1,0:T(8,128)(2,1)S(1)}, bf16[128,4224]{1,0:T(8,128)(2,1)S(1)}, u32[]{:S(2)}, u32[]{:S(2)}) collective-permute-start(bf16[128,4224]{1,0:T(8,128)(2,1)S(1)} %constant_dynamic-update-slice_fusion.5.own), channel_id=1, source_target_pairs={{0,8},{1,9},{2,10},{3,11},{4,12},{5,13},{6,14},{7,15},{8,0},{9,1},... | collective-permute-start | bytes 3244040 | tf_op jit(solution)/shard_map/ppermute | solution.py:87
  52.1 9.4 %collective-permute-start.13 = (bf16[64,4224]{1,0:T(8,128)(2,1)S(1)}, bf16[64,4224]{1,0:T(8,128)(2,1)S(1)}, u32[]{:S(2)}, u32[]{:S(2)}) collective-permute-start(bf16[64,4224]{1,0:T(8,128)(2,1)S(1)} %pad_maximum_fusion.2), channel_id=1, source_target_pairs={{0,16},{1,17},{2,18},{3,19},{4,20},{5,21},{6,22},{7,23},{8,9},{9,8... | collective-permute-start | bytes 1622024 | tf_op jit(solution)/shard_map/ppermute | solution.py:87
  68.0 2.7 %collective-permute-start.17 = (bf16[128,4096]{1,0:T(8,128)(2,1)S(1)}, bf16[128,4096]{1,0:T(8,128)(2,1)S(1)}, u32[]{:S(2)}, u32[]{:S(2)}) collective-permute-start(bf16[128,4096]{1,0:T(8,128)(2,1)S(1)} %get-tuple-element.72), channel_id=1, source_target_pairs={{0,8},{1,9},{2,10},{3,11},{4,12},{5,13},{6,14},{7,15},{8,0},{9,1},... | collective-permute-start | bytes 3145736 | tf_op jit(solution)/shard_map/ppermute | solution.py:87
  68.1 4.3 %copy-start.2 = (bf16[1,4096,512]{2,1,0:T(8,128)(2,1)S(1)}, bf16[1,4096,512]{2,1,0:T(8,128)(2,1)}, u32[]{:S(2)}) copy-start(bf16[1,4096,512]{2,1,0:T(8,128)(2,1)} %param.14) | copy-start | bytes 12582916
  68.2 4.3 %collective-permute-start.16 = (bf16[128,4224]{1,0:T(8,128)(2,1)S(1)}, bf16[128,4224]{1,0:T(8,128)(2,1)S(1)}, u32[]{:S(2)}, u32[]{:S(2)}) collective-permute-start(bf16[128,4224]{1,0:T(8,128)(2,1)S(1)} %constant_dynamic-update-slice_fusion.10.own), channel_id=1, source_target_pairs={{0,8},{1,9},{2,10},{3,11},{4,12},{5,13},{6,14},{7,15},{8,0},{9,1},... | collective-permute-start | bytes 3244040 | tf_op jit(solution)/shard_map/ppermute | solution.py:87
  68.8 10.1 %collective-permute-start.14 = (bf16[64,4096]{1,0:T(8,128)(2,1)S(1)}, bf16[64,4096]{1,0:T(8,128)(2,1)S(1)}, u32[]{:S(2)}, u32[]{:S(2)}) collective-permute-start(bf16[64,4096]{1,0:T(8,128)(2,1)S(1)} %add_convert_fusion.2), channel_id=1, source_target_pairs={{0,16},{1,17},{2,18},{3,19},{4,20},{5,21},{6,22},{7,23},{8,9},{9,8... | collective-permute-start | bytes 1572872 | tf_op jit(solution)/shard_map/ppermute | solution.py:87
  70.9 14.8 %collective-permute-start.23 = (bf16[64,4096]{1,0:T(8,128)(2,1)S(1)}, bf16[64,4096]{1,0:T(8,128)(2,1)S(1)}, u32[]{:S(2)}, u32[]{:S(2)}) collective-permute-start(bf16[64,4096]{1,0:T(8,128)(2,1)S(1)} %add_convert_fusion), channel_id=1, source_target_pairs={{0,16},{1,17},{2,18},{3,19},{4,20},{5,21},{6,22},{7,23},{8,9},{9,8... | collective-permute-start | bytes 1572872 | tf_op jit(solution)/shard_map/ppermute | solution.py:87
  79.0 6.6 %collective-permute-start.18 = (bf16[32,4096]{1,0:T(8,128)(2,1)S(1)}, bf16[32,4096]{1,0:T(8,128)(2,1)S(1)}, u32[]{:S(2)}, u32[]{:S(2)}) collective-permute-start(bf16[32,4096]{1,0:T(8,128)(2,1)S(1)} %add_convert_fusion.5), channel_id=1, source_target_pairs={{0,1},{1,0},{2,3},{3,2},{4,5},{5,4},{6,7},{7,6},{8,24},{9,25},{10,... | collective-permute-start | bytes 786440 | tf_op jit(solution)/shard_map/ppermute | solution.py:87
  80.4 6.7 %collective-permute-start.19 = (bf16[128,4096]{1,0:T(8,128)(2,1)S(1)}, bf16[128,4096]{1,0:T(8,128)(2,1)S(1)}, u32[]{:S(2)}, u32[]{:S(2)}) collective-permute-start(bf16[128,4096]{1,0:T(8,128)(2,1)S(1)} %get-tuple-element.77), channel_id=1, source_target_pairs={{0,8},{1,9},{2,10},{3,11},{4,12},{5,13},{6,14},{7,15},{8,0},{9,1},... | collective-permute-start | bytes 3145736 | tf_op jit(solution)/shard_map/ppermute | solution.py:87
  85.8 6.5 %collective-permute-start.25 = (bf16[32,4096]{1,0:T(8,128)(2,1)S(1)}, bf16[32,4096]{1,0:T(8,128)(2,1)S(1)}, u32[]{:S(2)}, u32[]{:S(2)}) collective-permute-start(bf16[32,4096]{1,0:T(8,128)(2,1)S(1)} %add_convert_fusion.3), channel_id=1, source_target_pairs={{0,1},{1,0},{2,3},{3,2},{4,5},{5,4},{6,7},{7,6},{8,24},{9,25},{10,... | collective-permute-start | bytes 786440 | tf_op jit(solution)/shard_map/ppermute | solution.py:87
  87.2 6.0 %collective-permute-start.20 = (bf16[16,4096]{1,0:T(8,128)(2,1)S(1)}, bf16[16,4096]{1,0:T(8,128)(2,1)S(1)}, u32[]{:S(2)}, u32[]{:S(2)}) collective-permute-start(bf16[16,4096]{1,0:T(8,128)(2,1)S(1)} %add_convert_fusion.8), channel_id=1, source_target_pairs={{0,2},{1,3},{2,0},{3,1},{4,6},{5,7},{6,4},{7,5},{8,10},{9,11},{10,... | collective-permute-start | bytes 393224 | tf_op jit(solution)/shard_map/ppermute | solution.py:87
  89.0 9.2 %collective-permute-start.21 = (bf16[64,4096]{1,0:T(8,128)(2,1)S(1)}, bf16[64,4096]{1,0:T(8,128)(2,1)S(1)}, u32[]{:S(2)}, u32[]{:S(2)}) collective-permute-start(bf16[64,4096]{1,0:T(8,128)(2,1)S(1)} %add_convert_fusion.1), channel_id=1, source_target_pairs={{0,16},{1,17},{2,18},{3,19},{4,20},{5,21},{6,22},{7,23},{8,9},{9,8... | collective-permute-start | bytes 1572872 | tf_op jit(solution)/shard_map/ppermute | solution.py:87
  93.3 12.6 %collective-permute-start.27 = (bf16[16,4096]{1,0:T(8,128)(2,1)S(1)}, bf16[16,4096]{1,0:T(8,128)(2,1)S(1)}, u32[]{:S(2)}, u32[]{:S(2)}) collective-permute-start(bf16[16,4096]{1,0:T(8,128)(2,1)S(1)} %add_convert_fusion.6), channel_id=1, source_target_pairs={{0,2},{1,3},{2,0},{3,1},{4,6},{5,7},{6,4},{7,5},{8,10},{9,11},{10,... | collective-permute-start | bytes 393224 | tf_op jit(solution)/shard_map/ppermute | solution.py:87
  98.4 6.4 %collective-permute-start.24 = (bf16[32,4096]{1,0:T(8,128)(2,1)S(1)}, bf16[32,4096]{1,0:T(8,128)(2,1)S(1)}, u32[]{:S(2)}, u32[]{:S(2)}) collective-permute-start(bf16[32,4096]{1,0:T(8,128)(2,1)S(1)} %add_convert_fusion.4), channel_id=1, source_target_pairs={{0,1},{1,0},{2,3},{3,2},{4,5},{5,4},{6,7},{7,6},{8,24},{9,25},{10,... | collective-permute-start | bytes 786440 | tf_op jit(solution)/shard_map/ppermute | solution.py:87
  99.3 10.1 %collective-permute-start.22 = (bf16[8,4096]{1,0:T(8,128)(2,1)S(1)}, bf16[8,4096]{1,0:T(8,128)(2,1)S(1)}, u32[]{:S(2)}, u32[]{:S(2)}) collective-permute-start(bf16[8,4096]{1,0:T(8,128)(2,1)S(1)} %add_convert_fusion.14), channel_id=1, source_target_pairs={{0,4},{1,5},{2,6},{3,7},{4,0},{5,1},{6,2},{7,3},{8,12},{9,13},{10,... | collective-permute-start | bytes 196616 | tf_op jit(solution)/shard_map/ppermute | solution.py:87
  104.9 7.1 %collective-permute-start.26 = (bf16[16,4096]{1,0:T(8,128)(2,1)S(1)}, bf16[16,4096]{1,0:T(8,128)(2,1)S(1)}, u32[]{:S(2)}, u32[]{:S(2)}) collective-permute-start(bf16[16,4096]{1,0:T(8,128)(2,1)S(1)} %add_convert_fusion.7), channel_id=1, source_target_pairs={{0,2},{1,3},{2,0},{3,1},{4,6},{5,7},{6,4},{7,5},{8,10},{9,11},{10,... | collective-permute-start | bytes 393224 | tf_op jit(solution)/shard_map/ppermute | solution.py:87
  106.0 6.0 %collective-permute-start.28 = (bf16[8,4096]{1,0:T(8,128)(2,1)S(1)}, bf16[8,4096]{1,0:T(8,128)(2,1)S(1)}, u32[]{:S(2)}, u32[]{:S(2)}) collective-permute-start(bf16[8,4096]{1,0:T(8,128)(2,1)S(1)} %add_convert_fusion.12), channel_id=1, source_target_pairs={{0,4},{1,5},{2,6},{3,7},{4,0},{5,1},{6,2},{7,3},{8,12},{9,13},{10,... | collective-permute-start | bytes 196616 | tf_op jit(solution)/shard_map/ppermute | solution.py:87
  112.0 5.2 %collective-permute-start.29 = (bf16[8,4096]{1,0:T(8,128)(2,1)S(1)}, bf16[8,4096]{1,0:T(8,128)(2,1)S(1)}, u32[]{:S(2)}, u32[]{:S(2)}) collective-permute-start(bf16[8,4096]{1,0:T(8,128)(2,1)S(1)} %add_convert_fusion.10), channel_id=1, source_target_pairs={{0,4},{1,5},{2,6},{3,7},{4,0},{5,1},{6,2},{7,3},{8,12},{9,13},{10,... | collective-permute-start | bytes 196616 | tf_op jit(solution)/shard_map/ppermute | solution.py:87

commit v7 on v6

--- a/solution.py
+++ b/solution.py
@@ -10,8 +10,9 @@
 AXES = ("dp", "expert")
 LANES = 128
 PARTS = 4
+VMEM_MIB = 8
 ROWS_AT_ONCE = 8
-ORDER = [0, 1, 0, 1, 0, 2, 1, 0, 2, 1, 0, 2, 0, 1, 2, 0, 1, 1, 2, 0, 1, 2, 2, 0, 2, 0, 1, 2, 0, 1, 2, 1, 2, 0, 1, 2]
+GUARDS = []
 
 
 def partner(value, axis, distance):
@@ -120,71 +121,39 @@
     return jnp.sum(jnp.where(ids == mine, hi + mid + lo, 0.0), axis=1, keepdims=True)
 
 
-def serve_kernel(
-    top_count, mine, own, sib, w_gate, w_up, w_down, out_own, out_sib, x, gate, up, down, y, in_sem, out_sem
-):
-    rows, packed_width = own.shape
+def serve_kernel(top_count, mine, own, sib, w_gate, w_up, w_down, out_own, out_sib):
+    rows = own.shape[0]
     width, hidden_width = w_gate.shape
     depth = width // PARTS
-    loads = [
-        pltpu.make_async_copy(own, x.at[:rows], in_sem.at[0]),
-        pltpu.make_async_copy(sib, x.at[rows:], in_sem.at[1]),
-    ]
-    for k in range(PARTS):
-        part = pl.ds(k * depth, depth)
-        loads.append(pltpu.make_async_copy(w_gate.at[part], gate.at[part], in_sem.at[2 + 2 * k]))
-        loads.append(pltpu.make_async_copy(w_up.at[part], up.at[part], in_sem.at[3 + 2 * k]))
-    load_down = pltpu.make_async_copy(w_down, down, in_sem.at[2 + 2 * PARTS])
-    for load in loads:
-        load.start()
-    load_down.start()
-    loads[0].wait()
-    loads[1].wait()
     gate_sum = jnp.zeros((2 * rows, hidden_width), jnp.float32)
     up_sum = jnp.zeros((2 * rows, hidden_width), jnp.float32)
     for k in range(PARTS):
         part = pl.ds(k * depth, depth)
-        loads[2 + 2 * k].wait()
-        gate_sum += jnp.dot(x[:, part], gate[part], preferred_element_type=jnp.float32)
-        loads[3 + 2 * k].wait()
-        up_sum += jnp.dot(x[:, part], up[part], preferred_element_type=jnp.float32)
+        x = jnp.concatenate([own[:, part], sib[:, part]])
+        gate_sum += jnp.dot(x, w_gate[part], preferred_element_type=jnp.float32)
+        up_sum += jnp.dot(x, w_up[part], preferred_element_type=jnp.float32)
     hidden = (gate_sum / (1.0 + jnp.exp(-gate_sum)) * up_sum).astype(jnp.bfloat16)
-    scale = scale_of(x[:, width:], mine[0].astype(jnp.float32), top_count)
-    load_down.wait()
-    stores = []
+    extra = jnp.concatenate([own[:, width:], sib[:, width:]])
+    scale = scale_of(extra, mine[0].astype(jnp.float32), top_count)
     for k in range(PARTS):
         part = pl.ds(k * depth, depth)
-        served = jnp.dot(hidden, down[:, part], preferred_element_type=jnp.float32)
-        y[:, part] = (served * scale).astype(jnp.bfloat16)
-        stores.append(pltpu.make_async_copy(y.at[rows:, part], out_sib.at[:, part], out_sem.at[2 * k]))
-        stores.append(pltpu.make_async_copy(y.at[:rows, part], out_own.at[:, part], out_sem.at[2 * k + 1]))
-        stores[-2].start()
-        stores[-1].start()
-    for store in stores:
-        store.wait()
+        served = jnp.dot(hidden, w_down[:, part], preferred_element_type=jnp.float32) * scale
+        out_own[:, part] = served[:rows].astype(jnp.bfloat16)
+        out_sib[:, part] = served[rows:].astype(jnp.bfloat16)
 
 
 def serve_rows(own, sib, mine, top_count, w_gate, w_up, w_down):
     rows, packed_width = own.shape
     width, hidden_width = w_gate.shape
-    anywhere = pl.BlockSpec(memory_space=pl.ANY)
+    whole = pl.BlockSpec(memory_space=pltpu.VMEM)
     out = jax.ShapeDtypeStruct((rows, width), jnp.bfloat16)
     moved = 2 * (4 * rows * width + 3 * width * hidden_width)
     return pl.pallas_call(
         functools.partial(serve_kernel, top_count),
         out_shape=(out, out),
-        in_specs=[pl.BlockSpec(memory_space=pltpu.SMEM)] + [anywhere] * 5,
-        out_specs=(anywhere, anywhere),
-        scratch_shapes=[
-            pltpu.VMEM((2 * rows, packed_width), jnp.bfloat16),
-            pltpu.VMEM((width, hidden_width), jnp.bfloat16),
-            pltpu.VMEM((width, hidden_width), jnp.bfloat16),
-            pltpu.VMEM((hidden_width, width), jnp.bfloat16),
-            pltpu.VMEM((2 * rows, width), jnp.bfloat16),
-            pltpu.SemaphoreType.DMA((3 + 2 * PARTS,)),
-            pltpu.SemaphoreType.DMA((2 * PARTS,)),
-        ],
-        compiler_params=pltpu.CompilerParams(vmem_limit_bytes=40 * 2**20),
+        in_specs=[pl.BlockSpec(memory_space=pltpu.SMEM)] + [whole] * 5,
+        out_specs=(whole, whole),
+        compiler_params=pltpu.CompilerParams(vmem_limit_bytes=VMEM_MIB * 2**20),
         cost_estimate=pl.CostEstimate(
             flops=12 * rows * width * hidden_width, bytes_accessed=moved, transcendentals=2 * rows * hidden_width
         ),
@@ -203,9 +172,9 @@
         (got,) = yield (permute(held, move),)
         held = jnp.concatenate([held, got])
     (sib,) = yield (permute(held, to_sibling),)
-    out, out_sib = yield serve(held, sib)
+    out, out_sib = serve(held, sib)
+    (got,) = yield (permute(out_sib, to_sibling),)
     terms = [out]
-    (got,) = yield (permute(out_sib, to_sibling),)
     for move in moves[::-1]:
         terms.append(got)
         half = got.shape[0] // 2
@@ -215,25 +184,23 @@
     return total(*[term[:rows] for term in terms])
 
 
-def in_order(chunks, order):
-    waits = [next(chunk) for chunk in chunks]
+def run_steps(chunks, guards):
+    waits = [[next(chunk)[0]] for chunk in chunks]
     results = [None] * len(chunks)
-    before = ()
-    for number in order:
-        count = len(waits[number])
-        ready = lax.optimization_barrier(waits[number] + before)[:count]
-        before = waits[number]
-        try:
-            waits[number] = chunks[number].send(ready)
-        except StopIteration as end:
-            results[number] = end.value
+    while any(result is None for result in results):
+        for i, chunk in enumerate(chunks):
+            at = len(waits[i]) - 1
+            asked = [(j, t) for k, s, j, t in guards if (k, s) == (i, at)]
+            if results[i] is not None or any(len(waits[j]) <= t for j, t in asked):
+                continue
+            ready = tuple(waits[i][-1:])
+            if asked:
+                ready = lax.optimization_barrier(ready + tuple(waits[j][t] for j, t in asked))[:1]
+            try:
+                waits[i].append(chunk.send(ready)[0])
+            except StopIteration as end:
+                results[i] = end.value
     return results
-
-
-def step_order(chunk_count, step_count):
-    if chunk_count == 3 and step_count == len(ORDER) // 3:
-        return ORDER
-    return [number for _ in range(step_count) for number in range(chunk_count)]
 
 
 def dense(tokens, expert_ids, route_weight, slot_of, swap_flag, w_gate, w_up, w_down):
@@ -249,7 +216,8 @@
         own = jnp.concatenate([tokens[at : at + step], extra[at : at + step]], axis=1)
         serve = lambda held, sib: serve_rows(held, sib, mine, top_count, w_gate[0], w_up[0], w_down[0])
         chunks.append(chunk_steps(own, moves, serve))
-    return jnp.concatenate(in_order(chunks, step_order(len(chunks), 2 * len(moves) + 4)))
+    guards = GUARDS if len(chunks) == 3 and len(moves) == 4 else []
+    return jnp.concatenate(run_steps(chunks, guards))
 
 
 def on_device(tokens, expert_ids, *rest):

time: 118 us -> 115 us (0.975)
  other arithmetic: 4.23 us -> 11.5 us
  Pallas kernels: 19.4 us -> 12.7 us
  starting transfers between devices: 46.9 us -> 40.6 us
  local copies, waits for them, and re-layouts: 4.37 us -> 6.12 us
    pallas_call x3, Pallas kernels: 19.4 us -> 12.7 us  [serve_rows(): pl.pallas_call(functools.partial(serve_kernel, top_count), out_shape=(out...]
    ppermute x30, starting transfers between devices: 46.9 us -> 40.6 us  [permute(): return lax.ppermute(value, AXES, pairs)]
    concatenate x9, other arithmetic: 0.24 us -> 5.6 us  [chunk_steps(): held = jnp.concatenate([held, got])]
    concatenate x3, other arithmetic: 0.02 us -> 1.92 us  [dense(): own = jnp.concatenate([tokens[at:at + step], extra[at:at + step]], axis=1)]
    unnamed x21 -> x20, local copies, waits for them, and re-layouts: 3.14 us -> 4.89 us
  transfers between devices with their start and end apart: 30 -> 30, of which waited for: 17 -> 17; matrix products, arithmetic and copies ran while one was open for 2% -> 9% of each run, Pallas kernels for 5% -> 11%
where the time goes in v7:
time: 115 us; the launch traced here: 114 us
  waiting for transfers between devices  42.1 us (37%)
  starting transfers between devices  40.6 us (35%)
  Pallas kernels  12.7 us (11%)
  other arithmetic  11.5 us (10%)
  local copies, waits for them, and re-layouts  6.12 us (5%)
    ppermute x30, waiting for transfers between devices, permute(): return lax.ppermute(value, AXES, pairs)  42.1 us
    ppermute x30, starting transfers between devices, permute(): return lax.ppermute(value, AXES, pairs)  40.6 us
    pallas_call x3, Pallas kernels, serve_rows(): pl.pallas_call(functools.partial(serve_kernel, top_count), out_shape=(out...  12.7 us
    concatenate x9, other arithmetic, chunk_steps(): held = jnp.concatenate([held, got])  5.6 us
    unnamed x20, local copies, waits for them, and re-layouts  4.89 us
  transfers between devices with their start and end apart: 30, of which 17 were waited for; matrix products, arithmetic and copies ran while one was open for 9% of the time, Pallas kernels for 11%

profile of v7, /device:TPU:0, one launch (start us, length us, event | category | flops | bytes accessed | tf_op | source)
XLA Modules:
  0.0 113.9 jit_solution(3412037592039362984)
XLA Ops:
  0.0 0.7 reduce_precision.9
  0.7 0.8 copy.13
  1.4 0.7 convert_element_type.239
  2.4 0.9 fusion.10
  3.3 0.6 pad_maximum_fusion.10
  4.0 4.0 %collective-permute-start = (bf16[8,4224]{1,0:T(8,128)(2,1)}, bf16[8,4224]{1,0:T(8,128)(2,1)}, u32[]{:S(2)}, u32[]{:S(2)}) collective-permute-start(bf16[8,4224]{1,0:T(8,128)(2,1)} %get-tuple-element.20), channel_id=1, source_target_pairs={{0,4},{1,5},{2,6},{3,7},{4,0},{5,1},{6,2},{7,3},{8,12},{9,13},{10,... | collective-permute-start | bytes 202760 | tf_op jit(solution)/shard_map/ppermute | solution.py:88
  8.0 0.6 pad_maximum_fusion.12
  8.6 0.6 pad_maximum_fusion.11
  9.3 2.9 %collective-permute-start.10 = (bf16[8,4224]{1,0:T(8,128)(2,1)}, bf16[8,4224]{1,0:T(8,128)(2,1)S(1)}, u32[]{:S(2)}, u32[]{:S(2)}) collective-permute-start(bf16[8,4224]{1,0:T(8,128)(2,1)} %get-tuple-element.22), channel_id=1, source_target_pairs={{0,4},{1,5},{2,6},{3,7},{4,0},{5,1},{6,2},{7,3},{8,12},{9,13},{10,... | collective-permute-start | bytes 202760 | tf_op jit(solution)/shard_map/ppermute | solution.py:88
  12.9 0.9 pad_maximum_fusion.7
  13.8 2.0 %collective-permute-start.1 = (bf16[16,4224]{1,0:T(8,128)(2,1)S(1)}, bf16[16,4224]{1,0:T(8,128)(2,1)S(1)}, u32[]{:S(2)}, u32[]{:S(2)}) collective-permute-start(bf16[16,4224]{1,0:T(8,128)(2,1)S(1)} %pad_maximum_fusion.7), channel_id=1, source_target_pairs={{0,2},{1,3},{2,0},{3,1},{4,6},{5,7},{6,4},{7,5},{8,10},{9,11},{10,... | collective-permute-start | bytes 405512 | tf_op jit(solution)/shard_map/ppermute | solution.py:88
  15.8 1.4 %collective-permute-done.20 = bf16[8,4224]{1,0:T(8,128)(2,1)} collective-permute-done((bf16[8,4224]{1,0:T(8,128)(2,1)}, bf16[8,4224]{1,0:T(8,128)(2,1)}, u32[]{:S(2)}, u32[]{:S(2)}) %collective-permute-start.20) | collective-permute-done | bytes 67616 | tf_op jit(solution)/shard_map/ppermute | solution.py:88
  17.2 0.9 pad_maximum_fusion.9
  18.2 2.1 %collective-permute-start.11 = (bf16[16,4224]{1,0:T(8,128)(2,1)S(1)}, bf16[16,4224]{1,0:T(8,128)(2,1)S(1)}, u32[]{:S(2)}, u32[]{:S(2)}) collective-permute-start(bf16[16,4224]{1,0:T(8,128)(2,1)S(1)} %pad_maximum_fusion.8), channel_id=1, source_target_pairs={{0,2},{1,3},{2,0},{3,1},{4,6},{5,7},{6,4},{7,5},{8,10},{9,11},{10,... | collective-permute-start | bytes 405512 | tf_op jit(solution)/shard_map/ppermute | solution.py:88
  20.2 0.9 constant_dynamic-update-slice_fusion.3
  21.1 0.9 constant_dynamic-update-slice_fusion.13
  22.0 0.9 pad_maximum_fusion.3
  22.9 1.8 %collective-permute-start.2 = (bf16[32,4224]{1,0:T(8,128)(2,1)S(1)}, bf16[32,4224]{1,0:T(8,128)(2,1)S(1)}, u32[]{:S(2)}, u32[]{:S(2)}) collective-permute-start(bf16[32,4224]{1,0:T(8,128)(2,1)S(1)} %pad_maximum_fusion.3), channel_id=1, source_target_pairs={{0,1},{1,0},{2,3},{3,2},{4,5},{5,4},{6,7},{7,6},{8,24},{9,25},{10,... | collective-permute-start | bytes 811016 | tf_op jit(solution)/shard_map/ppermute | solution.py:88
  24.7 0.9 pad_maximum_fusion.5
  25.7 1.7 %collective-permute-start.22 = (bf16[32,4224]{1,0:T(8,128)(2,1)S(1)}, bf16[32,4224]{1,0:T(8,128)(2,1)S(1)}, u32[]{:S(2)}, u32[]{:S(2)}) collective-permute-start(bf16[32,4224]{1,0:T(8,128)(2,1)S(1)} %pad_maximum_fusion.5), channel_id=1, source_target_pairs={{0,1},{1,0},{2,3},{3,2},{4,5},{5,4},{6,7},{7,6},{8,24},{9,25},{10,... | collective-permute-start | bytes 811016 | tf_op jit(solution)/shard_map/ppermute | solution.py:88
  27.4 0.8 collective-permute-start.12
  28.3 1.2 %collective-permute-done.2 = bf16[32,4224]{1,0:T(8,128)(2,1)S(1)} collective-permute-done((bf16[32,4224]{1,0:T(8,128)(2,1)S(1)}, bf16[32,4224]{1,0:T(8,128)(2,1)S(1)}, u32[]{:S(2)}, u32[]{:S(2)}) %collective-permute-start.2) | collective-permute-done | bytes 270368 | tf_op jit(solution)/shard_map/ppermute | solution.py:88
  29.5 1.0 pad_maximum_fusion
  30.5 1.7 %collective-permute-start.3 = (bf16[64,4224]{1,0:T(8,128)(2,1)S(1)}, bf16[64,4224]{1,0:T(8,128)(2,1)S(1)}, u32[]{:S(2)}, u32[]{:S(2)}) collective-permute-start(bf16[64,4224]{1,0:T(8,128)(2,1)S(1)} %pad_maximum_fusion), channel_id=1, source_target_pairs={{0,16},{1,17},{2,18},{3,19},{4,20},{5,21},{6,22},{7,23},{8,9},{9,8... | collective-permute-start | bytes 1622024 | tf_op jit(solution)/shard_map/ppermute | solution.py:88
  32.2 1.4 %collective-permute-done.22 = bf16[32,4224]{1,0:T(8,128)(2,1)S(1)} collective-permute-done((bf16[32,4224]{1,0:T(8,128)(2,1)S(1)}, bf16[32,4224]{1,0:T(8,128)(2,1)S(1)}, u32[]{:S(2)}, u32[]{:S(2)}) %collective-permute-start.22) | collective-permute-done | bytes 270368 | tf_op jit(solution)/shard_map/ppermute | solution.py:88
  33.6 0.9 pad_maximum_fusion.2
  34.5 2.0 %collective-permute-start.23 = (bf16[64,4224]{1,0:T(8,128)(2,1)S(1)}, bf16[64,4224]{1,0:T(8,128)(2,1)S(1)}, u32[]{:S(2)}, u32[]{:S(2)}) collective-permute-start(bf16[64,4224]{1,0:T(8,128)(2,1)S(1)} %pad_maximum_fusion.2), channel_id=1, source_target_pairs={{0,16},{1,17},{2,18},{3,19},{4,20},{5,21},{6,22},{7,23},{8,9},{9,8... | collective-permute-start | bytes 1622024 | tf_op jit(solution)/shard_map/ppermute | solution.py:88
  36.6 2.8 %collective-permute-done.12 = bf16[32,4224]{1,0:T(8,128)(2,1)S(1)} collective-permute-done((bf16[32,4224]{1,0:T(8,128)(2,1)S(1)}, bf16[32,4224]{1,0:T(8,128)(2,1)S(1)}, u32[]{:S(2)}, u32[]{:S(2)}) %collective-permute-start.12) | collective-permute-done | bytes 270368 | tf_op jit(solution)/shard_map/ppermute | solution.py:88
  39.4 2.0 %collective-permute-start.13 = (bf16[64,4224]{1,0:T(8,128)(2,1)S(1)}, bf16[64,4224]{1,0:T(8,128)(2,1)S(1)}, u32[]{:S(2)}, u32[]{:S(2)}) collective-permute-start(bf16[64,4224]{1,0:T(8,128)(2,1)S(1)} %pad_maximum_fusion.1), channel_id=1, source_target_pairs={{0,16},{1,17},{2,18},{3,19},{4,20},{5,21},{6,22},{7,23},{8,9},{9,8... | collective-permute-start | bytes 1622024 | tf_op jit(solution)/shard_map/ppermute | solution.py:88
  41.7 3.9 %collective-permute-done.23 = bf16[64,4224]{1,0:T(8,128)(2,1)S(1)} collective-permute-done((bf16[64,4224]{1,0:T(8,128)(2,1)S(1)}, bf16[64,4224]{1,0:T(8,128)(2,1)S(1)}, u32[]{:S(2)}, u32[]{:S(2)}) %collective-permute-start.23) | collective-permute-done | bytes 540704 | tf_op jit(solution)/shard_map/ppermute | solution.py:88
  45.7 1.3 %collective-permute-start.24 = (bf16[128,4224]{1,0:T(8,128)(2,1)S(1)}, bf16[128,4224]{1,0:T(8,128)(2,1)S(1)}, u32[]{:S(2)}, u32[]{:S(2)}) collective-permute-start(bf16[128,4224]{1,0:T(8,128)(2,1)S(1)} %constant_dynamic-update-slice_fusion.10.own), channel_id=1, source_target_pairs={{0,8},{1,9},{2,10},{3,11},{4,12},{5,13},{6,14},{7,15},{8,0},{9,1},... | collective-permute-start | bytes 3244040 | tf_op jit(solution)/shard_map/ppermute | solution.py:88
  47.1 4.4 %collective-permute-done.13 = bf16[64,4224]{1,0:T(8,128)(2,1)S(1)} collective-permute-done((bf16[64,4224]{1,0:T(8,128)(2,1)S(1)}, bf16[64,4224]{1,0:T(8,128)(2,1)S(1)}, u32[]{:S(2)}, u32[]{:S(2)}) %collective-permute-start.13) | collective-permute-done | bytes 540704 | tf_op jit(solution)/shard_map/ppermute | solution.py:88
  51.5 1.0 collective-permute-start.14
  52.6 0.6 fusion.9
  53.2 2.2 %copy-done.2 = bf16[1,512,4096]{2,1,0:T(8,128)(2,1)S(1)} copy-done((bf16[1,512,4096]{2,1,0:T(8,128)(2,1)S(1)}, bf16[1,512,4096]{2,1,0:T(8,128)(2,1)}, u32[]{:S(2)}) %copy-start.2) | copy-done | bytes 4194328
  55.4 4.3 %serve_rows.3 = (bf16[128,4096]{1,0:T(8,128)(2,1)S(1)}, bf16[128,4096]{1,0:T(8,128)(2,1)S(1)}) custom-call(s32[1]{0:T(128)} %bitcast.1.mine, bf16[128,4224]{1,0:T(8,128)(2,1)S(1)} %constant_dynamic-update-slice_fusion.own, bf16[128,4224]{1,0:T(8,128)(2,1)S(1)} %collective-permute-done.4.sib, bf16[4096,512]{1,0:T(8,128)(2,1)S(1)} %bitcast.5, ...), custom_call_target="tpu_custom_call" | custom-call | flops 3221225472 | bytes 16777216 | tf_op jit(solution)/shard_map/serve_rows/pallas_call | solution.py:151
  59.8 4.2 %serve_rows.5 = (bf16[128,4096]{1,0:T(8,128)(2,1)S(1)}, bf16[128,4096]{1,0:T(8,128)(2,1)S(1)}) custom-call(s32[1]{0:T(128)} %bitcast.1.mine, bf16[128,4224]{1,0:T(8,128)(2,1)S(1)} %constant_dynamic-update-slice_fusion.10.own, bf16[128,4224]{1,0:T(8,128)(2,1)S(1)} %collective-permute-done.24.sib, bf16[4096,512]{1,0:T(8,128)(2,1)S(1)} %bitcast.6, ...), custom_call_target="tpu_custom_call" | custom-call | flops 3221225472 | bytes 16777216 | tf_op jit(solution)/shard_map/serve_rows/pallas_call | solution.py:151
  64.0 0.6 collective-permute-start.25
  64.6 4.2 %serve_rows.4 = (bf16[128,4096]{1,0:T(8,128)(2,1)S(1)}, bf16[128,4096]{1,0:T(8,128)(2,1)S(1)}) custom-call(s32[1]{0:T(128)} %bitcast.1.mine, bf16[128,4224]{1,0:T(8,128)(2,1)S(1)} %constant_dynamic-update-slice_fusion.5.own, bf16[128,4224]{1,0:T(8,128)(2,1)S(1)} %collective-permute-done.14.sib, bf16[4096,512]{1,0:T(8,128)(2,1)S(1)} %bitcast.7, ...), custom_call_target="tpu_custom_call" | custom-call | flops 3221225472 | bytes 16777216 | tf_op jit(solution)/shard_map/serve_rows/pallas_call | solution.py:151
  68.9 0.1 add_convert_fusion.2
  69.0 1.8 %collective-permute-start.6 = (bf16[64,4096]{1,0:T(8,128)(2,1)S(1)}, bf16[64,4096]{1,0:T(8,128)(2,1)S(1)}, u32[]{:S(2)}, u32[]{:S(2)}) collective-permute-start(bf16[64,4096]{1,0:T(8,128)(2,1)S(1)} %add_convert_fusion.2), channel_id=1, source_target_pairs={{0,16},{1,17},{2,18},{3,19},{4,20},{5,21},{6,22},{7,23},{8,9},{9,8... | collective-permute-start | bytes 1572872 | tf_op jit(solution)/shard_map/ppermute | solution.py:88
  70.8 0.1 add_convert_fusion
  70.9 0.4 collective-permute-start.26
  71.3 0.2 collective-permute-done.15
  71.5 0.1 add_convert_fusion.1
  71.6 1.8 %collective-permute-start.16 = (bf16[64,4096]{1,0:T(8,128)(2,1)S(1)}, bf16[64,4096]{1,0:T(8,128)(2,1)S(1)}, u32[]{:S(2)}, u32[]{:S(2)}) collective-permute-start(bf16[64,4096]{1,0:T(8,128)(2,1)S(1)} %add_convert_fusion.1), channel_id=1, source_target_pairs={{0,16},{1,17},{2,18},{3,19},{4,20},{5,21},{6,22},{7,23},{8,9},{9,8... | collective-permute-start | bytes 1572872 | tf_op jit(solution)/shard_map/ppermute | solution.py:88
  73.4 4.8 %collective-permute-done.6 = bf16[64,4096]{1,0:T(8,128)(2,1)S(1)} collective-permute-done((bf16[64,4096]{1,0:T(8,128)(2,1)S(1)}, bf16[64,4096]{1,0:T(8,128)(2,1)S(1)}, u32[]{:S(2)}, u32[]{:S(2)}) %collective-permute-start.6) | collective-permute-done | bytes 524320 | tf_op jit(solution)/shard_map/ppermute | solution.py:88
  78.3 1.8 %collective-permute-start.7 = (bf16[32,4096]{1,0:T(8,128)(2,1)S(1)}, bf16[32,4096]{1,0:T(8,128)(2,1)S(1)}, u32[]{:S(2)}, u32[]{:S(2)}) collective-permute-start(bf16[32,4096]{1,0:T(8,128)(2,1)S(1)} %add_convert_fusion.5), channel_id=1, source_target_pairs={{0,1},{1,0},{2,3},{3,2},{4,5},{5,4},{6,7},{7,6},{8,24},{9,25},{10,... | collective-permute-start | bytes 786440 | tf_op jit(solution)/shard_map/ppermute | solution.py:88
  80.2 6.5 %collective-permute-done.26 = bf16[64,4096]{1,0:T(8,128)(2,1)S(1)} collective-permute-done((bf16[64,4096]{1,0:T(8,128)(2,1)S(1)}, bf16[64,4096]{1,0:T(8,128)(2,1)S(1)}, u32[]{:S(2)}, u32[]{:S(2)}) %collective-permute-start.26) | collective-permute-done | bytes 524320 | tf_op jit(solution)/shard_map/ppermute | solution.py:88
  86.8 1.8 %collective-permute-start.27 = (bf16[32,4096]{1,0:T(8,128)(2,1)S(1)}, bf16[32,4096]{1,0:T(8,128)(2,1)S(1)}, u32[]{:S(2)}, u32[]{:S(2)}) collective-permute-start(bf16[32,4096]{1,0:T(8,128)(2,1)S(1)} %add_convert_fusion.3), channel_id=1, source_target_pairs={{0,1},{1,0},{2,3},{3,2},{4,5},{5,4},{6,7},{7,6},{8,24},{9,25},{10,... | collective-permute-start | bytes 786440 | tf_op jit(solution)/shard_map/ppermute | solution.py:88
  88.6 6.5 %collective-permute-done.16 = bf16[64,4096]{1,0:T(8,128)(2,1)S(1)} collective-permute-done((bf16[64,4096]{1,0:T(8,128)(2,1)S(1)}, bf16[64,4096]{1,0:T(8,128)(2,1)S(1)}, u32[]{:S(2)}, u32[]{:S(2)}) %collective-permute-start.16) | collective-permute-done | bytes 524320 | tf_op jit(solution)/shard_map/ppermute | solution.py:88
  95.2 1.8 %collective-permute-start.17 = (bf16[32,4096]{1,0:T(8,128)(2,1)S(1)}, bf16[32,4096]{1,0:T(8,128)(2,1)S(1)}, u32[]{:S(2)}, u32[]{:S(2)}) collective-permute-start(bf16[32,4096]{1,0:T(8,128)(2,1)S(1)} %add_convert_fusion.4), channel_id=1, source_target_pairs={{0,1},{1,0},{2,3},{3,2},{4,5},{5,4},{6,7},{7,6},{8,24},{9,25},{10,... | collective-permute-start | bytes 786440 | tf_op jit(solution)/shard_map/ppermute | solution.py:88
  97.3 2.1 %collective-permute-start.28 = (bf16[16,4096]{1,0:T(8,128)(2,1)S(1)}, bf16[16,4096]{1,0:T(8,128)(2,1)S(1)}, u32[]{:S(2)}, u32[]{:S(2)}) collective-permute-start(bf16[16,4096]{1,0:T(8,128)(2,1)S(1)} %add_convert_fusion.6), channel_id=1, source_target_pairs={{0,2},{1,3},{2,0},{3,1},{4,6},{5,7},{6,4},{7,5},{8,10},{9,11},{10,... | collective-permute-start | bytes 393224 | tf_op jit(solution)/shard_map/ppermute | solution.py:88
  99.3 2.3 %collective-permute-done.17 = bf16[32,4096]{1,0:T(8,128)(2,1)S(1)} collective-permute-done((bf16[32,4096]{1,0:T(8,128)(2,1)S(1)}, bf16[32,4096]{1,0:T(8,128)(2,1)S(1)}, u32[]{:S(2)}, u32[]{:S(2)}) %collective-permute-start.17) | collective-permute-done | bytes 262176 | tf_op jit(solution)/shard_map/ppermute | solution.py:88
  101.8 1.8 %collective-permute-done.8 = bf16[16,4096]{1,0:T(8,128)(2,1)S(1)} collective-permute-done((bf16[16,4096]{1,0:T(8,128)(2,1)S(1)}, bf16[16,4096]{1,0:T(8,128)(2,1)S(1)}, u32[]{:S(2)}, u32[]{:S(2)}) %collective-permute-start.8) | collective-permute-done | bytes 131104 | tf_op jit(solution)/shard_map/ppermute | solution.py:88
  103.7 1.5 %collective-permute-start.9 = (bf16[8,4096]{1,0:T(8,128)(2,1)S(1)}, bf16[8,4096]{1,0:T(8,128)(2,1)S(1)}, u32[]{:S(2)}, u32[]{:S(2)}) collective-permute-start(bf16[8,4096]{1,0:T(8,128)(2,1)S(1)} %add_convert_fusion.14), channel_id=1, source_target_pairs={{0,4},{1,5},{2,6},{3,7},{4,0},{5,1},{6,2},{7,3},{8,12},{9,13},{10,... | collective-permute-start | bytes 196616 | tf_op jit(solution)/shard_map/ppermute | solution.py:88
  105.2 1.1 collective-permute-done.28
  106.4 1.1 collective-permute-start.29
  107.4 0.3 collective-permute-done.18
  107.8 1.9 %collective-permute-start.19 = (bf16[8,4096]{1,0:T(8,128)(2,1)S(1)}, bf16[8,4096]{1,0:T(8,128)(2,1)S(1)}, u32[]{:S(2)}, u32[]{:S(2)}) collective-permute-start(bf16[8,4096]{1,0:T(8,128)(2,1)S(1)} %add_convert_fusion.12), channel_id=1, source_target_pairs={{0,4},{1,5},{2,6},{3,7},{4,0},{5,1},{6,2},{7,3},{8,12},{9,13},{10,... | collective-permute-start | bytes 196616 | tf_op jit(solution)/shard_map/ppermute | solution.py:88
  109.7 1.8 %collective-permute-done.9 = bf16[8,4096]{1,0:T(8,128)(2,1)S(1)} collective-permute-done((bf16[8,4096]{1,0:T(8,128)(2,1)S(1)}, bf16[8,4096]{1,0:T(8,128)(2,1)S(1)}, u32[]{:S(2)}, u32[]{:S(2)}) %collective-permute-start.9) | collective-permute-done | bytes 65568 | tf_op jit(solution)/shard_map/ppermute | solution.py:88
  111.5 0.9 collective-permute-done.29
  112.5 0.6 collective-permute-done.19
  113.2 0.7 pad_maximum_fusion.6
  (59 shorter events, 2.0 us)
Async XLA Ops:
  4.0 8.9 %collective-permute-start = (bf16[8,4224]{1,0:T(8,128)(2,1)}, bf16[8,4224]{1,0:T(8,128)(2,1)}, u32[]{:S(2)}, u32[]{:S(2)}) collective-permute-start(bf16[8,4224]{1,0:T(8,128)(2,1)} %get-tuple-element.20), channel_id=1, source_target_pairs={{0,4},{1,5},{2,6},{3,7},{4,0},{5,1},{6,2},{7,3},{8,12},{9,13},{10,... | collective-permute-start | bytes 202760 | tf_op jit(solution)/shard_map/ppermute | solution.py:88
  8.6 8.5 %collective-permute-start.20 = (bf16[8,4224]{1,0:T(8,128)(2,1)}, bf16[8,4224]{1,0:T(8,128)(2,1)}, u32[]{:S(2)}, u32[]{:S(2)}) collective-permute-start(bf16[8,4224]{1,0:T(8,128)(2,1)} %get-tuple-element.24), channel_id=1, source_target_pairs={{0,4},{1,5},{2,6},{3,7},{4,0},{5,1},{6,2},{7,3},{8,12},{9,13},{10,... | collective-permute-start | bytes 202760 | tf_op jit(solution)/shard_map/ppermute | solution.py:88
  9.3 8.8 %collective-permute-start.10 = (bf16[8,4224]{1,0:T(8,128)(2,1)}, bf16[8,4224]{1,0:T(8,128)(2,1)S(1)}, u32[]{:S(2)}, u32[]{:S(2)}) collective-permute-start(bf16[8,4224]{1,0:T(8,128)(2,1)} %get-tuple-element.22), channel_id=1, source_target_pairs={{0,4},{1,5},{2,6},{3,7},{4,0},{5,1},{6,2},{7,3},{8,12},{9,13},{10,... | collective-permute-start | bytes 202760 | tf_op jit(solution)/shard_map/ppermute | solution.py:88
  13.8 8.3 %collective-permute-start.1 = (bf16[16,4224]{1,0:T(8,128)(2,1)S(1)}, bf16[16,4224]{1,0:T(8,128)(2,1)S(1)}, u32[]{:S(2)}, u32[]{:S(2)}) collective-permute-start(bf16[16,4224]{1,0:T(8,128)(2,1)S(1)} %pad_maximum_fusion.7), channel_id=1, source_target_pairs={{0,2},{1,3},{2,0},{3,1},{4,6},{5,7},{6,4},{7,5},{8,10},{9,11},{10,... | collective-permute-start | bytes 405512 | tf_op jit(solution)/shard_map/ppermute | solution.py:88
  18.0 6.7 %collective-permute-start.21 = (bf16[16,4224]{1,0:T(8,128)(2,1)S(1)}, bf16[16,4224]{1,0:T(8,128)(2,1)S(1)}, u32[]{:S(2)}, u32[]{:S(2)}) collective-permute-start(bf16[16,4224]{1,0:T(8,128)(2,1)S(1)} %pad_maximum_fusion.9), channel_id=1, source_target_pairs={{0,2},{1,3},{2,0},{3,1},{4,6},{5,7},{6,4},{7,5},{8,10},{9,11},{10,... | collective-permute-start | bytes 405512 | tf_op jit(solution)/shard_map/ppermute | solution.py:88
  18.2 9.2 %collective-permute-start.11 = (bf16[16,4224]{1,0:T(8,128)(2,1)S(1)}, bf16[16,4224]{1,0:T(8,128)(2,1)S(1)}, u32[]{:S(2)}, u32[]{:S(2)}) collective-permute-start(bf16[16,4224]{1,0:T(8,128)(2,1)S(1)} %pad_maximum_fusion.8), channel_id=1, source_target_pairs={{0,2},{1,3},{2,0},{3,1},{4,6},{5,7},{6,4},{7,5},{8,10},{9,11},{10,... | collective-permute-start | bytes 405512 | tf_op jit(solution)/shard_map/ppermute | solution.py:88
  22.9 6.5 %collective-permute-start.2 = (bf16[32,4224]{1,0:T(8,128)(2,1)S(1)}, bf16[32,4224]{1,0:T(8,128)(2,1)S(1)}, u32[]{:S(2)}, u32[]{:S(2)}) collective-permute-start(bf16[32,4224]{1,0:T(8,128)(2,1)S(1)} %pad_maximum_fusion.3), channel_id=1, source_target_pairs={{0,1},{1,0},{2,3},{3,2},{4,5},{5,4},{6,7},{7,6},{8,24},{9,25},{10,... | collective-permute-start | bytes 811016 | tf_op jit(solution)/shard_map/ppermute | solution.py:88
  25.7 7.9 %collective-permute-start.22 = (bf16[32,4224]{1,0:T(8,128)(2,1)S(1)}, bf16[32,4224]{1,0:T(8,128)(2,1)S(1)}, u32[]{:S(2)}, u32[]{:S(2)}) collective-permute-start(bf16[32,4224]{1,0:T(8,128)(2,1)S(1)} %pad_maximum_fusion.5), channel_id=1, source_target_pairs={{0,1},{1,0},{2,3},{3,2},{4,5},{5,4},{6,7},{7,6},{8,24},{9,25},{10,... | collective-permute-start | bytes 811016 | tf_op jit(solution)/shard_map/ppermute | solution.py:88
  27.4 12.0 %collective-permute-start.12 = (bf16[32,4224]{1,0:T(8,128)(2,1)S(1)}, bf16[32,4224]{1,0:T(8,128)(2,1)S(1)}, u32[]{:S(2)}, u32[]{:S(2)}) collective-permute-start(bf16[32,4224]{1,0:T(8,128)(2,1)S(1)} %pad_maximum_fusion.4), channel_id=1, source_target_pairs={{0,1},{1,0},{2,3},{3,2},{4,5},{5,4},{6,7},{7,6},{8,24},{9,25},{10,... | collective-permute-start | bytes 811016 | tf_op jit(solution)/shard_map/ppermute | solution.py:88
  28.3 24.9 %copy-start.1 = (bf16[1,4096,512]{2,1,0:T(8,128)(2,1)S(1)}, bf16[1,4096,512]{2,1,0:T(8,128)(2,1)}, u32[]{:S(2)}) copy-start(bf16[1,4096,512]{2,1,0:T(8,128)(2,1)} %param.14) | copy-start | bytes 12582916
  30.5 11.1 %collective-permute-start.3 = (bf16[64,4224]{1,0:T(8,128)(2,1)S(1)}, bf16[64,4224]{1,0:T(8,128)(2,1)S(1)}, u32[]{:S(2)}, u32[]{:S(2)}) collective-permute-start(bf16[64,4224]{1,0:T(8,128)(2,1)S(1)} %pad_maximum_fusion), channel_id=1, source_target_pairs={{0,16},{1,17},{2,18},{3,19},{4,20},{5,21},{6,22},{7,23},{8,9},{9,8... | collective-permute-start | bytes 1622024 | tf_op jit(solution)/shard_map/ppermute | solution.py:88
  34.5 11.2 %collective-permute-start.23 = (bf16[64,4224]{1,0:T(8,128)(2,1)S(1)}, bf16[64,4224]{1,0:T(8,128)(2,1)S(1)}, u32[]{:S(2)}, u32[]{:S(2)}) collective-permute-start(bf16[64,4224]{1,0:T(8,128)(2,1)S(1)} %pad_maximum_fusion.2), channel_id=1, source_target_pairs={{0,16},{1,17},{2,18},{3,19},{4,20},{5,21},{6,22},{7,23},{8,9},{9,8... | collective-permute-start | bytes 1622024 | tf_op jit(solution)/shard_map/ppermute | solution.py:88
  39.4 12.0 %collective-permute-start.13 = (bf16[64,4224]{1,0:T(8,128)(2,1)S(1)}, bf16[64,4224]{1,0:T(8,128)(2,1)S(1)}, u32[]{:S(2)}, u32[]{:S(2)}) collective-permute-start(bf16[64,4224]{1,0:T(8,128)(2,1)S(1)} %pad_maximum_fusion.1), channel_id=1, source_target_pairs={{0,16},{1,17},{2,18},{3,19},{4,20},{5,21},{6,22},{7,23},{8,9},{9,8... | collective-permute-start | bytes 1622024 | tf_op jit(solution)/shard_map/ppermute | solution.py:88
  41.5 11.1 %copy-start.4 = (s32[16,2]{0,1:T(2,128)S(1)}, s32[16,2]{0,1:T(2,128)}, u32[]{:S(2)}) copy-start(s32[16,2]{0,1:T(2,128)} %param.11) | copy-start | bytes 388
  41.5 11.7 %copy-start = (bf16[1,4096,512]{2,1,0:T(8,128)(2,1)S(1)}, bf16[1,4096,512]{2,1,0:T(8,128)(2,1)}, u32[]{:S(2)}) copy-start(bf16[1,4096,512]{2,1,0:T(8,128)(2,1)} %param.13) | copy-start | bytes 12582916
  41.6 11.6 %collective-permute-start.4 = (bf16[128,4224]{1,0:T(8,128)(2,1)S(1)}, bf16[128,4224]{1,0:T(8,128)(2,1)S(1)}, u32[]{:S(2)}, u32[]{:S(2)}) collective-permute-start(bf16[128,4224]{1,0:T(8,128)(2,1)S(1)} %constant_dynamic-update-slice_fusion.own), channel_id=1, source_target_pairs={{0,8},{1,9},{2,10},{3,11},{4,12},{5,13},{6,14},{7,15},{8,0},{9,1},... | collective-permute-start | bytes 3244040 | tf_op jit(solution)/shard_map/ppermute | solution.py:88
  45.7 14.1 %collective-permute-start.24 = (bf16[128,4224]{1,0:T(8,128)(2,1)S(1)}, bf16[128,4224]{1,0:T(8,128)(2,1)S(1)}, u32[]{:S(2)}, u32[]{:S(2)}) collective-permute-start(bf16[128,4224]{1,0:T(8,128)(2,1)S(1)} %constant_dynamic-update-slice_fusion.10.own), channel_id=1, source_target_pairs={{0,8},{1,9},{2,10},{3,11},{4,12},{5,13},{6,14},{7,15},{8,0},{9,1},... | collective-permute-start | bytes 3244040 | tf_op jit(solution)/shard_map/ppermute | solution.py:88
  51.5 13.1 %collective-permute-start.14 = (bf16[128,4224]{1,0:T(8,128)(2,1)S(1)}, bf16[128,4224]{1,0:T(8,128)(2,1)S(1)}, u32[]{:S(2)}, u32[]{:S(2)}) collective-permute-start(bf16[128,4224]{1,0:T(8,128)(2,1)S(1)} %constant_dynamic-update-slice_fusion.5.own), channel_id=1, source_target_pairs={{0,8},{1,9},{2,10},{3,11},{4,12},{5,13},{6,14},{7,15},{8,0},{9,1},... | collective-permute-start | bytes 3244040 | tf_op jit(solution)/shard_map/ppermute | solution.py:88
  53.2 2.2 %copy-start.2 = (bf16[1,512,4096]{2,1,0:T(8,128)(2,1)S(1)}, bf16[1,512,4096]{2,1,0:T(8,128)(2,1)}, u32[]{:S(2)}) copy-start(bf16[1,512,4096]{2,1,0:T(8,128)(2,1)} %param.15) | copy-start | bytes 12582916
  55.4 4.4 %copy-start.3 = (bf16[1,512,4096]{2,1,0:T(8,128)(2,1)S(1)}, bf16[1,512,4096]{2,1,0:T(8,128)(2,1)}, u32[]{:S(2)}) copy-start(bf16[1,512,4096]{2,1,0:T(8,128)(2,1)} %param.15) | copy-start | bytes 12582916
  59.7 9.1 %collective-permute-start.5 = (bf16[128,4096]{1,0:T(8,128)(2,1)S(1)}, bf16[128,4096]{1,0:T(8,128)(2,1)S(1)}, u32[]{:S(2)}, u32[]{:S(2)}) collective-permute-start(bf16[128,4096]{1,0:T(8,128)(2,1)S(1)} %get-tuple-element.12), channel_id=1, source_target_pairs={{0,8},{1,9},{2,10},{3,11},{4,12},{5,13},{6,14},{7,15},{8,0},{9,1},... | collective-permute-start | bytes 3145736 | tf_op jit(solution)/shard_map/ppermute | solution.py:88
  64.0 6.7 %collective-permute-start.25 = (bf16[128,4096]{1,0:T(8,128)(2,1)S(1)}, bf16[128,4096]{1,0:T(8,128)(2,1)S(1)}, u32[]{:S(2)}, u32[]{:S(2)}) collective-permute-start(bf16[128,4096]{1,0:T(8,128)(2,1)S(1)} %get-tuple-element.16), channel_id=1, source_target_pairs={{0,8},{1,9},{2,10},{3,11},{4,12},{5,13},{6,14},{7,15},{8,0},{9,1},... | collective-permute-start | bytes 3145736 | tf_op jit(solution)/shard_map/ppermute | solution.py:88
  68.8 2.7 %collective-permute-start.15 = (bf16[128,4096]{1,0:T(8,128)(2,1)S(1)}, bf16[128,4096]{1,0:T(8,128)(2,1)S(1)}, u32[]{:S(2)}, u32[]{:S(2)}) collective-permute-start(bf16[128,4096]{1,0:T(8,128)(2,1)S(1)} %get-tuple-element.14), channel_id=1, source_target_pairs={{0,8},{1,9},{2,10},{3,11},{4,12},{5,13},{6,14},{7,15},{8,0},{9,1},... | collective-permute-start | bytes 3145736 | tf_op jit(solution)/shard_map/ppermute | solution.py:88
  69.0 9.2 %collective-permute-start.6 = (bf16[64,4096]{1,0:T(8,128)(2,1)S(1)}, bf16[64,4096]{1,0:T(8,128)(2,1)S(1)}, u32[]{:S(2)}, u32[]{:S(2)}) collective-permute-start(bf16[64,4096]{1,0:T(8,128)(2,1)S(1)} %add_convert_fusion.2), channel_id=1, source_target_pairs={{0,16},{1,17},{2,18},{3,19},{4,20},{5,21},{6,22},{7,23},{8,9},{9,8... | collective-permute-start | bytes 1572872 | tf_op jit(solution)/shard_map/ppermute | solution.py:88
  70.9 15.8 %collective-permute-start.26 = (bf16[64,4096]{1,0:T(8,128)(2,1)S(1)}, bf16[64,4096]{1,0:T(8,128)(2,1)S(1)}, u32[]{:S(2)}, u32[]{:S(2)}) collective-permute-start(bf16[64,4096]{1,0:T(8,128)(2,1)S(1)} %add_convert_fusion), channel_id=1, source_target_pairs={{0,16},{1,17},{2,18},{3,19},{4,20},{5,21},{6,22},{7,23},{8,9},{9,8... | collective-permute-start | bytes 1572872 | tf_op jit(solution)/shard_map/ppermute | solution.py:88
  71.6 23.5 %collective-permute-start.16 = (bf16[64,4096]{1,0:T(8,128)(2,1)S(1)}, bf16[64,4096]{1,0:T(8,128)(2,1)S(1)}, u32[]{:S(2)}, u32[]{:S(2)}) collective-permute-start(bf16[64,4096]{1,0:T(8,128)(2,1)S(1)} %add_convert_fusion.1), channel_id=1, source_target_pairs={{0,16},{1,17},{2,18},{3,19},{4,20},{5,21},{6,22},{7,23},{8,9},{9,8... | collective-permute-start | bytes 1572872 | tf_op jit(solution)/shard_map/ppermute | solution.py:88
  78.3 18.7 %collective-permute-start.7 = (bf16[32,4096]{1,0:T(8,128)(2,1)S(1)}, bf16[32,4096]{1,0:T(8,128)(2,1)S(1)}, u32[]{:S(2)}, u32[]{:S(2)}) collective-permute-start(bf16[32,4096]{1,0:T(8,128)(2,1)S(1)} %add_convert_fusion.5), channel_id=1, source_target_pairs={{0,1},{1,0},{2,3},{3,2},{4,5},{5,4},{6,7},{7,6},{8,24},{9,25},{10,... | collective-permute-start | bytes 786440 | tf_op jit(solution)/shard_map/ppermute | solution.py:88
  86.8 10.4 %collective-permute-start.27 = (bf16[32,4096]{1,0:T(8,128)(2,1)S(1)}, bf16[32,4096]{1,0:T(8,128)(2,1)S(1)}, u32[]{:S(2)}, u32[]{:S(2)}) collective-permute-start(bf16[32,4096]{1,0:T(8,128)(2,1)S(1)} %add_convert_fusion.3), channel_id=1, source_target_pairs={{0,1},{1,0},{2,3},{3,2},{4,5},{5,4},{6,7},{7,6},{8,24},{9,25},{10,... | collective-permute-start | bytes 786440 | tf_op jit(solution)/shard_map/ppermute | solution.py:88
  95.2 6.4 %collective-permute-start.17 = (bf16[32,4096]{1,0:T(8,128)(2,1)S(1)}, bf16[32,4096]{1,0:T(8,128)(2,1)S(1)}, u32[]{:S(2)}, u32[]{:S(2)}) collective-permute-start(bf16[32,4096]{1,0:T(8,128)(2,1)S(1)} %add_convert_fusion.4), channel_id=1, source_target_pairs={{0,1},{1,0},{2,3},{3,2},{4,5},{5,4},{6,7},{7,6},{8,24},{9,25},{10,... | collective-permute-start | bytes 786440 | tf_op jit(solution)/shard_map/ppermute | solution.py:88
  97.1 6.5 %collective-permute-start.8 = (bf16[16,4096]{1,0:T(8,128)(2,1)S(1)}, bf16[16,4096]{1,0:T(8,128)(2,1)S(1)}, u32[]{:S(2)}, u32[]{:S(2)}) collective-permute-start(bf16[16,4096]{1,0:T(8,128)(2,1)S(1)} %add_convert_fusion.8), channel_id=1, source_target_pairs={{0,2},{1,3},{2,0},{3,1},{4,6},{5,7},{6,4},{7,5},{8,10},{9,11},{10,... | collective-permute-start | bytes 393224 | tf_op jit(solution)/shard_map/ppermute | solution.py:88
  97.3 9.1 %collective-permute-start.28 = (bf16[16,4096]{1,0:T(8,128)(2,1)S(1)}, bf16[16,4096]{1,0:T(8,128)(2,1)S(1)}, u32[]{:S(2)}, u32[]{:S(2)}) collective-permute-start(bf16[16,4096]{1,0:T(8,128)(2,1)S(1)} %add_convert_fusion.6), channel_id=1, source_target_pairs={{0,2},{1,3},{2,0},{3,1},{4,6},{5,7},{6,4},{7,5},{8,10},{9,11},{10,... | collective-permute-start | bytes 393224 | tf_op jit(solution)/shard_map/ppermute | solution.py:88
  101.7 6.0 %collective-permute-start.18 = (bf16[16,4096]{1,0:T(8,128)(2,1)S(1)}, bf16[16,4096]{1,0:T(8,128)(2,1)S(1)}, u32[]{:S(2)}, u32[]{:S(2)}) collective-permute-start(bf16[16,4096]{1,0:T(8,128)(2,1)S(1)} %add_convert_fusion.7), channel_id=1, source_target_pairs={{0,2},{1,3},{2,0},{3,1},{4,6},{5,7},{6,4},{7,5},{8,10},{9,11},{10,... | collective-permute-start | bytes 393224 | tf_op jit(solution)/shard_map/ppermute | solution.py:88
  103.7 7.8 %collective-permute-start.9 = (bf16[8,4096]{1,0:T(8,128)(2,1)S(1)}, bf16[8,4096]{1,0:T(8,128)(2,1)S(1)}, u32[]{:S(2)}, u32[]{:S(2)}) collective-permute-start(bf16[8,4096]{1,0:T(8,128)(2,1)S(1)} %add_convert_fusion.14), channel_id=1, source_target_pairs={{0,4},{1,5},{2,6},{3,7},{4,0},{5,1},{6,2},{7,3},{8,12},{9,13},{10,... | collective-permute-start | bytes 196616 | tf_op jit(solution)/shard_map/ppermute | solution.py:88
  106.4 6.1 %collective-permute-start.29 = (bf16[8,4096]{1,0:T(8,128)(2,1)S(1)}, bf16[8,4096]{1,0:T(8,128)(2,1)S(1)}, u32[]{:S(2)}, u32[]{:S(2)}) collective-permute-start(bf16[8,4096]{1,0:T(8,128)(2,1)S(1)} %add_convert_fusion.10), channel_id=1, source_target_pairs={{0,4},{1,5},{2,6},{3,7},{4,0},{5,1},{6,2},{7,3},{8,12},{9,13},{10,... | collective-permute-start | bytes 196616 | tf_op jit(solution)/shard_map/ppermute | solution.py:88
  107.8 5.4 %collective-permute-start.19 = (bf16[8,4096]{1,0:T(8,128)(2,1)S(1)}, bf16[8,4096]{1,0:T(8,128)(2,1)S(1)}, u32[]{:S(2)}, u32[]{:S(2)}) collective-permute-start(bf16[8,4096]{1,0:T(8,128)(2,1)S(1)} %add_convert_fusion.12), channel_id=1, source_target_pairs={{0,4},{1,5},{2,6},{3,7},{4,0},{5,1},{6,2},{7,3},{8,12},{9,13},{10,... | collective-permute-start | bytes 196616 | tf_op jit(solution)/shard_map/ppermute | solution.py:88

commit v8 on v7

--- a/solution.py
+++ b/solution.py
@@ -10,7 +10,7 @@
 AXES = ("dp", "expert")
 LANES = 128
 PARTS = 4
-VMEM_MIB = 8
+VMEM_MIB = 12
 ROWS_AT_ONCE = 8
 GUARDS = []
 
@@ -115,13 +115,36 @@
     return jnp.pad(extra, ((0, 0), (0, -extra.shape[1] % LANES)))
 
 
+def pack_kernel(tokens, extra, *outs):
+    at = 0
+    for out in outs:
+        rows, packed_width = out.shape
+        out[...] = jnp.concatenate([tokens[at : at + rows], extra[at : at + rows]], axis=1)
+        at += rows
+
+
+def packed(tokens, extra, rows):
+    tok_rows, width = tokens.shape
+    whole = pl.BlockSpec(memory_space=pltpu.VMEM)
+    out = jax.ShapeDtypeStruct((rows, width + extra.shape[1]), tokens.dtype)
+    return pl.pallas_call(
+        pack_kernel,
+        out_shape=(out,) * (tok_rows // rows),
+        in_specs=[whole, whole],
+        out_specs=(whole,) * (tok_rows // rows),
+        name="pack_rows",
+    )(tokens, extra)
+
+
 def scale_of(extra, mine, top_count):
     extra = extra.astype(jnp.float32)
     ids, hi, mid, lo = (extra[:, k * top_count : (k + 1) * top_count] for k in range(4))
     return jnp.sum(jnp.where(ids == mine, hi + mid + lo, 0.0), axis=1, keepdims=True)
 
 
-def serve_kernel(top_count, mine, own, sib, w_gate, w_up, w_down, out_own, out_sib):
+def serve_kernel(top_count, mine, own, sib, w_gate, w_up, w_down, out_own, out_sib, down, sem):
+    load = pltpu.make_async_copy(w_down, down, sem)
+    load.start()
     rows = own.shape[0]
     width, hidden_width = w_gate.shape
     depth = width // PARTS
@@ -135,9 +158,10 @@
     hidden = (gate_sum / (1.0 + jnp.exp(-gate_sum)) * up_sum).astype(jnp.bfloat16)
     extra = jnp.concatenate([own[:, width:], sib[:, width:]])
     scale = scale_of(extra, mine[0].astype(jnp.float32), top_count)
+    load.wait()
     for k in range(PARTS):
         part = pl.ds(k * depth, depth)
-        served = jnp.dot(hidden, w_down[:, part], preferred_element_type=jnp.float32) * scale
+        served = jnp.dot(hidden, down[:, part], preferred_element_type=jnp.float32) * scale
         out_own[:, part] = served[:rows].astype(jnp.bfloat16)
         out_sib[:, part] = served[rows:].astype(jnp.bfloat16)
 
@@ -151,8 +175,9 @@
     return pl.pallas_call(
         functools.partial(serve_kernel, top_count),
         out_shape=(out, out),
-        in_specs=[pl.BlockSpec(memory_space=pltpu.SMEM)] + [whole] * 5,
+        in_specs=[pl.BlockSpec(memory_space=pltpu.SMEM)] + [whole] * 4 + [pl.BlockSpec(memory_space=pltpu.HBM)],
         out_specs=(whole, whole),
+        scratch_shapes=[pltpu.VMEM((hidden_width, width), jnp.bfloat16), pltpu.SemaphoreType.DMA],
         compiler_params=pltpu.CompilerParams(vmem_limit_bytes=VMEM_MIB * 2**20),
         cost_estimate=pl.CostEstimate(
             flops=12 * rows * width * hidden_width, bytes_accessed=moved, transcendentals=2 * rows * hidden_width
@@ -173,6 +198,7 @@
         held = jnp.concatenate([held, got])
     (sib,) = yield (permute(held, to_sibling),)
     out, out_sib = serve(held, sib)
+    (out_sib,) = yield (out_sib,)
     (got,) = yield (permute(out_sib, to_sibling),)
     terms = [out]
     for move in moves[::-1]:
@@ -211,11 +237,8 @@
     moves = [along_line(2**bit) for bit in range(line_bits)][::-1] + [over_first, over_second]
     step = ROWS_AT_ONCE if tok_rows % ROWS_AT_ONCE == 0 else tok_rows
     extra = choices(expert_ids, route_weight)
-    chunks = []
-    for at in range(0, tok_rows, step):
-        own = jnp.concatenate([tokens[at : at + step], extra[at : at + step]], axis=1)
-        serve = lambda held, sib: serve_rows(held, sib, mine, top_count, w_gate[0], w_up[0], w_down[0])
-        chunks.append(chunk_steps(own, moves, serve))
+    serve = lambda held, sib: serve_rows(held, sib, mine, top_count, w_gate[0], w_up[0], w_down[0])
+    chunks = [chunk_steps(own, moves, serve) for own in packed(tokens, extra, step)]
     guards = GUARDS if len(chunks) == 3 and len(moves) == 4 else []
     return jnp.concatenate(run_steps(chunks, guards))
 

time: 115 us -> 117 us (1.017)
  starting transfers between devices: 40.6 us -> 47.1 us
  waiting for transfers between devices: 42.1 us -> 37.8 us
  Pallas kernels: 12.7 us -> 15.3 us
  other arithmetic: 11.5 us -> 9.35 us
    ppermute x30, starting transfers between devices: 40.6 us -> 47.1 us  [permute(): return lax.ppermute(value, AXES, pairs)]
    ppermute x30, waiting for transfers between devices: 42.1 us -> 37.8 us  [permute(): return lax.ppermute(value, AXES, pairs)]
    concatenate x3 -> x0, other arithmetic: 1.92 us -> none  [dense(): own = jnp.concatenate([tokens[at:at + step], extra[at:at + step]], axis=1)]
    pallas_call x0 -> x1, Pallas kernels: none -> 1.59 us  [packed(): pl.pallas_call(pack_kernel, out_shape=(out,) * (tok_rows // rows), in_spe...]
    unnamed x20 -> x26, local copies, waits for them, and re-layouts: 4.89 us -> 5.83 us
  transfers between devices with their start and end apart: 30 -> 30, of which waited for: 17 -> 15; matrix products, arithmetic and copies ran while one was open for 9% -> 8% of each run, Pallas kernels for 11% -> 12%
where the time goes in v8:
time: 117 us
  starting transfers between devices  47.1 us (40%)
  waiting for transfers between devices  37.8 us (32%)
  Pallas kernels  15.3 us (13%)
  other arithmetic  9.35 us (8%)
  local copies, waits for them, and re-layouts  6.14 us (5%)
    ppermute x30, starting transfers between devices, permute(): return lax.ppermute(value, AXES, pairs)  47.1 us
    ppermute x30, waiting for transfers between devices, permute(): return lax.ppermute(value, AXES, pairs)  37.8 us
    pallas_call x3, Pallas kernels, serve_rows(): pl.pallas_call(functools.partial(serve_kernel, top_count), out_shape=(out...  13.7 us
    unnamed x26, local copies, waits for them, and re-layouts  5.83 us
    concatenate x9, other arithmetic, chunk_steps(): held = jnp.concatenate([held, got])  4.82 us
  transfers between devices with their start and end apart: 30, of which 15 were waited for; matrix products, arithmetic and copies ran while one was open for 8% of the time, Pallas kernels for 12%

profile of v8, /device:TPU:0, one launch (start us, length us, event | category | flops | bytes accessed | tf_op | source)
XLA Modules:
  0.0 116.6 jit_solution(18036627485264215714)
XLA Ops:
  0.0 0.8 copy.13
  0.8 0.7 reduce_precision.9
  1.5 0.7 convert_element_type.239
  2.3 0.7 fusion.8.extra
  3.0 1.6 %pack_rows.1 = (bf16[8,4224]{1,0:T(8,128)(2,1)}, bf16[8,4224]{1,0:T(8,128)(2,1)}, bf16[8,4224]{1,0:T(8,128)(2,1)}) custom-call(bf16[24,4096]{1,0:T(8,128)(2,1)} %tokens.1, bf16[24,128]{1,0:T(8,128)(2,1)} %fusion.8.extra), custom_call_target="tpu_custom_call" | custom-call | tf_op jit(solution)/shard_map/pack_rows/pallas_call | solution.py:130
  4.6 4.0 %collective-permute-start.20 = (bf16[8,4224]{1,0:T(8,128)(2,1)}, bf16[8,4224]{1,0:T(8,128)(2,1)}, u32[]{:S(2)}, u32[]{:S(2)}) collective-permute-start(bf16[8,4224]{1,0:T(8,128)(2,1)} %get-tuple-element.20), channel_id=1, source_target_pairs={{0,4},{1,5},{2,6},{3,7},{4,0},{5,1},{6,2},{7,3},{8,12},{9,13},{10,... | collective-permute-start | bytes 202760 | tf_op jit(solution)/shard_map/ppermute | solution.py:88
  8.7 2.9 %collective-permute-start = (bf16[8,4224]{1,0:T(8,128)(2,1)}, bf16[8,4224]{1,0:T(8,128)(2,1)S(1)}, u32[]{:S(2)}, u32[]{:S(2)}) collective-permute-start(bf16[8,4224]{1,0:T(8,128)(2,1)} %get-tuple-element.14), channel_id=1, source_target_pairs={{0,4},{1,5},{2,6},{3,7},{4,0},{5,1},{6,2},{7,3},{8,12},{9,13},{10,... | collective-permute-start | bytes 202760 | tf_op jit(solution)/shard_map/ppermute | solution.py:88
  11.5 0.9 constant_dynamic-update-slice_fusion.4
  12.5 0.9 constant_dynamic-update-slice_fusion.14
  14.0 0.9 pad_maximum_fusion.9
  15.0 2.3 %collective-permute-start.21 = (bf16[16,4224]{1,0:T(8,128)(2,1)S(1)}, bf16[16,4224]{1,0:T(8,128)(2,1)S(1)}, u32[]{:S(2)}, u32[]{:S(2)}) collective-permute-start(bf16[16,4224]{1,0:T(8,128)(2,1)S(1)} %pad_maximum_fusion.9), channel_id=1, source_target_pairs={{0,2},{1,3},{2,0},{3,1},{4,6},{5,7},{6,4},{7,5},{8,10},{9,11},{10,... | collective-permute-start | bytes 405512 | tf_op jit(solution)/shard_map/ppermute | solution.py:88
  17.2 0.1 collective-permute-done.10
  17.4 0.9 pad_maximum_fusion.8
  18.3 0.4 collective-permute-start.11
  18.6 0.9 pad_maximum_fusion.7
  19.5 1.8 %collective-permute-start.1 = (bf16[16,4224]{1,0:T(8,128)(2,1)S(1)}, bf16[16,4224]{1,0:T(8,128)(2,1)S(1)}, u32[]{:S(2)}, u32[]{:S(2)}) collective-permute-start(bf16[16,4224]{1,0:T(8,128)(2,1)S(1)} %pad_maximum_fusion.7), channel_id=1, source_target_pairs={{0,2},{1,3},{2,0},{3,1},{4,6},{5,7},{6,4},{7,5},{8,10},{9,11},{10,... | collective-permute-start | bytes 405512 | tf_op jit(solution)/shard_map/ppermute | solution.py:88
  21.3 0.9 constant_dynamic-update-slice_fusion.13
  22.3 0.9 pad_maximum_fusion.5
  23.2 2.9 %collective-permute-start.22 = (bf16[32,4224]{1,0:T(8,128)(2,1)S(1)}, bf16[32,4224]{1,0:T(8,128)(2,1)S(1)}, u32[]{:S(2)}, u32[]{:S(2)}) collective-permute-start(bf16[32,4224]{1,0:T(8,128)(2,1)S(1)} %pad_maximum_fusion.5), channel_id=1, source_target_pairs={{0,1},{1,0},{2,3},{3,2},{4,5},{5,4},{6,7},{7,6},{8,24},{9,25},{10,... | collective-permute-start | bytes 811016 | tf_op jit(solution)/shard_map/ppermute | solution.py:88
  26.1 1.8 %collective-permute-start.12 = (bf16[32,4224]{1,0:T(8,128)(2,1)S(1)}, bf16[32,4224]{1,0:T(8,128)(2,1)S(1)}, u32[]{:S(2)}, u32[]{:S(2)}) collective-permute-start(bf16[32,4224]{1,0:T(8,128)(2,1)S(1)} %pad_maximum_fusion.4), channel_id=1, source_target_pairs={{0,1},{1,0},{2,3},{3,2},{4,5},{5,4},{6,7},{7,6},{8,24},{9,25},{10,... | collective-permute-start | bytes 811016 | tf_op jit(solution)/shard_map/ppermute | solution.py:88
  27.9 1.4 %collective-permute-start.2 = (bf16[32,4224]{1,0:T(8,128)(2,1)S(1)}, bf16[32,4224]{1,0:T(8,128)(2,1)S(1)}, u32[]{:S(2)}, u32[]{:S(2)}) collective-permute-start(bf16[32,4224]{1,0:T(8,128)(2,1)S(1)} %pad_maximum_fusion.3), channel_id=1, source_target_pairs={{0,1},{1,0},{2,3},{3,2},{4,5},{5,4},{6,7},{7,6},{8,24},{9,25},{10,... | collective-permute-start | bytes 811016 | tf_op jit(solution)/shard_map/ppermute | solution.py:88
  29.4 1.1 collective-permute-done.22
  30.5 1.1 pad_maximum_fusion.2
  31.5 1.9 %collective-permute-start.23 = (bf16[64,4224]{1,0:T(8,128)(2,1)S(1)}, bf16[64,4224]{1,0:T(8,128)(2,1)S(1)}, u32[]{:S(2)}, u32[]{:S(2)}) collective-permute-start(bf16[64,4224]{1,0:T(8,128)(2,1)S(1)} %pad_maximum_fusion.2), channel_id=1, source_target_pairs={{0,16},{1,17},{2,18},{3,19},{4,20},{5,21},{6,22},{7,23},{8,9},{9,8... | collective-permute-start | bytes 1622024 | tf_op jit(solution)/shard_map/ppermute | solution.py:88
  33.5 1.7 %collective-permute-done.12 = bf16[32,4224]{1,0:T(8,128)(2,1)S(1)} collective-permute-done((bf16[32,4224]{1,0:T(8,128)(2,1)S(1)}, bf16[32,4224]{1,0:T(8,128)(2,1)S(1)}, u32[]{:S(2)}, u32[]{:S(2)}) %collective-permute-start.12) | collective-permute-done | bytes 270368 | tf_op jit(solution)/shard_map/ppermute | solution.py:88
  35.2 2.3 %collective-permute-start.13 = (bf16[64,4224]{1,0:T(8,128)(2,1)S(1)}, bf16[64,4224]{1,0:T(8,128)(2,1)S(1)}, u32[]{:S(2)}, u32[]{:S(2)}) collective-permute-start(bf16[64,4224]{1,0:T(8,128)(2,1)S(1)} %pad_maximum_fusion.1), channel_id=1, source_target_pairs={{0,16},{1,17},{2,18},{3,19},{4,20},{5,21},{6,22},{7,23},{8,9},{9,8... | collective-permute-start | bytes 1622024 | tf_op jit(solution)/shard_map/ppermute | solution.py:88
  37.5 3.4 %collective-permute-done.2 = bf16[32,4224]{1,0:T(8,128)(2,1)S(1)} collective-permute-done((bf16[32,4224]{1,0:T(8,128)(2,1)S(1)}, bf16[32,4224]{1,0:T(8,128)(2,1)S(1)}, u32[]{:S(2)}, u32[]{:S(2)}) %collective-permute-start.2) | collective-permute-done | bytes 270368 | tf_op jit(solution)/shard_map/ppermute | solution.py:88
  41.0 2.3 %collective-permute-start.3 = (bf16[64,4224]{1,0:T(8,128)(2,1)S(1)}, bf16[64,4224]{1,0:T(8,128)(2,1)S(1)}, u32[]{:S(2)}, u32[]{:S(2)}) collective-permute-start(bf16[64,4224]{1,0:T(8,128)(2,1)S(1)} %pad_maximum_fusion), channel_id=1, source_target_pairs={{0,16},{1,17},{2,18},{3,19},{4,20},{5,21},{6,22},{7,23},{8,9},{9,8... | collective-permute-start | bytes 1622024 | tf_op jit(solution)/shard_map/ppermute | solution.py:88
  43.6 3.2 %collective-permute-done.13 = bf16[64,4224]{1,0:T(8,128)(2,1)S(1)} collective-permute-done((bf16[64,4224]{1,0:T(8,128)(2,1)S(1)}, bf16[64,4224]{1,0:T(8,128)(2,1)S(1)}, u32[]{:S(2)}, u32[]{:S(2)}) %collective-permute-start.13) | collective-permute-done | bytes 540704 | tf_op jit(solution)/shard_map/ppermute | solution.py:88
  46.8 1.3 %collective-permute-start.14 = (bf16[128,4224]{1,0:T(8,128)(2,1)S(1)}, bf16[128,4224]{1,0:T(8,128)(2,1)S(1)}, u32[]{:S(2)}, u32[]{:S(2)}) collective-permute-start(bf16[128,4224]{1,0:T(8,128)(2,1)S(1)} %constant_dynamic-update-slice_fusion.5.own), channel_id=1, source_target_pairs={{0,8},{1,9},{2,10},{3,11},{4,12},{5,13},{6,14},{7,15},{8,0},{9,1},... | collective-permute-start | bytes 3244040 | tf_op jit(solution)/shard_map/ppermute | solution.py:88
  48.1 4.5 %collective-permute-done.3 = bf16[64,4224]{1,0:T(8,128)(2,1)S(1)} collective-permute-done((bf16[64,4224]{1,0:T(8,128)(2,1)S(1)}, bf16[64,4224]{1,0:T(8,128)(2,1)S(1)}, u32[]{:S(2)}, u32[]{:S(2)}) %collective-permute-start.3) | collective-permute-done | bytes 540704 | tf_op jit(solution)/shard_map/ppermute | solution.py:88
  52.6 1.0 collective-permute-start.4
  53.6 0.6 fusion.9
  54.2 2.2 %copy-done.2 = bf16[1,512,4096]{2,1,0:T(8,128)(2,1)S(1)} copy-done((bf16[1,512,4096]{2,1,0:T(8,128)(2,1)S(1)}, bf16[1,512,4096]{2,1,0:T(8,128)(2,1)}, u32[]{:S(2)}) %copy-start.2) | copy-done | bytes 4194328
  56.4 4.6 %serve_rows.5 = (bf16[128,4096]{1,0:T(8,128)(2,1)S(1)}, bf16[128,4096]{1,0:T(8,128)(2,1)S(1)}) custom-call(s32[1]{0:T(128)} %bitcast.1.mine, bf16[128,4224]{1,0:T(8,128)(2,1)S(1)} %constant_dynamic-update-slice_fusion.10.own, bf16[128,4224]{1,0:T(8,128)(2,1)S(1)} %collective-permute-done.24.sib, bf16[4096,512]{1,0:T(8,128)(2,1)S(1)} %bitcast.5, ...), custom_call_target="tpu_custom_call" | custom-call | flops 3221225472 | bytes 16777216 | tf_op jit(solution)/shard_map/serve_rows/pallas_call | solution.py:175
  61.1 4.6 %serve_rows.4 = (bf16[128,4096]{1,0:T(8,128)(2,1)S(1)}, bf16[128,4096]{1,0:T(8,128)(2,1)S(1)}) custom-call(s32[1]{0:T(128)} %bitcast.1.mine, bf16[128,4224]{1,0:T(8,128)(2,1)S(1)} %constant_dynamic-update-slice_fusion.5.own, bf16[128,4224]{1,0:T(8,128)(2,1)S(1)} %collective-permute-done.14.sib, bf16[4096,512]{1,0:T(8,128)(2,1)S(1)} %bitcast.6, ...), custom_call_target="tpu_custom_call" | custom-call | flops 3221225472 | bytes 16777216 | tf_op jit(solution)/shard_map/serve_rows/pallas_call | solution.py:175
  65.6 0.6 collective-permute-start.15
  66.2 4.6 %serve_rows.3 = (bf16[128,4096]{1,0:T(8,128)(2,1)S(1)}, bf16[128,4096]{1,0:T(8,128)(2,1)S(1)}) custom-call(s32[1]{0:T(128)} %bitcast.1.mine, bf16[128,4224]{1,0:T(8,128)(2,1)S(1)} %constant_dynamic-update-slice_fusion.own, bf16[128,4224]{1,0:T(8,128)(2,1)S(1)} %collective-permute-done.4.sib, bf16[4096,512]{1,0:T(8,128)(2,1)S(1)} %bitcast.7, ...), custom_call_target="tpu_custom_call" | custom-call | flops 3221225472 | bytes 16777216 | tf_op jit(solution)/shard_map/serve_rows/pallas_call | solution.py:175
  70.9 0.1 add_convert_fusion
  71.0 2.1 %collective-permute-start.26 = (bf16[64,4096]{1,0:T(8,128)(2,1)S(1)}, bf16[64,4096]{1,0:T(8,128)(2,1)S(1)}, u32[]{:S(2)}, u32[]{:S(2)}) collective-permute-start(bf16[64,4096]{1,0:T(8,128)(2,1)S(1)} %add_convert_fusion), channel_id=1, source_target_pairs={{0,16},{1,17},{2,18},{3,19},{4,20},{5,21},{6,22},{7,23},{8,9},{9,8... | collective-permute-start | bytes 1572872 | tf_op jit(solution)/shard_map/ppermute | solution.py:88
  73.1 0.1 add_convert_fusion.1
  73.2 0.1 collective-permute-start.16
  73.3 0.2 collective-permute-done.5
  73.5 0.1 add_convert_fusion.2
  73.6 2.1 %collective-permute-start.6 = (bf16[64,4096]{1,0:T(8,128)(2,1)S(1)}, bf16[64,4096]{1,0:T(8,128)(2,1)S(1)}, u32[]{:S(2)}, u32[]{:S(2)}) collective-permute-start(bf16[64,4096]{1,0:T(8,128)(2,1)S(1)} %add_convert_fusion.2), channel_id=1, source_target_pairs={{0,16},{1,17},{2,18},{3,19},{4,20},{5,21},{6,22},{7,23},{8,9},{9,8... | collective-permute-start | bytes 1572872 | tf_op jit(solution)/shard_map/ppermute | solution.py:88
  75.7 4.6 %collective-permute-done.26 = bf16[64,4096]{1,0:T(8,128)(2,1)S(1)} collective-permute-done((bf16[64,4096]{1,0:T(8,128)(2,1)S(1)}, bf16[64,4096]{1,0:T(8,128)(2,1)S(1)}, u32[]{:S(2)}, u32[]{:S(2)}) %collective-permute-start.26) | collective-permute-done | bytes 524320 | tf_op jit(solution)/shard_map/ppermute | solution.py:88
  80.2 0.1 add_convert_fusion.3
  80.3 2.1 %collective-permute-start.27 = (bf16[32,4096]{1,0:T(8,128)(2,1)S(1)}, bf16[32,4096]{1,0:T(8,128)(2,1)S(1)}, u32[]{:S(2)}, u32[]{:S(2)}) collective-permute-start(bf16[32,4096]{1,0:T(8,128)(2,1)S(1)} %add_convert_fusion.3), channel_id=1, source_target_pairs={{0,1},{1,0},{2,3},{3,2},{4,5},{5,4},{6,7},{7,6},{8,24},{9,25},{10,... | collective-permute-start | bytes 786440 | tf_op jit(solution)/shard_map/ppermute | solution.py:88
  82.4 6.2 %collective-permute-done.16 = bf16[64,4096]{1,0:T(8,128)(2,1)S(1)} collective-permute-done((bf16[64,4096]{1,0:T(8,128)(2,1)S(1)}, bf16[64,4096]{1,0:T(8,128)(2,1)S(1)}, u32[]{:S(2)}, u32[]{:S(2)}) %collective-permute-start.16) | collective-permute-done | bytes 524320 | tf_op jit(solution)/shard_map/ppermute | solution.py:88
  88.7 0.1 add_convert_fusion.4
  88.8 2.1 %collective-permute-start.17 = (bf16[32,4096]{1,0:T(8,128)(2,1)S(1)}, bf16[32,4096]{1,0:T(8,128)(2,1)S(1)}, u32[]{:S(2)}, u32[]{:S(2)}) collective-permute-start(bf16[32,4096]{1,0:T(8,128)(2,1)S(1)} %add_convert_fusion.4), channel_id=1, source_target_pairs={{0,1},{1,0},{2,3},{3,2},{4,5},{5,4},{6,7},{7,6},{8,24},{9,25},{10,... | collective-permute-start | bytes 786440 | tf_op jit(solution)/shard_map/ppermute | solution.py:88
  90.9 6.2 %collective-permute-done.6 = bf16[64,4096]{1,0:T(8,128)(2,1)S(1)} collective-permute-done((bf16[64,4096]{1,0:T(8,128)(2,1)S(1)}, bf16[64,4096]{1,0:T(8,128)(2,1)S(1)}, u32[]{:S(2)}, u32[]{:S(2)}) %collective-permute-start.6) | collective-permute-done | bytes 524320 | tf_op jit(solution)/shard_map/ppermute | solution.py:88
  97.2 2.1 %collective-permute-start.7 = (bf16[32,4096]{1,0:T(8,128)(2,1)S(1)}, bf16[32,4096]{1,0:T(8,128)(2,1)S(1)}, u32[]{:S(2)}, u32[]{:S(2)}) collective-permute-start(bf16[32,4096]{1,0:T(8,128)(2,1)S(1)} %add_convert_fusion.5), channel_id=1, source_target_pairs={{0,1},{1,0},{2,3},{3,2},{4,5},{5,4},{6,7},{7,6},{8,24},{9,25},{10,... | collective-permute-start | bytes 786440 | tf_op jit(solution)/shard_map/ppermute | solution.py:88
  99.4 0.5 collective-permute-start.28
  99.9 1.6 %collective-permute-start.18 = (bf16[16,4096]{1,0:T(8,128)(2,1)S(1)}, bf16[16,4096]{1,0:T(8,128)(2,1)S(1)}, u32[]{:S(2)}, u32[]{:S(2)}) collective-permute-start(bf16[16,4096]{1,0:T(8,128)(2,1)S(1)} %add_convert_fusion.7), channel_id=1, source_target_pairs={{0,2},{1,3},{2,0},{3,1},{4,6},{5,7},{6,4},{7,5},{8,10},{9,11},{10,... | collective-permute-start | bytes 393224 | tf_op jit(solution)/shard_map/ppermute | solution.py:88
  101.6 2.0 %collective-permute-done.7 = bf16[32,4096]{1,0:T(8,128)(2,1)S(1)} collective-permute-done((bf16[32,4096]{1,0:T(8,128)(2,1)S(1)}, bf16[32,4096]{1,0:T(8,128)(2,1)S(1)}, u32[]{:S(2)}, u32[]{:S(2)}) %collective-permute-start.7) | collective-permute-done | bytes 262176 | tf_op jit(solution)/shard_map/ppermute | solution.py:88
  103.7 0.7 collective-permute-start.8
  104.6 3.4 %collective-permute-start.29 = (bf16[8,4096]{1,0:T(8,128)(2,1)S(1)}, bf16[8,4096]{1,0:T(8,128)(2,1)S(1)}, u32[]{:S(2)}, u32[]{:S(2)}) collective-permute-start(bf16[8,4096]{1,0:T(8,128)(2,1)S(1)} %add_convert_fusion.10), channel_id=1, source_target_pairs={{0,4},{1,5},{2,6},{3,7},{4,0},{5,1},{6,2},{7,3},{8,12},{9,13},{10,... | collective-permute-start | bytes 196616 | tf_op jit(solution)/shard_map/ppermute | solution.py:88
  108.0 1.8 %collective-permute-start.19 = (bf16[8,4096]{1,0:T(8,128)(2,1)S(1)}, bf16[8,4096]{1,0:T(8,128)(2,1)S(1)}, u32[]{:S(2)}, u32[]{:S(2)}) collective-permute-start(bf16[8,4096]{1,0:T(8,128)(2,1)S(1)} %add_convert_fusion.12), channel_id=1, source_target_pairs={{0,4},{1,5},{2,6},{3,7},{4,0},{5,1},{6,2},{7,3},{8,12},{9,13},{10,... | collective-permute-start | bytes 196616 | tf_op jit(solution)/shard_map/ppermute | solution.py:88
  109.8 0.7 collective-permute-done.8
  110.6 1.5 %collective-permute-start.9 = (bf16[8,4096]{1,0:T(8,128)(2,1)S(1)}, bf16[8,4096]{1,0:T(8,128)(2,1)S(1)}, u32[]{:S(2)}, u32[]{:S(2)}) collective-permute-start(bf16[8,4096]{1,0:T(8,128)(2,1)S(1)} %add_convert_fusion.14), channel_id=1, source_target_pairs={{0,4},{1,5},{2,6},{3,7},{4,0},{5,1},{6,2},{7,3},{8,12},{9,13},{10,... | collective-permute-start | bytes 196616 | tf_op jit(solution)/shard_map/ppermute | solution.py:88
  112.1 2.8 %collective-permute-done.19 = bf16[8,4096]{1,0:T(8,128)(2,1)S(1)} collective-permute-done((bf16[8,4096]{1,0:T(8,128)(2,1)S(1)}, bf16[8,4096]{1,0:T(8,128)(2,1)S(1)}, u32[]{:S(2)}, u32[]{:S(2)}) %collective-permute-start.19) | collective-permute-done | bytes 65568 | tf_op jit(solution)/shard_map/ppermute | solution.py:88
  115.0 0.9 collective-permute-done.9
  115.9 0.7 pad_maximum_fusion.6
  (61 shorter events, 1.7 us)
Async XLA Ops:
  4.6 17.7 %copy-start.5 = (bf16[8,4224]{1,0:T(8,128)(2,1)S(1)}, bf16[8,4224]{1,0:T(8,128)(2,1)}, u32[]{:S(2)}) copy-start(bf16[8,4224]{1,0:T(8,128)(2,1)} %get-tuple-element.20) | copy-start | bytes 202756
  4.6 9.4 %collective-permute-start.20 = (bf16[8,4224]{1,0:T(8,128)(2,1)}, bf16[8,4224]{1,0:T(8,128)(2,1)}, u32[]{:S(2)}, u32[]{:S(2)}) collective-permute-start(bf16[8,4224]{1,0:T(8,128)(2,1)} %get-tuple-element.20), channel_id=1, source_target_pairs={{0,4},{1,5},{2,6},{3,7},{4,0},{5,1},{6,2},{7,3},{8,12},{9,13},{10,... | collective-permute-start | bytes 202760 | tf_op jit(solution)/shard_map/ppermute | solution.py:88
  8.6 8.8 %collective-permute-start.10 = (bf16[8,4224]{1,0:T(8,128)(2,1)}, bf16[8,4224]{1,0:T(8,128)(2,1)S(1)}, u32[]{:S(2)}, u32[]{:S(2)}) collective-permute-start(bf16[8,4224]{1,0:T(8,128)(2,1)} %get-tuple-element.17), channel_id=1, source_target_pairs={{0,4},{1,5},{2,6},{3,7},{4,0},{5,1},{6,2},{7,3},{8,12},{9,13},{10,... | collective-permute-start | bytes 202760 | tf_op jit(solution)/shard_map/ppermute | solution.py:88
  8.7 17.4 %copy-start.4 = (bf16[8,4224]{1,0:T(8,128)(2,1)S(1)}, bf16[8,4224]{1,0:T(8,128)(2,1)}, u32[]{:S(2)}) copy-start(bf16[8,4224]{1,0:T(8,128)(2,1)} %get-tuple-element.17) | copy-start | bytes 202756
  8.7 10.0 %collective-permute-start = (bf16[8,4224]{1,0:T(8,128)(2,1)}, bf16[8,4224]{1,0:T(8,128)(2,1)S(1)}, u32[]{:S(2)}, u32[]{:S(2)}) collective-permute-start(bf16[8,4224]{1,0:T(8,128)(2,1)} %get-tuple-element.14), channel_id=1, source_target_pairs={{0,4},{1,5},{2,6},{3,7},{4,0},{5,1},{6,2},{7,3},{8,12},{9,13},{10,... | collective-permute-start | bytes 202760 | tf_op jit(solution)/shard_map/ppermute | solution.py:88
  15.0 12.9 %copy-start.3 = (bf16[8,4224]{1,0:T(8,128)(2,1)S(1)}, bf16[8,4224]{1,0:T(8,128)(2,1)}, u32[]{:S(2)}) copy-start(bf16[8,4224]{1,0:T(8,128)(2,1)} %get-tuple-element.14) | copy-start | bytes 202756
  15.0 7.3 %collective-permute-start.21 = (bf16[16,4224]{1,0:T(8,128)(2,1)S(1)}, bf16[16,4224]{1,0:T(8,128)(2,1)S(1)}, u32[]{:S(2)}, u32[]{:S(2)}) collective-permute-start(bf16[16,4224]{1,0:T(8,128)(2,1)S(1)} %pad_maximum_fusion.9), channel_id=1, source_target_pairs={{0,2},{1,3},{2,0},{3,1},{4,6},{5,7},{6,4},{7,5},{8,10},{9,11},{10,... | collective-permute-start | bytes 405512 | tf_op jit(solution)/shard_map/ppermute | solution.py:88
  18.3 7.8 %collective-permute-start.11 = (bf16[16,4224]{1,0:T(8,128)(2,1)S(1)}, bf16[16,4224]{1,0:T(8,128)(2,1)S(1)}, u32[]{:S(2)}, u32[]{:S(2)}) collective-permute-start(bf16[16,4224]{1,0:T(8,128)(2,1)S(1)} %pad_maximum_fusion.8), channel_id=1, source_target_pairs={{0,2},{1,3},{2,0},{3,1},{4,6},{5,7},{6,4},{7,5},{8,10},{9,11},{10,... | collective-permute-start | bytes 405512 | tf_op jit(solution)/shard_map/ppermute | solution.py:88
  19.5 8.3 %collective-permute-start.1 = (bf16[16,4224]{1,0:T(8,128)(2,1)S(1)}, bf16[16,4224]{1,0:T(8,128)(2,1)S(1)}, u32[]{:S(2)}, u32[]{:S(2)}) collective-permute-start(bf16[16,4224]{1,0:T(8,128)(2,1)S(1)} %pad_maximum_fusion.7), channel_id=1, source_target_pairs={{0,2},{1,3},{2,0},{3,1},{4,6},{5,7},{6,4},{7,5},{8,10},{9,11},{10,... | collective-permute-start | bytes 405512 | tf_op jit(solution)/shard_map/ppermute | solution.py:88
  23.2 7.3 %collective-permute-start.22 = (bf16[32,4224]{1,0:T(8,128)(2,1)S(1)}, bf16[32,4224]{1,0:T(8,128)(2,1)S(1)}, u32[]{:S(2)}, u32[]{:S(2)}) collective-permute-start(bf16[32,4224]{1,0:T(8,128)(2,1)S(1)} %pad_maximum_fusion.5), channel_id=1, source_target_pairs={{0,1},{1,0},{2,3},{3,2},{4,5},{5,4},{6,7},{7,6},{8,24},{9,25},{10,... | collective-permute-start | bytes 811016 | tf_op jit(solution)/shard_map/ppermute | solution.py:88
  26.1 9.1 %collective-permute-start.12 = (bf16[32,4224]{1,0:T(8,128)(2,1)S(1)}, bf16[32,4224]{1,0:T(8,128)(2,1)S(1)}, u32[]{:S(2)}, u32[]{:S(2)}) collective-permute-start(bf16[32,4224]{1,0:T(8,128)(2,1)S(1)} %pad_maximum_fusion.4), channel_id=1, source_target_pairs={{0,1},{1,0},{2,3},{3,2},{4,5},{5,4},{6,7},{7,6},{8,24},{9,25},{10,... | collective-permute-start | bytes 811016 | tf_op jit(solution)/shard_map/ppermute | solution.py:88
  27.9 13.1 %collective-permute-start.2 = (bf16[32,4224]{1,0:T(8,128)(2,1)S(1)}, bf16[32,4224]{1,0:T(8,128)(2,1)S(1)}, u32[]{:S(2)}, u32[]{:S(2)}) collective-permute-start(bf16[32,4224]{1,0:T(8,128)(2,1)S(1)} %pad_maximum_fusion.3), channel_id=1, source_target_pairs={{0,1},{1,0},{2,3},{3,2},{4,5},{5,4},{6,7},{7,6},{8,24},{9,25},{10,... | collective-permute-start | bytes 811016 | tf_op jit(solution)/shard_map/ppermute | solution.py:88
  29.4 24.9 %copy-start.1 = (bf16[1,4096,512]{2,1,0:T(8,128)(2,1)S(1)}, bf16[1,4096,512]{2,1,0:T(8,128)(2,1)}, u32[]{:S(2)}) copy-start(bf16[1,4096,512]{2,1,0:T(8,128)(2,1)} %param.14) | copy-start | bytes 12582916
  31.5 11.9 %collective-permute-start.23 = (bf16[64,4224]{1,0:T(8,128)(2,1)S(1)}, bf16[64,4224]{1,0:T(8,128)(2,1)S(1)}, u32[]{:S(2)}, u32[]{:S(2)}) collective-permute-start(bf16[64,4224]{1,0:T(8,128)(2,1)S(1)} %pad_maximum_fusion.2), channel_id=1, source_target_pairs={{0,16},{1,17},{2,18},{3,19},{4,20},{5,21},{6,22},{7,23},{8,9},{9,8... | collective-permute-start | bytes 1622024 | tf_op jit(solution)/shard_map/ppermute | solution.py:88
  35.2 11.6 %collective-permute-start.13 = (bf16[64,4224]{1,0:T(8,128)(2,1)S(1)}, bf16[64,4224]{1,0:T(8,128)(2,1)S(1)}, u32[]{:S(2)}, u32[]{:S(2)}) collective-permute-start(bf16[64,4224]{1,0:T(8,128)(2,1)S(1)} %pad_maximum_fusion.1), channel_id=1, source_target_pairs={{0,16},{1,17},{2,18},{3,19},{4,20},{5,21},{6,22},{7,23},{8,9},{9,8... | collective-permute-start | bytes 1622024 | tf_op jit(solution)/shard_map/ppermute | solution.py:88
  41.0 11.5 %collective-permute-start.3 = (bf16[64,4224]{1,0:T(8,128)(2,1)S(1)}, bf16[64,4224]{1,0:T(8,128)(2,1)S(1)}, u32[]{:S(2)}, u32[]{:S(2)}) collective-permute-start(bf16[64,4224]{1,0:T(8,128)(2,1)S(1)} %pad_maximum_fusion), channel_id=1, source_target_pairs={{0,16},{1,17},{2,18},{3,19},{4,20},{5,21},{6,22},{7,23},{8,9},{9,8... | collective-permute-start | bytes 1622024 | tf_op jit(solution)/shard_map/ppermute | solution.py:88
  43.3 10.3 %copy-start.6 = (s32[16,2]{0,1:T(2,128)S(1)}, s32[16,2]{0,1:T(2,128)}, u32[]{:S(2)}) copy-start(s32[16,2]{0,1:T(2,128)} %param.11) | copy-start | bytes 388
  43.3 10.9 %copy-start = (bf16[1,4096,512]{2,1,0:T(8,128)(2,1)S(1)}, bf16[1,4096,512]{2,1,0:T(8,128)(2,1)}, u32[]{:S(2)}) copy-start(bf16[1,4096,512]{2,1,0:T(8,128)(2,1)} %param.13) | copy-start | bytes 12582916
  43.5 10.7 %collective-permute-start.24 = (bf16[128,4224]{1,0:T(8,128)(2,1)S(1)}, bf16[128,4224]{1,0:T(8,128)(2,1)S(1)}, u32[]{:S(2)}, u32[]{:S(2)}) collective-permute-start(bf16[128,4224]{1,0:T(8,128)(2,1)S(1)} %constant_dynamic-update-slice_fusion.10.own), channel_id=1, source_target_pairs={{0,8},{1,9},{2,10},{3,11},{4,12},{5,13},{6,14},{7,15},{8,0},{9,1},... | collective-permute-start | bytes 3244040 | tf_op jit(solution)/shard_map/ppermute | solution.py:88
  46.8 14.3 %collective-permute-start.14 = (bf16[128,4224]{1,0:T(8,128)(2,1)S(1)}, bf16[128,4224]{1,0:T(8,128)(2,1)S(1)}, u32[]{:S(2)}, u32[]{:S(2)}) collective-permute-start(bf16[128,4224]{1,0:T(8,128)(2,1)S(1)} %constant_dynamic-update-slice_fusion.5.own), channel_id=1, source_target_pairs={{0,8},{1,9},{2,10},{3,11},{4,12},{5,13},{6,14},{7,15},{8,0},{9,1},... | collective-permute-start | bytes 3244040 | tf_op jit(solution)/shard_map/ppermute | solution.py:88
  52.6 13.6 %collective-permute-start.4 = (bf16[128,4224]{1,0:T(8,128)(2,1)S(1)}, bf16[128,4224]{1,0:T(8,128)(2,1)S(1)}, u32[]{:S(2)}, u32[]{:S(2)}) collective-permute-start(bf16[128,4224]{1,0:T(8,128)(2,1)S(1)} %constant_dynamic-update-slice_fusion.own), channel_id=1, source_target_pairs={{0,8},{1,9},{2,10},{3,11},{4,12},{5,13},{6,14},{7,15},{8,0},{9,1},... | collective-permute-start | bytes 3244040 | tf_op jit(solution)/shard_map/ppermute | solution.py:88
  54.2 2.2 %copy-start.2 = (bf16[1,512,4096]{2,1,0:T(8,128)(2,1)S(1)}, bf16[1,512,4096]{2,1,0:T(8,128)(2,1)}, u32[]{:S(2)}) copy-start(bf16[1,512,4096]{2,1,0:T(8,128)(2,1)} %param.15) | copy-start | bytes 12582916
  61.0 9.9 %collective-permute-start.25 = (bf16[128,4096]{1,0:T(8,128)(2,1)S(1)}, bf16[128,4096]{1,0:T(8,128)(2,1)S(1)}, u32[]{:S(2)}, u32[]{:S(2)}) collective-permute-start(bf16[128,4096]{1,0:T(8,128)(2,1)S(1)} %get-tuple-element.22), channel_id=1, source_target_pairs={{0,8},{1,9},{2,10},{3,11},{4,12},{5,13},{6,14},{7,15},{8,0},{9,1},... | collective-permute-start | bytes 3145736 | tf_op jit(solution)/shard_map/ppermute | solution.py:88
  65.6 7.4 %collective-permute-start.15 = (bf16[128,4096]{1,0:T(8,128)(2,1)S(1)}, bf16[128,4096]{1,0:T(8,128)(2,1)S(1)}, u32[]{:S(2)}, u32[]{:S(2)}) collective-permute-start(bf16[128,4096]{1,0:T(8,128)(2,1)S(1)} %get-tuple-element.19), channel_id=1, source_target_pairs={{0,8},{1,9},{2,10},{3,11},{4,12},{5,13},{6,14},{7,15},{8,0},{9,1},... | collective-permute-start | bytes 3145736 | tf_op jit(solution)/shard_map/ppermute | solution.py:88
  70.8 2.7 %collective-permute-start.5 = (bf16[128,4096]{1,0:T(8,128)(2,1)S(1)}, bf16[128,4096]{1,0:T(8,128)(2,1)S(1)}, u32[]{:S(2)}, u32[]{:S(2)}) collective-permute-start(bf16[128,4096]{1,0:T(8,128)(2,1)S(1)} %get-tuple-element.16), channel_id=1, source_target_pairs={{0,8},{1,9},{2,10},{3,11},{4,12},{5,13},{6,14},{7,15},{8,0},{9,1},... | collective-permute-start | bytes 3145736 | tf_op jit(solution)/shard_map/ppermute | solution.py:88
  71.0 9.2 %collective-permute-start.26 = (bf16[64,4096]{1,0:T(8,128)(2,1)S(1)}, bf16[64,4096]{1,0:T(8,128)(2,1)S(1)}, u32[]{:S(2)}, u32[]{:S(2)}) collective-permute-start(bf16[64,4096]{1,0:T(8,128)(2,1)S(1)} %add_convert_fusion), channel_id=1, source_target_pairs={{0,16},{1,17},{2,18},{3,19},{4,20},{5,21},{6,22},{7,23},{8,9},{9,8... | collective-permute-start | bytes 1572872 | tf_op jit(solution)/shard_map/ppermute | solution.py:88
  73.2 15.5 %collective-permute-start.16 = (bf16[64,4096]{1,0:T(8,128)(2,1)S(1)}, bf16[64,4096]{1,0:T(8,128)(2,1)S(1)}, u32[]{:S(2)}, u32[]{:S(2)}) collective-permute-start(bf16[64,4096]{1,0:T(8,128)(2,1)S(1)} %add_convert_fusion.1), channel_id=1, source_target_pairs={{0,16},{1,17},{2,18},{3,19},{4,20},{5,21},{6,22},{7,23},{8,9},{9,8... | collective-permute-start | bytes 1572872 | tf_op jit(solution)/shard_map/ppermute | solution.py:88
  73.6 23.5 %collective-permute-start.6 = (bf16[64,4096]{1,0:T(8,128)(2,1)S(1)}, bf16[64,4096]{1,0:T(8,128)(2,1)S(1)}, u32[]{:S(2)}, u32[]{:S(2)}) collective-permute-start(bf16[64,4096]{1,0:T(8,128)(2,1)S(1)} %add_convert_fusion.2), channel_id=1, source_target_pairs={{0,16},{1,17},{2,18},{3,19},{4,20},{5,21},{6,22},{7,23},{8,9},{9,8... | collective-permute-start | bytes 1572872 | tf_op jit(solution)/shard_map/ppermute | solution.py:88
  80.3 18.9 %collective-permute-start.27 = (bf16[32,4096]{1,0:T(8,128)(2,1)S(1)}, bf16[32,4096]{1,0:T(8,128)(2,1)S(1)}, u32[]{:S(2)}, u32[]{:S(2)}) collective-permute-start(bf16[32,4096]{1,0:T(8,128)(2,1)S(1)} %add_convert_fusion.3), channel_id=1, source_target_pairs={{0,1},{1,0},{2,3},{3,2},{4,5},{5,4},{6,7},{7,6},{8,24},{9,25},{10,... | collective-permute-start | bytes 786440 | tf_op jit(solution)/shard_map/ppermute | solution.py:88
  88.8 11.1 %collective-permute-start.17 = (bf16[32,4096]{1,0:T(8,128)(2,1)S(1)}, bf16[32,4096]{1,0:T(8,128)(2,1)S(1)}, u32[]{:S(2)}, u32[]{:S(2)}) collective-permute-start(bf16[32,4096]{1,0:T(8,128)(2,1)S(1)} %add_convert_fusion.4), channel_id=1, source_target_pairs={{0,1},{1,0},{2,3},{3,2},{4,5},{5,4},{6,7},{7,6},{8,24},{9,25},{10,... | collective-permute-start | bytes 786440 | tf_op jit(solution)/shard_map/ppermute | solution.py:88
  97.2 6.4 %collective-permute-start.7 = (bf16[32,4096]{1,0:T(8,128)(2,1)S(1)}, bf16[32,4096]{1,0:T(8,128)(2,1)S(1)}, u32[]{:S(2)}, u32[]{:S(2)}) collective-permute-start(bf16[32,4096]{1,0:T(8,128)(2,1)S(1)} %add_convert_fusion.5), channel_id=1, source_target_pairs={{0,1},{1,0},{2,3},{3,2},{4,5},{5,4},{6,7},{7,6},{8,24},{9,25},{10,... | collective-permute-start | bytes 786440 | tf_op jit(solution)/shard_map/ppermute | solution.py:88
  99.4 5.2 %collective-permute-start.28 = (bf16[16,4096]{1,0:T(8,128)(2,1)S(1)}, bf16[16,4096]{1,0:T(8,128)(2,1)S(1)}, u32[]{:S(2)}, u32[]{:S(2)}) collective-permute-start(bf16[16,4096]{1,0:T(8,128)(2,1)S(1)} %add_convert_fusion.6), channel_id=1, source_target_pairs={{0,2},{1,3},{2,0},{3,1},{4,6},{5,7},{6,4},{7,5},{8,10},{9,11},{10,... | collective-permute-start | bytes 393224 | tf_op jit(solution)/shard_map/ppermute | solution.py:88
  99.9 8.0 %collective-permute-start.18 = (bf16[16,4096]{1,0:T(8,128)(2,1)S(1)}, bf16[16,4096]{1,0:T(8,128)(2,1)S(1)}, u32[]{:S(2)}, u32[]{:S(2)}) collective-permute-start(bf16[16,4096]{1,0:T(8,128)(2,1)S(1)} %add_convert_fusion.7), channel_id=1, source_target_pairs={{0,2},{1,3},{2,0},{3,1},{4,6},{5,7},{6,4},{7,5},{8,10},{9,11},{10,... | collective-permute-start | bytes 393224 | tf_op jit(solution)/shard_map/ppermute | solution.py:88
  103.7 6.8 %collective-permute-start.8 = (bf16[16,4096]{1,0:T(8,128)(2,1)S(1)}, bf16[16,4096]{1,0:T(8,128)(2,1)S(1)}, u32[]{:S(2)}, u32[]{:S(2)}) collective-permute-start(bf16[16,4096]{1,0:T(8,128)(2,1)S(1)} %add_convert_fusion.8), channel_id=1, source_target_pairs={{0,2},{1,3},{2,0},{3,1},{4,6},{5,7},{6,4},{7,5},{8,10},{9,11},{10,... | collective-permute-start | bytes 393224 | tf_op jit(solution)/shard_map/ppermute | solution.py:88
  104.6 7.5 %collective-permute-start.29 = (bf16[8,4096]{1,0:T(8,128)(2,1)S(1)}, bf16[8,4096]{1,0:T(8,128)(2,1)S(1)}, u32[]{:S(2)}, u32[]{:S(2)}) collective-permute-start(bf16[8,4096]{1,0:T(8,128)(2,1)S(1)} %add_convert_fusion.10), channel_id=1, source_target_pairs={{0,4},{1,5},{2,6},{3,7},{4,0},{5,1},{6,2},{7,3},{8,12},{9,13},{10,... | collective-permute-start | bytes 196616 | tf_op jit(solution)/shard_map/ppermute | solution.py:88
  108.0 6.9 %collective-permute-start.19 = (bf16[8,4096]{1,0:T(8,128)(2,1)S(1)}, bf16[8,4096]{1,0:T(8,128)(2,1)S(1)}, u32[]{:S(2)}, u32[]{:S(2)}) collective-permute-start(bf16[8,4096]{1,0:T(8,128)(2,1)S(1)} %add_convert_fusion.12), channel_id=1, source_target_pairs={{0,4},{1,5},{2,6},{3,7},{4,0},{5,1},{6,2},{7,3},{8,12},{9,13},{10,... | collective-permute-start | bytes 196616 | tf_op jit(solution)/shard_map/ppermute | solution.py:88
  110.6 5.2 %collective-permute-start.9 = (bf16[8,4096]{1,0:T(8,128)(2,1)S(1)}, bf16[8,4096]{1,0:T(8,128)(2,1)S(1)}, u32[]{:S(2)}, u32[]{:S(2)}) collective-permute-start(bf16[8,4096]{1,0:T(8,128)(2,1)S(1)} %add_convert_fusion.14), channel_id=1, source_target_pairs={{0,4},{1,5},{2,6},{3,7},{4,0},{5,1},{6,2},{7,3},{8,12},{9,13},{10,... | collective-permute-start | bytes 196616 | tf_op jit(solution)/shard_map/ppermute | solution.py:88

commit v9 on v8

--- a/solution.py
+++ b/solution.py
@@ -126,7 +126,7 @@
 def packed(tokens, extra, rows):
     tok_rows, width = tokens.shape
     whole = pl.BlockSpec(memory_space=pltpu.VMEM)
-    out = jax.ShapeDtypeStruct((rows, width + extra.shape[1]), tokens.dtype)
+    out = pltpu.VMEM((rows, width + extra.shape[1]), tokens.dtype)
     return pl.pallas_call(
         pack_kernel,
         out_shape=(out,) * (tok_rows // rows),
@@ -183,7 +183,7 @@
             flops=12 * rows * width * hidden_width, bytes_accessed=moved, transcendentals=2 * rows * hidden_width
         ),
         name="serve_rows",
-    )(mine.reshape(1), own, sib, w_gate, w_up, w_down)
+    )(mine.reshape(1), own, sib, w_gate, w_up, pltpu.with_memory_space_constraint(w_down, pltpu.HBM))
 
 
 def total(*terms):
@@ -234,12 +234,15 @@
     top_count = expert_ids.shape[1]
     mine = served_expert(slot_of, swap_flag)
     line_bits = (lax.axis_size("expert") // 2).bit_length() - 1
-    moves = [along_line(2**bit) for bit in range(line_bits)][::-1] + [over_first, over_second]
+    along = [along_line(2**bit) for bit in range(line_bits)][::-1]
+    across = [over_first, over_second]
+    routes = [along[:1] + across + along[1:], along + across, along + across]
     step = ROWS_AT_ONCE if tok_rows % ROWS_AT_ONCE == 0 else tok_rows
     extra = choices(expert_ids, route_weight)
     serve = lambda held, sib: serve_rows(held, sib, mine, top_count, w_gate[0], w_up[0], w_down[0])
-    chunks = [chunk_steps(own, moves, serve) for own in packed(tokens, extra, step)]
-    guards = GUARDS if len(chunks) == 3 and len(moves) == 4 else []
+    owns = packed(tokens, extra, step)
+    chunks = [chunk_steps(own, routes[i % len(routes)], serve) for i, own in enumerate(owns)]
+    guards = GUARDS if len(chunks) == 3 and line_bits == 2 else []
     return jnp.concatenate(run_steps(chunks, guards))
 
 

time: 117 us -> 112 us (0.957)
  starting transfers between devices: 47.1 us -> 35.1 us
  Pallas kernels: 15.3 us -> 20 us
  waiting for transfers between devices: 37.8 us -> 41.8 us
  local copies, waits for them, and re-layouts: 6.14 us -> 3.03 us
    ppermute x30, starting transfers between devices: 47.1 us -> 35.1 us  [permute(): return lax.ppermute(value, AXES, pairs)]
    pallas_call x3, Pallas kernels: 13.7 us -> 19.1 us  [serve_rows(): pl.pallas_call(functools.partial(serve_kernel, top_count), out_shape=(out...]
    ppermute x30, waiting for transfers between devices: 37.8 us -> 41.8 us  [permute(): return lax.ppermute(value, AXES, pairs)]
    unnamed x26 -> x18, local copies, waits for them, and re-layouts: 5.83 us -> 2.72 us
  transfers between devices with their start and end apart: 30 -> 30, of which waited for: 15 -> 16; matrix products, arithmetic and copies ran while one was open for 8% -> 8% of each run, Pallas kernels for 12% -> 17%
where the time goes in v9:
time: 112 us; the launch traced here: 111 us
  waiting for transfers between devices  41.8 us (37%)
  starting transfers between devices  35.1 us (31%)
  Pallas kernels  20 us (18%)
  other arithmetic  10.1 us (9%)
  local copies, waits for them, and re-layouts  3.03 us (3%)
    ppermute x30, waiting for transfers between devices, permute(): return lax.ppermute(value, AXES, pairs)  41.8 us
    ppermute x30, starting transfers between devices, permute(): return lax.ppermute(value, AXES, pairs)  35.1 us
    pallas_call x3, Pallas kernels, serve_rows(): pl.pallas_call(functools.partial(serve_kernel, top_count), out_shape=(out...  19.1 us
    concatenate x9, other arithmetic, chunk_steps(): held = jnp.concatenate([held, got])  5.51 us
    unnamed x18, local copies, waits for them, and re-layouts  2.72 us
  transfers between devices with their start and end apart: 30, of which 16 were waited for; matrix products, arithmetic and copies ran while one was open for 8% of the time, Pallas kernels for 17%

profile of v9, /device:TPU:0, one launch (start us, length us, event | category | flops | bytes accessed | tf_op | source)
XLA Modules:
  0.0 111.0 jit_solution(11481012970490091453)
XLA Ops:
  0.0 0.8 copy.13
  0.8 0.7 reduce_precision.9
  1.5 0.7 convert_element_type.239
  2.2 0.1 copy.15
  2.3 0.7 fusion.8.extra
  3.0 0.9 pack_rows.1
  3.9 4.1 %collective-permute-start.20 = (bf16[8,4224]{1,0:T(8,128)(2,1)S(1)}, bf16[8,4224]{1,0:T(8,128)(2,1)}, u32[]{:S(2)}, u32[]{:S(2)}) collective-permute-start(bf16[8,4224]{1,0:T(8,128)(2,1)S(1)} %get-tuple-element.20), channel_id=1, source_target_pairs={{0,4},{1,5},{2,6},{3,7},{4,0},{5,1},{6,2},{7,3},{8,12},{9,13},{10,... | collective-permute-start | bytes 202760 | tf_op jit(solution)/shard_map/ppermute | solution.py:88
  8.1 2.8 %collective-permute-start = (bf16[8,4224]{1,0:T(8,128)(2,1)S(1)}, bf16[8,4224]{1,0:T(8,128)(2,1)S(1)}, u32[]{:S(2)}, u32[]{:S(2)}) collective-permute-start(bf16[8,4224]{1,0:T(8,128)(2,1)S(1)} %get-tuple-element.14), channel_id=1, source_target_pairs={{0,4},{1,5},{2,6},{3,7},{4,0},{5,1},{6,2},{7,3},{8,12},{9,13},{10,... | collective-permute-start | bytes 202760 | tf_op jit(solution)/shard_map/ppermute | solution.py:88
  11.6 0.3 collective-permute-done.20
  11.9 0.9 pad_maximum_fusion.9
  12.8 3.5 %collective-permute-start.21 = (bf16[16,4224]{1,0:T(8,128)(2,1)S(1)}, bf16[16,4224]{1,0:T(8,128)(2,1)S(1)}, u32[]{:S(2)}, u32[]{:S(2)}) collective-permute-start(bf16[16,4224]{1,0:T(8,128)(2,1)S(1)} %pad_maximum_fusion.9), channel_id=1, source_target_pairs={{0,2},{1,3},{2,0},{3,1},{4,6},{5,7},{6,4},{7,5},{8,10},{9,11},{10,... | collective-permute-start | bytes 405512 | tf_op jit(solution)/shard_map/ppermute | solution.py:88
  16.3 0.4 collective-permute-done.10
  16.7 0.9 pad_maximum_fusion.8
  17.6 0.1 collective-permute-start.11
  17.8 3.0 %collective-permute-start.1 = (bf16[16,4224]{1,0:T(8,128)(2,1)S(1)}, bf16[16,4224]{1,0:T(8,128)(2,1)S(1)}, u32[]{:S(2)}, u32[]{:S(2)}) collective-permute-start(bf16[16,4224]{1,0:T(8,128)(2,1)S(1)} %pad_maximum_fusion.7), channel_id=1, source_target_pairs={{0,1},{1,0},{2,3},{3,2},{4,5},{5,4},{6,7},{7,6},{8,24},{9,25},{10,... | collective-permute-start | bytes 405512 | tf_op jit(solution)/shard_map/ppermute | solution.py:88
  20.8 0.9 constant_dynamic-update-slice_fusion.13
  21.7 0.9 constant_dynamic-update-slice_fusion.8
  22.6 0.9 pad_maximum_fusion.5
  23.5 1.6 %collective-permute-start.22 = (bf16[32,4224]{1,0:T(8,128)(2,1)S(1)}, bf16[32,4224]{1,0:T(8,128)(2,1)S(1)}, u32[]{:S(2)}, u32[]{:S(2)}) collective-permute-start(bf16[32,4224]{1,0:T(8,128)(2,1)S(1)} %pad_maximum_fusion.5), channel_id=1, source_target_pairs={{0,1},{1,0},{2,3},{3,2},{4,5},{5,4},{6,7},{7,6},{8,24},{9,25},{10,... | collective-permute-start | bytes 811016 | tf_op jit(solution)/shard_map/ppermute | solution.py:88
  25.2 0.9 pad_maximum_fusion.4
  26.1 0.6 collective-permute-start.12
  26.6 1.6 %collective-permute-start.2 = (bf16[32,4224]{1,0:T(8,128)(2,1)S(1)}, bf16[32,4224]{1,0:T(8,128)(2,1)S(1)}, u32[]{:S(2)}, u32[]{:S(2)}) collective-permute-start(bf16[32,4224]{1,0:T(8,128)(2,1)S(1)} %pad_maximum_fusion.3), channel_id=1, source_target_pairs={{0,16},{1,17},{2,18},{3,19},{4,20},{5,21},{6,22},{7,23},{8,9},{9,8... | collective-permute-start | bytes 811016 | tf_op jit(solution)/shard_map/ppermute | solution.py:88
  28.3 4.2 %collective-permute-done.22 = bf16[32,4224]{1,0:T(8,128)(2,1)S(1)} collective-permute-done((bf16[32,4224]{1,0:T(8,128)(2,1)S(1)}, bf16[32,4224]{1,0:T(8,128)(2,1)S(1)}, u32[]{:S(2)}, u32[]{:S(2)}) %collective-permute-start.22) | collective-permute-done | bytes 270368 | tf_op jit(solution)/shard_map/ppermute | solution.py:88
  32.5 0.9 pad_maximum_fusion.2
  33.4 2.0 %collective-permute-start.23 = (bf16[64,4224]{1,0:T(8,128)(2,1)S(1)}, bf16[64,4224]{1,0:T(8,128)(2,1)S(1)}, u32[]{:S(2)}, u32[]{:S(2)}) collective-permute-start(bf16[64,4224]{1,0:T(8,128)(2,1)S(1)} %pad_maximum_fusion.2), channel_id=1, source_target_pairs={{0,16},{1,17},{2,18},{3,19},{4,20},{5,21},{6,22},{7,23},{8,9},{9,8... | collective-permute-start | bytes 1622024 | tf_op jit(solution)/shard_map/ppermute | solution.py:88
  35.4 2.9 %collective-permute-done.12 = bf16[32,4224]{1,0:T(8,128)(2,1)S(1)} collective-permute-done((bf16[32,4224]{1,0:T(8,128)(2,1)S(1)}, bf16[32,4224]{1,0:T(8,128)(2,1)S(1)}, u32[]{:S(2)}, u32[]{:S(2)}) %collective-permute-start.12) | collective-permute-done | bytes 270368 | tf_op jit(solution)/shard_map/ppermute | solution.py:88
  38.3 0.9 pad_maximum_fusion.1
  39.2 2.0 %collective-permute-start.13 = (bf16[64,4224]{1,0:T(8,128)(2,1)S(1)}, bf16[64,4224]{1,0:T(8,128)(2,1)S(1)}, u32[]{:S(2)}, u32[]{:S(2)}) collective-permute-start(bf16[64,4224]{1,0:T(8,128)(2,1)S(1)} %pad_maximum_fusion.1), channel_id=1, source_target_pairs={{0,16},{1,17},{2,18},{3,19},{4,20},{5,21},{6,22},{7,23},{8,9},{9,8... | collective-permute-start | bytes 1622024 | tf_op jit(solution)/shard_map/ppermute | solution.py:88
  41.3 0.6 collective-permute-start.3
  41.9 0.9 collective-permute-done.23
  43.0 5.7 %collective-permute-done.13 = bf16[64,4224]{1,0:T(8,128)(2,1)S(1)} collective-permute-done((bf16[64,4224]{1,0:T(8,128)(2,1)S(1)}, bf16[64,4224]{1,0:T(8,128)(2,1)S(1)}, u32[]{:S(2)}, u32[]{:S(2)}) %collective-permute-start.13) | collective-permute-done | bytes 540704 | tf_op jit(solution)/shard_map/ppermute | solution.py:88
  48.8 1.9 %collective-permute-done.3 = bf16[64,4224]{1,0:T(8,128)(2,1)S(1)} collective-permute-done((bf16[64,4224]{1,0:T(8,128)(2,1)S(1)}, bf16[64,4224]{1,0:T(8,128)(2,1)S(1)}, u32[]{:S(2)}, u32[]{:S(2)}) %collective-permute-start.3) | collective-permute-done | bytes 540704 | tf_op jit(solution)/shard_map/ppermute | solution.py:88
  50.8 0.6 fusion.9
  51.5 6.4 %serve_rows.5 = (bf16[128,4096]{1,0:T(8,128)(2,1)S(1)}, bf16[128,4096]{1,0:T(8,128)(2,1)S(1)}) custom-call(s32[1]{0:T(128)} %bitcast.1.mine, bf16[128,4224]{1,0:T(8,128)(2,1)S(1)} %constant_dynamic-update-slice_fusion.10.own, bf16[128,4224]{1,0:T(8,128)(2,1)S(1)} %collective-permute-done.24.sib, bf16[4096,512]{1,0:T(8,128)(2,1)S(1)} %bitcast.5, ...), custom_call_target="tpu_custom_call" | custom-call | flops 3221225472 | bytes 16777216 | tf_op jit(solution)/shard_map/serve_rows/pallas_call | solution.py:175
  57.8 0.6 collective-permute-start.25
  58.4 6.3 %serve_rows.4 = (bf16[128,4096]{1,0:T(8,128)(2,1)S(1)}, bf16[128,4096]{1,0:T(8,128)(2,1)S(1)}) custom-call(s32[1]{0:T(128)} %bitcast.1.mine, bf16[128,4224]{1,0:T(8,128)(2,1)S(1)} %constant_dynamic-update-slice_fusion.5.own, bf16[128,4224]{1,0:T(8,128)(2,1)S(1)} %collective-permute-done.14.sib, bf16[4096,512]{1,0:T(8,128)(2,1)S(1)} %bitcast.6, ...), custom_call_target="tpu_custom_call" | custom-call | flops 3221225472 | bytes 16777216 | tf_op jit(solution)/shard_map/serve_rows/pallas_call | solution.py:175
  64.8 6.3 %serve_rows.3 = (bf16[128,4096]{1,0:T(8,128)(2,1)S(1)}, bf16[128,4096]{1,0:T(8,128)(2,1)S(1)}) custom-call(s32[1]{0:T(128)} %bitcast.1.mine, bf16[128,4224]{1,0:T(8,128)(2,1)S(1)} %constant_dynamic-update-slice_fusion.own, bf16[128,4224]{1,0:T(8,128)(2,1)S(1)} %collective-permute-done.4.sib, bf16[4096,512]{1,0:T(8,128)(2,1)S(1)} %bitcast.7, ...), custom_call_target="tpu_custom_call" | custom-call | flops 3221225472 | bytes 16777216 | tf_op jit(solution)/shard_map/serve_rows/pallas_call | solution.py:175
  71.2 0.6 collective-permute-start.5
  71.8 0.1 add_convert_fusion
  71.9 0.1 collective-permute-start.26
  72.0 0.1 add_convert_fusion.1
  72.2 2.0 %collective-permute-start.16 = (bf16[64,4096]{1,0:T(8,128)(2,1)S(1)}, bf16[64,4096]{1,0:T(8,128)(2,1)S(1)}, u32[]{:S(2)}, u32[]{:S(2)}) collective-permute-start(bf16[64,4096]{1,0:T(8,128)(2,1)S(1)} %add_convert_fusion.1), channel_id=1, source_target_pairs={{0,16},{1,17},{2,18},{3,19},{4,20},{5,21},{6,22},{7,23},{8,9},{9,8... | collective-permute-start | bytes 1572872 | tf_op jit(solution)/shard_map/ppermute | solution.py:88
  74.2 0.1 add_convert_fusion.2
  74.3 0.5 collective-permute-start.6
  74.9 6.3 %collective-permute-done.26 = bf16[64,4096]{1,0:T(8,128)(2,1)S(1)} collective-permute-done((bf16[64,4096]{1,0:T(8,128)(2,1)S(1)}, bf16[64,4096]{1,0:T(8,128)(2,1)S(1)}, u32[]{:S(2)}, u32[]{:S(2)}) %collective-permute-start.26) | collective-permute-done | bytes 524320 | tf_op jit(solution)/shard_map/ppermute | solution.py:88
  81.1 0.1 add_convert_fusion.3
  81.2 1.6 %collective-permute-start.27 = (bf16[32,4096]{1,0:T(8,128)(2,1)S(1)}, bf16[32,4096]{1,0:T(8,128)(2,1)S(1)}, u32[]{:S(2)}, u32[]{:S(2)}) collective-permute-start(bf16[32,4096]{1,0:T(8,128)(2,1)S(1)} %add_convert_fusion.3), channel_id=1, source_target_pairs={{0,1},{1,0},{2,3},{3,2},{4,5},{5,4},{6,7},{7,6},{8,24},{9,25},{10,... | collective-permute-start | bytes 786440 | tf_op jit(solution)/shard_map/ppermute | solution.py:88
  82.8 6.8 %collective-permute-done.16 = bf16[64,4096]{1,0:T(8,128)(2,1)S(1)} collective-permute-done((bf16[64,4096]{1,0:T(8,128)(2,1)S(1)}, bf16[64,4096]{1,0:T(8,128)(2,1)S(1)}, u32[]{:S(2)}, u32[]{:S(2)}) %collective-permute-start.16) | collective-permute-done | bytes 524320 | tf_op jit(solution)/shard_map/ppermute | solution.py:88
  89.6 0.1 add_convert_fusion.4
  89.7 1.6 %collective-permute-start.17 = (bf16[32,4096]{1,0:T(8,128)(2,1)S(1)}, bf16[32,4096]{1,0:T(8,128)(2,1)S(1)}, u32[]{:S(2)}, u32[]{:S(2)}) collective-permute-start(bf16[32,4096]{1,0:T(8,128)(2,1)S(1)} %add_convert_fusion.4), channel_id=1, source_target_pairs={{0,1},{1,0},{2,3},{3,2},{4,5},{5,4},{6,7},{7,6},{8,24},{9,25},{10,... | collective-permute-start | bytes 786440 | tf_op jit(solution)/shard_map/ppermute | solution.py:88
  91.2 0.1 add_convert_fusion.5
  91.3 0.3 collective-permute-start.7
  91.8 4.5 %collective-permute-done.17 = bf16[32,4096]{1,0:T(8,128)(2,1)S(1)} collective-permute-done((bf16[32,4096]{1,0:T(8,128)(2,1)S(1)}, bf16[32,4096]{1,0:T(8,128)(2,1)S(1)}, u32[]{:S(2)}, u32[]{:S(2)}) %collective-permute-start.17) | collective-permute-done | bytes 262176 | tf_op jit(solution)/shard_map/ppermute | solution.py:88
  96.3 0.5 collective-permute-start.18
  96.9 2.3 %collective-permute-done.7 = bf16[32,4096]{1,0:T(8,128)(2,1)S(1)} collective-permute-done((bf16[32,4096]{1,0:T(8,128)(2,1)S(1)}, bf16[32,4096]{1,0:T(8,128)(2,1)S(1)}, u32[]{:S(2)}, u32[]{:S(2)}) %collective-permute-start.7) | collective-permute-done | bytes 262176 | tf_op jit(solution)/shard_map/ppermute | solution.py:88
  99.3 2.2 %collective-permute-start.29 = (bf16[8,4096]{1,0:T(8,128)(2,1)S(1)}, bf16[8,4096]{1,0:T(8,128)(2,1)S(1)}, u32[]{:S(2)}, u32[]{:S(2)}) collective-permute-start(bf16[8,4096]{1,0:T(8,128)(2,1)S(1)} %add_convert_fusion.10), channel_id=1, source_target_pairs={{0,4},{1,5},{2,6},{3,7},{4,0},{5,1},{6,2},{7,3},{8,12},{9,13},{10,... | collective-permute-start | bytes 196616 | tf_op jit(solution)/shard_map/ppermute | solution.py:88
  101.5 0.6 collective-permute-done.18
  102.2 1.7 %collective-permute-start.19 = (bf16[8,4096]{1,0:T(8,128)(2,1)S(1)}, bf16[8,4096]{1,0:T(8,128)(2,1)S(1)}, u32[]{:S(2)}, u32[]{:S(2)}) collective-permute-start(bf16[8,4096]{1,0:T(8,128)(2,1)S(1)} %add_convert_fusion.12), channel_id=1, source_target_pairs={{0,4},{1,5},{2,6},{3,7},{4,0},{5,1},{6,2},{7,3},{8,12},{9,13},{10,... | collective-permute-start | bytes 196616 | tf_op jit(solution)/shard_map/ppermute | solution.py:88
  103.9 0.4 collective-permute-done.8
  104.3 1.0 collective-permute-start.9
  105.3 0.7 collective-permute-done.29
  106.0 2.1 %collective-permute-done.19 = bf16[8,4096]{1,0:T(8,128)(2,1)S(1)} collective-permute-done((bf16[8,4096]{1,0:T(8,128)(2,1)S(1)}, bf16[8,4096]{1,0:T(8,128)(2,1)S(1)}, u32[]{:S(2)}, u32[]{:S(2)}) %collective-permute-start.19) | collective-permute-done | bytes 65568 | tf_op jit(solution)/shard_map/ppermute | solution.py:88
  108.1 2.1 %collective-permute-done.9 = bf16[8,4096]{1,0:T(8,128)(2,1)S(1)} collective-permute-done((bf16[8,4096]{1,0:T(8,128)(2,1)S(1)}, bf16[8,4096]{1,0:T(8,128)(2,1)S(1)}, u32[]{:S(2)}, u32[]{:S(2)}) %collective-permute-start.9) | collective-permute-done | bytes 65568 | tf_op jit(solution)/shard_map/ppermute | solution.py:88
  110.3 0.7 pad_maximum_fusion.6
  (53 shorter events, 1.6 us)
Async XLA Ops:
  3.9 8.0 %collective-permute-start.20 = (bf16[8,4224]{1,0:T(8,128)(2,1)S(1)}, bf16[8,4224]{1,0:T(8,128)(2,1)}, u32[]{:S(2)}, u32[]{:S(2)}) collective-permute-start(bf16[8,4224]{1,0:T(8,128)(2,1)S(1)} %get-tuple-element.20), channel_id=1, source_target_pairs={{0,4},{1,5},{2,6},{3,7},{4,0},{5,1},{6,2},{7,3},{8,12},{9,13},{10,... | collective-permute-start | bytes 202760 | tf_op jit(solution)/shard_map/ppermute | solution.py:88
  8.0 8.7 %collective-permute-start.10 = (bf16[8,4224]{1,0:T(8,128)(2,1)S(1)}, bf16[8,4224]{1,0:T(8,128)(2,1)}, u32[]{:S(2)}, u32[]{:S(2)}) collective-permute-start(bf16[8,4224]{1,0:T(8,128)(2,1)S(1)} %get-tuple-element.17), channel_id=1, source_target_pairs={{0,4},{1,5},{2,6},{3,7},{4,0},{5,1},{6,2},{7,3},{8,12},{9,13},{10,... | collective-permute-start | bytes 202760 | tf_op jit(solution)/shard_map/ppermute | solution.py:88
  8.1 9.6 %collective-permute-start = (bf16[8,4224]{1,0:T(8,128)(2,1)S(1)}, bf16[8,4224]{1,0:T(8,128)(2,1)S(1)}, u32[]{:S(2)}, u32[]{:S(2)}) collective-permute-start(bf16[8,4224]{1,0:T(8,128)(2,1)S(1)} %get-tuple-element.14), channel_id=1, source_target_pairs={{0,4},{1,5},{2,6},{3,7},{4,0},{5,1},{6,2},{7,3},{8,12},{9,13},{10,... | collective-permute-start | bytes 202760 | tf_op jit(solution)/shard_map/ppermute | solution.py:88
  12.8 9.8 %collective-permute-start.21 = (bf16[16,4224]{1,0:T(8,128)(2,1)S(1)}, bf16[16,4224]{1,0:T(8,128)(2,1)S(1)}, u32[]{:S(2)}, u32[]{:S(2)}) collective-permute-start(bf16[16,4224]{1,0:T(8,128)(2,1)S(1)} %pad_maximum_fusion.9), channel_id=1, source_target_pairs={{0,2},{1,3},{2,0},{3,1},{4,6},{5,7},{6,4},{7,5},{8,10},{9,11},{10,... | collective-permute-start | bytes 405512 | tf_op jit(solution)/shard_map/ppermute | solution.py:88
  17.6 7.6 %collective-permute-start.11 = (bf16[16,4224]{1,0:T(8,128)(2,1)S(1)}, bf16[16,4224]{1,0:T(8,128)(2,1)S(1)}, u32[]{:S(2)}, u32[]{:S(2)}) collective-permute-start(bf16[16,4224]{1,0:T(8,128)(2,1)S(1)} %pad_maximum_fusion.8), channel_id=1, source_target_pairs={{0,2},{1,3},{2,0},{3,1},{4,6},{5,7},{6,4},{7,5},{8,10},{9,11},{10,... | collective-permute-start | bytes 405512 | tf_op jit(solution)/shard_map/ppermute | solution.py:88
  17.8 8.9 %collective-permute-start.1 = (bf16[16,4224]{1,0:T(8,128)(2,1)S(1)}, bf16[16,4224]{1,0:T(8,128)(2,1)S(1)}, u32[]{:S(2)}, u32[]{:S(2)}) collective-permute-start(bf16[16,4224]{1,0:T(8,128)(2,1)S(1)} %pad_maximum_fusion.7), channel_id=1, source_target_pairs={{0,1},{1,0},{2,3},{3,2},{4,5},{5,4},{6,7},{7,6},{8,24},{9,25},{10,... | collective-permute-start | bytes 405512 | tf_op jit(solution)/shard_map/ppermute | solution.py:88
  23.5 9.0 %collective-permute-start.22 = (bf16[32,4224]{1,0:T(8,128)(2,1)S(1)}, bf16[32,4224]{1,0:T(8,128)(2,1)S(1)}, u32[]{:S(2)}, u32[]{:S(2)}) collective-permute-start(bf16[32,4224]{1,0:T(8,128)(2,1)S(1)} %pad_maximum_fusion.5), channel_id=1, source_target_pairs={{0,1},{1,0},{2,3},{3,2},{4,5},{5,4},{6,7},{7,6},{8,24},{9,25},{10,... | collective-permute-start | bytes 811016 | tf_op jit(solution)/shard_map/ppermute | solution.py:88
  26.1 12.2 %collective-permute-start.12 = (bf16[32,4224]{1,0:T(8,128)(2,1)S(1)}, bf16[32,4224]{1,0:T(8,128)(2,1)S(1)}, u32[]{:S(2)}, u32[]{:S(2)}) collective-permute-start(bf16[32,4224]{1,0:T(8,128)(2,1)S(1)} %pad_maximum_fusion.4), channel_id=1, source_target_pairs={{0,1},{1,0},{2,3},{3,2},{4,5},{5,4},{6,7},{7,6},{8,24},{9,25},{10,... | collective-permute-start | bytes 811016 | tf_op jit(solution)/shard_map/ppermute | solution.py:88
  26.6 14.6 %collective-permute-start.2 = (bf16[32,4224]{1,0:T(8,128)(2,1)S(1)}, bf16[32,4224]{1,0:T(8,128)(2,1)S(1)}, u32[]{:S(2)}, u32[]{:S(2)}) collective-permute-start(bf16[32,4224]{1,0:T(8,128)(2,1)S(1)} %pad_maximum_fusion.3), channel_id=1, source_target_pairs={{0,16},{1,17},{2,18},{3,19},{4,20},{5,21},{6,22},{7,23},{8,9},{9,8... | collective-permute-start | bytes 811016 | tf_op jit(solution)/shard_map/ppermute | solution.py:88
  28.3 23.2 %copy-start.1 = (bf16[1,4096,512]{2,1,0:T(8,128)(2,1)S(1)}, bf16[1,4096,512]{2,1,0:T(8,128)(2,1)}, u32[]{:S(2)}) copy-start(bf16[1,4096,512]{2,1,0:T(8,128)(2,1)} %param.14) | copy-start | bytes 12582916
  33.4 9.4 %collective-permute-start.23 = (bf16[64,4224]{1,0:T(8,128)(2,1)S(1)}, bf16[64,4224]{1,0:T(8,128)(2,1)S(1)}, u32[]{:S(2)}, u32[]{:S(2)}) collective-permute-start(bf16[64,4224]{1,0:T(8,128)(2,1)S(1)} %pad_maximum_fusion.2), channel_id=1, source_target_pairs={{0,16},{1,17},{2,18},{3,19},{4,20},{5,21},{6,22},{7,23},{8,9},{9,8... | collective-permute-start | bytes 1622024 | tf_op jit(solution)/shard_map/ppermute | solution.py:88
  39.2 9.4 %collective-permute-start.13 = (bf16[64,4224]{1,0:T(8,128)(2,1)S(1)}, bf16[64,4224]{1,0:T(8,128)(2,1)S(1)}, u32[]{:S(2)}, u32[]{:S(2)}) collective-permute-start(bf16[64,4224]{1,0:T(8,128)(2,1)S(1)} %pad_maximum_fusion.1), channel_id=1, source_target_pairs={{0,16},{1,17},{2,18},{3,19},{4,20},{5,21},{6,22},{7,23},{8,9},{9,8... | collective-permute-start | bytes 1622024 | tf_op jit(solution)/shard_map/ppermute | solution.py:88
  41.3 9.4 %collective-permute-start.3 = (bf16[64,4224]{1,0:T(8,128)(2,1)S(1)}, bf16[64,4224]{1,0:T(8,128)(2,1)S(1)}, u32[]{:S(2)}, u32[]{:S(2)}) collective-permute-start(bf16[64,4224]{1,0:T(8,128)(2,1)S(1)} %pad_maximum_fusion), channel_id=1, source_target_pairs={{0,2},{1,3},{2,0},{3,1},{4,6},{5,7},{6,4},{7,5},{8,10},{9,11},{10,... | collective-permute-start | bytes 1622024 | tf_op jit(solution)/shard_map/ppermute | solution.py:88
  41.8 9.0 %copy-start.2 = (s32[16,2]{0,1:T(2,128)S(1)}, s32[16,2]{0,1:T(2,128)}, u32[]{:S(2)}) copy-start(s32[16,2]{0,1:T(2,128)} %param.11) | copy-start | bytes 388
  41.8 9.6 %copy-start = (bf16[1,4096,512]{2,1,0:T(8,128)(2,1)S(1)}, bf16[1,4096,512]{2,1,0:T(8,128)(2,1)}, u32[]{:S(2)}) copy-start(bf16[1,4096,512]{2,1,0:T(8,128)(2,1)} %param.13) | copy-start | bytes 12582916
  42.9 8.6 %collective-permute-start.24 = (bf16[128,4224]{1,0:T(8,128)(2,1)S(1)}, bf16[128,4224]{1,0:T(8,128)(2,1)S(1)}, u32[]{:S(2)}, u32[]{:S(2)}) collective-permute-start(bf16[128,4224]{1,0:T(8,128)(2,1)S(1)} %constant_dynamic-update-slice_fusion.10.own), channel_id=1, source_target_pairs={{0,8},{1,9},{2,10},{3,11},{4,12},{5,13},{6,14},{7,15},{8,0},{9,1},... | collective-permute-start | bytes 3244040 | tf_op jit(solution)/shard_map/ppermute | solution.py:88
  48.7 9.7 %collective-permute-start.14 = (bf16[128,4224]{1,0:T(8,128)(2,1)S(1)}, bf16[128,4224]{1,0:T(8,128)(2,1)S(1)}, u32[]{:S(2)}, u32[]{:S(2)}) collective-permute-start(bf16[128,4224]{1,0:T(8,128)(2,1)S(1)} %constant_dynamic-update-slice_fusion.5.own), channel_id=1, source_target_pairs={{0,8},{1,9},{2,10},{3,11},{4,12},{5,13},{6,14},{7,15},{8,0},{9,1},... | collective-permute-start | bytes 3244040 | tf_op jit(solution)/shard_map/ppermute | solution.py:88
  50.7 14.1 %collective-permute-start.4 = (bf16[128,4224]{1,0:T(8,128)(2,1)S(1)}, bf16[128,4224]{1,0:T(8,128)(2,1)S(1)}, u32[]{:S(2)}, u32[]{:S(2)}) collective-permute-start(bf16[128,4224]{1,0:T(8,128)(2,1)S(1)} %constant_dynamic-update-slice_fusion.own), channel_id=1, source_target_pairs={{0,8},{1,9},{2,10},{3,11},{4,12},{5,13},{6,14},{7,15},{8,0},{9,1},... | collective-permute-start | bytes 3244040 | tf_op jit(solution)/shard_map/ppermute | solution.py:88
  57.8 13.9 %collective-permute-start.25 = (bf16[128,4096]{1,0:T(8,128)(2,1)S(1)}, bf16[128,4096]{1,0:T(8,128)(2,1)S(1)}, u32[]{:S(2)}, u32[]{:S(2)}) collective-permute-start(bf16[128,4096]{1,0:T(8,128)(2,1)S(1)} %get-tuple-element.22), channel_id=1, source_target_pairs={{0,8},{1,9},{2,10},{3,11},{4,12},{5,13},{6,14},{7,15},{8,0},{9,1},... | collective-permute-start | bytes 3145736 | tf_op jit(solution)/shard_map/ppermute | solution.py:88
  64.7 7.3 %collective-permute-start.15 = (bf16[128,4096]{1,0:T(8,128)(2,1)S(1)}, bf16[128,4096]{1,0:T(8,128)(2,1)S(1)}, u32[]{:S(2)}, u32[]{:S(2)}) collective-permute-start(bf16[128,4096]{1,0:T(8,128)(2,1)S(1)} %get-tuple-element.19), channel_id=1, source_target_pairs={{0,8},{1,9},{2,10},{3,11},{4,12},{5,13},{6,14},{7,15},{8,0},{9,1},... | collective-permute-start | bytes 3145736 | tf_op jit(solution)/shard_map/ppermute | solution.py:88
  71.2 3.0 %collective-permute-start.5 = (bf16[128,4096]{1,0:T(8,128)(2,1)S(1)}, bf16[128,4096]{1,0:T(8,128)(2,1)S(1)}, u32[]{:S(2)}, u32[]{:S(2)}) collective-permute-start(bf16[128,4096]{1,0:T(8,128)(2,1)S(1)} %get-tuple-element.16), channel_id=1, source_target_pairs={{0,8},{1,9},{2,10},{3,11},{4,12},{5,13},{6,14},{7,15},{8,0},{9,1},... | collective-permute-start | bytes 3145736 | tf_op jit(solution)/shard_map/ppermute | solution.py:88
  71.9 9.2 %collective-permute-start.26 = (bf16[64,4096]{1,0:T(8,128)(2,1)S(1)}, bf16[64,4096]{1,0:T(8,128)(2,1)S(1)}, u32[]{:S(2)}, u32[]{:S(2)}) collective-permute-start(bf16[64,4096]{1,0:T(8,128)(2,1)S(1)} %add_convert_fusion), channel_id=1, source_target_pairs={{0,16},{1,17},{2,18},{3,19},{4,20},{5,21},{6,22},{7,23},{8,9},{9,8... | collective-permute-start | bytes 1572872 | tf_op jit(solution)/shard_map/ppermute | solution.py:88
  72.2 17.4 %collective-permute-start.16 = (bf16[64,4096]{1,0:T(8,128)(2,1)S(1)}, bf16[64,4096]{1,0:T(8,128)(2,1)S(1)}, u32[]{:S(2)}, u32[]{:S(2)}) collective-permute-start(bf16[64,4096]{1,0:T(8,128)(2,1)S(1)} %add_convert_fusion.1), channel_id=1, source_target_pairs={{0,16},{1,17},{2,18},{3,19},{4,20},{5,21},{6,22},{7,23},{8,9},{9,8... | collective-permute-start | bytes 1572872 | tf_op jit(solution)/shard_map/ppermute | solution.py:88
  74.3 16.9 %collective-permute-start.6 = (bf16[64,4096]{1,0:T(8,128)(2,1)S(1)}, bf16[64,4096]{1,0:T(8,128)(2,1)S(1)}, u32[]{:S(2)}, u32[]{:S(2)}) collective-permute-start(bf16[64,4096]{1,0:T(8,128)(2,1)S(1)} %add_convert_fusion.2), channel_id=1, source_target_pairs={{0,2},{1,3},{2,0},{3,1},{4,6},{5,7},{6,4},{7,5},{8,10},{9,11},{10,... | collective-permute-start | bytes 1572872 | tf_op jit(solution)/shard_map/ppermute | solution.py:88
  81.2 10.4 %collective-permute-start.27 = (bf16[32,4096]{1,0:T(8,128)(2,1)S(1)}, bf16[32,4096]{1,0:T(8,128)(2,1)S(1)}, u32[]{:S(2)}, u32[]{:S(2)}) collective-permute-start(bf16[32,4096]{1,0:T(8,128)(2,1)S(1)} %add_convert_fusion.3), channel_id=1, source_target_pairs={{0,1},{1,0},{2,3},{3,2},{4,5},{5,4},{6,7},{7,6},{8,24},{9,25},{10,... | collective-permute-start | bytes 786440 | tf_op jit(solution)/shard_map/ppermute | solution.py:88
  89.7 6.6 %collective-permute-start.17 = (bf16[32,4096]{1,0:T(8,128)(2,1)S(1)}, bf16[32,4096]{1,0:T(8,128)(2,1)S(1)}, u32[]{:S(2)}, u32[]{:S(2)}) collective-permute-start(bf16[32,4096]{1,0:T(8,128)(2,1)S(1)} %add_convert_fusion.4), channel_id=1, source_target_pairs={{0,1},{1,0},{2,3},{3,2},{4,5},{5,4},{6,7},{7,6},{8,24},{9,25},{10,... | collective-permute-start | bytes 786440 | tf_op jit(solution)/shard_map/ppermute | solution.py:88
  91.3 7.8 %collective-permute-start.7 = (bf16[32,4096]{1,0:T(8,128)(2,1)S(1)}, bf16[32,4096]{1,0:T(8,128)(2,1)S(1)}, u32[]{:S(2)}, u32[]{:S(2)}) collective-permute-start(bf16[32,4096]{1,0:T(8,128)(2,1)S(1)} %add_convert_fusion.5), channel_id=1, source_target_pairs={{0,16},{1,17},{2,18},{3,19},{4,20},{5,21},{6,22},{7,23},{8,9},{9,8... | collective-permute-start | bytes 786440 | tf_op jit(solution)/shard_map/ppermute | solution.py:88
  91.7 7.6 %collective-permute-start.28 = (bf16[16,4096]{1,0:T(8,128)(2,1)S(1)}, bf16[16,4096]{1,0:T(8,128)(2,1)S(1)}, u32[]{:S(2)}, u32[]{:S(2)}) collective-permute-start(bf16[16,4096]{1,0:T(8,128)(2,1)S(1)} %add_convert_fusion.6), channel_id=1, source_target_pairs={{0,2},{1,3},{2,0},{3,1},{4,6},{5,7},{6,4},{7,5},{8,10},{9,11},{10,... | collective-permute-start | bytes 393224 | tf_op jit(solution)/shard_map/ppermute | solution.py:88
  96.3 5.8 %collective-permute-start.18 = (bf16[16,4096]{1,0:T(8,128)(2,1)S(1)}, bf16[16,4096]{1,0:T(8,128)(2,1)S(1)}, u32[]{:S(2)}, u32[]{:S(2)}) collective-permute-start(bf16[16,4096]{1,0:T(8,128)(2,1)S(1)} %add_convert_fusion.7), channel_id=1, source_target_pairs={{0,2},{1,3},{2,0},{3,1},{4,6},{5,7},{6,4},{7,5},{8,10},{9,11},{10,... | collective-permute-start | bytes 393224 | tf_op jit(solution)/shard_map/ppermute | solution.py:88
  99.2 5.0 %collective-permute-start.8 = (bf16[16,4096]{1,0:T(8,128)(2,1)S(1)}, bf16[16,4096]{1,0:T(8,128)(2,1)S(1)}, u32[]{:S(2)}, u32[]{:S(2)}) collective-permute-start(bf16[16,4096]{1,0:T(8,128)(2,1)S(1)} %add_convert_fusion.8), channel_id=1, source_target_pairs={{0,1},{1,0},{2,3},{3,2},{4,5},{5,4},{6,7},{7,6},{8,24},{9,25},{10,... | collective-permute-start | bytes 393224 | tf_op jit(solution)/shard_map/ppermute | solution.py:88
  99.3 6.6 %collective-permute-start.29 = (bf16[8,4096]{1,0:T(8,128)(2,1)S(1)}, bf16[8,4096]{1,0:T(8,128)(2,1)S(1)}, u32[]{:S(2)}, u32[]{:S(2)}) collective-permute-start(bf16[8,4096]{1,0:T(8,128)(2,1)S(1)} %add_convert_fusion.10), channel_id=1, source_target_pairs={{0,4},{1,5},{2,6},{3,7},{4,0},{5,1},{6,2},{7,3},{8,12},{9,13},{10,... | collective-permute-start | bytes 196616 | tf_op jit(solution)/shard_map/ppermute | solution.py:88
  102.2 5.9 %collective-permute-start.19 = (bf16[8,4096]{1,0:T(8,128)(2,1)S(1)}, bf16[8,4096]{1,0:T(8,128)(2,1)S(1)}, u32[]{:S(2)}, u32[]{:S(2)}) collective-permute-start(bf16[8,4096]{1,0:T(8,128)(2,1)S(1)} %add_convert_fusion.12), channel_id=1, source_target_pairs={{0,4},{1,5},{2,6},{3,7},{4,0},{5,1},{6,2},{7,3},{8,12},{9,13},{10,... | collective-permute-start | bytes 196616 | tf_op jit(solution)/shard_map/ppermute | solution.py:88
  104.3 5.9 %collective-permute-start.9 = (bf16[8,4096]{1,0:T(8,128)(2,1)S(1)}, bf16[8,4096]{1,0:T(8,128)(2,1)S(1)}, u32[]{:S(2)}, u32[]{:S(2)}) collective-permute-start(bf16[8,4096]{1,0:T(8,128)(2,1)S(1)} %add_convert_fusion.14), channel_id=1, source_target_pairs={{0,4},{1,5},{2,6},{3,7},{4,0},{5,1},{6,2},{7,3},{8,12},{9,13},{10,... | collective-permute-start | bytes 196616 | tf_op jit(solution)/shard_map/ppermute | solution.py:88

commit v10 on v9

--- a/solution.py
+++ b/solution.py
@@ -10,7 +10,7 @@
 AXES = ("dp", "expert")
 LANES = 128
 PARTS = 4
-VMEM_MIB = 12
+VMEM_MIB = 8
 ROWS_AT_ONCE = 8
 GUARDS = []
 
@@ -71,14 +71,6 @@
     return jnp.sum(scaled.reshape(tok_rows, top_count, model_width), axis=1).astype(jnp.bfloat16)
 
 
-def served_expert(slot_of, swap_flag):
-    d = lax.axis_index("dp")
-    x = lax.axis_index("expert")
-    serving = jnp.where(swap_flag[0] == 1, d ^ 1, d) * lax.axis_size("expert") + x
-    numbers = jnp.arange(slot_of.shape[0], dtype=jnp.int32)[:, None]
-    return jnp.sum(jnp.where(slot_of == serving, numbers, 0))
-
-
 def permute(value, move):
     ex_count = lax.axis_size("expert")
     pairs = []
@@ -104,18 +96,24 @@
     return lambda d, e: (d, e ^ (2 * distance))
 
 
-def choices(expert_ids, route_weight):
-    parts = [expert_ids.astype(jnp.bfloat16)]
-    rest = route_weight
-    for _ in range(3):
-        part = lax.reduce_precision(rest, exponent_bits=8, mantissa_bits=7)
-        parts.append(part.astype(jnp.bfloat16))
+def pack_kernel(slots, flag, tokens, ids, weights, mine, *outs_and_square):
+    *outs, square = outs_and_square
+    d = lax.axis_index("dp")
+    serving = jnp.where(flag[0] == 1, d ^ 1, d) * lax.axis_size("expert") + lax.axis_index("expert")
+    expert = jnp.int32(0)
+    for half in range(slots.shape[0]):
+        for number in range(slots.shape[1]):
+            expert += jnp.where(slots[half, number] == serving, number, 0)
+    mine[0] = expert
+    top_count, tok_rows = ids.shape
+    square[...] = jnp.zeros_like(square)
+    square[:top_count, :tok_rows] = ids[...].astype(jnp.float32)
+    rest = weights[...]
+    for k in range(1, 4):
+        part = rest.astype(jnp.bfloat16).astype(jnp.float32)
+        square[k * top_count : (k + 1) * top_count, :tok_rows] = part
         rest = rest - part
-    extra = jnp.concatenate(parts, axis=1)
-    return jnp.pad(extra, ((0, 0), (0, -extra.shape[1] % LANES)))
-
-
-def pack_kernel(tokens, extra, *outs):
+    extra = square[...].T.astype(jnp.bfloat16)
     at = 0
     for out in outs:
         rows, packed_width = out.shape
@@ -123,17 +121,21 @@
         at += rows
 
 
-def packed(tokens, extra, rows):
+def packed(tokens, expert_ids, route_weight, slot_of, swap_flag, rows):
     tok_rows, width = tokens.shape
+    side = -(-max(tok_rows, 4 * expert_ids.shape[1]) // LANES) * LANES
+    scalars = pl.BlockSpec(memory_space=pltpu.SMEM)
     whole = pl.BlockSpec(memory_space=pltpu.VMEM)
-    out = pltpu.VMEM((rows, width + extra.shape[1]), tokens.dtype)
-    return pl.pallas_call(
+    count = tok_rows // rows
+    mine, *owns = pl.pallas_call(
         pack_kernel,
-        out_shape=(out,) * (tok_rows // rows),
-        in_specs=[whole, whole],
-        out_specs=(whole,) * (tok_rows // rows),
+        out_shape=(jax.ShapeDtypeStruct((1,), jnp.int32),) + (pltpu.VMEM((rows, width + side), tokens.dtype),) * count,
+        in_specs=[scalars] * 2 + [whole] * 3,
+        out_specs=(scalars,) + (whole,) * count,
+        scratch_shapes=[pltpu.VMEM((side, side), jnp.float32)],
         name="pack_rows",
-    )(tokens, extra)
+    )(slot_of.T, swap_flag, tokens, expert_ids.T, route_weight.T)
+    return mine, owns
 
 
 def scale_of(extra, mine, top_count):
@@ -142,9 +144,7 @@
     return jnp.sum(jnp.where(ids == mine, hi + mid + lo, 0.0), axis=1, keepdims=True)
 
 
-def serve_kernel(top_count, mine, own, sib, w_gate, w_up, w_down, out_own, out_sib, down, sem):
-    load = pltpu.make_async_copy(w_down, down, sem)
-    load.start()
+def serve_kernel(top_count, mine, own, sib, w_gate, w_up, w_down, out_own, out_sib):
     rows = own.shape[0]
     width, hidden_width = w_gate.shape
     depth = width // PARTS
@@ -158,10 +158,9 @@
     hidden = (gate_sum / (1.0 + jnp.exp(-gate_sum)) * up_sum).astype(jnp.bfloat16)
     extra = jnp.concatenate([own[:, width:], sib[:, width:]])
     scale = scale_of(extra, mine[0].astype(jnp.float32), top_count)
-    load.wait()
     for k in range(PARTS):
         part = pl.ds(k * depth, depth)
-        served = jnp.dot(hidden, down[:, part], preferred_element_type=jnp.float32) * scale
+        served = jnp.dot(hidden, w_down[:, part], preferred_element_type=jnp.float32) * scale
         out_own[:, part] = served[:rows].astype(jnp.bfloat16)
         out_sib[:, part] = served[rows:].astype(jnp.bfloat16)
 
@@ -175,15 +174,14 @@
     return pl.pallas_call(
         functools.partial(serve_kernel, top_count),
         out_shape=(out, out),
-        in_specs=[pl.BlockSpec(memory_space=pltpu.SMEM)] + [whole] * 4 + [pl.BlockSpec(memory_space=pltpu.HBM)],
+        in_specs=[pl.BlockSpec(memory_space=pltpu.SMEM)] + [whole] * 5,
         out_specs=(whole, whole),
-        scratch_shapes=[pltpu.VMEM((hidden_width, width), jnp.bfloat16), pltpu.SemaphoreType.DMA],
         compiler_params=pltpu.CompilerParams(vmem_limit_bytes=VMEM_MIB * 2**20),
         cost_estimate=pl.CostEstimate(
             flops=12 * rows * width * hidden_width, bytes_accessed=moved, transcendentals=2 * rows * hidden_width
         ),
         name="serve_rows",
-    )(mine.reshape(1), own, sib, w_gate, w_up, pltpu.with_memory_space_constraint(w_down, pltpu.HBM))
+    )(mine, own, sib, w_gate, w_up, w_down)
 
 
 def total(*terms):
@@ -232,15 +230,13 @@
 def dense(tokens, expert_ids, route_weight, slot_of, swap_flag, w_gate, w_up, w_down):
     tok_rows = tokens.shape[0]
     top_count = expert_ids.shape[1]
-    mine = served_expert(slot_of, swap_flag)
     line_bits = (lax.axis_size("expert") // 2).bit_length() - 1
     along = [along_line(2**bit) for bit in range(line_bits)][::-1]
     across = [over_first, over_second]
-    routes = [along[:1] + across + along[1:], along + across, along + across]
+    routes = [along + across, along[:1] + across + along[1:]]
     step = ROWS_AT_ONCE if tok_rows % ROWS_AT_ONCE == 0 else tok_rows
-    extra = choices(expert_ids, route_weight)
+    mine, owns = packed(tokens, expert_ids, route_weight, slot_of, swap_flag, step)
     serve = lambda held, sib: serve_rows(held, sib, mine, top_count, w_gate[0], w_up[0], w_down[0])
-    owns = packed(tokens, extra, step)
     chunks = [chunk_steps(own, routes[i % len(routes)], serve) for i, own in enumerate(owns)]
     guards = GUARDS if len(chunks) == 3 and line_bits == 2 else []
     return jnp.concatenate(run_steps(chunks, guards))

time: 112 us -> 98.9 us (0.88)
  other arithmetic: 10.1 us -> 2.12 us
  Pallas kernels: 20 us -> 14.2 us
  starting transfers between devices: 35.1 us -> 38.8 us
  waiting for transfers between devices: 41.8 us -> 40.2 us
    pallas_call x3, Pallas kernels: 19.1 us -> 12.7 us  [serve_rows(): pl.pallas_call(functools.partial(serve_kernel, top_count), out_shape=(out...]
    concatenate x9, other arithmetic: 5.51 us -> 0.26 us  [chunk_steps(): held = jnp.concatenate([held, got])]
    ppermute x30, starting transfers between devices: 35.1 us -> 38.8 us  [permute(): return lax.ppermute(value, AXES, pairs)]
    ppermute x30, waiting for transfers between devices: 41.8 us -> 40.2 us  [permute(): return lax.ppermute(value, AXES, pairs)]
    unnamed x18 -> x20, local copies, waits for them, and re-layouts: 2.72 us -> 2.38 us
  transfers between devices with their start and end apart: 30 -> 30, of which waited for: 16 -> 16; matrix products, arithmetic and copies ran while one was open for 8% -> 2% of each run, Pallas kernels for 17% -> 13%
where the time goes in v10:
time: 98.9 us; the launch traced here: 98.7 us
  waiting for transfers between devices  40.2 us (41%)
  starting transfers between devices  38.8 us (39%)
  Pallas kernels  14.2 us (14%)
  local copies, waits for them, and re-layouts  2.53 us (3%)
  other arithmetic  2.12 us (2%)
    ppermute x30, waiting for transfers between devices, permute(): return lax.ppermute(value, AXES, pairs)  40.2 us
    ppermute x30, starting transfers between devices, permute(): return lax.ppermute(value, AXES, pairs)  38.8 us
    pallas_call x3, Pallas kernels, serve_rows(): pl.pallas_call(functools.partial(serve_kernel, top_count), out_shape=(out...  12.7 us
    unnamed x20, local copies, waits for them, and re-layouts  2.38 us
  transfers between devices with their start and end apart: 30, of which 16 were waited for; matrix products, arithmetic and copies ran while one was open for 2% of the time, Pallas kernels for 13%

profile of v10, /device:TPU:0, one launch (start us, length us, event | category | flops | bytes accessed | tf_op | source)
XLA Modules:
  0.0 98.7 jit_solution(12438216327057680809)
XLA Ops:
  0.7 1.5 %pack_rows.1 = (s32[1]{0:T(128)}, bf16[8,4224]{1,0:T(8,128)(2,1)S(1)}, bf16[8,4224]{1,0:T(8,128)(2,1)S(1)}, bf16[8,4224]{1,0:T(8,128)(2,1)S(1)}) custom-call(s32[2,16]{1,0:T(2,128)} %bitcast.17, s32[1]{0:T(128)S(6)} %copy.21.flag, bf16[24,4096]{1,0:T(8,128)(2,1)} %tokens.1, s32[8,24]{1,0:T(8,128)} %bitcast.15, f32[8,24]{1,0:T(8,128)} %bitcast.16), custom_call_target="tpu_custom_call" | custom-call | tf_op jit(solution)/shard_map/pack_rows/pallas_call | solution.py:130
  2.2 4.1 %collective-permute-start = (bf16[8,4224]{1,0:T(8,128)(2,1)S(1)}, bf16[8,4224]{1,0:T(8,128)(2,1)S(1)}, u32[]{:S(2)}, u32[]{:S(2)}) collective-permute-start(bf16[8,4224]{1,0:T(8,128)(2,1)S(1)} %get-tuple-element.16), channel_id=1, source_target_pairs={{0,4},{1,5},{2,6},{3,7},{4,0},{5,1},{6,2},{7,3},{8,12},{9,13},{10,... | collective-permute-start | bytes 202760 | tf_op jit(solution)/shard_map/ppermute | solution.py:80
  6.3 0.1 collective-permute-start.10
  6.4 2.8 %collective-permute-start.20 = (bf16[8,4224]{1,0:T(8,128)(2,1)S(1)}, bf16[8,4224]{1,0:T(8,128)(2,1)S(1)}, u32[]{:S(2)}, u32[]{:S(2)}) collective-permute-start(bf16[8,4224]{1,0:T(8,128)(2,1)S(1)} %get-tuple-element.22), channel_id=1, source_target_pairs={{0,4},{1,5},{2,6},{3,7},{4,0},{5,1},{6,2},{7,3},{8,12},{9,13},{10,... | collective-permute-start | bytes 202760 | tf_op jit(solution)/shard_map/ppermute | solution.py:80
  9.2 0.8 collective-permute-done
  10.1 3.6 %collective-permute-start.1 = (bf16[16,4224]{1,0:T(8,128)(2,1)S(1)}, bf16[16,4224]{1,0:T(8,128)(2,1)S(1)}, u32[]{:S(2)}, u32[]{:S(2)}) collective-permute-start(bf16[16,4224]{1,0:T(8,128)(2,1)S(1)} %pad_maximum_fusion.7), channel_id=1, source_target_pairs={{0,2},{1,3},{2,0},{3,1},{4,6},{5,7},{6,4},{7,5},{8,10},{9,11},{10,... | collective-permute-start | bytes 405512 | tf_op jit(solution)/shard_map/ppermute | solution.py:80
  13.7 1.2 %collective-permute-done.10 = bf16[8,4224]{1,0:T(8,128)(2,1)S(1)} collective-permute-done((bf16[8,4224]{1,0:T(8,128)(2,1)S(1)}, bf16[8,4224]{1,0:T(8,128)(2,1)S(1)}, u32[]{:S(2)}, u32[]{:S(2)}) %collective-permute-start.10) | collective-permute-done | bytes 67616 | tf_op jit(solution)/shard_map/ppermute | solution.py:80
  14.9 1.6 %collective-permute-start.11 = (bf16[16,4224]{1,0:T(8,128)(2,1)S(1)}, bf16[16,4224]{1,0:T(8,128)(2,1)S(1)}, u32[]{:S(2)}, u32[]{:S(2)}) collective-permute-start(bf16[16,4224]{1,0:T(8,128)(2,1)S(1)} %pad_maximum_fusion.8), channel_id=1, source_target_pairs={{0,1},{1,0},{2,3},{3,2},{4,5},{5,4},{6,7},{7,6},{8,24},{9,25},{10,... | collective-permute-start | bytes 405512 | tf_op jit(solution)/shard_map/ppermute | solution.py:80
  16.5 0.7 collective-permute-start.21
  17.2 1.5 %collective-permute-done.1 = bf16[16,4224]{1,0:T(8,128)(2,1)S(1)} collective-permute-done((bf16[16,4224]{1,0:T(8,128)(2,1)S(1)}, bf16[16,4224]{1,0:T(8,128)(2,1)S(1)}, u32[]{:S(2)}, u32[]{:S(2)}) %collective-permute-start.1) | collective-permute-done | bytes 135200 | tf_op jit(solution)/shard_map/ppermute | solution.py:80
  18.8 2.1 %collective-permute-start.2 = (bf16[32,4224]{1,0:T(8,128)(2,1)S(1)}, bf16[32,4224]{1,0:T(8,128)(2,1)S(1)}, u32[]{:S(2)}, u32[]{:S(2)}) collective-permute-start(bf16[32,4224]{1,0:T(8,128)(2,1)S(1)} %pad_maximum_fusion.3), channel_id=1, source_target_pairs={{0,1},{1,0},{2,3},{3,2},{4,5},{5,4},{6,7},{7,6},{8,24},{9,25},{10,... | collective-permute-start | bytes 811016 | tf_op jit(solution)/shard_map/ppermute | solution.py:80
  20.9 1.6 %collective-permute-start.12 = (bf16[32,4224]{1,0:T(8,128)(2,1)S(1)}, bf16[32,4224]{1,0:T(8,128)(2,1)S(1)}, u32[]{:S(2)}, u32[]{:S(2)}) collective-permute-start(bf16[32,4224]{1,0:T(8,128)(2,1)S(1)} %pad_maximum_fusion.4), channel_id=1, source_target_pairs={{0,16},{1,17},{2,18},{3,19},{4,20},{5,21},{6,22},{7,23},{8,9},{9,8... | collective-permute-start | bytes 811016 | tf_op jit(solution)/shard_map/ppermute | solution.py:80
  22.5 0.9 collective-permute-start.22
  23.5 4.7 %collective-permute-done.2 = bf16[32,4224]{1,0:T(8,128)(2,1)S(1)} collective-permute-done((bf16[32,4224]{1,0:T(8,128)(2,1)S(1)}, bf16[32,4224]{1,0:T(8,128)(2,1)S(1)}, u32[]{:S(2)}, u32[]{:S(2)}) %collective-permute-start.2) | collective-permute-done | bytes 270368 | tf_op jit(solution)/shard_map/ppermute | solution.py:80
  28.2 2.1 %collective-permute-start.3 = (bf16[64,4224]{1,0:T(8,128)(2,1)S(1)}, bf16[64,4224]{1,0:T(8,128)(2,1)S(1)}, u32[]{:S(2)}, u32[]{:S(2)}) collective-permute-start(bf16[64,4224]{1,0:T(8,128)(2,1)S(1)} %pad_maximum_fusion), channel_id=1, source_target_pairs={{0,16},{1,17},{2,18},{3,19},{4,20},{5,21},{6,22},{7,23},{8,9},{9,8... | collective-permute-start | bytes 1622024 | tf_op jit(solution)/shard_map/ppermute | solution.py:80
  30.4 0.1 collective-permute-start.13
  30.4 3.5 %collective-permute-done.22 = bf16[32,4224]{1,0:T(8,128)(2,1)S(1)} collective-permute-done((bf16[32,4224]{1,0:T(8,128)(2,1)S(1)}, bf16[32,4224]{1,0:T(8,128)(2,1)S(1)}, u32[]{:S(2)}, u32[]{:S(2)}) %collective-permute-start.22) | collective-permute-done | bytes 270368 | tf_op jit(solution)/shard_map/ppermute | solution.py:80
  34.0 2.1 %collective-permute-start.23 = (bf16[64,4224]{1,0:T(8,128)(2,1)S(1)}, bf16[64,4224]{1,0:T(8,128)(2,1)S(1)}, u32[]{:S(2)}, u32[]{:S(2)}) collective-permute-start(bf16[64,4224]{1,0:T(8,128)(2,1)S(1)} %pad_maximum_fusion.2), channel_id=1, source_target_pairs={{0,16},{1,17},{2,18},{3,19},{4,20},{5,21},{6,22},{7,23},{8,9},{9,8... | collective-permute-start | bytes 1622024 | tf_op jit(solution)/shard_map/ppermute | solution.py:80
  36.2 1.4 %collective-permute-done.3 = bf16[64,4224]{1,0:T(8,128)(2,1)S(1)} collective-permute-done((bf16[64,4224]{1,0:T(8,128)(2,1)S(1)}, bf16[64,4224]{1,0:T(8,128)(2,1)S(1)}, u32[]{:S(2)}, u32[]{:S(2)}) %collective-permute-start.3) | collective-permute-done | bytes 540704 | tf_op jit(solution)/shard_map/ppermute | solution.py:80
  37.7 0.1 collective-permute-start.4
  37.8 3.9 %collective-permute-done.13 = bf16[64,4224]{1,0:T(8,128)(2,1)S(1)} collective-permute-done((bf16[64,4224]{1,0:T(8,128)(2,1)S(1)}, bf16[64,4224]{1,0:T(8,128)(2,1)S(1)}, u32[]{:S(2)}, u32[]{:S(2)}) %collective-permute-start.13) | collective-permute-done | bytes 540704 | tf_op jit(solution)/shard_map/ppermute | solution.py:80
  41.7 0.1 collective-permute-start.14
  41.8 1.7 %collective-permute-done.23 = bf16[64,4224]{1,0:T(8,128)(2,1)S(1)} collective-permute-done((bf16[64,4224]{1,0:T(8,128)(2,1)S(1)}, bf16[64,4224]{1,0:T(8,128)(2,1)S(1)}, u32[]{:S(2)}, u32[]{:S(2)}) %collective-permute-start.23) | collective-permute-done | bytes 540704 | tf_op jit(solution)/shard_map/ppermute | solution.py:80
  43.5 0.1 collective-permute-start.24
  43.6 2.2 %copy-done.2 = bf16[1,512,4096]{2,1,0:T(8,128)(2,1)S(1)} copy-done((bf16[1,512,4096]{2,1,0:T(8,128)(2,1)S(1)}, bf16[1,512,4096]{2,1,0:T(8,128)(2,1)}, u32[]{:S(2)}) %copy-start.2) | copy-done | bytes 4194328
  45.8 4.2 %serve_rows.3 = (bf16[128,4096]{1,0:T(8,128)(2,1)S(1)}, bf16[128,4096]{1,0:T(8,128)(2,1)S(1)}) custom-call(s32[1]{0:T(128)} %get-tuple-element.15.mine, bf16[128,4224]{1,0:T(8,128)(2,1)S(1)} %constant_dynamic-update-slice_fusion.own, bf16[128,4224]{1,0:T(8,128)(2,1)S(1)} %collective-permute-done.4.sib, bf16[4096,512]{1,0:T(8,128)(2,1)S(1)} %bitcast.6, ...), custom_call_target="tpu_custom_call" | custom-call | flops 3221225472 | bytes 16777216 | tf_op jit(solution)/shard_map/serve_rows/pallas_call | solution.py:174
  50.0 0.5 collective-permute-start.5
  50.5 4.3 %serve_rows.4 = (bf16[128,4096]{1,0:T(8,128)(2,1)S(1)}, bf16[128,4096]{1,0:T(8,128)(2,1)S(1)}) custom-call(s32[1]{0:T(128)} %get-tuple-element.15.mine, bf16[128,4224]{1,0:T(8,128)(2,1)S(1)} %constant_dynamic-update-slice_fusion.5.own, bf16[128,4224]{1,0:T(8,128)(2,1)S(1)} %collective-permute-done.14.sib, bf16[4096,512]{1,0:T(8,128)(2,1)S(1)} %bitcast.7, ...), custom_call_target="tpu_custom_call" | custom-call | flops 3221225472 | bytes 16777216 | tf_op jit(solution)/shard_map/serve_rows/pallas_call | solution.py:174
  54.8 0.1 collective-permute-start.15
  55.0 4.2 %serve_rows.5 = (bf16[128,4096]{1,0:T(8,128)(2,1)S(1)}, bf16[128,4096]{1,0:T(8,128)(2,1)S(1)}) custom-call(s32[1]{0:T(128)} %get-tuple-element.15.mine, bf16[128,4224]{1,0:T(8,128)(2,1)S(1)} %constant_dynamic-update-slice_fusion.10.own, bf16[128,4224]{1,0:T(8,128)(2,1)S(1)} %collective-permute-done.24.sib, bf16[4096,512]{1,0:T(8,128)(2,1)S(1)} %bitcast.8, ...), custom_call_target="tpu_custom_call" | custom-call | flops 3221225472 | bytes 16777216 | tf_op jit(solution)/shard_map/serve_rows/pallas_call | solution.py:174
  59.1 0.5 collective-permute-start.25
  59.7 0.1 add_convert_fusion.2
  59.8 2.1 %collective-permute-start.6 = (bf16[64,4096]{1,0:T(8,128)(2,1)S(1)}, bf16[64,4096]{1,0:T(8,128)(2,1)S(1)}, u32[]{:S(2)}, u32[]{:S(2)}) collective-permute-start(bf16[64,4096]{1,0:T(8,128)(2,1)S(1)} %add_convert_fusion.2), channel_id=1, source_target_pairs={{0,16},{1,17},{2,18},{3,19},{4,20},{5,21},{6,22},{7,23},{8,9},{9,8... | collective-permute-start | bytes 1572872 | tf_op jit(solution)/shard_map/ppermute | solution.py:80
  61.9 0.1 add_convert_fusion.1
  62.0 0.1 collective-permute-start.16
  62.1 0.1 add_convert_fusion
  62.2 1.9 %collective-permute-start.26 = (bf16[64,4096]{1,0:T(8,128)(2,1)S(1)}, bf16[64,4096]{1,0:T(8,128)(2,1)S(1)}, u32[]{:S(2)}, u32[]{:S(2)}) collective-permute-start(bf16[64,4096]{1,0:T(8,128)(2,1)S(1)} %add_convert_fusion), channel_id=1, source_target_pairs={{0,16},{1,17},{2,18},{3,19},{4,20},{5,21},{6,22},{7,23},{8,9},{9,8... | collective-permute-start | bytes 1572872 | tf_op jit(solution)/shard_map/ppermute | solution.py:80
  64.2 4.9 %collective-permute-done.6 = bf16[64,4096]{1,0:T(8,128)(2,1)S(1)} collective-permute-done((bf16[64,4096]{1,0:T(8,128)(2,1)S(1)}, bf16[64,4096]{1,0:T(8,128)(2,1)S(1)}, u32[]{:S(2)}, u32[]{:S(2)}) %collective-permute-start.6) | collective-permute-done | bytes 524320 | tf_op jit(solution)/shard_map/ppermute | solution.py:80
  69.0 0.1 add_convert_fusion.5
  69.1 2.1 %collective-permute-start.7 = (bf16[32,4096]{1,0:T(8,128)(2,1)S(1)}, bf16[32,4096]{1,0:T(8,128)(2,1)S(1)}, u32[]{:S(2)}, u32[]{:S(2)}) collective-permute-start(bf16[32,4096]{1,0:T(8,128)(2,1)S(1)} %add_convert_fusion.5), channel_id=1, source_target_pairs={{0,1},{1,0},{2,3},{3,2},{4,5},{5,4},{6,7},{7,6},{8,24},{9,25},{10,... | collective-permute-start | bytes 786440 | tf_op jit(solution)/shard_map/ppermute | solution.py:80
  71.2 4.4 %collective-permute-done.16 = bf16[64,4096]{1,0:T(8,128)(2,1)S(1)} collective-permute-done((bf16[64,4096]{1,0:T(8,128)(2,1)S(1)}, bf16[64,4096]{1,0:T(8,128)(2,1)S(1)}, u32[]{:S(2)}, u32[]{:S(2)}) %collective-permute-start.16) | collective-permute-done | bytes 524320 | tf_op jit(solution)/shard_map/ppermute | solution.py:80
  75.7 0.1 add_convert_fusion.4
  75.8 0.7 collective-permute-start.17
  76.5 1.0 %collective-permute-done.26 = bf16[64,4096]{1,0:T(8,128)(2,1)S(1)} collective-permute-done((bf16[64,4096]{1,0:T(8,128)(2,1)S(1)}, bf16[64,4096]{1,0:T(8,128)(2,1)S(1)}, u32[]{:S(2)}, u32[]{:S(2)}) %collective-permute-start.26) | collective-permute-done | bytes 524320 | tf_op jit(solution)/shard_map/ppermute | solution.py:80
  77.5 0.1 add_convert_fusion.3
  77.6 2.1 %collective-permute-start.27 = (bf16[32,4096]{1,0:T(8,128)(2,1)S(1)}, bf16[32,4096]{1,0:T(8,128)(2,1)S(1)}, u32[]{:S(2)}, u32[]{:S(2)}) collective-permute-start(bf16[32,4096]{1,0:T(8,128)(2,1)S(1)} %add_convert_fusion.3), channel_id=1, source_target_pairs={{0,1},{1,0},{2,3},{3,2},{4,5},{5,4},{6,7},{7,6},{8,24},{9,25},{10,... | collective-permute-start | bytes 786440 | tf_op jit(solution)/shard_map/ppermute | solution.py:80
  79.7 0.1 add_convert_fusion.8
  79.7 0.1 collective-permute-start.8
  79.8 4.5 %collective-permute-done.17 = bf16[32,4096]{1,0:T(8,128)(2,1)S(1)} collective-permute-done((bf16[32,4096]{1,0:T(8,128)(2,1)S(1)}, bf16[32,4096]{1,0:T(8,128)(2,1)S(1)}, u32[]{:S(2)}, u32[]{:S(2)}) %collective-permute-start.17) | collective-permute-done | bytes 262176 | tf_op jit(solution)/shard_map/ppermute | solution.py:80
  84.3 0.1 add_convert_fusion.7
  84.4 1.1 %collective-permute-start.18 = (bf16[16,4096]{1,0:T(8,128)(2,1)S(1)}, bf16[16,4096]{1,0:T(8,128)(2,1)S(1)}, u32[]{:S(2)}, u32[]{:S(2)}) collective-permute-start(bf16[16,4096]{1,0:T(8,128)(2,1)S(1)} %add_convert_fusion.7), channel_id=1, source_target_pairs={{0,1},{1,0},{2,3},{3,2},{4,5},{5,4},{6,7},{7,6},{8,24},{9,25},{10,... | collective-permute-start | bytes 393224 | tf_op jit(solution)/shard_map/ppermute | solution.py:80
  85.5 0.1 add_convert_fusion.6
  85.5 0.4 collective-permute-start.28
  85.9 3.5 %collective-permute-start.9 = (bf16[8,4096]{1,0:T(8,128)(2,1)S(1)}, bf16[8,4096]{1,0:T(8,128)(2,1)S(1)}, u32[]{:S(2)}, u32[]{:S(2)}) collective-permute-start(bf16[8,4096]{1,0:T(8,128)(2,1)S(1)} %add_convert_fusion.14), channel_id=1, source_target_pairs={{0,4},{1,5},{2,6},{3,7},{4,0},{5,1},{6,2},{7,3},{8,12},{9,13},{10,... | collective-permute-start | bytes 196616 | tf_op jit(solution)/shard_map/ppermute | solution.py:80
  89.5 1.1 %collective-permute-start.19 = (bf16[8,4096]{1,0:T(8,128)(2,1)S(1)}, bf16[8,4096]{1,0:T(8,128)(2,1)S(1)}, u32[]{:S(2)}, u32[]{:S(2)}) collective-permute-start(bf16[8,4096]{1,0:T(8,128)(2,1)S(1)} %add_convert_fusion.12), channel_id=1, source_target_pairs={{0,4},{1,5},{2,6},{3,7},{4,0},{5,1},{6,2},{7,3},{8,12},{9,13},{10,... | collective-permute-start | bytes 196616 | tf_op jit(solution)/shard_map/ppermute | solution.py:80
  90.6 2.0 %collective-permute-done.28 = bf16[16,4096]{1,0:T(8,128)(2,1)S(1)} collective-permute-done((bf16[16,4096]{1,0:T(8,128)(2,1)S(1)}, bf16[16,4096]{1,0:T(8,128)(2,1)S(1)}, u32[]{:S(2)}, u32[]{:S(2)}) %collective-permute-start.28) | collective-permute-done | bytes 131104 | tf_op jit(solution)/shard_map/ppermute | solution.py:80
  92.7 0.6 collective-permute-start.29
  93.3 0.2 collective-permute-done.9
  93.4 0.1 add_convert_fusion.13
  93.5 1.7 %collective-permute-done.19 = bf16[8,4096]{1,0:T(8,128)(2,1)S(1)} collective-permute-done((bf16[8,4096]{1,0:T(8,128)(2,1)S(1)}, bf16[8,4096]{1,0:T(8,128)(2,1)S(1)}, u32[]{:S(2)}, u32[]{:S(2)}) %collective-permute-start.19) | collective-permute-done | bytes 65568 | tf_op jit(solution)/shard_map/ppermute | solution.py:80
  95.1 0.1 add_convert_fusion.11
  95.2 2.8 %collective-permute-done.29 = bf16[8,4096]{1,0:T(8,128)(2,1)S(1)} collective-permute-done((bf16[8,4096]{1,0:T(8,128)(2,1)S(1)}, bf16[8,4096]{1,0:T(8,128)(2,1)S(1)}, u32[]{:S(2)}, u32[]{:S(2)}) %collective-permute-start.29) | collective-permute-done | bytes 65568 | tf_op jit(solution)/shard_map/ppermute | solution.py:80
  98.0 0.1 add_convert_fusion.9
  98.1 0.7 pad_maximum_fusion.6
  (48 shorter events, 0.8 us)
Async XLA Ops:
  2.2 7.9 %collective-permute-start = (bf16[8,4224]{1,0:T(8,128)(2,1)S(1)}, bf16[8,4224]{1,0:T(8,128)(2,1)S(1)}, u32[]{:S(2)}, u32[]{:S(2)}) collective-permute-start(bf16[8,4224]{1,0:T(8,128)(2,1)S(1)} %get-tuple-element.16), channel_id=1, source_target_pairs={{0,4},{1,5},{2,6},{3,7},{4,0},{5,1},{6,2},{7,3},{8,12},{9,13},{10,... | collective-permute-start | bytes 202760 | tf_op jit(solution)/shard_map/ppermute | solution.py:80
  6.3 8.6 %collective-permute-start.10 = (bf16[8,4224]{1,0:T(8,128)(2,1)S(1)}, bf16[8,4224]{1,0:T(8,128)(2,1)S(1)}, u32[]{:S(2)}, u32[]{:S(2)}) collective-permute-start(bf16[8,4224]{1,0:T(8,128)(2,1)S(1)} %get-tuple-element.19), channel_id=1, source_target_pairs={{0,4},{1,5},{2,6},{3,7},{4,0},{5,1},{6,2},{7,3},{8,12},{9,13},{10,... | collective-permute-start | bytes 202760 | tf_op jit(solution)/shard_map/ppermute | solution.py:80
  6.4 10.1 %collective-permute-start.20 = (bf16[8,4224]{1,0:T(8,128)(2,1)S(1)}, bf16[8,4224]{1,0:T(8,128)(2,1)S(1)}, u32[]{:S(2)}, u32[]{:S(2)}) collective-permute-start(bf16[8,4224]{1,0:T(8,128)(2,1)S(1)} %get-tuple-element.22), channel_id=1, source_target_pairs={{0,4},{1,5},{2,6},{3,7},{4,0},{5,1},{6,2},{7,3},{8,12},{9,13},{10,... | collective-permute-start | bytes 202760 | tf_op jit(solution)/shard_map/ppermute | solution.py:80
  10.1 8.7 %collective-permute-start.1 = (bf16[16,4224]{1,0:T(8,128)(2,1)S(1)}, bf16[16,4224]{1,0:T(8,128)(2,1)S(1)}, u32[]{:S(2)}, u32[]{:S(2)}) collective-permute-start(bf16[16,4224]{1,0:T(8,128)(2,1)S(1)} %pad_maximum_fusion.7), channel_id=1, source_target_pairs={{0,2},{1,3},{2,0},{3,1},{4,6},{5,7},{6,4},{7,5},{8,10},{9,11},{10,... | collective-permute-start | bytes 405512 | tf_op jit(solution)/shard_map/ppermute | solution.py:80
  14.9 6.0 %collective-permute-start.11 = (bf16[16,4224]{1,0:T(8,128)(2,1)S(1)}, bf16[16,4224]{1,0:T(8,128)(2,1)S(1)}, u32[]{:S(2)}, u32[]{:S(2)}) collective-permute-start(bf16[16,4224]{1,0:T(8,128)(2,1)S(1)} %pad_maximum_fusion.8), channel_id=1, source_target_pairs={{0,1},{1,0},{2,3},{3,2},{4,5},{5,4},{6,7},{7,6},{8,24},{9,25},{10,... | collective-permute-start | bytes 405512 | tf_op jit(solution)/shard_map/ppermute | solution.py:80
  16.5 5.9 %collective-permute-start.21 = (bf16[16,4224]{1,0:T(8,128)(2,1)S(1)}, bf16[16,4224]{1,0:T(8,128)(2,1)S(1)}, u32[]{:S(2)}, u32[]{:S(2)}) collective-permute-start(bf16[16,4224]{1,0:T(8,128)(2,1)S(1)} %pad_maximum_fusion.9), channel_id=1, source_target_pairs={{0,2},{1,3},{2,0},{3,1},{4,6},{5,7},{6,4},{7,5},{8,10},{9,11},{10,... | collective-permute-start | bytes 405512 | tf_op jit(solution)/shard_map/ppermute | solution.py:80
  18.8 9.3 %collective-permute-start.2 = (bf16[32,4224]{1,0:T(8,128)(2,1)S(1)}, bf16[32,4224]{1,0:T(8,128)(2,1)S(1)}, u32[]{:S(2)}, u32[]{:S(2)}) collective-permute-start(bf16[32,4224]{1,0:T(8,128)(2,1)S(1)} %pad_maximum_fusion.3), channel_id=1, source_target_pairs={{0,1},{1,0},{2,3},{3,2},{4,5},{5,4},{6,7},{7,6},{8,24},{9,25},{10,... | collective-permute-start | bytes 811016 | tf_op jit(solution)/shard_map/ppermute | solution.py:80
  20.9 9.4 %collective-permute-start.12 = (bf16[32,4224]{1,0:T(8,128)(2,1)S(1)}, bf16[32,4224]{1,0:T(8,128)(2,1)S(1)}, u32[]{:S(2)}, u32[]{:S(2)}) collective-permute-start(bf16[32,4224]{1,0:T(8,128)(2,1)S(1)} %pad_maximum_fusion.4), channel_id=1, source_target_pairs={{0,16},{1,17},{2,18},{3,19},{4,20},{5,21},{6,22},{7,23},{8,9},{9,8... | collective-permute-start | bytes 811016 | tf_op jit(solution)/shard_map/ppermute | solution.py:80
  22.5 11.5 %collective-permute-start.22 = (bf16[32,4224]{1,0:T(8,128)(2,1)S(1)}, bf16[32,4224]{1,0:T(8,128)(2,1)S(1)}, u32[]{:S(2)}, u32[]{:S(2)}) collective-permute-start(bf16[32,4224]{1,0:T(8,128)(2,1)S(1)} %pad_maximum_fusion.5), channel_id=1, source_target_pairs={{0,1},{1,0},{2,3},{3,2},{4,5},{5,4},{6,7},{7,6},{8,24},{9,25},{10,... | collective-permute-start | bytes 811016 | tf_op jit(solution)/shard_map/ppermute | solution.py:80
  23.4 20.2 %copy-start.1 = (bf16[1,4096,512]{2,1,0:T(8,128)(2,1)S(1)}, bf16[1,4096,512]{2,1,0:T(8,128)(2,1)}, u32[]{:S(2)}) copy-start(bf16[1,4096,512]{2,1,0:T(8,128)(2,1)} %param.14) | copy-start | bytes 12582916
  28.2 9.5 %collective-permute-start.3 = (bf16[64,4224]{1,0:T(8,128)(2,1)S(1)}, bf16[64,4224]{1,0:T(8,128)(2,1)S(1)}, u32[]{:S(2)}, u32[]{:S(2)}) collective-permute-start(bf16[64,4224]{1,0:T(8,128)(2,1)S(1)} %pad_maximum_fusion), channel_id=1, source_target_pairs={{0,16},{1,17},{2,18},{3,19},{4,20},{5,21},{6,22},{7,23},{8,9},{9,8... | collective-permute-start | bytes 1622024 | tf_op jit(solution)/shard_map/ppermute | solution.py:80
  30.4 11.3 %collective-permute-start.13 = (bf16[64,4224]{1,0:T(8,128)(2,1)S(1)}, bf16[64,4224]{1,0:T(8,128)(2,1)S(1)}, u32[]{:S(2)}, u32[]{:S(2)}) collective-permute-start(bf16[64,4224]{1,0:T(8,128)(2,1)S(1)} %pad_maximum_fusion.1), channel_id=1, source_target_pairs={{0,2},{1,3},{2,0},{3,1},{4,6},{5,7},{6,4},{7,5},{8,10},{9,11},{10,... | collective-permute-start | bytes 1622024 | tf_op jit(solution)/shard_map/ppermute | solution.py:80
  34.0 9.5 %collective-permute-start.23 = (bf16[64,4224]{1,0:T(8,128)(2,1)S(1)}, bf16[64,4224]{1,0:T(8,128)(2,1)S(1)}, u32[]{:S(2)}, u32[]{:S(2)}) collective-permute-start(bf16[64,4224]{1,0:T(8,128)(2,1)S(1)} %pad_maximum_fusion.2), channel_id=1, source_target_pairs={{0,16},{1,17},{2,18},{3,19},{4,20},{5,21},{6,22},{7,23},{8,9},{9,8... | collective-permute-start | bytes 1622024 | tf_op jit(solution)/shard_map/ppermute | solution.py:80
  36.1 7.5 %copy-start = (bf16[1,4096,512]{2,1,0:T(8,128)(2,1)S(1)}, bf16[1,4096,512]{2,1,0:T(8,128)(2,1)}, u32[]{:S(2)}) copy-start(bf16[1,4096,512]{2,1,0:T(8,128)(2,1)} %param.13) | copy-start | bytes 12582916
  37.7 5.9 %collective-permute-start.4 = (bf16[128,4224]{1,0:T(8,128)(2,1)S(1)}, bf16[128,4224]{1,0:T(8,128)(2,1)S(1)}, u32[]{:S(2)}, u32[]{:S(2)}) collective-permute-start(bf16[128,4224]{1,0:T(8,128)(2,1)S(1)} %constant_dynamic-update-slice_fusion.own), channel_id=1, source_target_pairs={{0,8},{1,9},{2,10},{3,11},{4,12},{5,13},{6,14},{7,15},{8,0},{9,1},... | collective-permute-start | bytes 3244040 | tf_op jit(solution)/shard_map/ppermute | solution.py:80
  41.7 8.8 %collective-permute-start.14 = (bf16[128,4224]{1,0:T(8,128)(2,1)S(1)}, bf16[128,4224]{1,0:T(8,128)(2,1)S(1)}, u32[]{:S(2)}, u32[]{:S(2)}) collective-permute-start(bf16[128,4224]{1,0:T(8,128)(2,1)S(1)} %constant_dynamic-update-slice_fusion.5.own), channel_id=1, source_target_pairs={{0,8},{1,9},{2,10},{3,11},{4,12},{5,13},{6,14},{7,15},{8,0},{9,1},... | collective-permute-start | bytes 3244040 | tf_op jit(solution)/shard_map/ppermute | solution.py:80
  43.5 11.5 %collective-permute-start.24 = (bf16[128,4224]{1,0:T(8,128)(2,1)S(1)}, bf16[128,4224]{1,0:T(8,128)(2,1)S(1)}, u32[]{:S(2)}, u32[]{:S(2)}) collective-permute-start(bf16[128,4224]{1,0:T(8,128)(2,1)S(1)} %constant_dynamic-update-slice_fusion.10.own), channel_id=1, source_target_pairs={{0,8},{1,9},{2,10},{3,11},{4,12},{5,13},{6,14},{7,15},{8,0},{9,1},... | collective-permute-start | bytes 3244040 | tf_op jit(solution)/shard_map/ppermute | solution.py:80
  43.6 2.2 %copy-start.2 = (bf16[1,512,4096]{2,1,0:T(8,128)(2,1)S(1)}, bf16[1,512,4096]{2,1,0:T(8,128)(2,1)}, u32[]{:S(2)}) copy-start(bf16[1,512,4096]{2,1,0:T(8,128)(2,1)} %param.15) | copy-start | bytes 12582916
  50.0 9.7 %collective-permute-start.5 = (bf16[128,4096]{1,0:T(8,128)(2,1)S(1)}, bf16[128,4096]{1,0:T(8,128)(2,1)S(1)}, u32[]{:S(2)}, u32[]{:S(2)}) collective-permute-start(bf16[128,4096]{1,0:T(8,128)(2,1)S(1)} %get-tuple-element.18), channel_id=1, source_target_pairs={{0,8},{1,9},{2,10},{3,11},{4,12},{5,13},{6,14},{7,15},{8,0},{9,1},... | collective-permute-start | bytes 3145736 | tf_op jit(solution)/shard_map/ppermute | solution.py:80
  50.5 4.4 %copy-start.3 = (bf16[1,512,4096]{2,1,0:T(8,128)(2,1)S(1)}, bf16[1,512,4096]{2,1,0:T(8,128)(2,1)}, u32[]{:S(2)}) copy-start(bf16[1,512,4096]{2,1,0:T(8,128)(2,1)} %param.15) | copy-start | bytes 12582916
  54.8 7.0 %collective-permute-start.15 = (bf16[128,4096]{1,0:T(8,128)(2,1)S(1)}, bf16[128,4096]{1,0:T(8,128)(2,1)S(1)}, u32[]{:S(2)}, u32[]{:S(2)}) collective-permute-start(bf16[128,4096]{1,0:T(8,128)(2,1)S(1)} %get-tuple-element.21), channel_id=1, source_target_pairs={{0,8},{1,9},{2,10},{3,11},{4,12},{5,13},{6,14},{7,15},{8,0},{9,1},... | collective-permute-start | bytes 3145736 | tf_op jit(solution)/shard_map/ppermute | solution.py:80
  59.1 3.0 %collective-permute-start.25 = (bf16[128,4096]{1,0:T(8,128)(2,1)S(1)}, bf16[128,4096]{1,0:T(8,128)(2,1)S(1)}, u32[]{:S(2)}, u32[]{:S(2)}) collective-permute-start(bf16[128,4096]{1,0:T(8,128)(2,1)S(1)} %get-tuple-element.24), channel_id=1, source_target_pairs={{0,8},{1,9},{2,10},{3,11},{4,12},{5,13},{6,14},{7,15},{8,0},{9,1},... | collective-permute-start | bytes 3145736 | tf_op jit(solution)/shard_map/ppermute | solution.py:80
  59.8 9.2 %collective-permute-start.6 = (bf16[64,4096]{1,0:T(8,128)(2,1)S(1)}, bf16[64,4096]{1,0:T(8,128)(2,1)S(1)}, u32[]{:S(2)}, u32[]{:S(2)}) collective-permute-start(bf16[64,4096]{1,0:T(8,128)(2,1)S(1)} %add_convert_fusion.2), channel_id=1, source_target_pairs={{0,16},{1,17},{2,18},{3,19},{4,20},{5,21},{6,22},{7,23},{8,9},{9,8... | collective-permute-start | bytes 1572872 | tf_op jit(solution)/shard_map/ppermute | solution.py:80
  62.0 13.7 %collective-permute-start.16 = (bf16[64,4096]{1,0:T(8,128)(2,1)S(1)}, bf16[64,4096]{1,0:T(8,128)(2,1)S(1)}, u32[]{:S(2)}, u32[]{:S(2)}) collective-permute-start(bf16[64,4096]{1,0:T(8,128)(2,1)S(1)} %add_convert_fusion.1), channel_id=1, source_target_pairs={{0,2},{1,3},{2,0},{3,1},{4,6},{5,7},{6,4},{7,5},{8,10},{9,11},{10,... | collective-permute-start | bytes 1572872 | tf_op jit(solution)/shard_map/ppermute | solution.py:80
  62.2 15.2 %collective-permute-start.26 = (bf16[64,4096]{1,0:T(8,128)(2,1)S(1)}, bf16[64,4096]{1,0:T(8,128)(2,1)S(1)}, u32[]{:S(2)}, u32[]{:S(2)}) collective-permute-start(bf16[64,4096]{1,0:T(8,128)(2,1)S(1)} %add_convert_fusion), channel_id=1, source_target_pairs={{0,16},{1,17},{2,18},{3,19},{4,20},{5,21},{6,22},{7,23},{8,9},{9,8... | collective-permute-start | bytes 1572872 | tf_op jit(solution)/shard_map/ppermute | solution.py:80
  69.1 10.5 %collective-permute-start.7 = (bf16[32,4096]{1,0:T(8,128)(2,1)S(1)}, bf16[32,4096]{1,0:T(8,128)(2,1)S(1)}, u32[]{:S(2)}, u32[]{:S(2)}) collective-permute-start(bf16[32,4096]{1,0:T(8,128)(2,1)S(1)} %add_convert_fusion.5), channel_id=1, source_target_pairs={{0,1},{1,0},{2,3},{3,2},{4,5},{5,4},{6,7},{7,6},{8,24},{9,25},{10,... | collective-permute-start | bytes 786440 | tf_op jit(solution)/shard_map/ppermute | solution.py:80
  75.8 8.5 %collective-permute-start.17 = (bf16[32,4096]{1,0:T(8,128)(2,1)S(1)}, bf16[32,4096]{1,0:T(8,128)(2,1)S(1)}, u32[]{:S(2)}, u32[]{:S(2)}) collective-permute-start(bf16[32,4096]{1,0:T(8,128)(2,1)S(1)} %add_convert_fusion.4), channel_id=1, source_target_pairs={{0,16},{1,17},{2,18},{3,19},{4,20},{5,21},{6,22},{7,23},{8,9},{9,8... | collective-permute-start | bytes 786440 | tf_op jit(solution)/shard_map/ppermute | solution.py:80
  77.6 7.9 %collective-permute-start.27 = (bf16[32,4096]{1,0:T(8,128)(2,1)S(1)}, bf16[32,4096]{1,0:T(8,128)(2,1)S(1)}, u32[]{:S(2)}, u32[]{:S(2)}) collective-permute-start(bf16[32,4096]{1,0:T(8,128)(2,1)S(1)} %add_convert_fusion.3), channel_id=1, source_target_pairs={{0,1},{1,0},{2,3},{3,2},{4,5},{5,4},{6,7},{7,6},{8,24},{9,25},{10,... | collective-permute-start | bytes 786440 | tf_op jit(solution)/shard_map/ppermute | solution.py:80
  79.7 6.1 %collective-permute-start.8 = (bf16[16,4096]{1,0:T(8,128)(2,1)S(1)}, bf16[16,4096]{1,0:T(8,128)(2,1)S(1)}, u32[]{:S(2)}, u32[]{:S(2)}) collective-permute-start(bf16[16,4096]{1,0:T(8,128)(2,1)S(1)} %add_convert_fusion.8), channel_id=1, source_target_pairs={{0,2},{1,3},{2,0},{3,1},{4,6},{5,7},{6,4},{7,5},{8,10},{9,11},{10,... | collective-permute-start | bytes 393224 | tf_op jit(solution)/shard_map/ppermute | solution.py:80
  84.4 5.0 %collective-permute-start.18 = (bf16[16,4096]{1,0:T(8,128)(2,1)S(1)}, bf16[16,4096]{1,0:T(8,128)(2,1)S(1)}, u32[]{:S(2)}, u32[]{:S(2)}) collective-permute-start(bf16[16,4096]{1,0:T(8,128)(2,1)S(1)} %add_convert_fusion.7), channel_id=1, source_target_pairs={{0,1},{1,0},{2,3},{3,2},{4,5},{5,4},{6,7},{7,6},{8,24},{9,25},{10,... | collective-permute-start | bytes 393224 | tf_op jit(solution)/shard_map/ppermute | solution.py:80
  85.5 7.1 %collective-permute-start.28 = (bf16[16,4096]{1,0:T(8,128)(2,1)S(1)}, bf16[16,4096]{1,0:T(8,128)(2,1)S(1)}, u32[]{:S(2)}, u32[]{:S(2)}) collective-permute-start(bf16[16,4096]{1,0:T(8,128)(2,1)S(1)} %add_convert_fusion.6), channel_id=1, source_target_pairs={{0,2},{1,3},{2,0},{3,1},{4,6},{5,7},{6,4},{7,5},{8,10},{9,11},{10,... | collective-permute-start | bytes 393224 | tf_op jit(solution)/shard_map/ppermute | solution.py:80
  85.9 7.5 %collective-permute-start.9 = (bf16[8,4096]{1,0:T(8,128)(2,1)S(1)}, bf16[8,4096]{1,0:T(8,128)(2,1)S(1)}, u32[]{:S(2)}, u32[]{:S(2)}) collective-permute-start(bf16[8,4096]{1,0:T(8,128)(2,1)S(1)} %add_convert_fusion.14), channel_id=1, source_target_pairs={{0,4},{1,5},{2,6},{3,7},{4,0},{5,1},{6,2},{7,3},{8,12},{9,13},{10,... | collective-permute-start | bytes 196616 | tf_op jit(solution)/shard_map/ppermute | solution.py:80
  89.5 5.7 %collective-permute-start.19 = (bf16[8,4096]{1,0:T(8,128)(2,1)S(1)}, bf16[8,4096]{1,0:T(8,128)(2,1)S(1)}, u32[]{:S(2)}, u32[]{:S(2)}) collective-permute-start(bf16[8,4096]{1,0:T(8,128)(2,1)S(1)} %add_convert_fusion.12), channel_id=1, source_target_pairs={{0,4},{1,5},{2,6},{3,7},{4,0},{5,1},{6,2},{7,3},{8,12},{9,13},{10,... | collective-permute-start | bytes 196616 | tf_op jit(solution)/shard_map/ppermute | solution.py:80
  92.7 5.3 %collective-permute-start.29 = (bf16[8,4096]{1,0:T(8,128)(2,1)S(1)}, bf16[8,4096]{1,0:T(8,128)(2,1)S(1)}, u32[]{:S(2)}, u32[]{:S(2)}) collective-permute-start(bf16[8,4096]{1,0:T(8,128)(2,1)S(1)} %add_convert_fusion.10), channel_id=1, source_target_pairs={{0,4},{1,5},{2,6},{3,7},{4,0},{5,1},{6,2},{7,3},{8,12},{9,13},{10,... | collective-permute-start | bytes 196616 | tf_op jit(solution)/shard_map/ppermute | solution.py:80

commit v11 on v10

--- a/solution.py
+++ b/solution.py
@@ -12,7 +12,6 @@
 PARTS = 4
 VMEM_MIB = 8
 ROWS_AT_ONCE = 8
-GUARDS = []
 
 
 def partner(value, axis, distance):
@@ -96,8 +95,14 @@
     return lambda d, e: (d, e ^ (2 * distance))
 
 
-def pack_kernel(slots, flag, tokens, ids, weights, mine, *outs_and_square):
-    *outs, square = outs_and_square
+def pack_kernel(slots, flag, tokens_hbm, ids_hbm, weights_hbm, mine, *outs_and_scratch):
+    *outs, square, tokens, ids, weights, sems = outs_and_scratch
+    loads = [
+        pltpu.make_async_copy(source, target, sems.at[k])
+        for k, (source, target) in enumerate(((ids_hbm, ids), (weights_hbm, weights), (tokens_hbm, tokens)))
+    ]
+    for load in loads:
+        load.start()
     d = lax.axis_index("dp")
     serving = jnp.where(flag[0] == 1, d ^ 1, d) * lax.axis_size("expert") + lax.axis_index("expert")
     expert = jnp.int32(0)
@@ -107,6 +112,8 @@
     mine[0] = expert
     top_count, tok_rows = ids.shape
     square[...] = jnp.zeros_like(square)
+    loads[0].wait()
+    loads[1].wait()
     square[:top_count, :tok_rows] = ids[...].astype(jnp.float32)
     rest = weights[...]
     for k in range(1, 4):
@@ -114,11 +121,16 @@
         square[k * top_count : (k + 1) * top_count, :tok_rows] = part
         rest = rest - part
     extra = square[...].T.astype(jnp.bfloat16)
+    loads[2].wait()
     at = 0
     for out in outs:
         rows, packed_width = out.shape
         out[...] = jnp.concatenate([tokens[at : at + rows], extra[at : at + rows]], axis=1)
         at += rows
+
+
+def in_hbm(*arrays):
+    return [pltpu.with_memory_space_constraint(array, pltpu.HBM) for array in arrays]
 
 
 def packed(tokens, expert_ids, route_weight, slot_of, swap_flag, rows):
@@ -130,11 +142,19 @@
     mine, *owns = pl.pallas_call(
         pack_kernel,
         out_shape=(jax.ShapeDtypeStruct((1,), jnp.int32),) + (pltpu.VMEM((rows, width + side), tokens.dtype),) * count,
-        in_specs=[scalars] * 2 + [whole] * 3,
+        in_specs=[scalars] * 2 + [pl.BlockSpec(memory_space=pl.ANY)] * 3,
         out_specs=(scalars,) + (whole,) * count,
-        scratch_shapes=[pltpu.VMEM((side, side), jnp.float32)],
+        scratch_shapes=[
+            pltpu.VMEM((side, side), jnp.float32),
+            pltpu.VMEM(tokens.shape, tokens.dtype),
+            pltpu.VMEM(expert_ids.shape[::-1], expert_ids.dtype),
+            pltpu.VMEM(route_weight.shape[::-1], route_weight.dtype),
+            pltpu.SemaphoreType.DMA((3,)),
+        ],
+        compiler_params=pltpu.CompilerParams(vmem_limit_bytes=VMEM_MIB * 2**20),
+        cost_estimate=pl.CostEstimate(flops=10**10, bytes_accessed=4 * tok_rows * width, transcendentals=0),
         name="pack_rows",
-    )(slot_of.T, swap_flag, tokens, expert_ids.T, route_weight.T)
+    )(*in_hbm(slot_of.T), swap_flag, *in_hbm(tokens, expert_ids.T, route_weight.T))
     return mine, owns
 
 
@@ -208,20 +228,13 @@
     return total(*[term[:rows] for term in terms])
 
 
-def run_steps(chunks, guards):
-    waits = [[next(chunk)[0]] for chunk in chunks]
+def run_steps(chunks):
+    waits = [next(chunk) for chunk in chunks]
     results = [None] * len(chunks)
     while any(result is None for result in results):
         for i, chunk in enumerate(chunks):
-            at = len(waits[i]) - 1
-            asked = [(j, t) for k, s, j, t in guards if (k, s) == (i, at)]
-            if results[i] is not None or any(len(waits[j]) <= t for j, t in asked):
-                continue
-            ready = tuple(waits[i][-1:])
-            if asked:
-                ready = lax.optimization_barrier(ready + tuple(waits[j][t] for j, t in asked))[:1]
             try:
-                waits[i].append(chunk.send(ready)[0])
+                waits[i] = chunk.send(waits[i]) if results[i] is None else None
             except StopIteration as end:
                 results[i] = end.value
     return results
@@ -238,8 +251,7 @@
     mine, owns = packed(tokens, expert_ids, route_weight, slot_of, swap_flag, step)
     serve = lambda held, sib: serve_rows(held, sib, mine, top_count, w_gate[0], w_up[0], w_down[0])
     chunks = [chunk_steps(own, routes[i % len(routes)], serve) for i, own in enumerate(owns)]
-    guards = GUARDS if len(chunks) == 3 and line_bits == 2 else []
-    return jnp.concatenate(run_steps(chunks, guards))
+    return jnp.concatenate(run_steps(chunks))
 
 
 def on_device(tokens, expert_ids, *rest):

time: 98.9 us -> 97.9 us (0.990)
  local copies, waits for them, and re-layouts: 2.53 us -> 0.34 us
  Pallas kernels: 14.2 us -> 15.3 us
    unnamed x20 -> x18, local copies, waits for them, and re-layouts: 2.38 us -> 0.2 us
    pallas_call x1, Pallas kernels: 1.52 us -> 2.72 us  [packed(): pl.pallas_call(pack_kernel, out_shape=(jax.ShapeDtypeStruct((1,), jnp.int...]
where the time goes in v11:
time: 97.9 us; the launch traced here: 97.7 us
  waiting for transfers between devices  40.3 us (41%)
  starting transfers between devices  38.7 us (40%)
  Pallas kernels  15.3 us (16%)
  other arithmetic  2.11 us (2%)
    ppermute x30, waiting for transfers between devices, permute(): return lax.ppermute(value, AXES, pairs)  40.3 us
    ppermute x30, starting transfers between devices, permute(): return lax.ppermute(value, AXES, pairs)  38.7 us
    pallas_call x3, Pallas kernels, serve_rows(): pl.pallas_call(functools.partial(serve_kernel, top_count), out_shape=(out...  12.6 us
    pallas_call x1, Pallas kernels, packed(): pl.pallas_call(pack_kernel, out_shape=(jax.ShapeDtypeStruct((1,), jnp.int...  2.72 us
  transfers between devices with their start and end apart: 30, of which 16 were waited for; matrix products, arithmetic and copies ran while one was open for 2% of the time, Pallas kernels for 13%

profile of v11, /device:TPU:0, one launch (start us, length us, event | category | flops | bytes accessed | tf_op | source)
XLA Modules:
  0.0 97.7 jit_solution(1624641049140910839)
XLA Ops:
  0.7 2.7 %pack_rows.1 = (s32[1]{0:T(128)}, bf16[8,4224]{1,0:T(8,128)(2,1)S(1)}, bf16[8,4224]{1,0:T(8,128)(2,1)S(1)}, bf16[8,4224]{1,0:T(8,128)(2,1)S(1)}) custom-call(s32[2,16]{1,0:T(2,128)} %bitcast.17, s32[1]{0:T(128)S(6)} %copy.21.flag, bf16[24,4096]{1,0:T(8,128)(2,1)} %tokens_hbm.1, s32[8,24]{1,0:T(8,128)} %bitcast.15, f32[8,24]{1,0:T(8,128)} %bitcast.16), custom_call_target="tpu_custom_call" | custom-call | flops 10000000000 | bytes 393216 | tf_op jit(solution)/shard_map/pack_rows/pallas_call | solution.py:142
  3.4 4.1 %collective-permute-start = (bf16[8,4224]{1,0:T(8,128)(2,1)S(1)}, bf16[8,4224]{1,0:T(8,128)(2,1)S(1)}, u32[]{:S(2)}, u32[]{:S(2)}) collective-permute-start(bf16[8,4224]{1,0:T(8,128)(2,1)S(1)} %get-tuple-element.16), channel_id=1, source_target_pairs={{0,4},{1,5},{2,6},{3,7},{4,0},{5,1},{6,2},{7,3},{8,12},{9,13},{10,... | collective-permute-start | bytes 202760 | tf_op jit(solution)/shard_map/ppermute | solution.py:79
  7.5 0.1 collective-permute-start.10
  7.6 2.8 %collective-permute-start.20 = (bf16[8,4224]{1,0:T(8,128)(2,1)S(1)}, bf16[8,4224]{1,0:T(8,128)(2,1)S(1)}, u32[]{:S(2)}, u32[]{:S(2)}) collective-permute-start(bf16[8,4224]{1,0:T(8,128)(2,1)S(1)} %get-tuple-element.22), channel_id=1, source_target_pairs={{0,4},{1,5},{2,6},{3,7},{4,0},{5,1},{6,2},{7,3},{8,12},{9,13},{10,... | collective-permute-start | bytes 202760 | tf_op jit(solution)/shard_map/ppermute | solution.py:79
  10.5 0.8 collective-permute-done
  11.3 3.6 %collective-permute-start.1 = (bf16[16,4224]{1,0:T(8,128)(2,1)S(1)}, bf16[16,4224]{1,0:T(8,128)(2,1)S(1)}, u32[]{:S(2)}, u32[]{:S(2)}) collective-permute-start(bf16[16,4224]{1,0:T(8,128)(2,1)S(1)} %pad_maximum_fusion.7), channel_id=1, source_target_pairs={{0,2},{1,3},{2,0},{3,1},{4,6},{5,7},{6,4},{7,5},{8,10},{9,11},{10,... | collective-permute-start | bytes 405512 | tf_op jit(solution)/shard_map/ppermute | solution.py:79
  14.9 1.2 %collective-permute-done.10 = bf16[8,4224]{1,0:T(8,128)(2,1)S(1)} collective-permute-done((bf16[8,4224]{1,0:T(8,128)(2,1)S(1)}, bf16[8,4224]{1,0:T(8,128)(2,1)S(1)}, u32[]{:S(2)}, u32[]{:S(2)}) %collective-permute-start.10) | collective-permute-done | bytes 67616 | tf_op jit(solution)/shard_map/ppermute | solution.py:79
  16.1 1.6 %collective-permute-start.11 = (bf16[16,4224]{1,0:T(8,128)(2,1)S(1)}, bf16[16,4224]{1,0:T(8,128)(2,1)S(1)}, u32[]{:S(2)}, u32[]{:S(2)}) collective-permute-start(bf16[16,4224]{1,0:T(8,128)(2,1)S(1)} %pad_maximum_fusion.8), channel_id=1, source_target_pairs={{0,1},{1,0},{2,3},{3,2},{4,5},{5,4},{6,7},{7,6},{8,24},{9,25},{10,... | collective-permute-start | bytes 405512 | tf_op jit(solution)/shard_map/ppermute | solution.py:79
  17.7 0.7 collective-permute-start.21
  18.4 1.5 %collective-permute-done.1 = bf16[16,4224]{1,0:T(8,128)(2,1)S(1)} collective-permute-done((bf16[16,4224]{1,0:T(8,128)(2,1)S(1)}, bf16[16,4224]{1,0:T(8,128)(2,1)S(1)}, u32[]{:S(2)}, u32[]{:S(2)}) %collective-permute-start.1) | collective-permute-done | bytes 135200 | tf_op jit(solution)/shard_map/ppermute | solution.py:79
  20.0 2.1 %collective-permute-start.2 = (bf16[32,4224]{1,0:T(8,128)(2,1)S(1)}, bf16[32,4224]{1,0:T(8,128)(2,1)S(1)}, u32[]{:S(2)}, u32[]{:S(2)}) collective-permute-start(bf16[32,4224]{1,0:T(8,128)(2,1)S(1)} %pad_maximum_fusion.3), channel_id=1, source_target_pairs={{0,1},{1,0},{2,3},{3,2},{4,5},{5,4},{6,7},{7,6},{8,24},{9,25},{10,... | collective-permute-start | bytes 811016 | tf_op jit(solution)/shard_map/ppermute | solution.py:79
  22.1 1.6 %collective-permute-start.12 = (bf16[32,4224]{1,0:T(8,128)(2,1)S(1)}, bf16[32,4224]{1,0:T(8,128)(2,1)S(1)}, u32[]{:S(2)}, u32[]{:S(2)}) collective-permute-start(bf16[32,4224]{1,0:T(8,128)(2,1)S(1)} %pad_maximum_fusion.4), channel_id=1, source_target_pairs={{0,16},{1,17},{2,18},{3,19},{4,20},{5,21},{6,22},{7,23},{8,9},{9,8... | collective-permute-start | bytes 811016 | tf_op jit(solution)/shard_map/ppermute | solution.py:79
  23.7 0.9 collective-permute-start.22
  24.7 4.7 %collective-permute-done.2 = bf16[32,4224]{1,0:T(8,128)(2,1)S(1)} collective-permute-done((bf16[32,4224]{1,0:T(8,128)(2,1)S(1)}, bf16[32,4224]{1,0:T(8,128)(2,1)S(1)}, u32[]{:S(2)}, u32[]{:S(2)}) %collective-permute-start.2) | collective-permute-done | bytes 270368 | tf_op jit(solution)/shard_map/ppermute | solution.py:79
  29.4 2.1 %collective-permute-start.3 = (bf16[64,4224]{1,0:T(8,128)(2,1)S(1)}, bf16[64,4224]{1,0:T(8,128)(2,1)S(1)}, u32[]{:S(2)}, u32[]{:S(2)}) collective-permute-start(bf16[64,4224]{1,0:T(8,128)(2,1)S(1)} %pad_maximum_fusion), channel_id=1, source_target_pairs={{0,16},{1,17},{2,18},{3,19},{4,20},{5,21},{6,22},{7,23},{8,9},{9,8... | collective-permute-start | bytes 1622024 | tf_op jit(solution)/shard_map/ppermute | solution.py:79
  31.6 0.1 collective-permute-start.13
  31.6 3.5 %collective-permute-done.22 = bf16[32,4224]{1,0:T(8,128)(2,1)S(1)} collective-permute-done((bf16[32,4224]{1,0:T(8,128)(2,1)S(1)}, bf16[32,4224]{1,0:T(8,128)(2,1)S(1)}, u32[]{:S(2)}, u32[]{:S(2)}) %collective-permute-start.22) | collective-permute-done | bytes 270368 | tf_op jit(solution)/shard_map/ppermute | solution.py:79
  35.1 0.1 pad_maximum_fusion.2
  35.2 2.1 %collective-permute-start.23 = (bf16[64,4224]{1,0:T(8,128)(2,1)S(1)}, bf16[64,4224]{1,0:T(8,128)(2,1)S(1)}, u32[]{:S(2)}, u32[]{:S(2)}) collective-permute-start(bf16[64,4224]{1,0:T(8,128)(2,1)S(1)} %pad_maximum_fusion.2), channel_id=1, source_target_pairs={{0,16},{1,17},{2,18},{3,19},{4,20},{5,21},{6,22},{7,23},{8,9},{9,8... | collective-permute-start | bytes 1622024 | tf_op jit(solution)/shard_map/ppermute | solution.py:79
  37.4 1.4 %collective-permute-done.3 = bf16[64,4224]{1,0:T(8,128)(2,1)S(1)} collective-permute-done((bf16[64,4224]{1,0:T(8,128)(2,1)S(1)}, bf16[64,4224]{1,0:T(8,128)(2,1)S(1)}, u32[]{:S(2)}, u32[]{:S(2)}) %collective-permute-start.3) | collective-permute-done | bytes 540704 | tf_op jit(solution)/shard_map/ppermute | solution.py:79
  38.9 0.1 collective-permute-start.4
  39.0 3.9 %collective-permute-done.13 = bf16[64,4224]{1,0:T(8,128)(2,1)S(1)} collective-permute-done((bf16[64,4224]{1,0:T(8,128)(2,1)S(1)}, bf16[64,4224]{1,0:T(8,128)(2,1)S(1)}, u32[]{:S(2)}, u32[]{:S(2)}) %collective-permute-start.13) | collective-permute-done | bytes 540704 | tf_op jit(solution)/shard_map/ppermute | solution.py:79
  42.9 0.1 collective-permute-start.14
  43.0 1.7 %collective-permute-done.23 = bf16[64,4224]{1,0:T(8,128)(2,1)S(1)} collective-permute-done((bf16[64,4224]{1,0:T(8,128)(2,1)S(1)}, bf16[64,4224]{1,0:T(8,128)(2,1)S(1)}, u32[]{:S(2)}, u32[]{:S(2)}) %collective-permute-start.23) | collective-permute-done | bytes 540704 | tf_op jit(solution)/shard_map/ppermute | solution.py:79
  44.7 0.1 collective-permute-start.24
  44.8 4.2 %serve_rows.3 = (bf16[128,4096]{1,0:T(8,128)(2,1)S(1)}, bf16[128,4096]{1,0:T(8,128)(2,1)S(1)}) custom-call(s32[1]{0:T(128)} %get-tuple-element.15.mine, bf16[128,4224]{1,0:T(8,128)(2,1)S(1)} %constant_dynamic-update-slice_fusion.own, bf16[128,4224]{1,0:T(8,128)(2,1)S(1)} %collective-permute-done.4.sib, bf16[4096,512]{1,0:T(8,128)(2,1)S(1)} %bitcast.6, ...), custom_call_target="tpu_custom_call" | custom-call | flops 3221225472 | bytes 16777216 | tf_op jit(solution)/shard_map/serve_rows/pallas_call | solution.py:194
  49.0 0.5 collective-permute-start.5
  49.6 4.2 %serve_rows.4 = (bf16[128,4096]{1,0:T(8,128)(2,1)S(1)}, bf16[128,4096]{1,0:T(8,128)(2,1)S(1)}) custom-call(s32[1]{0:T(128)} %get-tuple-element.15.mine, bf16[128,4224]{1,0:T(8,128)(2,1)S(1)} %constant_dynamic-update-slice_fusion.5.own, bf16[128,4224]{1,0:T(8,128)(2,1)S(1)} %collective-permute-done.14.sib, bf16[4096,512]{1,0:T(8,128)(2,1)S(1)} %bitcast.7, ...), custom_call_target="tpu_custom_call" | custom-call | flops 3221225472 | bytes 16777216 | tf_op jit(solution)/shard_map/serve_rows/pallas_call | solution.py:194
  53.8 0.1 collective-permute-start.15
  53.9 4.2 %serve_rows.5 = (bf16[128,4096]{1,0:T(8,128)(2,1)S(1)}, bf16[128,4096]{1,0:T(8,128)(2,1)S(1)}) custom-call(s32[1]{0:T(128)} %get-tuple-element.15.mine, bf16[128,4224]{1,0:T(8,128)(2,1)S(1)} %constant_dynamic-update-slice_fusion.10.own, bf16[128,4224]{1,0:T(8,128)(2,1)S(1)} %collective-permute-done.24.sib, bf16[4096,512]{1,0:T(8,128)(2,1)S(1)} %bitcast.8, ...), custom_call_target="tpu_custom_call" | custom-call | flops 3221225472 | bytes 16777216 | tf_op jit(solution)/shard_map/serve_rows/pallas_call | solution.py:194
  58.1 0.5 collective-permute-start.25
  58.6 0.1 add_convert_fusion.2
  58.7 2.1 %collective-permute-start.6 = (bf16[64,4096]{1,0:T(8,128)(2,1)S(1)}, bf16[64,4096]{1,0:T(8,128)(2,1)S(1)}, u32[]{:S(2)}, u32[]{:S(2)}) collective-permute-start(bf16[64,4096]{1,0:T(8,128)(2,1)S(1)} %add_convert_fusion.2), channel_id=1, source_target_pairs={{0,16},{1,17},{2,18},{3,19},{4,20},{5,21},{6,22},{7,23},{8,9},{9,8... | collective-permute-start | bytes 1572872 | tf_op jit(solution)/shard_map/ppermute | solution.py:79
  60.8 0.1 add_convert_fusion.1
  60.9 0.1 collective-permute-start.16
  61.0 0.1 add_convert_fusion
  61.2 1.9 %collective-permute-start.26 = (bf16[64,4096]{1,0:T(8,128)(2,1)S(1)}, bf16[64,4096]{1,0:T(8,128)(2,1)S(1)}, u32[]{:S(2)}, u32[]{:S(2)}) collective-permute-start(bf16[64,4096]{1,0:T(8,128)(2,1)S(1)} %add_convert_fusion), channel_id=1, source_target_pairs={{0,16},{1,17},{2,18},{3,19},{4,20},{5,21},{6,22},{7,23},{8,9},{9,8... | collective-permute-start | bytes 1572872 | tf_op jit(solution)/shard_map/ppermute | solution.py:79
  63.1 4.9 %collective-permute-done.6 = bf16[64,4096]{1,0:T(8,128)(2,1)S(1)} collective-permute-done((bf16[64,4096]{1,0:T(8,128)(2,1)S(1)}, bf16[64,4096]{1,0:T(8,128)(2,1)S(1)}, u32[]{:S(2)}, u32[]{:S(2)}) %collective-permute-start.6) | collective-permute-done | bytes 524320 | tf_op jit(solution)/shard_map/ppermute | solution.py:79
  68.0 0.1 add_convert_fusion.5
  68.1 2.1 %collective-permute-start.7 = (bf16[32,4096]{1,0:T(8,128)(2,1)S(1)}, bf16[32,4096]{1,0:T(8,128)(2,1)S(1)}, u32[]{:S(2)}, u32[]{:S(2)}) collective-permute-start(bf16[32,4096]{1,0:T(8,128)(2,1)S(1)} %add_convert_fusion.5), channel_id=1, source_target_pairs={{0,1},{1,0},{2,3},{3,2},{4,5},{5,4},{6,7},{7,6},{8,24},{9,25},{10,... | collective-permute-start | bytes 786440 | tf_op jit(solution)/shard_map/ppermute | solution.py:79
  70.2 4.4 %collective-permute-done.16 = bf16[64,4096]{1,0:T(8,128)(2,1)S(1)} collective-permute-done((bf16[64,4096]{1,0:T(8,128)(2,1)S(1)}, bf16[64,4096]{1,0:T(8,128)(2,1)S(1)}, u32[]{:S(2)}, u32[]{:S(2)}) %collective-permute-start.16) | collective-permute-done | bytes 524320 | tf_op jit(solution)/shard_map/ppermute | solution.py:79
  74.6 0.1 add_convert_fusion.4
  74.7 0.7 collective-permute-start.17
  75.4 1.0 %collective-permute-done.26 = bf16[64,4096]{1,0:T(8,128)(2,1)S(1)} collective-permute-done((bf16[64,4096]{1,0:T(8,128)(2,1)S(1)}, bf16[64,4096]{1,0:T(8,128)(2,1)S(1)}, u32[]{:S(2)}, u32[]{:S(2)}) %collective-permute-start.26) | collective-permute-done | bytes 524320 | tf_op jit(solution)/shard_map/ppermute | solution.py:79
  76.4 0.1 add_convert_fusion.3
  76.5 2.1 %collective-permute-start.27 = (bf16[32,4096]{1,0:T(8,128)(2,1)S(1)}, bf16[32,4096]{1,0:T(8,128)(2,1)S(1)}, u32[]{:S(2)}, u32[]{:S(2)}) collective-permute-start(bf16[32,4096]{1,0:T(8,128)(2,1)S(1)} %add_convert_fusion.3), channel_id=1, source_target_pairs={{0,1},{1,0},{2,3},{3,2},{4,5},{5,4},{6,7},{7,6},{8,24},{9,25},{10,... | collective-permute-start | bytes 786440 | tf_op jit(solution)/shard_map/ppermute | solution.py:79
  78.6 0.1 add_convert_fusion.8
  78.7 0.1 collective-permute-start.8
  78.8 4.5 %collective-permute-done.17 = bf16[32,4096]{1,0:T(8,128)(2,1)S(1)} collective-permute-done((bf16[32,4096]{1,0:T(8,128)(2,1)S(1)}, bf16[32,4096]{1,0:T(8,128)(2,1)S(1)}, u32[]{:S(2)}, u32[]{:S(2)}) %collective-permute-start.17) | collective-permute-done | bytes 262176 | tf_op jit(solution)/shard_map/ppermute | solution.py:79
  83.3 0.1 add_convert_fusion.7
  83.3 1.1 %collective-permute-start.18 = (bf16[16,4096]{1,0:T(8,128)(2,1)S(1)}, bf16[16,4096]{1,0:T(8,128)(2,1)S(1)}, u32[]{:S(2)}, u32[]{:S(2)}) collective-permute-start(bf16[16,4096]{1,0:T(8,128)(2,1)S(1)} %add_convert_fusion.7), channel_id=1, source_target_pairs={{0,1},{1,0},{2,3},{3,2},{4,5},{5,4},{6,7},{7,6},{8,24},{9,25},{10,... | collective-permute-start | bytes 393224 | tf_op jit(solution)/shard_map/ppermute | solution.py:79
  84.4 0.1 add_convert_fusion.6
  84.5 0.4 collective-permute-start.28
  84.9 3.5 %collective-permute-start.9 = (bf16[8,4096]{1,0:T(8,128)(2,1)S(1)}, bf16[8,4096]{1,0:T(8,128)(2,1)S(1)}, u32[]{:S(2)}, u32[]{:S(2)}) collective-permute-start(bf16[8,4096]{1,0:T(8,128)(2,1)S(1)} %add_convert_fusion.14), channel_id=1, source_target_pairs={{0,4},{1,5},{2,6},{3,7},{4,0},{5,1},{6,2},{7,3},{8,12},{9,13},{10,... | collective-permute-start | bytes 196616 | tf_op jit(solution)/shard_map/ppermute | solution.py:79
  88.4 1.1 %collective-permute-start.19 = (bf16[8,4096]{1,0:T(8,128)(2,1)S(1)}, bf16[8,4096]{1,0:T(8,128)(2,1)S(1)}, u32[]{:S(2)}, u32[]{:S(2)}) collective-permute-start(bf16[8,4096]{1,0:T(8,128)(2,1)S(1)} %add_convert_fusion.12), channel_id=1, source_target_pairs={{0,4},{1,5},{2,6},{3,7},{4,0},{5,1},{6,2},{7,3},{8,12},{9,13},{10,... | collective-permute-start | bytes 196616 | tf_op jit(solution)/shard_map/ppermute | solution.py:79
  89.5 2.1 %collective-permute-done.28 = bf16[16,4096]{1,0:T(8,128)(2,1)S(1)} collective-permute-done((bf16[16,4096]{1,0:T(8,128)(2,1)S(1)}, bf16[16,4096]{1,0:T(8,128)(2,1)S(1)}, u32[]{:S(2)}, u32[]{:S(2)}) %collective-permute-start.28) | collective-permute-done | bytes 131104 | tf_op jit(solution)/shard_map/ppermute | solution.py:79
  91.6 0.5 collective-permute-start.29
  92.2 0.1 collective-permute-done.9
  92.3 0.1 add_convert_fusion.13
  92.4 1.7 %collective-permute-done.19 = bf16[8,4096]{1,0:T(8,128)(2,1)S(1)} collective-permute-done((bf16[8,4096]{1,0:T(8,128)(2,1)S(1)}, bf16[8,4096]{1,0:T(8,128)(2,1)S(1)}, u32[]{:S(2)}, u32[]{:S(2)}) %collective-permute-start.19) | collective-permute-done | bytes 65568 | tf_op jit(solution)/shard_map/ppermute | solution.py:79
  94.0 0.1 add_convert_fusion.11
  94.1 2.8 %collective-permute-done.29 = bf16[8,4096]{1,0:T(8,128)(2,1)S(1)} collective-permute-done((bf16[8,4096]{1,0:T(8,128)(2,1)S(1)}, bf16[8,4096]{1,0:T(8,128)(2,1)S(1)}, u32[]{:S(2)}, u32[]{:S(2)}) %collective-permute-start.29) | collective-permute-done | bytes 65568 | tf_op jit(solution)/shard_map/ppermute | solution.py:79
  96.9 0.1 add_convert_fusion.9
  97.0 0.7 pad_maximum_fusion.6
  (46 shorter events, 0.7 us)
Async XLA Ops:
  0.7 44.1 %copy-start.2 = (bf16[1,512,4096]{2,1,0:T(8,128)(2,1)S(1)}, bf16[1,512,4096]{2,1,0:T(8,128)(2,1)}, u32[]{:S(2)}) copy-start(bf16[1,512,4096]{2,1,0:T(8,128)(2,1)} %param.15) | copy-start | bytes 12582916
  3.4 7.9 %collective-permute-start = (bf16[8,4224]{1,0:T(8,128)(2,1)S(1)}, bf16[8,4224]{1,0:T(8,128)(2,1)S(1)}, u32[]{:S(2)}, u32[]{:S(2)}) collective-permute-start(bf16[8,4224]{1,0:T(8,128)(2,1)S(1)} %get-tuple-element.16), channel_id=1, source_target_pairs={{0,4},{1,5},{2,6},{3,7},{4,0},{5,1},{6,2},{7,3},{8,12},{9,13},{10,... | collective-permute-start | bytes 202760 | tf_op jit(solution)/shard_map/ppermute | solution.py:79
  7.5 8.6 %collective-permute-start.10 = (bf16[8,4224]{1,0:T(8,128)(2,1)S(1)}, bf16[8,4224]{1,0:T(8,128)(2,1)S(1)}, u32[]{:S(2)}, u32[]{:S(2)}) collective-permute-start(bf16[8,4224]{1,0:T(8,128)(2,1)S(1)} %get-tuple-element.19), channel_id=1, source_target_pairs={{0,4},{1,5},{2,6},{3,7},{4,0},{5,1},{6,2},{7,3},{8,12},{9,13},{10,... | collective-permute-start | bytes 202760 | tf_op jit(solution)/shard_map/ppermute | solution.py:79
  7.6 10.1 %collective-permute-start.20 = (bf16[8,4224]{1,0:T(8,128)(2,1)S(1)}, bf16[8,4224]{1,0:T(8,128)(2,1)S(1)}, u32[]{:S(2)}, u32[]{:S(2)}) collective-permute-start(bf16[8,4224]{1,0:T(8,128)(2,1)S(1)} %get-tuple-element.22), channel_id=1, source_target_pairs={{0,4},{1,5},{2,6},{3,7},{4,0},{5,1},{6,2},{7,3},{8,12},{9,13},{10,... | collective-permute-start | bytes 202760 | tf_op jit(solution)/shard_map/ppermute | solution.py:79
  11.3 8.7 %collective-permute-start.1 = (bf16[16,4224]{1,0:T(8,128)(2,1)S(1)}, bf16[16,4224]{1,0:T(8,128)(2,1)S(1)}, u32[]{:S(2)}, u32[]{:S(2)}) collective-permute-start(bf16[16,4224]{1,0:T(8,128)(2,1)S(1)} %pad_maximum_fusion.7), channel_id=1, source_target_pairs={{0,2},{1,3},{2,0},{3,1},{4,6},{5,7},{6,4},{7,5},{8,10},{9,11},{10,... | collective-permute-start | bytes 405512 | tf_op jit(solution)/shard_map/ppermute | solution.py:79
  16.1 6.0 %collective-permute-start.11 = (bf16[16,4224]{1,0:T(8,128)(2,1)S(1)}, bf16[16,4224]{1,0:T(8,128)(2,1)S(1)}, u32[]{:S(2)}, u32[]{:S(2)}) collective-permute-start(bf16[16,4224]{1,0:T(8,128)(2,1)S(1)} %pad_maximum_fusion.8), channel_id=1, source_target_pairs={{0,1},{1,0},{2,3},{3,2},{4,5},{5,4},{6,7},{7,6},{8,24},{9,25},{10,... | collective-permute-start | bytes 405512 | tf_op jit(solution)/shard_map/ppermute | solution.py:79
  17.7 5.9 %collective-permute-start.21 = (bf16[16,4224]{1,0:T(8,128)(2,1)S(1)}, bf16[16,4224]{1,0:T(8,128)(2,1)S(1)}, u32[]{:S(2)}, u32[]{:S(2)}) collective-permute-start(bf16[16,4224]{1,0:T(8,128)(2,1)S(1)} %pad_maximum_fusion.9), channel_id=1, source_target_pairs={{0,2},{1,3},{2,0},{3,1},{4,6},{5,7},{6,4},{7,5},{8,10},{9,11},{10,... | collective-permute-start | bytes 405512 | tf_op jit(solution)/shard_map/ppermute | solution.py:79
  20.0 9.3 %collective-permute-start.2 = (bf16[32,4224]{1,0:T(8,128)(2,1)S(1)}, bf16[32,4224]{1,0:T(8,128)(2,1)S(1)}, u32[]{:S(2)}, u32[]{:S(2)}) collective-permute-start(bf16[32,4224]{1,0:T(8,128)(2,1)S(1)} %pad_maximum_fusion.3), channel_id=1, source_target_pairs={{0,1},{1,0},{2,3},{3,2},{4,5},{5,4},{6,7},{7,6},{8,24},{9,25},{10,... | collective-permute-start | bytes 811016 | tf_op jit(solution)/shard_map/ppermute | solution.py:79
  22.1 9.4 %collective-permute-start.12 = (bf16[32,4224]{1,0:T(8,128)(2,1)S(1)}, bf16[32,4224]{1,0:T(8,128)(2,1)S(1)}, u32[]{:S(2)}, u32[]{:S(2)}) collective-permute-start(bf16[32,4224]{1,0:T(8,128)(2,1)S(1)} %pad_maximum_fusion.4), channel_id=1, source_target_pairs={{0,16},{1,17},{2,18},{3,19},{4,20},{5,21},{6,22},{7,23},{8,9},{9,8... | collective-permute-start | bytes 811016 | tf_op jit(solution)/shard_map/ppermute | solution.py:79
  23.7 11.5 %collective-permute-start.22 = (bf16[32,4224]{1,0:T(8,128)(2,1)S(1)}, bf16[32,4224]{1,0:T(8,128)(2,1)S(1)}, u32[]{:S(2)}, u32[]{:S(2)}) collective-permute-start(bf16[32,4224]{1,0:T(8,128)(2,1)S(1)} %pad_maximum_fusion.5), channel_id=1, source_target_pairs={{0,1},{1,0},{2,3},{3,2},{4,5},{5,4},{6,7},{7,6},{8,24},{9,25},{10,... | collective-permute-start | bytes 811016 | tf_op jit(solution)/shard_map/ppermute | solution.py:79
  24.6 20.2 %copy-start.1 = (bf16[1,4096,512]{2,1,0:T(8,128)(2,1)S(1)}, bf16[1,4096,512]{2,1,0:T(8,128)(2,1)}, u32[]{:S(2)}) copy-start(bf16[1,4096,512]{2,1,0:T(8,128)(2,1)} %param.14) | copy-start | bytes 12582916
  29.4 9.5 %collective-permute-start.3 = (bf16[64,4224]{1,0:T(8,128)(2,1)S(1)}, bf16[64,4224]{1,0:T(8,128)(2,1)S(1)}, u32[]{:S(2)}, u32[]{:S(2)}) collective-permute-start(bf16[64,4224]{1,0:T(8,128)(2,1)S(1)} %pad_maximum_fusion), channel_id=1, source_target_pairs={{0,16},{1,17},{2,18},{3,19},{4,20},{5,21},{6,22},{7,23},{8,9},{9,8... | collective-permute-start | bytes 1622024 | tf_op jit(solution)/shard_map/ppermute | solution.py:79
  31.6 11.3 %collective-permute-start.13 = (bf16[64,4224]{1,0:T(8,128)(2,1)S(1)}, bf16[64,4224]{1,0:T(8,128)(2,1)S(1)}, u32[]{:S(2)}, u32[]{:S(2)}) collective-permute-start(bf16[64,4224]{1,0:T(8,128)(2,1)S(1)} %pad_maximum_fusion.1), channel_id=1, source_target_pairs={{0,2},{1,3},{2,0},{3,1},{4,6},{5,7},{6,4},{7,5},{8,10},{9,11},{10,... | collective-permute-start | bytes 1622024 | tf_op jit(solution)/shard_map/ppermute | solution.py:79
  35.2 9.5 %collective-permute-start.23 = (bf16[64,4224]{1,0:T(8,128)(2,1)S(1)}, bf16[64,4224]{1,0:T(8,128)(2,1)S(1)}, u32[]{:S(2)}, u32[]{:S(2)}) collective-permute-start(bf16[64,4224]{1,0:T(8,128)(2,1)S(1)} %pad_maximum_fusion.2), channel_id=1, source_target_pairs={{0,16},{1,17},{2,18},{3,19},{4,20},{5,21},{6,22},{7,23},{8,9},{9,8... | collective-permute-start | bytes 1622024 | tf_op jit(solution)/shard_map/ppermute | solution.py:79
  37.3 7.5 %copy-start = (bf16[1,4096,512]{2,1,0:T(8,128)(2,1)S(1)}, bf16[1,4096,512]{2,1,0:T(8,128)(2,1)}, u32[]{:S(2)}) copy-start(bf16[1,4096,512]{2,1,0:T(8,128)(2,1)} %param.13) | copy-start | bytes 12582916
  38.9 5.9 %collective-permute-start.4 = (bf16[128,4224]{1,0:T(8,128)(2,1)S(1)}, bf16[128,4224]{1,0:T(8,128)(2,1)S(1)}, u32[]{:S(2)}, u32[]{:S(2)}) collective-permute-start(bf16[128,4224]{1,0:T(8,128)(2,1)S(1)} %constant_dynamic-update-slice_fusion.own), channel_id=1, source_target_pairs={{0,8},{1,9},{2,10},{3,11},{4,12},{5,13},{6,14},{7,15},{8,0},{9,1},... | collective-permute-start | bytes 3244040 | tf_op jit(solution)/shard_map/ppermute | solution.py:79
  42.9 6.7 %collective-permute-start.14 = (bf16[128,4224]{1,0:T(8,128)(2,1)S(1)}, bf16[128,4224]{1,0:T(8,128)(2,1)S(1)}, u32[]{:S(2)}, u32[]{:S(2)}) collective-permute-start(bf16[128,4224]{1,0:T(8,128)(2,1)S(1)} %constant_dynamic-update-slice_fusion.5.own), channel_id=1, source_target_pairs={{0,8},{1,9},{2,10},{3,11},{4,12},{5,13},{6,14},{7,15},{8,0},{9,1},... | collective-permute-start | bytes 3244040 | tf_op jit(solution)/shard_map/ppermute | solution.py:79
  44.7 9.2 %collective-permute-start.24 = (bf16[128,4224]{1,0:T(8,128)(2,1)S(1)}, bf16[128,4224]{1,0:T(8,128)(2,1)S(1)}, u32[]{:S(2)}, u32[]{:S(2)}) collective-permute-start(bf16[128,4224]{1,0:T(8,128)(2,1)S(1)} %constant_dynamic-update-slice_fusion.10.own), channel_id=1, source_target_pairs={{0,8},{1,9},{2,10},{3,11},{4,12},{5,13},{6,14},{7,15},{8,0},{9,1},... | collective-permute-start | bytes 3244040 | tf_op jit(solution)/shard_map/ppermute | solution.py:79
  49.0 9.6 %collective-permute-start.5 = (bf16[128,4096]{1,0:T(8,128)(2,1)S(1)}, bf16[128,4096]{1,0:T(8,128)(2,1)S(1)}, u32[]{:S(2)}, u32[]{:S(2)}) collective-permute-start(bf16[128,4096]{1,0:T(8,128)(2,1)S(1)} %get-tuple-element.18), channel_id=1, source_target_pairs={{0,8},{1,9},{2,10},{3,11},{4,12},{5,13},{6,14},{7,15},{8,0},{9,1},... | collective-permute-start | bytes 3145736 | tf_op jit(solution)/shard_map/ppermute | solution.py:79
  53.8 7.0 %collective-permute-start.15 = (bf16[128,4096]{1,0:T(8,128)(2,1)S(1)}, bf16[128,4096]{1,0:T(8,128)(2,1)S(1)}, u32[]{:S(2)}, u32[]{:S(2)}) collective-permute-start(bf16[128,4096]{1,0:T(8,128)(2,1)S(1)} %get-tuple-element.21), channel_id=1, source_target_pairs={{0,8},{1,9},{2,10},{3,11},{4,12},{5,13},{6,14},{7,15},{8,0},{9,1},... | collective-permute-start | bytes 3145736 | tf_op jit(solution)/shard_map/ppermute | solution.py:79
  58.1 3.0 %collective-permute-start.25 = (bf16[128,4096]{1,0:T(8,128)(2,1)S(1)}, bf16[128,4096]{1,0:T(8,128)(2,1)S(1)}, u32[]{:S(2)}, u32[]{:S(2)}) collective-permute-start(bf16[128,4096]{1,0:T(8,128)(2,1)S(1)} %get-tuple-element.24), channel_id=1, source_target_pairs={{0,8},{1,9},{2,10},{3,11},{4,12},{5,13},{6,14},{7,15},{8,0},{9,1},... | collective-permute-start | bytes 3145736 | tf_op jit(solution)/shard_map/ppermute | solution.py:79
  58.7 9.2 %collective-permute-start.6 = (bf16[64,4096]{1,0:T(8,128)(2,1)S(1)}, bf16[64,4096]{1,0:T(8,128)(2,1)S(1)}, u32[]{:S(2)}, u32[]{:S(2)}) collective-permute-start(bf16[64,4096]{1,0:T(8,128)(2,1)S(1)} %add_convert_fusion.2), channel_id=1, source_target_pairs={{0,16},{1,17},{2,18},{3,19},{4,20},{5,21},{6,22},{7,23},{8,9},{9,8... | collective-permute-start | bytes 1572872 | tf_op jit(solution)/shard_map/ppermute | solution.py:79
  60.9 13.7 %collective-permute-start.16 = (bf16[64,4096]{1,0:T(8,128)(2,1)S(1)}, bf16[64,4096]{1,0:T(8,128)(2,1)S(1)}, u32[]{:S(2)}, u32[]{:S(2)}) collective-permute-start(bf16[64,4096]{1,0:T(8,128)(2,1)S(1)} %add_convert_fusion.1), channel_id=1, source_target_pairs={{0,2},{1,3},{2,0},{3,1},{4,6},{5,7},{6,4},{7,5},{8,10},{9,11},{10,... | collective-permute-start | bytes 1572872 | tf_op jit(solution)/shard_map/ppermute | solution.py:79
  61.2 15.2 %collective-permute-start.26 = (bf16[64,4096]{1,0:T(8,128)(2,1)S(1)}, bf16[64,4096]{1,0:T(8,128)(2,1)S(1)}, u32[]{:S(2)}, u32[]{:S(2)}) collective-permute-start(bf16[64,4096]{1,0:T(8,128)(2,1)S(1)} %add_convert_fusion), channel_id=1, source_target_pairs={{0,16},{1,17},{2,18},{3,19},{4,20},{5,21},{6,22},{7,23},{8,9},{9,8... | collective-permute-start | bytes 1572872 | tf_op jit(solution)/shard_map/ppermute | solution.py:79
  68.1 10.5 %collective-permute-start.7 = (bf16[32,4096]{1,0:T(8,128)(2,1)S(1)}, bf16[32,4096]{1,0:T(8,128)(2,1)S(1)}, u32[]{:S(2)}, u32[]{:S(2)}) collective-permute-start(bf16[32,4096]{1,0:T(8,128)(2,1)S(1)} %add_convert_fusion.5), channel_id=1, source_target_pairs={{0,1},{1,0},{2,3},{3,2},{4,5},{5,4},{6,7},{7,6},{8,24},{9,25},{10,... | collective-permute-start | bytes 786440 | tf_op jit(solution)/shard_map/ppermute | solution.py:79
  74.7 8.6 %collective-permute-start.17 = (bf16[32,4096]{1,0:T(8,128)(2,1)S(1)}, bf16[32,4096]{1,0:T(8,128)(2,1)S(1)}, u32[]{:S(2)}, u32[]{:S(2)}) collective-permute-start(bf16[32,4096]{1,0:T(8,128)(2,1)S(1)} %add_convert_fusion.4), channel_id=1, source_target_pairs={{0,16},{1,17},{2,18},{3,19},{4,20},{5,21},{6,22},{7,23},{8,9},{9,8... | collective-permute-start | bytes 786440 | tf_op jit(solution)/shard_map/ppermute | solution.py:79
  76.5 7.9 %collective-permute-start.27 = (bf16[32,4096]{1,0:T(8,128)(2,1)S(1)}, bf16[32,4096]{1,0:T(8,128)(2,1)S(1)}, u32[]{:S(2)}, u32[]{:S(2)}) collective-permute-start(bf16[32,4096]{1,0:T(8,128)(2,1)S(1)} %add_convert_fusion.3), channel_id=1, source_target_pairs={{0,1},{1,0},{2,3},{3,2},{4,5},{5,4},{6,7},{7,6},{8,24},{9,25},{10,... | collective-permute-start | bytes 786440 | tf_op jit(solution)/shard_map/ppermute | solution.py:79
  78.7 6.1 %collective-permute-start.8 = (bf16[16,4096]{1,0:T(8,128)(2,1)S(1)}, bf16[16,4096]{1,0:T(8,128)(2,1)S(1)}, u32[]{:S(2)}, u32[]{:S(2)}) collective-permute-start(bf16[16,4096]{1,0:T(8,128)(2,1)S(1)} %add_convert_fusion.8), channel_id=1, source_target_pairs={{0,2},{1,3},{2,0},{3,1},{4,6},{5,7},{6,4},{7,5},{8,10},{9,11},{10,... | collective-permute-start | bytes 393224 | tf_op jit(solution)/shard_map/ppermute | solution.py:79
  83.3 5.0 %collective-permute-start.18 = (bf16[16,4096]{1,0:T(8,128)(2,1)S(1)}, bf16[16,4096]{1,0:T(8,128)(2,1)S(1)}, u32[]{:S(2)}, u32[]{:S(2)}) collective-permute-start(bf16[16,4096]{1,0:T(8,128)(2,1)S(1)} %add_convert_fusion.7), channel_id=1, source_target_pairs={{0,1},{1,0},{2,3},{3,2},{4,5},{5,4},{6,7},{7,6},{8,24},{9,25},{10,... | collective-permute-start | bytes 393224 | tf_op jit(solution)/shard_map/ppermute | solution.py:79
  84.5 7.1 %collective-permute-start.28 = (bf16[16,4096]{1,0:T(8,128)(2,1)S(1)}, bf16[16,4096]{1,0:T(8,128)(2,1)S(1)}, u32[]{:S(2)}, u32[]{:S(2)}) collective-permute-start(bf16[16,4096]{1,0:T(8,128)(2,1)S(1)} %add_convert_fusion.6), channel_id=1, source_target_pairs={{0,2},{1,3},{2,0},{3,1},{4,6},{5,7},{6,4},{7,5},{8,10},{9,11},{10,... | collective-permute-start | bytes 393224 | tf_op jit(solution)/shard_map/ppermute | solution.py:79
  84.9 7.4 %collective-permute-start.9 = (bf16[8,4096]{1,0:T(8,128)(2,1)S(1)}, bf16[8,4096]{1,0:T(8,128)(2,1)S(1)}, u32[]{:S(2)}, u32[]{:S(2)}) collective-permute-start(bf16[8,4096]{1,0:T(8,128)(2,1)S(1)} %add_convert_fusion.14), channel_id=1, source_target_pairs={{0,4},{1,5},{2,6},{3,7},{4,0},{5,1},{6,2},{7,3},{8,12},{9,13},{10,... | collective-permute-start | bytes 196616 | tf_op jit(solution)/shard_map/ppermute | solution.py:79
  88.4 5.6 %collective-permute-start.19 = (bf16[8,4096]{1,0:T(8,128)(2,1)S(1)}, bf16[8,4096]{1,0:T(8,128)(2,1)S(1)}, u32[]{:S(2)}, u32[]{:S(2)}) collective-permute-start(bf16[8,4096]{1,0:T(8,128)(2,1)S(1)} %add_convert_fusion.12), channel_id=1, source_target_pairs={{0,4},{1,5},{2,6},{3,7},{4,0},{5,1},{6,2},{7,3},{8,12},{9,13},{10,... | collective-permute-start | bytes 196616 | tf_op jit(solution)/shard_map/ppermute | solution.py:79
  91.6 5.3 %collective-permute-start.29 = (bf16[8,4096]{1,0:T(8,128)(2,1)S(1)}, bf16[8,4096]{1,0:T(8,128)(2,1)S(1)}, u32[]{:S(2)}, u32[]{:S(2)}) collective-permute-start(bf16[8,4096]{1,0:T(8,128)(2,1)S(1)} %add_convert_fusion.10), channel_id=1, source_target_pairs={{0,4},{1,5},{2,6},{3,7},{4,0},{5,1},{6,2},{7,3},{8,12},{9,13},{10,... | collective-permute-start | bytes 196616 | tf_op jit(solution)/shard_map/ppermute | solution.py:79

commit v12 on v11

--- a/solution.py
+++ b/solution.py
@@ -9,8 +9,8 @@
 
 AXES = ("dp", "expert")
 LANES = 128
-PARTS = 4
-VMEM_MIB = 8
+COLUMNS = 256
+VMEM_MIB = 10
 ROWS_AT_ONCE = 8
 
 
@@ -95,7 +95,30 @@
     return lambda d, e: (d, e ^ (2 * distance))
 
 
-def pack_kernel(slots, flag, tokens_hbm, ids_hbm, weights_hbm, mine, *outs_and_scratch):
+def expert_kernel(slots, flag, mine):
+    d = lax.axis_index("dp")
+    serving = jnp.where(flag[0] == 1, d ^ 1, d) * lax.axis_size("expert") + lax.axis_index("expert")
+    expert = jnp.int32(0)
+    for half in range(slots.shape[0]):
+        for number in range(slots.shape[1]):
+            expert += jnp.where(slots[half, number] == serving, number, 0)
+    mine[0] = expert
+
+
+def served_expert(slot_of, swap_flag):
+    scalars = pl.BlockSpec(memory_space=pltpu.SMEM)
+    return pl.pallas_call(
+        expert_kernel,
+        out_shape=jax.ShapeDtypeStruct((1,), jnp.int32),
+        in_specs=[scalars] * 2,
+        out_specs=scalars,
+        compiler_params=pltpu.CompilerParams(vmem_limit_bytes=2**20),
+        cost_estimate=pl.CostEstimate(flops=10**10, bytes_accessed=0, transcendentals=0),
+        name="served_expert",
+    )(*in_hbm(slot_of.T), swap_flag)
+
+
+def pack_kernel(tokens_hbm, ids_hbm, weights_hbm, *outs_and_scratch):
     *outs, square, tokens, ids, weights, sems = outs_and_scratch
     loads = [
         pltpu.make_async_copy(source, target, sems.at[k])
@@ -103,13 +126,6 @@
     ]
     for load in loads:
         load.start()
-    d = lax.axis_index("dp")
-    serving = jnp.where(flag[0] == 1, d ^ 1, d) * lax.axis_size("expert") + lax.axis_index("expert")
-    expert = jnp.int32(0)
-    for half in range(slots.shape[0]):
-        for number in range(slots.shape[1]):
-            expert += jnp.where(slots[half, number] == serving, number, 0)
-    mine[0] = expert
     top_count, tok_rows = ids.shape
     square[...] = jnp.zeros_like(square)
     loads[0].wait()
@@ -133,17 +149,16 @@
     return [pltpu.with_memory_space_constraint(array, pltpu.HBM) for array in arrays]
 
 
-def packed(tokens, expert_ids, route_weight, slot_of, swap_flag, rows):
+def packed(tokens, expert_ids, route_weight, rows):
     tok_rows, width = tokens.shape
     side = -(-max(tok_rows, 4 * expert_ids.shape[1]) // LANES) * LANES
-    scalars = pl.BlockSpec(memory_space=pltpu.SMEM)
     whole = pl.BlockSpec(memory_space=pltpu.VMEM)
     count = tok_rows // rows
-    mine, *owns = pl.pallas_call(
+    return pl.pallas_call(
         pack_kernel,
-        out_shape=(jax.ShapeDtypeStruct((1,), jnp.int32),) + (pltpu.VMEM((rows, width + side), tokens.dtype),) * count,
-        in_specs=[scalars] * 2 + [pl.BlockSpec(memory_space=pl.ANY)] * 3,
-        out_specs=(scalars,) + (whole,) * count,
+        out_shape=(pltpu.VMEM((rows, width + side), tokens.dtype),) * count,
+        in_specs=[pl.BlockSpec(memory_space=pl.ANY)] * 3,
+        out_specs=(whole,) * count,
         scratch_shapes=[
             pltpu.VMEM((side, side), jnp.float32),
             pltpu.VMEM(tokens.shape, tokens.dtype),
@@ -152,10 +167,9 @@
             pltpu.SemaphoreType.DMA((3,)),
         ],
         compiler_params=pltpu.CompilerParams(vmem_limit_bytes=VMEM_MIB * 2**20),
-        cost_estimate=pl.CostEstimate(flops=10**10, bytes_accessed=4 * tok_rows * width, transcendentals=0),
+        cost_estimate=pl.CostEstimate(flops=0, bytes_accessed=4 * tok_rows * width, transcendentals=0),
         name="pack_rows",
-    )(*in_hbm(slot_of.T), swap_flag, *in_hbm(tokens, expert_ids.T, route_weight.T))
-    return mine, owns
+    )(*in_hbm(tokens, expert_ids.T, route_weight.T))
 
 
 def scale_of(extra, mine, top_count):
@@ -164,23 +178,21 @@
     return jnp.sum(jnp.where(ids == mine, hi + mid + lo, 0.0), axis=1, keepdims=True)
 
 
-def serve_kernel(top_count, mine, own, sib, w_gate, w_up, w_down, out_own, out_sib):
+def serve_kernel(top_count, mine, own, sib, w_gate, w_up, w_down, out_own, out_sib, x, hidden):
     rows = own.shape[0]
     width, hidden_width = w_gate.shape
-    depth = width // PARTS
-    gate_sum = jnp.zeros((2 * rows, hidden_width), jnp.float32)
-    up_sum = jnp.zeros((2 * rows, hidden_width), jnp.float32)
-    for k in range(PARTS):
-        part = pl.ds(k * depth, depth)
-        x = jnp.concatenate([own[:, part], sib[:, part]])
-        gate_sum += jnp.dot(x, w_gate[part], preferred_element_type=jnp.float32)
-        up_sum += jnp.dot(x, w_up[part], preferred_element_type=jnp.float32)
-    hidden = (gate_sum / (1.0 + jnp.exp(-gate_sum)) * up_sum).astype(jnp.bfloat16)
+    x[:rows] = own[:, :width]
+    x[rows:] = sib[:, :width]
+    for at in range(0, hidden_width, COLUMNS):
+        part = pl.ds(at, COLUMNS)
+        gate_sum = jnp.dot(x[...], w_gate[:, part], preferred_element_type=jnp.float32)
+        up_sum = jnp.dot(x[...], w_up[:, part], preferred_element_type=jnp.float32)
+        hidden[:, part] = (gate_sum / (1.0 + jnp.exp(-gate_sum)) * up_sum).astype(jnp.bfloat16)
     extra = jnp.concatenate([own[:, width:], sib[:, width:]])
     scale = scale_of(extra, mine[0].astype(jnp.float32), top_count)
-    for k in range(PARTS):
-        part = pl.ds(k * depth, depth)
-        served = jnp.dot(hidden, w_down[:, part], preferred_element_type=jnp.float32) * scale
+    for at in range(0, width, COLUMNS):
+        part = pl.ds(at, COLUMNS)
+        served = jnp.dot(hidden[...], w_down[:, part], preferred_element_type=jnp.float32) * scale
         out_own[:, part] = served[:rows].astype(jnp.bfloat16)
         out_sib[:, part] = served[rows:].astype(jnp.bfloat16)
 
@@ -196,6 +208,10 @@
         out_shape=(out, out),
         in_specs=[pl.BlockSpec(memory_space=pltpu.SMEM)] + [whole] * 5,
         out_specs=(whole, whole),
+        scratch_shapes=[
+            pltpu.VMEM((2 * rows, width), jnp.bfloat16),
+            pltpu.VMEM((2 * rows, hidden_width), jnp.bfloat16),
+        ],
         compiler_params=pltpu.CompilerParams(vmem_limit_bytes=VMEM_MIB * 2**20),
         cost_estimate=pl.CostEstimate(
             flops=12 * rows * width * hidden_width, bytes_accessed=moved, transcendentals=2 * rows * hidden_width
@@ -208,11 +224,13 @@
     return sum(term.astype(jnp.float32) for term in terms).astype(jnp.bfloat16)
 
 
-def chunk_steps(own, moves, serve):
+def chunk_steps(own, moves, serve, beside):
     rows = own.shape[0]
     (held,) = yield (own,)
     for move in moves:
         (got,) = yield (permute(held, move),)
+        if move is moves[0] and beside:
+            got = lax.optimization_barrier((got, *beside))[0]
         held = jnp.concatenate([held, got])
     (sib,) = yield (permute(held, to_sibling),)
     out, out_sib = serve(held, sib)
@@ -248,9 +266,10 @@
     across = [over_first, over_second]
     routes = [along + across, along[:1] + across + along[1:]]
     step = ROWS_AT_ONCE if tok_rows % ROWS_AT_ONCE == 0 else tok_rows
-    mine, owns = packed(tokens, expert_ids, route_weight, slot_of, swap_flag, step)
+    owns = packed(tokens, expert_ids, route_weight, step)
+    mine = served_expert(slot_of, lax.optimization_barrier((swap_flag, owns[0]))[0])
     serve = lambda held, sib: serve_rows(held, sib, mine, top_count, w_gate[0], w_up[0], w_down[0])
-    chunks = [chunk_steps(own, routes[i % len(routes)], serve) for i, own in enumerate(owns)]
+    chunks = [chunk_steps(own, routes[i % len(routes)], serve, (mine,) if i == 1 else ()) for i, own in enumerate(owns)]
     return jnp.concatenate(run_steps(chunks))
 
 

time: 97.9 us -> 95.4 us (0.974)
  starting transfers between devices: 38.7 us -> 37.6 us
    ppermute x30, starting transfers between devices: 38.7 us -> 37.6 us  [permute(): return lax.ppermute(value, AXES, pairs)]
    pallas_call x1 -> x2, Pallas kernels: 2.72 us -> 2.38 us  [the longest x1 1.38 us: served_expert(): pl.pallas_call(expert_kernel, out_shape=jax.ShapeDtypeStruct((1,), jnp.in...]
  transfers between devices with their start and end apart: 30 -> 30, of which waited for: 16 -> 14; matrix products, arithmetic and copies ran while one was open for 2% -> 2% of each run, Pallas kernels for 13% -> 14%
where the time goes in v12:
time: 95.4 us; the launch traced here: 95.2 us
  waiting for transfers between devices  39.4 us (41%)
  starting transfers between devices  37.6 us (39%)
  Pallas kernels  14.8 us (16%)
  other arithmetic  2.14 us (2%)
    ppermute x30, waiting for transfers between devices, permute(): return lax.ppermute(value, AXES, pairs)  39.4 us
    ppermute x30, starting transfers between devices, permute(): return lax.ppermute(value, AXES, pairs)  37.6 us
    pallas_call x3, Pallas kernels, serve_rows(): pl.pallas_call(functools.partial(serve_kernel, top_count), out_shape=(out...  12.4 us
  transfers between devices with their start and end apart: 30, of which 14 were waited for; matrix products, arithmetic and copies ran while one was open for 2% of the time, Pallas kernels for 14%

profile of v12, /device:TPU:0, one launch (start us, length us, event | category | flops | bytes accessed | tf_op | source)
XLA Modules:
  0.0 95.2 jit_solution(2697952487428732099)
XLA Ops:
  0.0 1.0 %pack_rows.1 = (bf16[8,4224]{1,0:T(8,128)(2,1)S(1)}, bf16[8,4224]{1,0:T(8,128)(2,1)S(1)}, bf16[8,4224]{1,0:T(8,128)(2,1)S(1)}) custom-call(bf16[24,4096]{1,0:T(8,128)(2,1)} %tokens_hbm.1, s32[8,24]{1,0:T(8,128)} %bitcast.15, f32[8,24]{1,0:T(8,128)} %bitcast.16), custom_call_target="tpu_custom_call" | custom-call | bytes 393216 | tf_op jit(solution)/shard_map/pack_rows/pallas_call | solution.py:157
  1.0 4.1 %collective-permute-start.20 = (bf16[8,4224]{1,0:T(8,128)(2,1)S(1)}, bf16[8,4224]{1,0:T(8,128)(2,1)S(1)}, u32[]{:S(2)}, u32[]{:S(2)}) collective-permute-start(bf16[8,4224]{1,0:T(8,128)(2,1)S(1)} %get-tuple-element.24), channel_id=1, source_target_pairs={{0,4},{1,5},{2,6},{3,7},{4,0},{5,1},{6,2},{7,3},{8,12},{9,13},{10,... | collective-permute-start | bytes 202760 | tf_op jit(solution)/shard_map/ppermute | solution.py:79
  5.1 0.1 collective-permute-start.10
  5.2 2.8 %collective-permute-start = (bf16[8,4224]{1,0:T(8,128)(2,1)S(1)}, bf16[8,4224]{1,0:T(8,128)(2,1)S(1)}, u32[]{:S(2)}, u32[]{:S(2)}) collective-permute-start(bf16[8,4224]{1,0:T(8,128)(2,1)S(1)} %get-tuple-element.16), channel_id=1, source_target_pairs={{0,4},{1,5},{2,6},{3,7},{4,0},{5,1},{6,2},{7,3},{8,12},{9,13},{10,... | collective-permute-start | bytes 202760 | tf_op jit(solution)/shard_map/ppermute | solution.py:79
  8.7 1.4 %served_expert.1.mine = s32[1]{0:T(128)} custom-call(s32[2,16]{1,0:T(2,128)} %bitcast.17, s32[1]{0:T(128)S(6)} %copy.21.flag), custom_call_target="tpu_custom_call" | custom-call | flops 10000000000 | tf_op jit(solution)/shard_map/served_expert/pallas_call | solution.py:110
  10.2 2.3 %collective-permute-start.21 = (bf16[16,4224]{1,0:T(8,128)(2,1)S(1)}, bf16[16,4224]{1,0:T(8,128)(2,1)S(1)}, u32[]{:S(2)}, u32[]{:S(2)}) collective-permute-start(bf16[16,4224]{1,0:T(8,128)(2,1)S(1)} %pad_maximum_fusion.9), channel_id=1, source_target_pairs={{0,2},{1,3},{2,0},{3,1},{4,6},{5,7},{6,4},{7,5},{8,10},{9,11},{10,... | collective-permute-start | bytes 405512 | tf_op jit(solution)/shard_map/ppermute | solution.py:79
  12.5 1.2 %collective-permute-done.10 = bf16[8,4224]{1,0:T(8,128)(2,1)S(1)} collective-permute-done((bf16[8,4224]{1,0:T(8,128)(2,1)S(1)}, bf16[8,4224]{1,0:T(8,128)(2,1)S(1)}, u32[]{:S(2)}, u32[]{:S(2)}) %collective-permute-start.10) | collective-permute-done | bytes 67616 | tf_op jit(solution)/shard_map/ppermute | solution.py:79
  13.7 1.6 %collective-permute-start.11 = (bf16[16,4224]{1,0:T(8,128)(2,1)S(1)}, bf16[16,4224]{1,0:T(8,128)(2,1)S(1)}, u32[]{:S(2)}, u32[]{:S(2)}) collective-permute-start(bf16[16,4224]{1,0:T(8,128)(2,1)S(1)} %pad_maximum_fusion.8), channel_id=1, source_target_pairs={{0,1},{1,0},{2,3},{3,2},{4,5},{5,4},{6,7},{7,6},{8,24},{9,25},{10,... | collective-permute-start | bytes 405512 | tf_op jit(solution)/shard_map/ppermute | solution.py:79
  15.3 0.7 collective-permute-start.1
  16.1 1.5 %collective-permute-done.21 = bf16[16,4224]{1,0:T(8,128)(2,1)S(1)} collective-permute-done((bf16[16,4224]{1,0:T(8,128)(2,1)S(1)}, bf16[16,4224]{1,0:T(8,128)(2,1)S(1)}, u32[]{:S(2)}, u32[]{:S(2)}) %collective-permute-start.21) | collective-permute-done | bytes 135200 | tf_op jit(solution)/shard_map/ppermute | solution.py:79
  17.6 2.1 %collective-permute-start.22 = (bf16[32,4224]{1,0:T(8,128)(2,1)S(1)}, bf16[32,4224]{1,0:T(8,128)(2,1)S(1)}, u32[]{:S(2)}, u32[]{:S(2)}) collective-permute-start(bf16[32,4224]{1,0:T(8,128)(2,1)S(1)} %pad_maximum_fusion.5), channel_id=1, source_target_pairs={{0,1},{1,0},{2,3},{3,2},{4,5},{5,4},{6,7},{7,6},{8,24},{9,25},{10,... | collective-permute-start | bytes 811016 | tf_op jit(solution)/shard_map/ppermute | solution.py:79
  19.7 1.6 %collective-permute-start.12 = (bf16[32,4224]{1,0:T(8,128)(2,1)S(1)}, bf16[32,4224]{1,0:T(8,128)(2,1)S(1)}, u32[]{:S(2)}, u32[]{:S(2)}) collective-permute-start(bf16[32,4224]{1,0:T(8,128)(2,1)S(1)} %pad_maximum_fusion.4), channel_id=1, source_target_pairs={{0,16},{1,17},{2,18},{3,19},{4,20},{5,21},{6,22},{7,23},{8,9},{9,8... | collective-permute-start | bytes 811016 | tf_op jit(solution)/shard_map/ppermute | solution.py:79
  21.3 0.9 collective-permute-start.2
  22.3 4.7 %collective-permute-done.22 = bf16[32,4224]{1,0:T(8,128)(2,1)S(1)} collective-permute-done((bf16[32,4224]{1,0:T(8,128)(2,1)S(1)}, bf16[32,4224]{1,0:T(8,128)(2,1)S(1)}, u32[]{:S(2)}, u32[]{:S(2)}) %collective-permute-start.22) | collective-permute-done | bytes 270368 | tf_op jit(solution)/shard_map/ppermute | solution.py:79
  27.0 2.1 %collective-permute-start.23 = (bf16[64,4224]{1,0:T(8,128)(2,1)S(1)}, bf16[64,4224]{1,0:T(8,128)(2,1)S(1)}, u32[]{:S(2)}, u32[]{:S(2)}) collective-permute-start(bf16[64,4224]{1,0:T(8,128)(2,1)S(1)} %pad_maximum_fusion.2), channel_id=1, source_target_pairs={{0,16},{1,17},{2,18},{3,19},{4,20},{5,21},{6,22},{7,23},{8,9},{9,8... | collective-permute-start | bytes 1622024 | tf_op jit(solution)/shard_map/ppermute | solution.py:79
  29.2 0.1 collective-permute-start.13
  29.3 3.5 %collective-permute-done.2 = bf16[32,4224]{1,0:T(8,128)(2,1)S(1)} collective-permute-done((bf16[32,4224]{1,0:T(8,128)(2,1)S(1)}, bf16[32,4224]{1,0:T(8,128)(2,1)S(1)}, u32[]{:S(2)}, u32[]{:S(2)}) %collective-permute-start.2) | collective-permute-done | bytes 270368 | tf_op jit(solution)/shard_map/ppermute | solution.py:79
  32.7 0.1 pad_maximum_fusion
  32.8 2.1 %collective-permute-start.3 = (bf16[64,4224]{1,0:T(8,128)(2,1)S(1)}, bf16[64,4224]{1,0:T(8,128)(2,1)S(1)}, u32[]{:S(2)}, u32[]{:S(2)}) collective-permute-start(bf16[64,4224]{1,0:T(8,128)(2,1)S(1)} %pad_maximum_fusion), channel_id=1, source_target_pairs={{0,16},{1,17},{2,18},{3,19},{4,20},{5,21},{6,22},{7,23},{8,9},{9,8... | collective-permute-start | bytes 1622024 | tf_op jit(solution)/shard_map/ppermute | solution.py:79
  35.0 1.4 %collective-permute-done.23 = bf16[64,4224]{1,0:T(8,128)(2,1)S(1)} collective-permute-done((bf16[64,4224]{1,0:T(8,128)(2,1)S(1)}, bf16[64,4224]{1,0:T(8,128)(2,1)S(1)}, u32[]{:S(2)}, u32[]{:S(2)}) %collective-permute-start.23) | collective-permute-done | bytes 540704 | tf_op jit(solution)/shard_map/ppermute | solution.py:79
  36.5 0.1 collective-permute-start.24
  36.6 3.9 %collective-permute-done.13 = bf16[64,4224]{1,0:T(8,128)(2,1)S(1)} collective-permute-done((bf16[64,4224]{1,0:T(8,128)(2,1)S(1)}, bf16[64,4224]{1,0:T(8,128)(2,1)S(1)}, u32[]{:S(2)}, u32[]{:S(2)}) %collective-permute-start.13) | collective-permute-done | bytes 540704 | tf_op jit(solution)/shard_map/ppermute | solution.py:79
  40.5 0.1 collective-permute-start.14
  40.6 1.7 %collective-permute-done.3 = bf16[64,4224]{1,0:T(8,128)(2,1)S(1)} collective-permute-done((bf16[64,4224]{1,0:T(8,128)(2,1)S(1)}, bf16[64,4224]{1,0:T(8,128)(2,1)S(1)}, u32[]{:S(2)}, u32[]{:S(2)}) %collective-permute-start.3) | collective-permute-done | bytes 540704 | tf_op jit(solution)/shard_map/ppermute | solution.py:79
  42.3 0.1 collective-permute-start.4
  42.4 4.1 %serve_rows.5 = (bf16[128,4096]{1,0:T(8,128)(2,1)S(1)}, bf16[128,4096]{1,0:T(8,128)(2,1)S(1)}) custom-call(s32[1]{0:T(128)} %served_expert.1.mine, bf16[128,4224]{1,0:T(8,128)(2,1)S(1)} %constant_dynamic-update-slice_fusion.10.own, bf16[128,4224]{1,0:T(8,128)(2,1)S(1)} %collective-permute-done.24.sib, bf16[4096,512]{1,0:T(8,128)(2,1)S(1)} %bitcast.6, ...), custom_call_target="tpu_custom_call" | custom-call | flops 3221225472 | bytes 16777216 | tf_op jit(solution)/shard_map/serve_rows/pallas_call | solution.py:206
  46.6 0.5 collective-permute-start.25
  47.1 4.1 %serve_rows.4 = (bf16[128,4096]{1,0:T(8,128)(2,1)S(1)}, bf16[128,4096]{1,0:T(8,128)(2,1)S(1)}) custom-call(s32[1]{0:T(128)} %served_expert.1.mine, bf16[128,4224]{1,0:T(8,128)(2,1)S(1)} %constant_dynamic-update-slice_fusion.5.own, bf16[128,4224]{1,0:T(8,128)(2,1)S(1)} %collective-permute-done.14.sib, bf16[4096,512]{1,0:T(8,128)(2,1)S(1)} %bitcast.7, ...), custom_call_target="tpu_custom_call" | custom-call | flops 3221225472 | bytes 16777216 | tf_op jit(solution)/shard_map/serve_rows/pallas_call | solution.py:206
  51.3 0.1 collective-permute-start.15
  51.4 4.1 %serve_rows.3 = (bf16[128,4096]{1,0:T(8,128)(2,1)S(1)}, bf16[128,4096]{1,0:T(8,128)(2,1)S(1)}) custom-call(s32[1]{0:T(128)} %served_expert.1.mine, bf16[128,4224]{1,0:T(8,128)(2,1)S(1)} %constant_dynamic-update-slice_fusion.own, bf16[128,4224]{1,0:T(8,128)(2,1)S(1)} %collective-permute-done.4.sib, bf16[4096,512]{1,0:T(8,128)(2,1)S(1)} %bitcast.8, ...), custom_call_target="tpu_custom_call" | custom-call | flops 3221225472 | bytes 16777216 | tf_op jit(solution)/shard_map/serve_rows/pallas_call | solution.py:206
  55.5 0.5 collective-permute-start.5
  56.0 0.1 add_convert_fusion
  56.2 2.1 %collective-permute-start.26 = (bf16[64,4096]{1,0:T(8,128)(2,1)S(1)}, bf16[64,4096]{1,0:T(8,128)(2,1)S(1)}, u32[]{:S(2)}, u32[]{:S(2)}) collective-permute-start(bf16[64,4096]{1,0:T(8,128)(2,1)S(1)} %add_convert_fusion), channel_id=1, source_target_pairs={{0,16},{1,17},{2,18},{3,19},{4,20},{5,21},{6,22},{7,23},{8,9},{9,8... | collective-permute-start | bytes 1572872 | tf_op jit(solution)/shard_map/ppermute | solution.py:79
  58.3 0.1 add_convert_fusion.1
  58.4 0.1 collective-permute-start.16
  58.5 0.1 add_convert_fusion.2
  58.6 1.9 %collective-permute-start.6 = (bf16[64,4096]{1,0:T(8,128)(2,1)S(1)}, bf16[64,4096]{1,0:T(8,128)(2,1)S(1)}, u32[]{:S(2)}, u32[]{:S(2)}) collective-permute-start(bf16[64,4096]{1,0:T(8,128)(2,1)S(1)} %add_convert_fusion.2), channel_id=1, source_target_pairs={{0,16},{1,17},{2,18},{3,19},{4,20},{5,21},{6,22},{7,23},{8,9},{9,8... | collective-permute-start | bytes 1572872 | tf_op jit(solution)/shard_map/ppermute | solution.py:79
  60.5 4.9 %collective-permute-done.26 = bf16[64,4096]{1,0:T(8,128)(2,1)S(1)} collective-permute-done((bf16[64,4096]{1,0:T(8,128)(2,1)S(1)}, bf16[64,4096]{1,0:T(8,128)(2,1)S(1)}, u32[]{:S(2)}, u32[]{:S(2)}) %collective-permute-start.26) | collective-permute-done | bytes 524320 | tf_op jit(solution)/shard_map/ppermute | solution.py:79
  65.4 0.1 add_convert_fusion.3
  65.5 2.1 %collective-permute-start.27 = (bf16[32,4096]{1,0:T(8,128)(2,1)S(1)}, bf16[32,4096]{1,0:T(8,128)(2,1)S(1)}, u32[]{:S(2)}, u32[]{:S(2)}) collective-permute-start(bf16[32,4096]{1,0:T(8,128)(2,1)S(1)} %add_convert_fusion.3), channel_id=1, source_target_pairs={{0,1},{1,0},{2,3},{3,2},{4,5},{5,4},{6,7},{7,6},{8,24},{9,25},{10,... | collective-permute-start | bytes 786440 | tf_op jit(solution)/shard_map/ppermute | solution.py:79
  67.6 4.4 %collective-permute-done.16 = bf16[64,4096]{1,0:T(8,128)(2,1)S(1)} collective-permute-done((bf16[64,4096]{1,0:T(8,128)(2,1)S(1)}, bf16[64,4096]{1,0:T(8,128)(2,1)S(1)}, u32[]{:S(2)}, u32[]{:S(2)}) %collective-permute-start.16) | collective-permute-done | bytes 524320 | tf_op jit(solution)/shard_map/ppermute | solution.py:79
  72.0 0.1 add_convert_fusion.4
  72.1 0.7 collective-permute-start.17
  72.9 1.0 %collective-permute-done.6 = bf16[64,4096]{1,0:T(8,128)(2,1)S(1)} collective-permute-done((bf16[64,4096]{1,0:T(8,128)(2,1)S(1)}, bf16[64,4096]{1,0:T(8,128)(2,1)S(1)}, u32[]{:S(2)}, u32[]{:S(2)}) %collective-permute-start.6) | collective-permute-done | bytes 524320 | tf_op jit(solution)/shard_map/ppermute | solution.py:79
  73.8 0.1 add_convert_fusion.5
  74.0 2.1 %collective-permute-start.7 = (bf16[32,4096]{1,0:T(8,128)(2,1)S(1)}, bf16[32,4096]{1,0:T(8,128)(2,1)S(1)}, u32[]{:S(2)}, u32[]{:S(2)}) collective-permute-start(bf16[32,4096]{1,0:T(8,128)(2,1)S(1)} %add_convert_fusion.5), channel_id=1, source_target_pairs={{0,1},{1,0},{2,3},{3,2},{4,5},{5,4},{6,7},{7,6},{8,24},{9,25},{10,... | collective-permute-start | bytes 786440 | tf_op jit(solution)/shard_map/ppermute | solution.py:79
  76.1 0.1 add_convert_fusion.6
  76.1 0.1 collective-permute-start.28
  76.2 4.5 %collective-permute-done.17 = bf16[32,4096]{1,0:T(8,128)(2,1)S(1)} collective-permute-done((bf16[32,4096]{1,0:T(8,128)(2,1)S(1)}, bf16[32,4096]{1,0:T(8,128)(2,1)S(1)}, u32[]{:S(2)}, u32[]{:S(2)}) %collective-permute-start.17) | collective-permute-done | bytes 262176 | tf_op jit(solution)/shard_map/ppermute | solution.py:79
  80.7 0.1 add_convert_fusion.7
  80.8 1.1 %collective-permute-start.18 = (bf16[16,4096]{1,0:T(8,128)(2,1)S(1)}, bf16[16,4096]{1,0:T(8,128)(2,1)S(1)}, u32[]{:S(2)}, u32[]{:S(2)}) collective-permute-start(bf16[16,4096]{1,0:T(8,128)(2,1)S(1)} %add_convert_fusion.7), channel_id=1, source_target_pairs={{0,1},{1,0},{2,3},{3,2},{4,5},{5,4},{6,7},{7,6},{8,24},{9,25},{10,... | collective-permute-start | bytes 393224 | tf_op jit(solution)/shard_map/ppermute | solution.py:79
  81.8 0.1 add_convert_fusion.8
  81.9 0.4 collective-permute-start.8
  82.3 3.5 %collective-permute-start.29 = (bf16[8,4096]{1,0:T(8,128)(2,1)S(1)}, bf16[8,4096]{1,0:T(8,128)(2,1)S(1)}, u32[]{:S(2)}, u32[]{:S(2)}) collective-permute-start(bf16[8,4096]{1,0:T(8,128)(2,1)S(1)} %add_convert_fusion.10), channel_id=1, source_target_pairs={{0,4},{1,5},{2,6},{3,7},{4,0},{5,1},{6,2},{7,3},{8,12},{9,13},{10,... | collective-permute-start | bytes 196616 | tf_op jit(solution)/shard_map/ppermute | solution.py:79
  85.8 0.0 collective-permute-done.18
  85.9 1.1 %collective-permute-start.19 = (bf16[8,4096]{1,0:T(8,128)(2,1)S(1)}, bf16[8,4096]{1,0:T(8,128)(2,1)S(1)}, u32[]{:S(2)}, u32[]{:S(2)}) collective-permute-start(bf16[8,4096]{1,0:T(8,128)(2,1)S(1)} %add_convert_fusion.12), channel_id=1, source_target_pairs={{0,4},{1,5},{2,6},{3,7},{4,0},{5,1},{6,2},{7,3},{8,12},{9,13},{10,... | collective-permute-start | bytes 196616 | tf_op jit(solution)/shard_map/ppermute | solution.py:79
  87.0 2.1 %collective-permute-done.8 = bf16[16,4096]{1,0:T(8,128)(2,1)S(1)} collective-permute-done((bf16[16,4096]{1,0:T(8,128)(2,1)S(1)}, bf16[16,4096]{1,0:T(8,128)(2,1)S(1)}, u32[]{:S(2)}, u32[]{:S(2)}) %collective-permute-start.8) | collective-permute-done | bytes 131104 | tf_op jit(solution)/shard_map/ppermute | solution.py:79
  89.1 0.6 collective-permute-start.9
  89.7 0.1 add_convert_fusion.9
  89.8 1.7 %collective-permute-done.19 = bf16[8,4096]{1,0:T(8,128)(2,1)S(1)} collective-permute-done((bf16[8,4096]{1,0:T(8,128)(2,1)S(1)}, bf16[8,4096]{1,0:T(8,128)(2,1)S(1)}, u32[]{:S(2)}, u32[]{:S(2)}) %collective-permute-start.19) | collective-permute-done | bytes 65568 | tf_op jit(solution)/shard_map/ppermute | solution.py:79
  91.5 0.1 add_convert_fusion.11
  91.6 2.9 %collective-permute-done.9 = bf16[8,4096]{1,0:T(8,128)(2,1)S(1)} collective-permute-done((bf16[8,4096]{1,0:T(8,128)(2,1)S(1)}, bf16[8,4096]{1,0:T(8,128)(2,1)S(1)}, u32[]{:S(2)}, u32[]{:S(2)}) %collective-permute-start.9) | collective-permute-done | bytes 65568 | tf_op jit(solution)/shard_map/ppermute | solution.py:79
  94.4 0.1 add_convert_fusion.13
  94.5 0.7 pad_maximum_fusion.6
  (46 shorter events, 0.7 us)
Async XLA Ops:
  1.0 9.1 %collective-permute-start.20 = (bf16[8,4224]{1,0:T(8,128)(2,1)S(1)}, bf16[8,4224]{1,0:T(8,128)(2,1)S(1)}, u32[]{:S(2)}, u32[]{:S(2)}) collective-permute-start(bf16[8,4224]{1,0:T(8,128)(2,1)S(1)} %get-tuple-element.24), channel_id=1, source_target_pairs={{0,4},{1,5},{2,6},{3,7},{4,0},{5,1},{6,2},{7,3},{8,12},{9,13},{10,... | collective-permute-start | bytes 202760 | tf_op jit(solution)/shard_map/ppermute | solution.py:79
  5.1 8.6 %collective-permute-start.10 = (bf16[8,4224]{1,0:T(8,128)(2,1)S(1)}, bf16[8,4224]{1,0:T(8,128)(2,1)S(1)}, u32[]{:S(2)}, u32[]{:S(2)}) collective-permute-start(bf16[8,4224]{1,0:T(8,128)(2,1)S(1)} %get-tuple-element.20), channel_id=1, source_target_pairs={{0,4},{1,5},{2,6},{3,7},{4,0},{5,1},{6,2},{7,3},{8,12},{9,13},{10,... | collective-permute-start | bytes 202760 | tf_op jit(solution)/shard_map/ppermute | solution.py:79
  5.2 10.1 %collective-permute-start = (bf16[8,4224]{1,0:T(8,128)(2,1)S(1)}, bf16[8,4224]{1,0:T(8,128)(2,1)S(1)}, u32[]{:S(2)}, u32[]{:S(2)}) collective-permute-start(bf16[8,4224]{1,0:T(8,128)(2,1)S(1)} %get-tuple-element.16), channel_id=1, source_target_pairs={{0,4},{1,5},{2,6},{3,7},{4,0},{5,1},{6,2},{7,3},{8,12},{9,13},{10,... | collective-permute-start | bytes 202760 | tf_op jit(solution)/shard_map/ppermute | solution.py:79
  8.7 33.7 %copy-start.2 = (bf16[1,512,4096]{2,1,0:T(8,128)(2,1)S(1)}, bf16[1,512,4096]{2,1,0:T(8,128)(2,1)}, u32[]{:S(2)}) copy-start(bf16[1,512,4096]{2,1,0:T(8,128)(2,1)} %param.15) | copy-start | bytes 12582916
  10.2 7.4 %collective-permute-start.21 = (bf16[16,4224]{1,0:T(8,128)(2,1)S(1)}, bf16[16,4224]{1,0:T(8,128)(2,1)S(1)}, u32[]{:S(2)}, u32[]{:S(2)}) collective-permute-start(bf16[16,4224]{1,0:T(8,128)(2,1)S(1)} %pad_maximum_fusion.9), channel_id=1, source_target_pairs={{0,2},{1,3},{2,0},{3,1},{4,6},{5,7},{6,4},{7,5},{8,10},{9,11},{10,... | collective-permute-start | bytes 405512 | tf_op jit(solution)/shard_map/ppermute | solution.py:79
  13.7 5.9 %collective-permute-start.11 = (bf16[16,4224]{1,0:T(8,128)(2,1)S(1)}, bf16[16,4224]{1,0:T(8,128)(2,1)S(1)}, u32[]{:S(2)}, u32[]{:S(2)}) collective-permute-start(bf16[16,4224]{1,0:T(8,128)(2,1)S(1)} %pad_maximum_fusion.8), channel_id=1, source_target_pairs={{0,1},{1,0},{2,3},{3,2},{4,5},{5,4},{6,7},{7,6},{8,24},{9,25},{10,... | collective-permute-start | bytes 405512 | tf_op jit(solution)/shard_map/ppermute | solution.py:79
  15.3 5.9 %collective-permute-start.1 = (bf16[16,4224]{1,0:T(8,128)(2,1)S(1)}, bf16[16,4224]{1,0:T(8,128)(2,1)S(1)}, u32[]{:S(2)}, u32[]{:S(2)}) collective-permute-start(bf16[16,4224]{1,0:T(8,128)(2,1)S(1)} %pad_maximum_fusion.7), channel_id=1, source_target_pairs={{0,2},{1,3},{2,0},{3,1},{4,6},{5,7},{6,4},{7,5},{8,10},{9,11},{10,... | collective-permute-start | bytes 405512 | tf_op jit(solution)/shard_map/ppermute | solution.py:79
  17.6 9.3 %collective-permute-start.22 = (bf16[32,4224]{1,0:T(8,128)(2,1)S(1)}, bf16[32,4224]{1,0:T(8,128)(2,1)S(1)}, u32[]{:S(2)}, u32[]{:S(2)}) collective-permute-start(bf16[32,4224]{1,0:T(8,128)(2,1)S(1)} %pad_maximum_fusion.5), channel_id=1, source_target_pairs={{0,1},{1,0},{2,3},{3,2},{4,5},{5,4},{6,7},{7,6},{8,24},{9,25},{10,... | collective-permute-start | bytes 811016 | tf_op jit(solution)/shard_map/ppermute | solution.py:79
  19.7 9.4 %collective-permute-start.12 = (bf16[32,4224]{1,0:T(8,128)(2,1)S(1)}, bf16[32,4224]{1,0:T(8,128)(2,1)S(1)}, u32[]{:S(2)}, u32[]{:S(2)}) collective-permute-start(bf16[32,4224]{1,0:T(8,128)(2,1)S(1)} %pad_maximum_fusion.4), channel_id=1, source_target_pairs={{0,16},{1,17},{2,18},{3,19},{4,20},{5,21},{6,22},{7,23},{8,9},{9,8... | collective-permute-start | bytes 811016 | tf_op jit(solution)/shard_map/ppermute | solution.py:79
  21.3 11.5 %collective-permute-start.2 = (bf16[32,4224]{1,0:T(8,128)(2,1)S(1)}, bf16[32,4224]{1,0:T(8,128)(2,1)S(1)}, u32[]{:S(2)}, u32[]{:S(2)}) collective-permute-start(bf16[32,4224]{1,0:T(8,128)(2,1)S(1)} %pad_maximum_fusion.3), channel_id=1, source_target_pairs={{0,1},{1,0},{2,3},{3,2},{4,5},{5,4},{6,7},{7,6},{8,24},{9,25},{10,... | collective-permute-start | bytes 811016 | tf_op jit(solution)/shard_map/ppermute | solution.py:79
  22.2 20.2 %copy-start.1 = (bf16[1,4096,512]{2,1,0:T(8,128)(2,1)S(1)}, bf16[1,4096,512]{2,1,0:T(8,128)(2,1)}, u32[]{:S(2)}) copy-start(bf16[1,4096,512]{2,1,0:T(8,128)(2,1)} %param.14) | copy-start | bytes 12582916
  27.0 9.5 %collective-permute-start.23 = (bf16[64,4224]{1,0:T(8,128)(2,1)S(1)}, bf16[64,4224]{1,0:T(8,128)(2,1)S(1)}, u32[]{:S(2)}, u32[]{:S(2)}) collective-permute-start(bf16[64,4224]{1,0:T(8,128)(2,1)S(1)} %pad_maximum_fusion.2), channel_id=1, source_target_pairs={{0,16},{1,17},{2,18},{3,19},{4,20},{5,21},{6,22},{7,23},{8,9},{9,8... | collective-permute-start | bytes 1622024 | tf_op jit(solution)/shard_map/ppermute | solution.py:79
  29.2 11.3 %collective-permute-start.13 = (bf16[64,4224]{1,0:T(8,128)(2,1)S(1)}, bf16[64,4224]{1,0:T(8,128)(2,1)S(1)}, u32[]{:S(2)}, u32[]{:S(2)}) collective-permute-start(bf16[64,4224]{1,0:T(8,128)(2,1)S(1)} %pad_maximum_fusion.1), channel_id=1, source_target_pairs={{0,2},{1,3},{2,0},{3,1},{4,6},{5,7},{6,4},{7,5},{8,10},{9,11},{10,... | collective-permute-start | bytes 1622024 | tf_op jit(solution)/shard_map/ppermute | solution.py:79
  32.8 9.5 %collective-permute-start.3 = (bf16[64,4224]{1,0:T(8,128)(2,1)S(1)}, bf16[64,4224]{1,0:T(8,128)(2,1)S(1)}, u32[]{:S(2)}, u32[]{:S(2)}) collective-permute-start(bf16[64,4224]{1,0:T(8,128)(2,1)S(1)} %pad_maximum_fusion), channel_id=1, source_target_pairs={{0,16},{1,17},{2,18},{3,19},{4,20},{5,21},{6,22},{7,23},{8,9},{9,8... | collective-permute-start | bytes 1622024 | tf_op jit(solution)/shard_map/ppermute | solution.py:79
  35.0 7.5 %copy-start = (bf16[1,4096,512]{2,1,0:T(8,128)(2,1)S(1)}, bf16[1,4096,512]{2,1,0:T(8,128)(2,1)}, u32[]{:S(2)}) copy-start(bf16[1,4096,512]{2,1,0:T(8,128)(2,1)} %param.13) | copy-start | bytes 12582916
  36.5 5.9 %collective-permute-start.24 = (bf16[128,4224]{1,0:T(8,128)(2,1)S(1)}, bf16[128,4224]{1,0:T(8,128)(2,1)S(1)}, u32[]{:S(2)}, u32[]{:S(2)}) collective-permute-start(bf16[128,4224]{1,0:T(8,128)(2,1)S(1)} %constant_dynamic-update-slice_fusion.10.own), channel_id=1, source_target_pairs={{0,8},{1,9},{2,10},{3,11},{4,12},{5,13},{6,14},{7,15},{8,0},{9,1},... | collective-permute-start | bytes 3244040 | tf_op jit(solution)/shard_map/ppermute | solution.py:79
  40.5 6.6 %collective-permute-start.14 = (bf16[128,4224]{1,0:T(8,128)(2,1)S(1)}, bf16[128,4224]{1,0:T(8,128)(2,1)S(1)}, u32[]{:S(2)}, u32[]{:S(2)}) collective-permute-start(bf16[128,4224]{1,0:T(8,128)(2,1)S(1)} %constant_dynamic-update-slice_fusion.5.own), channel_id=1, source_target_pairs={{0,8},{1,9},{2,10},{3,11},{4,12},{5,13},{6,14},{7,15},{8,0},{9,1},... | collective-permute-start | bytes 3244040 | tf_op jit(solution)/shard_map/ppermute | solution.py:79
  42.3 9.0 %collective-permute-start.4 = (bf16[128,4224]{1,0:T(8,128)(2,1)S(1)}, bf16[128,4224]{1,0:T(8,128)(2,1)S(1)}, u32[]{:S(2)}, u32[]{:S(2)}) collective-permute-start(bf16[128,4224]{1,0:T(8,128)(2,1)S(1)} %constant_dynamic-update-slice_fusion.own), channel_id=1, source_target_pairs={{0,8},{1,9},{2,10},{3,11},{4,12},{5,13},{6,14},{7,15},{8,0},{9,1},... | collective-permute-start | bytes 3244040 | tf_op jit(solution)/shard_map/ppermute | solution.py:79
  46.6 9.5 %collective-permute-start.25 = (bf16[128,4096]{1,0:T(8,128)(2,1)S(1)}, bf16[128,4096]{1,0:T(8,128)(2,1)S(1)}, u32[]{:S(2)}, u32[]{:S(2)}) collective-permute-start(bf16[128,4096]{1,0:T(8,128)(2,1)S(1)} %get-tuple-element.26), channel_id=1, source_target_pairs={{0,8},{1,9},{2,10},{3,11},{4,12},{5,13},{6,14},{7,15},{8,0},{9,1},... | collective-permute-start | bytes 3145736 | tf_op jit(solution)/shard_map/ppermute | solution.py:79
  51.3 7.0 %collective-permute-start.15 = (bf16[128,4096]{1,0:T(8,128)(2,1)S(1)}, bf16[128,4096]{1,0:T(8,128)(2,1)S(1)}, u32[]{:S(2)}, u32[]{:S(2)}) collective-permute-start(bf16[128,4096]{1,0:T(8,128)(2,1)S(1)} %get-tuple-element.23), channel_id=1, source_target_pairs={{0,8},{1,9},{2,10},{3,11},{4,12},{5,13},{6,14},{7,15},{8,0},{9,1},... | collective-permute-start | bytes 3145736 | tf_op jit(solution)/shard_map/ppermute | solution.py:79
  55.5 3.0 %collective-permute-start.5 = (bf16[128,4096]{1,0:T(8,128)(2,1)S(1)}, bf16[128,4096]{1,0:T(8,128)(2,1)S(1)}, u32[]{:S(2)}, u32[]{:S(2)}) collective-permute-start(bf16[128,4096]{1,0:T(8,128)(2,1)S(1)} %get-tuple-element.19), channel_id=1, source_target_pairs={{0,8},{1,9},{2,10},{3,11},{4,12},{5,13},{6,14},{7,15},{8,0},{9,1},... | collective-permute-start | bytes 3145736 | tf_op jit(solution)/shard_map/ppermute | solution.py:79
  56.2 9.2 %collective-permute-start.26 = (bf16[64,4096]{1,0:T(8,128)(2,1)S(1)}, bf16[64,4096]{1,0:T(8,128)(2,1)S(1)}, u32[]{:S(2)}, u32[]{:S(2)}) collective-permute-start(bf16[64,4096]{1,0:T(8,128)(2,1)S(1)} %add_convert_fusion), channel_id=1, source_target_pairs={{0,16},{1,17},{2,18},{3,19},{4,20},{5,21},{6,22},{7,23},{8,9},{9,8... | collective-permute-start | bytes 1572872 | tf_op jit(solution)/shard_map/ppermute | solution.py:79
  58.4 13.7 %collective-permute-start.16 = (bf16[64,4096]{1,0:T(8,128)(2,1)S(1)}, bf16[64,4096]{1,0:T(8,128)(2,1)S(1)}, u32[]{:S(2)}, u32[]{:S(2)}) collective-permute-start(bf16[64,4096]{1,0:T(8,128)(2,1)S(1)} %add_convert_fusion.1), channel_id=1, source_target_pairs={{0,2},{1,3},{2,0},{3,1},{4,6},{5,7},{6,4},{7,5},{8,10},{9,11},{10,... | collective-permute-start | bytes 1572872 | tf_op jit(solution)/shard_map/ppermute | solution.py:79
  58.6 15.2 %collective-permute-start.6 = (bf16[64,4096]{1,0:T(8,128)(2,1)S(1)}, bf16[64,4096]{1,0:T(8,128)(2,1)S(1)}, u32[]{:S(2)}, u32[]{:S(2)}) collective-permute-start(bf16[64,4096]{1,0:T(8,128)(2,1)S(1)} %add_convert_fusion.2), channel_id=1, source_target_pairs={{0,16},{1,17},{2,18},{3,19},{4,20},{5,21},{6,22},{7,23},{8,9},{9,8... | collective-permute-start | bytes 1572872 | tf_op jit(solution)/shard_map/ppermute | solution.py:79
  65.5 10.5 %collective-permute-start.27 = (bf16[32,4096]{1,0:T(8,128)(2,1)S(1)}, bf16[32,4096]{1,0:T(8,128)(2,1)S(1)}, u32[]{:S(2)}, u32[]{:S(2)}) collective-permute-start(bf16[32,4096]{1,0:T(8,128)(2,1)S(1)} %add_convert_fusion.3), channel_id=1, source_target_pairs={{0,1},{1,0},{2,3},{3,2},{4,5},{5,4},{6,7},{7,6},{8,24},{9,25},{10,... | collective-permute-start | bytes 786440 | tf_op jit(solution)/shard_map/ppermute | solution.py:79
  72.1 8.6 %collective-permute-start.17 = (bf16[32,4096]{1,0:T(8,128)(2,1)S(1)}, bf16[32,4096]{1,0:T(8,128)(2,1)S(1)}, u32[]{:S(2)}, u32[]{:S(2)}) collective-permute-start(bf16[32,4096]{1,0:T(8,128)(2,1)S(1)} %add_convert_fusion.4), channel_id=1, source_target_pairs={{0,16},{1,17},{2,18},{3,19},{4,20},{5,21},{6,22},{7,23},{8,9},{9,8... | collective-permute-start | bytes 786440 | tf_op jit(solution)/shard_map/ppermute | solution.py:79
  74.0 7.9 %collective-permute-start.7 = (bf16[32,4096]{1,0:T(8,128)(2,1)S(1)}, bf16[32,4096]{1,0:T(8,128)(2,1)S(1)}, u32[]{:S(2)}, u32[]{:S(2)}) collective-permute-start(bf16[32,4096]{1,0:T(8,128)(2,1)S(1)} %add_convert_fusion.5), channel_id=1, source_target_pairs={{0,1},{1,0},{2,3},{3,2},{4,5},{5,4},{6,7},{7,6},{8,24},{9,25},{10,... | collective-permute-start | bytes 786440 | tf_op jit(solution)/shard_map/ppermute | solution.py:79
  76.1 6.1 %collective-permute-start.28 = (bf16[16,4096]{1,0:T(8,128)(2,1)S(1)}, bf16[16,4096]{1,0:T(8,128)(2,1)S(1)}, u32[]{:S(2)}, u32[]{:S(2)}) collective-permute-start(bf16[16,4096]{1,0:T(8,128)(2,1)S(1)} %add_convert_fusion.6), channel_id=1, source_target_pairs={{0,2},{1,3},{2,0},{3,1},{4,6},{5,7},{6,4},{7,5},{8,10},{9,11},{10,... | collective-permute-start | bytes 393224 | tf_op jit(solution)/shard_map/ppermute | solution.py:79
  80.8 5.0 %collective-permute-start.18 = (bf16[16,4096]{1,0:T(8,128)(2,1)S(1)}, bf16[16,4096]{1,0:T(8,128)(2,1)S(1)}, u32[]{:S(2)}, u32[]{:S(2)}) collective-permute-start(bf16[16,4096]{1,0:T(8,128)(2,1)S(1)} %add_convert_fusion.7), channel_id=1, source_target_pairs={{0,1},{1,0},{2,3},{3,2},{4,5},{5,4},{6,7},{7,6},{8,24},{9,25},{10,... | collective-permute-start | bytes 393224 | tf_op jit(solution)/shard_map/ppermute | solution.py:79
  81.9 7.1 %collective-permute-start.8 = (bf16[16,4096]{1,0:T(8,128)(2,1)S(1)}, bf16[16,4096]{1,0:T(8,128)(2,1)S(1)}, u32[]{:S(2)}, u32[]{:S(2)}) collective-permute-start(bf16[16,4096]{1,0:T(8,128)(2,1)S(1)} %add_convert_fusion.8), channel_id=1, source_target_pairs={{0,2},{1,3},{2,0},{3,1},{4,6},{5,7},{6,4},{7,5},{8,10},{9,11},{10,... | collective-permute-start | bytes 393224 | tf_op jit(solution)/shard_map/ppermute | solution.py:79
  82.3 7.4 %collective-permute-start.29 = (bf16[8,4096]{1,0:T(8,128)(2,1)S(1)}, bf16[8,4096]{1,0:T(8,128)(2,1)S(1)}, u32[]{:S(2)}, u32[]{:S(2)}) collective-permute-start(bf16[8,4096]{1,0:T(8,128)(2,1)S(1)} %add_convert_fusion.10), channel_id=1, source_target_pairs={{0,4},{1,5},{2,6},{3,7},{4,0},{5,1},{6,2},{7,3},{8,12},{9,13},{10,... | collective-permute-start | bytes 196616 | tf_op jit(solution)/shard_map/ppermute | solution.py:79
  85.9 5.6 %collective-permute-start.19 = (bf16[8,4096]{1,0:T(8,128)(2,1)S(1)}, bf16[8,4096]{1,0:T(8,128)(2,1)S(1)}, u32[]{:S(2)}, u32[]{:S(2)}) collective-permute-start(bf16[8,4096]{1,0:T(8,128)(2,1)S(1)} %add_convert_fusion.12), channel_id=1, source_target_pairs={{0,4},{1,5},{2,6},{3,7},{4,0},{5,1},{6,2},{7,3},{8,12},{9,13},{10,... | collective-permute-start | bytes 196616 | tf_op jit(solution)/shard_map/ppermute | solution.py:79
  89.1 5.3 %collective-permute-start.9 = (bf16[8,4096]{1,0:T(8,128)(2,1)S(1)}, bf16[8,4096]{1,0:T(8,128)(2,1)S(1)}, u32[]{:S(2)}, u32[]{:S(2)}) collective-permute-start(bf16[8,4096]{1,0:T(8,128)(2,1)S(1)} %add_convert_fusion.14), channel_id=1, source_target_pairs={{0,4},{1,5},{2,6},{3,7},{4,0},{5,1},{6,2},{7,3},{8,12},{9,13},{10,... | collective-permute-start | bytes 196616 | tf_op jit(solution)/shard_map/ppermute | solution.py:79

commit v13 on v12

--- a/solution.py
+++ b/solution.py
@@ -12,6 +12,7 @@
 COLUMNS = 256
 VMEM_MIB = 10
 ROWS_AT_ONCE = 8
+GUARDS = [(2, 5, 0, 7), (1, 5, 2, 4), (1, 4, 0, 6), (0, 8, 2, 7), (0, 9, 2, 8), (0, 10, 2, 9)]
 
 
 def partner(value, axis, distance):
@@ -224,8 +225,8 @@
     return sum(term.astype(jnp.float32) for term in terms).astype(jnp.bfloat16)
 
 
-def chunk_steps(own, moves, serve, beside):
-    rows = own.shape[0]
+def chunk_steps(own, moves, back, serve, beside):
+    rows, packed_width = own.shape
     (held,) = yield (own,)
     for move in moves:
         (got,) = yield (permute(held, move),)
@@ -236,23 +237,32 @@
     out, out_sib = serve(held, sib)
     (out_sib,) = yield (out_sib,)
     (got,) = yield (permute(out_sib, to_sibling),)
-    terms = [out]
-    for move in moves[::-1]:
-        terms.append(got)
-        half = got.shape[0] // 2
-        sent = total(*[term[half : 2 * half] for term in terms])
-        (got,) = yield (permute(sent, move),)
-    terms.append(got)
-    return total(*[term[:rows] for term in terms])
-
-
-def run_steps(chunks):
-    waits = [next(chunk) for chunk in chunks]
+    left = list(range(len(moves)))[::-1]
+    terms = [out.reshape((2,) * len(left) + (rows, -1)), got.reshape((2,) * len(left) + (rows, -1))]
+    for number in back:
+        at = left.index(number)
+        left.remove(number)
+        kept, sent = ([lax.index_in_dim(term, k, at, keepdims=False) for term in terms] for k in (0, 1))
+        sent = total(*sent).reshape(-1, out.shape[1])
+        (got,) = yield (permute(sent, moves[number]),)
+        terms = kept + [got.reshape((2,) * len(left) + (rows, -1))]
+    return total(*terms)
+
+
+def run_steps(chunks, guards):
+    waits = [[next(chunk)[0]] for chunk in chunks]
     results = [None] * len(chunks)
     while any(result is None for result in results):
         for i, chunk in enumerate(chunks):
+            at = len(waits[i]) - 1
+            asked = [(j, t) for k, s, j, t in guards if (k, s) == (i, at)]
+            if results[i] is not None or any(len(waits[j]) <= t for j, t in asked):
+                continue
+            ready = tuple(waits[i][-1:])
+            if asked:
+                ready = lax.optimization_barrier(ready + tuple(waits[j][t] for j, t in asked))[:1]
             try:
-                waits[i] = chunk.send(waits[i]) if results[i] is None else None
+                waits[i].append(chunk.send(ready)[0])
             except StopIteration as end:
                 results[i] = end.value
     return results
@@ -264,13 +274,15 @@
     line_bits = (lax.axis_size("expert") // 2).bit_length() - 1
     along = [along_line(2**bit) for bit in range(line_bits)][::-1]
     across = [over_first, over_second]
-    routes = [along + across, along[:1] + across + along[1:]]
+    routes = [along + across, along + across, along[:1] + across + along[1:]]
+    backs = [[3, 2, 1, 0], [3, 2, 1, 0], [2, 3, 1, 0]] if line_bits == 2 else [range(len(along + across))[::-1]]
     step = ROWS_AT_ONCE if tok_rows % ROWS_AT_ONCE == 0 else tok_rows
     owns = packed(tokens, expert_ids, route_weight, step)
     mine = served_expert(slot_of, lax.optimization_barrier((swap_flag, owns[0]))[0])
     serve = lambda held, sib: serve_rows(held, sib, mine, top_count, w_gate[0], w_up[0], w_down[0])
-    chunks = [chunk_steps(own, routes[i % len(routes)], serve, (mine,) if i == 1 else ()) for i, own in enumerate(owns)]
-    return jnp.concatenate(run_steps(chunks))
+    chunks = [chunk_steps(own, routes[i % len(routes)], backs[i % len(backs)], serve, (mine,) if i == 1 else ()) for i, own in enumerate(owns)]
+    guards = GUARDS if len(chunks) == 3 and line_bits == 2 else []
+    return jnp.concatenate(run_steps(chunks, guards))
 
 
 def on_device(tokens, expert_ids, *rest):

time: 95.4 us -> 94.5 us (level)
  waiting for transfers between devices: 39.4 us -> 32.2 us
  starting transfers between devices: 37.6 us -> 43.9 us
    ppermute x30, waiting for transfers between devices: 39.4 us -> 32.2 us  [permute(): return lax.ppermute(value, AXES, pairs)]
    ppermute x30, starting transfers between devices: 37.6 us -> 43.9 us  [permute(): return lax.ppermute(value, AXES, pairs)]
  transfers between devices with their start and end apart: 30 -> 30, of which waited for: 14 -> 17; matrix products, arithmetic and copies ran while one was open for 2% -> 2% of each run, Pallas kernels for 14% -> 15%
where the time goes in v13:
time: 94.5 us; the launch traced here: 94.3 us
  starting transfers between devices  43.9 us (46%)
  waiting for transfers between devices  32.2 us (34%)
  Pallas kernels  14.8 us (16%)
  other arithmetic  2.1 us (2%)
    ppermute x30, starting transfers between devices, permute(): return lax.ppermute(value, AXES, pairs)  43.9 us
    ppermute x30, waiting for transfers between devices, permute(): return lax.ppermute(value, AXES, pairs)  32.2 us
    pallas_call x3, Pallas kernels, serve_rows(): pl.pallas_call(functools.partial(serve_kernel, top_count), out_shape=(out...  12.4 us
  transfers between devices with their start and end apart: 30, of which 17 were waited for; matrix products, arithmetic and copies ran while one was open for 2% of the time, Pallas kernels for 15%

profile of v13, /device:TPU:0, one launch (start us, length us, event | category | flops | bytes accessed | tf_op | source)
XLA Modules:
  0.0 94.3 jit_solution(4948248486172367173)
XLA Ops:
  0.0 1.0 %pack_rows.1 = (bf16[8,4224]{1,0:T(8,128)(2,1)S(1)}, bf16[8,4224]{1,0:T(8,128)(2,1)S(1)}, bf16[8,4224]{1,0:T(8,128)(2,1)S(1)}) custom-call(bf16[24,4096]{1,0:T(8,128)(2,1)} %tokens_hbm.1, s32[8,24]{1,0:T(8,128)} %bitcast.57, f32[8,24]{1,0:T(8,128)} %bitcast.58), custom_call_target="tpu_custom_call" | custom-call | bytes 393216 | tf_op jit(solution)/shard_map/pack_rows/pallas_call | solution.py:158
  1.0 4.1 %collective-permute-start.7 = (bf16[8,4224]{1,0:T(8,128)(2,1)S(1)}, bf16[8,4224]{1,0:T(8,128)(2,1)S(1)}, u32[]{:S(2)}, u32[]{:S(2)}) collective-permute-start(bf16[8,4224]{1,0:T(8,128)(2,1)S(1)} %get-tuple-element.26), channel_id=1, source_target_pairs={{0,4},{1,5},{2,6},{3,7},{4,0},{5,1},{6,2},{7,3},{8,12},{9,13},{10,... | collective-permute-start | bytes 202760 | tf_op jit(solution)/shard_map/ppermute | solution.py:80
  5.1 0.1 collective-permute-start
  5.2 2.8 %collective-permute-start.18 = (bf16[8,4224]{1,0:T(8,128)(2,1)S(1)}, bf16[8,4224]{1,0:T(8,128)(2,1)S(1)}, u32[]{:S(2)}, u32[]{:S(2)}) collective-permute-start(bf16[8,4224]{1,0:T(8,128)(2,1)S(1)} %get-tuple-element.33), channel_id=1, source_target_pairs={{0,4},{1,5},{2,6},{3,7},{4,0},{5,1},{6,2},{7,3},{8,12},{9,13},{10,... | collective-permute-start | bytes 202760 | tf_op jit(solution)/shard_map/ppermute | solution.py:80
  8.7 1.4 %served_expert.1.mine = s32[1]{0:T(128)} custom-call(s32[2,16]{1,0:T(2,128)} %bitcast.59, s32[1]{0:T(128)S(6)} %copy.21.flag), custom_call_target="tpu_custom_call" | custom-call | flops 10000000000 | tf_op jit(solution)/shard_map/served_expert/pallas_call | solution.py:111
  10.2 3.7 %collective-permute-start.8 = (bf16[16,4224]{1,0:T(8,128)(2,1)S(1)}, bf16[16,4224]{1,0:T(8,128)(2,1)S(1)}, u32[]{:S(2)}, u32[]{:S(2)}) collective-permute-start(bf16[16,4224]{1,0:T(8,128)(2,1)S(1)} %pad_maximum_fusion.8), channel_id=1, source_target_pairs={{0,1},{1,0},{2,3},{3,2},{4,5},{5,4},{6,7},{7,6},{8,24},{9,25},{10,... | collective-permute-start | bytes 405512 | tf_op jit(solution)/shard_map/ppermute | solution.py:80
  13.8 0.3 collective-permute-start.1
  14.1 0.5 collective-permute-done.18
  14.6 1.4 %collective-permute-start.19 = (bf16[16,4224]{1,0:T(8,128)(2,1)S(1)}, bf16[16,4224]{1,0:T(8,128)(2,1)S(1)}, u32[]{:S(2)}, u32[]{:S(2)}) collective-permute-start(bf16[16,4224]{1,0:T(8,128)(2,1)S(1)} %pad_maximum_fusion.9), channel_id=1, source_target_pairs={{0,2},{1,3},{2,0},{3,1},{4,6},{5,7},{6,4},{7,5},{8,10},{9,11},{10,... | collective-permute-start | bytes 405512 | tf_op jit(solution)/shard_map/ppermute | solution.py:80
  16.1 0.8 collective-permute-done.8
  16.8 2.1 %collective-permute-start.9 = (bf16[32,4224]{1,0:T(8,128)(2,1)S(1)}, bf16[32,4224]{1,0:T(8,128)(2,1)S(1)}, u32[]{:S(2)}, u32[]{:S(2)}) collective-permute-start(bf16[32,4224]{1,0:T(8,128)(2,1)S(1)} %pad_maximum_fusion.4), channel_id=1, source_target_pairs={{0,16},{1,17},{2,18},{3,19},{4,20},{5,21},{6,22},{7,23},{8,9},{9,8... | collective-permute-start | bytes 811016 | tf_op jit(solution)/shard_map/ppermute | solution.py:80
  18.9 0.9 collective-permute-done.1
  19.9 1.9 %collective-permute-start.2 = (bf16[32,4224]{1,0:T(8,128)(2,1)S(1)}, bf16[32,4224]{1,0:T(8,128)(2,1)S(1)}, u32[]{:S(2)}, u32[]{:S(2)}) collective-permute-start(bf16[32,4224]{1,0:T(8,128)(2,1)S(1)} %pad_maximum_fusion.3), channel_id=1, source_target_pairs={{0,1},{1,0},{2,3},{3,2},{4,5},{5,4},{6,7},{7,6},{8,24},{9,25},{10,... | collective-permute-start | bytes 811016 | tf_op jit(solution)/shard_map/ppermute | solution.py:80
  21.8 1.4 %collective-permute-start.20 = (bf16[32,4224]{1,0:T(8,128)(2,1)S(1)}, bf16[32,4224]{1,0:T(8,128)(2,1)S(1)}, u32[]{:S(2)}, u32[]{:S(2)}) collective-permute-start(bf16[32,4224]{1,0:T(8,128)(2,1)S(1)} %pad_maximum_fusion.5), channel_id=1, source_target_pairs={{0,1},{1,0},{2,3},{3,2},{4,5},{5,4},{6,7},{7,6},{8,24},{9,25},{10,... | collective-permute-start | bytes 811016 | tf_op jit(solution)/shard_map/ppermute | solution.py:80
  23.3 2.9 %collective-permute-done.9 = bf16[32,4224]{1,0:T(8,128)(2,1)S(1)} collective-permute-done((bf16[32,4224]{1,0:T(8,128)(2,1)S(1)}, bf16[32,4224]{1,0:T(8,128)(2,1)S(1)}, u32[]{:S(2)}, u32[]{:S(2)}) %collective-permute-start.9) | collective-permute-done | bytes 270368 | tf_op jit(solution)/shard_map/ppermute | solution.py:80
  26.2 0.8 collective-permute-start.10
  27.1 1.6 %collective-permute-start.3 = (bf16[64,4224]{1,0:T(8,128)(2,1)S(1)}, bf16[64,4224]{1,0:T(8,128)(2,1)S(1)}, u32[]{:S(2)}, u32[]{:S(2)}) collective-permute-start(bf16[64,4224]{1,0:T(8,128)(2,1)S(1)} %pad_maximum_fusion), channel_id=1, source_target_pairs={{0,16},{1,17},{2,18},{3,19},{4,20},{5,21},{6,22},{7,23},{8,9},{9,8... | collective-permute-start | bytes 1622024 | tf_op jit(solution)/shard_map/ppermute | solution.py:80
  28.7 1.9 %collective-permute-done.20 = bf16[32,4224]{1,0:T(8,128)(2,1)S(1)} collective-permute-done((bf16[32,4224]{1,0:T(8,128)(2,1)S(1)}, bf16[32,4224]{1,0:T(8,128)(2,1)S(1)}, u32[]{:S(2)}, u32[]{:S(2)}) %collective-permute-start.20) | collective-permute-done | bytes 270368 | tf_op jit(solution)/shard_map/ppermute | solution.py:80
  30.6 2.4 %collective-permute-start.21 = (bf16[64,4224]{1,0:T(8,128)(2,1)S(1)}, bf16[64,4224]{1,0:T(8,128)(2,1)S(1)}, u32[]{:S(2)}, u32[]{:S(2)}) collective-permute-start(bf16[64,4224]{1,0:T(8,128)(2,1)S(1)} %pad_maximum_fusion.2), channel_id=1, source_target_pairs={{0,16},{1,17},{2,18},{3,19},{4,20},{5,21},{6,22},{7,23},{8,9},{9,8... | collective-permute-start | bytes 1622024 | tf_op jit(solution)/shard_map/ppermute | solution.py:80
  33.0 3.5 %collective-permute-done.3 = bf16[64,4224]{1,0:T(8,128)(2,1)S(1)} collective-permute-done((bf16[64,4224]{1,0:T(8,128)(2,1)S(1)}, bf16[64,4224]{1,0:T(8,128)(2,1)S(1)}, u32[]{:S(2)}, u32[]{:S(2)}) %collective-permute-start.3) | collective-permute-done | bytes 540704 | tf_op jit(solution)/shard_map/ppermute | solution.py:80
  36.6 0.1 collective-permute-start.4
  36.7 0.6 collective-permute-start.11
  37.3 2.0 %collective-permute-done.4.sib = bf16[128,4224]{1,0:T(8,128)(2,1)S(1)} collective-permute-done((bf16[128,4224]{1,0:T(8,128)(2,1)S(1)}, bf16[128,4224]{1,0:T(8,128)(2,1)S(1)}, u32[]{:S(2)}, u32[]{:S(2)}) %collective-permute-start.4) | collective-permute-done | bytes 1081376 | tf_op jit(solution)/shard_map/ppermute | solution.py:80
  39.4 4.1 %serve_rows.3 = (bf16[128,4096]{1,0:T(8,128)(2,1)S(1)}, bf16[128,4096]{1,0:T(8,128)(2,1)S(1)}) custom-call(s32[1]{0:T(128)} %served_expert.1.mine, bf16[128,4224]{1,0:T(8,128)(2,1)S(1)} %constant_dynamic-update-slice_fusion.own, bf16[128,4224]{1,0:T(8,128)(2,1)S(1)} %collective-permute-done.4.sib, bf16[4096,512]{1,0:T(8,128)(2,1)S(1)} %bitcast.37, ...), custom_call_target="tpu_custom_call" | custom-call | flops 3221225472 | bytes 16777216 | tf_op jit(solution)/shard_map/serve_rows/pallas_call | solution.py:207
  43.5 0.2 collective-permute-start.5
  43.8 0.4 collective-permute-start.22
  44.2 2.0 %collective-permute-done.5 = bf16[128,4096]{1,0:T(8,128)(2,1)S(1)} collective-permute-done((bf16[128,4096]{1,0:T(8,128)(2,1)S(1)}, bf16[128,4096]{1,0:T(8,128)(2,1)S(1)}, u32[]{:S(2)}, u32[]{:S(2)}) %collective-permute-start.5) | collective-permute-done | bytes 1048608 | tf_op jit(solution)/shard_map/ppermute | solution.py:80
  46.2 4.1 %serve_rows.4 = (bf16[128,4096]{1,0:T(8,128)(2,1)S(1)}, bf16[128,4096]{1,0:T(8,128)(2,1)S(1)}) custom-call(s32[1]{0:T(128)} %served_expert.1.mine, bf16[128,4224]{1,0:T(8,128)(2,1)S(1)} %constant_dynamic-update-slice_fusion.5.own, bf16[128,4224]{1,0:T(8,128)(2,1)S(1)} %collective-permute-done.11.sib, bf16[4096,512]{1,0:T(8,128)(2,1)S(1)} %bitcast.38, ...), custom_call_target="tpu_custom_call" | custom-call | flops 3221225472 | bytes 16777216 | tf_op jit(solution)/shard_map/serve_rows/pallas_call | solution.py:207
  50.4 0.2 collective-permute-start.12
  50.6 0.1 add_convert_fusion.2
  50.7 1.6 %collective-permute-start.6 = (bf16[64,4096]{1,0:T(8,128)(2,1)S(1)}, bf16[64,4096]{1,0:T(8,128)(2,1)S(1)}, u32[]{:S(2)}, u32[]{:S(2)}) collective-permute-start(bf16[64,4096]{1,0:T(8,128)(2,1)S(1)} %add_convert_fusion.2), channel_id=1, source_target_pairs={{0,16},{1,17},{2,18},{3,19},{4,20},{5,21},{6,22},{7,23},{8,9},{9,8... | collective-permute-start | bytes 1572872 | tf_op jit(solution)/shard_map/ppermute | solution.py:80
  52.2 4.1 %serve_rows.5 = (bf16[128,4096]{1,0:T(8,128)(2,1)S(1)}, bf16[128,4096]{1,0:T(8,128)(2,1)S(1)}) custom-call(s32[1]{0:T(128)} %served_expert.1.mine, bf16[128,4224]{1,0:T(8,128)(2,1)S(1)} %constant_dynamic-update-slice_fusion.10.own, bf16[128,4224]{1,0:T(8,128)(2,1)S(1)} %collective-permute-done.22.sib, bf16[4096,512]{1,0:T(8,128)(2,1)S(1)} %bitcast.39, ...), custom_call_target="tpu_custom_call" | custom-call | flops 3221225472 | bytes 16777216 | tf_op jit(solution)/shard_map/serve_rows/pallas_call | solution.py:207
  56.4 0.2 collective-permute-start.23
  56.6 0.1 add_convert_fusion.1
  56.7 1.6 %collective-permute-start.14 = (bf16[64,4096]{1,0:T(8,128)(2,1)S(1)}, bf16[64,4096]{1,0:T(8,128)(2,1)S(1)}, u32[]{:S(2)}, u32[]{:S(2)}) collective-permute-start(bf16[64,4096]{1,0:T(8,128)(2,1)S(1)} %bitcast.56), channel_id=1, source_target_pairs={{0,16},{1,17},{2,18},{3,19},{4,20},{5,21},{6,22},{7,23},{8,9},{9,8... | collective-permute-start | bytes 1572872 | tf_op jit(solution)/shard_map/ppermute | solution.py:80
  58.3 1.7 %collective-permute-done.6 = bf16[64,4096]{1,0:T(8,128)(2,1)S(1)} collective-permute-done((bf16[64,4096]{1,0:T(8,128)(2,1)S(1)}, bf16[64,4096]{1,0:T(8,128)(2,1)S(1)}, u32[]{:S(2)}, u32[]{:S(2)}) %collective-permute-start.6) | collective-permute-done | bytes 524320 | tf_op jit(solution)/shard_map/ppermute | solution.py:80
  59.9 0.1 add_convert_fusion.4
  60.0 1.6 %collective-permute-start.13 = (bf16[32,4096]{1,0:T(8,128)(2,1)S(1)}, bf16[32,4096]{1,0:T(8,128)(2,1)S(1)}, u32[]{:S(2)}, u32[]{:S(2)}) collective-permute-start(bf16[32,4096]{1,0:T(8,128)(2,1)S(1)} %add_convert_fusion.4), channel_id=1, source_target_pairs={{0,1},{1,0},{2,3},{3,2},{4,5},{5,4},{6,7},{7,6},{8,24},{9,25},{10,... | collective-permute-start | bytes 786440 | tf_op jit(solution)/shard_map/ppermute | solution.py:80
  61.6 0.1 convert_add_fusion
  61.7 0.1 add_convert_fusion
  61.8 1.6 %collective-permute-start.24 = (bf16[64,4096]{1,0:T(8,128)(2,1)S(1)}, bf16[64,4096]{1,0:T(8,128)(2,1)S(1)}, u32[]{:S(2)}, u32[]{:S(2)}) collective-permute-start(bf16[64,4096]{1,0:T(8,128)(2,1)S(1)} %add_convert_fusion), channel_id=1, source_target_pairs={{0,16},{1,17},{2,18},{3,19},{4,20},{5,21},{6,22},{7,23},{8,9},{9,8... | collective-permute-start | bytes 1572872 | tf_op jit(solution)/shard_map/ppermute | solution.py:80
  63.4 5.4 %collective-permute-done.14 = bf16[64,4096]{1,0:T(8,128)(2,1)S(1)} collective-permute-done((bf16[64,4096]{1,0:T(8,128)(2,1)S(1)}, bf16[64,4096]{1,0:T(8,128)(2,1)S(1)}, u32[]{:S(2)}, u32[]{:S(2)}) %collective-permute-start.14) | collective-permute-done | bytes 524320 | tf_op jit(solution)/shard_map/ppermute | solution.py:80
  68.8 1.9 %collective-permute-start.16 = (bf16[32,4096]{1,0:T(8,128)(2,1)S(1)}, bf16[32,4096]{1,0:T(8,128)(2,1)S(1)}, u32[]{:S(2)}, u32[]{:S(2)}) collective-permute-start(bf16[32,4096]{1,0:T(8,128)(2,1)S(1)} %fusion), channel_id=1, source_target_pairs={{0,2},{1,3},{2,0},{3,1},{4,6},{5,7},{6,4},{7,5},{8,10},{9,11},{10,... | collective-permute-start | bytes 786440 | tf_op jit(solution)/shard_map/ppermute | solution.py:80
  70.7 0.1 add_convert_fusion.6
  70.8 0.3 collective-permute-start.15
  71.0 3.3 %collective-permute-done.24 = bf16[64,4096]{1,0:T(8,128)(2,1)S(1)} collective-permute-done((bf16[64,4096]{1,0:T(8,128)(2,1)S(1)}, bf16[64,4096]{1,0:T(8,128)(2,1)S(1)}, u32[]{:S(2)}, u32[]{:S(2)}) %collective-permute-start.24) | collective-permute-done | bytes 524320 | tf_op jit(solution)/shard_map/ppermute | solution.py:80
  74.4 0.1 add_convert_fusion.3
  74.5 1.5 %collective-permute-start.25 = (bf16[32,4096]{1,0:T(8,128)(2,1)S(1)}, bf16[32,4096]{1,0:T(8,128)(2,1)S(1)}, u32[]{:S(2)}, u32[]{:S(2)}) collective-permute-start(bf16[32,4096]{1,0:T(8,128)(2,1)S(1)} %add_convert_fusion.3), channel_id=1, source_target_pairs={{0,1},{1,0},{2,3},{3,2},{4,5},{5,4},{6,7},{7,6},{8,24},{9,25},{10,... | collective-permute-start | bytes 786440 | tf_op jit(solution)/shard_map/ppermute | solution.py:80
  76.0 1.5 %collective-permute-done.16 = bf16[32,4096]{1,0:T(8,128)(2,1)S(1)} collective-permute-done((bf16[32,4096]{1,0:T(8,128)(2,1)S(1)}, bf16[32,4096]{1,0:T(8,128)(2,1)S(1)}, u32[]{:S(2)}, u32[]{:S(2)}) %collective-permute-start.16) | collective-permute-done | bytes 262176 | tf_op jit(solution)/shard_map/ppermute | solution.py:80
  77.4 0.1 fusion.2
  77.5 1.1 %collective-permute-start.28 = (bf16[16,4096]{1,0:T(8,128)(2,1)S(1)}, bf16[16,4096]{1,0:T(8,128)(2,1)S(1)}, u32[]{:S(2)}, u32[]{:S(2)}) collective-permute-start(bf16[16,4096]{1,0:T(8,128)(2,1)S(1)} %fusion.2), channel_id=1, source_target_pairs={{0,1},{1,0},{2,3},{3,2},{4,5},{5,4},{6,7},{7,6},{8,24},{9,25},{10,... | collective-permute-start | bytes 393224 | tf_op jit(solution)/shard_map/ppermute | solution.py:80
  78.6 0.3 collective-permute-done.15
  78.9 3.1 %collective-permute-start.17 = (bf16[8,4096]{1,0:T(8,128)(2,1)S(1)}, bf16[8,4096]{1,0:T(8,128)(2,1)S(1)}, u32[]{:S(2)}, u32[]{:S(2)}) collective-permute-start(bf16[8,4096]{1,0:T(8,128)(2,1)S(1)} %add_convert_fusion.10), channel_id=1, source_target_pairs={{0,4},{1,5},{2,6},{3,7},{4,0},{5,1},{6,2},{7,3},{8,12},{9,13},{10,... | collective-permute-start | bytes 196616 | tf_op jit(solution)/shard_map/ppermute | solution.py:80
  82.0 0.1 add_convert_fusion.5
  82.1 0.8 collective-permute-start.26
  82.9 1.5 %collective-permute-done.17 = bf16[8,4096]{1,0:T(8,128)(2,1)S(1)} collective-permute-done((bf16[8,4096]{1,0:T(8,128)(2,1)S(1)}, bf16[8,4096]{1,0:T(8,128)(2,1)S(1)}, u32[]{:S(2)}, u32[]{:S(2)}) %collective-permute-start.17) | collective-permute-done | bytes 65568 | tf_op jit(solution)/shard_map/ppermute | solution.py:80
  84.4 0.1 add_convert_fusion.9
  84.5 2.9 %collective-permute-start.29 = (bf16[8,4096]{1,0:T(8,128)(2,1)S(1)}, bf16[8,4096]{1,0:T(8,128)(2,1)S(1)}, u32[]{:S(2)}, u32[]{:S(2)}) collective-permute-start(bf16[8,4096]{1,0:T(8,128)(2,1)S(1)} %fusion.5), channel_id=1, source_target_pairs={{0,4},{1,5},{2,6},{3,7},{4,0},{5,1},{6,2},{7,3},{8,12},{9,13},{10,... | collective-permute-start | bytes 196616 | tf_op jit(solution)/shard_map/ppermute | solution.py:80
  87.4 0.2 collective-permute-done.26
  87.6 2.0 %collective-permute-start.27 = (bf16[8,4096]{1,0:T(8,128)(2,1)S(1)}, bf16[8,4096]{1,0:T(8,128)(2,1)S(1)}, u32[]{:S(2)}, u32[]{:S(2)}) collective-permute-start(bf16[8,4096]{1,0:T(8,128)(2,1)S(1)} %add_convert_fusion.8), channel_id=1, source_target_pairs={{0,4},{1,5},{2,6},{3,7},{4,0},{5,1},{6,2},{7,3},{8,12},{9,13},{10,... | collective-permute-start | bytes 196616 | tf_op jit(solution)/shard_map/ppermute | solution.py:80
  89.6 1.5 %collective-permute-done.29 = bf16[8,4096]{1,0:T(8,128)(2,1)S(1)} collective-permute-done((bf16[8,4096]{1,0:T(8,128)(2,1)S(1)}, bf16[8,4096]{1,0:T(8,128)(2,1)S(1)}, u32[]{:S(2)}, u32[]{:S(2)}) %collective-permute-start.29) | collective-permute-done | bytes 65568 | tf_op jit(solution)/shard_map/ppermute | solution.py:80
  91.1 2.4 %collective-permute-done.27 = bf16[8,4096]{1,0:T(8,128)(2,1)S(1)} collective-permute-done((bf16[8,4096]{1,0:T(8,128)(2,1)S(1)}, bf16[8,4096]{1,0:T(8,128)(2,1)S(1)}, u32[]{:S(2)}, u32[]{:S(2)}) %collective-permute-start.27) | collective-permute-done | bytes 65568 | tf_op jit(solution)/shard_map/ppermute | solution.py:80
  93.5 0.1 add_convert_fusion.7
  93.6 0.7 pad_maximum_fusion.6
  (47 shorter events, 0.8 us)
Async XLA Ops:
  1.0 9.1 %collective-permute-start.7 = (bf16[8,4224]{1,0:T(8,128)(2,1)S(1)}, bf16[8,4224]{1,0:T(8,128)(2,1)S(1)}, u32[]{:S(2)}, u32[]{:S(2)}) collective-permute-start(bf16[8,4224]{1,0:T(8,128)(2,1)S(1)} %get-tuple-element.26), channel_id=1, source_target_pairs={{0,4},{1,5},{2,6},{3,7},{4,0},{5,1},{6,2},{7,3},{8,12},{9,13},{10,... | collective-permute-start | bytes 202760 | tf_op jit(solution)/shard_map/ppermute | solution.py:80
  5.1 8.7 %collective-permute-start = (bf16[8,4224]{1,0:T(8,128)(2,1)S(1)}, bf16[8,4224]{1,0:T(8,128)(2,1)S(1)}, u32[]{:S(2)}, u32[]{:S(2)}) collective-permute-start(bf16[8,4224]{1,0:T(8,128)(2,1)S(1)} %get-tuple-element.22), channel_id=1, source_target_pairs={{0,4},{1,5},{2,6},{3,7},{4,0},{5,1},{6,2},{7,3},{8,12},{9,13},{10,... | collective-permute-start | bytes 202760 | tf_op jit(solution)/shard_map/ppermute | solution.py:80
  5.2 9.4 %collective-permute-start.18 = (bf16[8,4224]{1,0:T(8,128)(2,1)S(1)}, bf16[8,4224]{1,0:T(8,128)(2,1)S(1)}, u32[]{:S(2)}, u32[]{:S(2)}) collective-permute-start(bf16[8,4224]{1,0:T(8,128)(2,1)S(1)} %get-tuple-element.33), channel_id=1, source_target_pairs={{0,4},{1,5},{2,6},{3,7},{4,0},{5,1},{6,2},{7,3},{8,12},{9,13},{10,... | collective-permute-start | bytes 202760 | tf_op jit(solution)/shard_map/ppermute | solution.py:80
  8.7 30.6 %copy-start.2 = (bf16[1,512,4096]{2,1,0:T(8,128)(2,1)S(1)}, bf16[1,512,4096]{2,1,0:T(8,128)(2,1)}, u32[]{:S(2)}) copy-start(bf16[1,512,4096]{2,1,0:T(8,128)(2,1)} %param.15) | copy-start | bytes 12582916
  10.2 6.7 %collective-permute-start.8 = (bf16[16,4224]{1,0:T(8,128)(2,1)S(1)}, bf16[16,4224]{1,0:T(8,128)(2,1)S(1)}, u32[]{:S(2)}, u32[]{:S(2)}) collective-permute-start(bf16[16,4224]{1,0:T(8,128)(2,1)S(1)} %pad_maximum_fusion.8), channel_id=1, source_target_pairs={{0,1},{1,0},{2,3},{3,2},{4,5},{5,4},{6,7},{7,6},{8,24},{9,25},{10,... | collective-permute-start | bytes 405512 | tf_op jit(solution)/shard_map/ppermute | solution.py:80
  13.8 6.0 %collective-permute-start.1 = (bf16[16,4224]{1,0:T(8,128)(2,1)S(1)}, bf16[16,4224]{1,0:T(8,128)(2,1)S(1)}, u32[]{:S(2)}, u32[]{:S(2)}) collective-permute-start(bf16[16,4224]{1,0:T(8,128)(2,1)S(1)} %pad_maximum_fusion.7), channel_id=1, source_target_pairs={{0,2},{1,3},{2,0},{3,1},{4,6},{5,7},{6,4},{7,5},{8,10},{9,11},{10,... | collective-permute-start | bytes 405512 | tf_op jit(solution)/shard_map/ppermute | solution.py:80
  14.6 7.2 %collective-permute-start.19 = (bf16[16,4224]{1,0:T(8,128)(2,1)S(1)}, bf16[16,4224]{1,0:T(8,128)(2,1)S(1)}, u32[]{:S(2)}, u32[]{:S(2)}) collective-permute-start(bf16[16,4224]{1,0:T(8,128)(2,1)S(1)} %pad_maximum_fusion.9), channel_id=1, source_target_pairs={{0,2},{1,3},{2,0},{3,1},{4,6},{5,7},{6,4},{7,5},{8,10},{9,11},{10,... | collective-permute-start | bytes 405512 | tf_op jit(solution)/shard_map/ppermute | solution.py:80
  16.8 22.5 %copy-start.1 = (bf16[1,4096,512]{2,1,0:T(8,128)(2,1)S(1)}, bf16[1,4096,512]{2,1,0:T(8,128)(2,1)}, u32[]{:S(2)}) copy-start(bf16[1,4096,512]{2,1,0:T(8,128)(2,1)} %param.14) | copy-start | bytes 12582916
  16.8 9.4 %collective-permute-start.9 = (bf16[32,4224]{1,0:T(8,128)(2,1)S(1)}, bf16[32,4224]{1,0:T(8,128)(2,1)S(1)}, u32[]{:S(2)}, u32[]{:S(2)}) collective-permute-start(bf16[32,4224]{1,0:T(8,128)(2,1)S(1)} %pad_maximum_fusion.4), channel_id=1, source_target_pairs={{0,16},{1,17},{2,18},{3,19},{4,20},{5,21},{6,22},{7,23},{8,9},{9,8... | collective-permute-start | bytes 811016 | tf_op jit(solution)/shard_map/ppermute | solution.py:80
  19.9 7.2 %collective-permute-start.2 = (bf16[32,4224]{1,0:T(8,128)(2,1)S(1)}, bf16[32,4224]{1,0:T(8,128)(2,1)S(1)}, u32[]{:S(2)}, u32[]{:S(2)}) collective-permute-start(bf16[32,4224]{1,0:T(8,128)(2,1)S(1)} %pad_maximum_fusion.3), channel_id=1, source_target_pairs={{0,1},{1,0},{2,3},{3,2},{4,5},{5,4},{6,7},{7,6},{8,24},{9,25},{10,... | collective-permute-start | bytes 811016 | tf_op jit(solution)/shard_map/ppermute | solution.py:80
  21.8 8.7 %collective-permute-start.20 = (bf16[32,4224]{1,0:T(8,128)(2,1)S(1)}, bf16[32,4224]{1,0:T(8,128)(2,1)S(1)}, u32[]{:S(2)}, u32[]{:S(2)}) collective-permute-start(bf16[32,4224]{1,0:T(8,128)(2,1)S(1)} %pad_maximum_fusion.5), channel_id=1, source_target_pairs={{0,1},{1,0},{2,3},{3,2},{4,5},{5,4},{6,7},{7,6},{8,24},{9,25},{10,... | collective-permute-start | bytes 811016 | tf_op jit(solution)/shard_map/ppermute | solution.py:80
  26.2 10.4 %collective-permute-start.10 = (bf16[64,4224]{1,0:T(8,128)(2,1)S(1)}, bf16[64,4224]{1,0:T(8,128)(2,1)S(1)}, u32[]{:S(2)}, u32[]{:S(2)}) collective-permute-start(bf16[64,4224]{1,0:T(8,128)(2,1)S(1)} %pad_maximum_fusion.1), channel_id=1, source_target_pairs={{0,2},{1,3},{2,0},{3,1},{4,6},{5,7},{6,4},{7,5},{8,10},{9,11},{10,... | collective-permute-start | bytes 1622024 | tf_op jit(solution)/shard_map/ppermute | solution.py:80
  27.1 9.4 %collective-permute-start.3 = (bf16[64,4224]{1,0:T(8,128)(2,1)S(1)}, bf16[64,4224]{1,0:T(8,128)(2,1)S(1)}, u32[]{:S(2)}, u32[]{:S(2)}) collective-permute-start(bf16[64,4224]{1,0:T(8,128)(2,1)S(1)} %pad_maximum_fusion), channel_id=1, source_target_pairs={{0,16},{1,17},{2,18},{3,19},{4,20},{5,21},{6,22},{7,23},{8,9},{9,8... | collective-permute-start | bytes 1622024 | tf_op jit(solution)/shard_map/ppermute | solution.py:80
  30.6 8.8 %copy-start = (bf16[1,4096,512]{2,1,0:T(8,128)(2,1)S(1)}, bf16[1,4096,512]{2,1,0:T(8,128)(2,1)}, u32[]{:S(2)}) copy-start(bf16[1,4096,512]{2,1,0:T(8,128)(2,1)} %param.13) | copy-start | bytes 12582916
  30.6 13.1 %collective-permute-start.21 = (bf16[64,4224]{1,0:T(8,128)(2,1)S(1)}, bf16[64,4224]{1,0:T(8,128)(2,1)S(1)}, u32[]{:S(2)}, u32[]{:S(2)}) collective-permute-start(bf16[64,4224]{1,0:T(8,128)(2,1)S(1)} %pad_maximum_fusion.2), channel_id=1, source_target_pairs={{0,16},{1,17},{2,18},{3,19},{4,20},{5,21},{6,22},{7,23},{8,9},{9,8... | collective-permute-start | bytes 1622024 | tf_op jit(solution)/shard_map/ppermute | solution.py:80
  36.6 2.8 %collective-permute-start.4 = (bf16[128,4224]{1,0:T(8,128)(2,1)S(1)}, bf16[128,4224]{1,0:T(8,128)(2,1)S(1)}, u32[]{:S(2)}, u32[]{:S(2)}) collective-permute-start(bf16[128,4224]{1,0:T(8,128)(2,1)S(1)} %constant_dynamic-update-slice_fusion.own), channel_id=1, source_target_pairs={{0,8},{1,9},{2,10},{3,11},{4,12},{5,13},{6,14},{7,15},{8,0},{9,1},... | collective-permute-start | bytes 3244040 | tf_op jit(solution)/shard_map/ppermute | solution.py:80
  36.7 7.5 %collective-permute-start.11 = (bf16[128,4224]{1,0:T(8,128)(2,1)S(1)}, bf16[128,4224]{1,0:T(8,128)(2,1)S(1)}, u32[]{:S(2)}, u32[]{:S(2)}) collective-permute-start(bf16[128,4224]{1,0:T(8,128)(2,1)S(1)} %constant_dynamic-update-slice_fusion.5.own), channel_id=1, source_target_pairs={{0,8},{1,9},{2,10},{3,11},{4,12},{5,13},{6,14},{7,15},{8,0},{9,1},... | collective-permute-start | bytes 3244040 | tf_op jit(solution)/shard_map/ppermute | solution.py:80
  43.5 2.7 %collective-permute-start.5 = (bf16[128,4096]{1,0:T(8,128)(2,1)S(1)}, bf16[128,4096]{1,0:T(8,128)(2,1)S(1)}, u32[]{:S(2)}, u32[]{:S(2)}) collective-permute-start(bf16[128,4096]{1,0:T(8,128)(2,1)S(1)} %get-tuple-element.25), channel_id=1, source_target_pairs={{0,8},{1,9},{2,10},{3,11},{4,12},{5,13},{6,14},{7,15},{8,0},{9,1},... | collective-permute-start | bytes 3145736 | tf_op jit(solution)/shard_map/ppermute | solution.py:80
  43.8 8.5 %collective-permute-start.22 = (bf16[128,4224]{1,0:T(8,128)(2,1)S(1)}, bf16[128,4224]{1,0:T(8,128)(2,1)S(1)}, u32[]{:S(2)}, u32[]{:S(2)}) collective-permute-start(bf16[128,4224]{1,0:T(8,128)(2,1)S(1)} %constant_dynamic-update-slice_fusion.10.own), channel_id=1, source_target_pairs={{0,8},{1,9},{2,10},{3,11},{4,12},{5,13},{6,14},{7,15},{8,0},{9,1},... | collective-permute-start | bytes 3244040 | tf_op jit(solution)/shard_map/ppermute | solution.py:80
  50.4 6.2 %collective-permute-start.12 = (bf16[128,4096]{1,0:T(8,128)(2,1)S(1)}, bf16[128,4096]{1,0:T(8,128)(2,1)S(1)}, u32[]{:S(2)}, u32[]{:S(2)}) collective-permute-start(bf16[128,4096]{1,0:T(8,128)(2,1)S(1)} %get-tuple-element.28), channel_id=1, source_target_pairs={{0,8},{1,9},{2,10},{3,11},{4,12},{5,13},{6,14},{7,15},{8,0},{9,1},... | collective-permute-start | bytes 3145736 | tf_op jit(solution)/shard_map/ppermute | solution.py:80
  50.7 9.2 %collective-permute-start.6 = (bf16[64,4096]{1,0:T(8,128)(2,1)S(1)}, bf16[64,4096]{1,0:T(8,128)(2,1)S(1)}, u32[]{:S(2)}, u32[]{:S(2)}) collective-permute-start(bf16[64,4096]{1,0:T(8,128)(2,1)S(1)} %add_convert_fusion.2), channel_id=1, source_target_pairs={{0,16},{1,17},{2,18},{3,19},{4,20},{5,21},{6,22},{7,23},{8,9},{9,8... | collective-permute-start | bytes 1572872 | tf_op jit(solution)/shard_map/ppermute | solution.py:80
  56.4 5.3 %collective-permute-start.23 = (bf16[128,4096]{1,0:T(8,128)(2,1)S(1)}, bf16[128,4096]{1,0:T(8,128)(2,1)S(1)}, u32[]{:S(2)}, u32[]{:S(2)}) collective-permute-start(bf16[128,4096]{1,0:T(8,128)(2,1)S(1)} %get-tuple-element.38), channel_id=1, source_target_pairs={{0,8},{1,9},{2,10},{3,11},{4,12},{5,13},{6,14},{7,15},{8,0},{9,1},... | collective-permute-start | bytes 3145736 | tf_op jit(solution)/shard_map/ppermute | solution.py:80
  56.7 12.1 %collective-permute-start.14 = (bf16[64,4096]{1,0:T(8,128)(2,1)S(1)}, bf16[64,4096]{1,0:T(8,128)(2,1)S(1)}, u32[]{:S(2)}, u32[]{:S(2)}) collective-permute-start(bf16[64,4096]{1,0:T(8,128)(2,1)S(1)} %bitcast.56), channel_id=1, source_target_pairs={{0,16},{1,17},{2,18},{3,19},{4,20},{5,21},{6,22},{7,23},{8,9},{9,8... | collective-permute-start | bytes 1572872 | tf_op jit(solution)/shard_map/ppermute | solution.py:80
  60.0 10.7 %collective-permute-start.13 = (bf16[32,4096]{1,0:T(8,128)(2,1)S(1)}, bf16[32,4096]{1,0:T(8,128)(2,1)S(1)}, u32[]{:S(2)}, u32[]{:S(2)}) collective-permute-start(bf16[32,4096]{1,0:T(8,128)(2,1)S(1)} %add_convert_fusion.4), channel_id=1, source_target_pairs={{0,1},{1,0},{2,3},{3,2},{4,5},{5,4},{6,7},{7,6},{8,24},{9,25},{10,... | collective-permute-start | bytes 786440 | tf_op jit(solution)/shard_map/ppermute | solution.py:80
  61.8 12.6 %collective-permute-start.24 = (bf16[64,4096]{1,0:T(8,128)(2,1)S(1)}, bf16[64,4096]{1,0:T(8,128)(2,1)S(1)}, u32[]{:S(2)}, u32[]{:S(2)}) collective-permute-start(bf16[64,4096]{1,0:T(8,128)(2,1)S(1)} %add_convert_fusion), channel_id=1, source_target_pairs={{0,16},{1,17},{2,18},{3,19},{4,20},{5,21},{6,22},{7,23},{8,9},{9,8... | collective-permute-start | bytes 1572872 | tf_op jit(solution)/shard_map/ppermute | solution.py:80
  68.8 8.6 %collective-permute-start.16 = (bf16[32,4096]{1,0:T(8,128)(2,1)S(1)}, bf16[32,4096]{1,0:T(8,128)(2,1)S(1)}, u32[]{:S(2)}, u32[]{:S(2)}) collective-permute-start(bf16[32,4096]{1,0:T(8,128)(2,1)S(1)} %fusion), channel_id=1, source_target_pairs={{0,2},{1,3},{2,0},{3,1},{4,6},{5,7},{6,4},{7,5},{8,10},{9,11},{10,... | collective-permute-start | bytes 786440 | tf_op jit(solution)/shard_map/ppermute | solution.py:80
  70.8 8.1 %collective-permute-start.15 = (bf16[16,4096]{1,0:T(8,128)(2,1)S(1)}, bf16[16,4096]{1,0:T(8,128)(2,1)S(1)}, u32[]{:S(2)}, u32[]{:S(2)}) collective-permute-start(bf16[16,4096]{1,0:T(8,128)(2,1)S(1)} %add_convert_fusion.6), channel_id=1, source_target_pairs={{0,2},{1,3},{2,0},{3,1},{4,6},{5,7},{6,4},{7,5},{8,10},{9,11},{10,... | collective-permute-start | bytes 393224 | tf_op jit(solution)/shard_map/ppermute | solution.py:80
  74.5 7.5 %collective-permute-start.25 = (bf16[32,4096]{1,0:T(8,128)(2,1)S(1)}, bf16[32,4096]{1,0:T(8,128)(2,1)S(1)}, u32[]{:S(2)}, u32[]{:S(2)}) collective-permute-start(bf16[32,4096]{1,0:T(8,128)(2,1)S(1)} %add_convert_fusion.3), channel_id=1, source_target_pairs={{0,1},{1,0},{2,3},{3,2},{4,5},{5,4},{6,7},{7,6},{8,24},{9,25},{10,... | collective-permute-start | bytes 786440 | tf_op jit(solution)/shard_map/ppermute | solution.py:80
  77.5 6.9 %collective-permute-start.28 = (bf16[16,4096]{1,0:T(8,128)(2,1)S(1)}, bf16[16,4096]{1,0:T(8,128)(2,1)S(1)}, u32[]{:S(2)}, u32[]{:S(2)}) collective-permute-start(bf16[16,4096]{1,0:T(8,128)(2,1)S(1)} %fusion.2), channel_id=1, source_target_pairs={{0,1},{1,0},{2,3},{3,2},{4,5},{5,4},{6,7},{7,6},{8,24},{9,25},{10,... | collective-permute-start | bytes 393224 | tf_op jit(solution)/shard_map/ppermute | solution.py:80
  78.9 5.5 %collective-permute-start.17 = (bf16[8,4096]{1,0:T(8,128)(2,1)S(1)}, bf16[8,4096]{1,0:T(8,128)(2,1)S(1)}, u32[]{:S(2)}, u32[]{:S(2)}) collective-permute-start(bf16[8,4096]{1,0:T(8,128)(2,1)S(1)} %add_convert_fusion.10), channel_id=1, source_target_pairs={{0,4},{1,5},{2,6},{3,7},{4,0},{5,1},{6,2},{7,3},{8,12},{9,13},{10,... | collective-permute-start | bytes 196616 | tf_op jit(solution)/shard_map/ppermute | solution.py:80
  82.1 5.5 %collective-permute-start.26 = (bf16[16,4096]{1,0:T(8,128)(2,1)S(1)}, bf16[16,4096]{1,0:T(8,128)(2,1)S(1)}, u32[]{:S(2)}, u32[]{:S(2)}) collective-permute-start(bf16[16,4096]{1,0:T(8,128)(2,1)S(1)} %add_convert_fusion.5), channel_id=1, source_target_pairs={{0,2},{1,3},{2,0},{3,1},{4,6},{5,7},{6,4},{7,5},{8,10},{9,11},{10,... | collective-permute-start | bytes 393224 | tf_op jit(solution)/shard_map/ppermute | solution.py:80
  84.5 6.6 %collective-permute-start.29 = (bf16[8,4096]{1,0:T(8,128)(2,1)S(1)}, bf16[8,4096]{1,0:T(8,128)(2,1)S(1)}, u32[]{:S(2)}, u32[]{:S(2)}) collective-permute-start(bf16[8,4096]{1,0:T(8,128)(2,1)S(1)} %fusion.5), channel_id=1, source_target_pairs={{0,4},{1,5},{2,6},{3,7},{4,0},{5,1},{6,2},{7,3},{8,12},{9,13},{10,... | collective-permute-start | bytes 196616 | tf_op jit(solution)/shard_map/ppermute | solution.py:80
  87.6 5.9 %collective-permute-start.27 = (bf16[8,4096]{1,0:T(8,128)(2,1)S(1)}, bf16[8,4096]{1,0:T(8,128)(2,1)S(1)}, u32[]{:S(2)}, u32[]{:S(2)}) collective-permute-start(bf16[8,4096]{1,0:T(8,128)(2,1)S(1)} %add_convert_fusion.8), channel_id=1, source_target_pairs={{0,4},{1,5},{2,6},{3,7},{4,0},{5,1},{6,2},{7,3},{8,12},{9,13},{10,... | collective-permute-start | bytes 196616 | tf_op jit(solution)/shard_map/ppermute | solution.py:80

commit v14 on v13

--- a/solution.py
+++ b/solution.py
@@ -12,7 +12,7 @@
 COLUMNS = 256
 VMEM_MIB = 10
 ROWS_AT_ONCE = 8
-GUARDS = [(2, 5, 0, 7), (1, 5, 2, 4), (1, 4, 0, 6), (0, 8, 2, 7), (0, 9, 2, 8), (0, 10, 2, 9)]
+GUARDS = [(2, 6, 0, 7), (1, 5, 2, 4), (1, 4, 0, 6), (1, 7, 0, 5), (0, 9, 2, 8), (0, 10, 2, 9), (0, 8, 2, 8)]
 
 
 def partner(value, axis, distance):

time: 94.5 us -> 92.7 us (0.981)
  waiting for transfers between devices: 32.2 us -> 26.8 us
  starting transfers between devices: 43.9 us -> 47.5 us
    ppermute x30, waiting for transfers between devices: 32.2 us -> 26.8 us  [permute(): return lax.ppermute(value, AXES, pairs)]
    ppermute x30, starting transfers between devices: 43.9 us -> 47.5 us  [permute(): return lax.ppermute(value, AXES, pairs)]
  transfers between devices with their start and end apart: 30 -> 30, of which waited for: 17 -> 13; matrix products, arithmetic and copies ran while one was open for 2% -> 2% of each run, Pallas kernels for 15% -> 15%
where the time goes in v14:
time: 92.7 us; the launch traced here: 92.4 us
  starting transfers between devices  47.5 us (51%)
  waiting for transfers between devices  26.8 us (29%)
  Pallas kernels  14.8 us (16%)
  other arithmetic  2.1 us (2%)
    ppermute x30, starting transfers between devices, permute(): return lax.ppermute(value, AXES, pairs)  47.5 us
    ppermute x30, waiting for transfers between devices, permute(): return lax.ppermute(value, AXES, pairs)  26.8 us
    pallas_call x3, Pallas kernels, serve_rows(): pl.pallas_call(functools.partial(serve_kernel, top_count), out_shape=(out...  12.4 us
  transfers between devices with their start and end apart: 30, of which 13 were waited for; matrix products, arithmetic and copies ran while one was open for 2% of the time, Pallas kernels for 15%

profile of v14, /device:TPU:0, one launch (start us, length us, event | category | flops | bytes accessed | tf_op | source)
XLA Modules:
  0.0 92.4 jit_solution(5720507281148804909)
XLA Ops:
  0.0 1.0 %pack_rows.1 = (bf16[8,4224]{1,0:T(8,128)(2,1)S(1)}, bf16[8,4224]{1,0:T(8,128)(2,1)S(1)}, bf16[8,4224]{1,0:T(8,128)(2,1)S(1)}) custom-call(bf16[24,4096]{1,0:T(8,128)(2,1)} %tokens_hbm.1, s32[8,24]{1,0:T(8,128)} %bitcast.57, f32[8,24]{1,0:T(8,128)} %bitcast.58), custom_call_target="tpu_custom_call" | custom-call | bytes 393216 | tf_op jit(solution)/shard_map/pack_rows/pallas_call | solution.py:158
  1.0 4.1 %collective-permute-start.7 = (bf16[8,4224]{1,0:T(8,128)(2,1)S(1)}, bf16[8,4224]{1,0:T(8,128)(2,1)S(1)}, u32[]{:S(2)}, u32[]{:S(2)}) collective-permute-start(bf16[8,4224]{1,0:T(8,128)(2,1)S(1)} %get-tuple-element.27), channel_id=1, source_target_pairs={{0,4},{1,5},{2,6},{3,7},{4,0},{5,1},{6,2},{7,3},{8,12},{9,13},{10,... | collective-permute-start | bytes 202760 | tf_op jit(solution)/shard_map/ppermute | solution.py:80
  5.1 0.1 collective-permute-start
  5.2 2.8 %collective-permute-start.18 = (bf16[8,4224]{1,0:T(8,128)(2,1)S(1)}, bf16[8,4224]{1,0:T(8,128)(2,1)S(1)}, u32[]{:S(2)}, u32[]{:S(2)}) collective-permute-start(bf16[8,4224]{1,0:T(8,128)(2,1)S(1)} %get-tuple-element.34), channel_id=1, source_target_pairs={{0,4},{1,5},{2,6},{3,7},{4,0},{5,1},{6,2},{7,3},{8,12},{9,13},{10,... | collective-permute-start | bytes 202760 | tf_op jit(solution)/shard_map/ppermute | solution.py:80
  8.7 0.0 copy-start.2
  8.7 1.4 %served_expert.1.mine = s32[1]{0:T(128)} custom-call(s32[2,16]{1,0:T(2,128)} %bitcast.59, s32[1]{0:T(128)S(6)} %copy.21.flag), custom_call_target="tpu_custom_call" | custom-call | flops 10000000000 | tf_op jit(solution)/shard_map/served_expert/pallas_call | solution.py:111
  10.2 3.7 %collective-permute-start.8 = (bf16[16,4224]{1,0:T(8,128)(2,1)S(1)}, bf16[16,4224]{1,0:T(8,128)(2,1)S(1)}, u32[]{:S(2)}, u32[]{:S(2)}) collective-permute-start(bf16[16,4224]{1,0:T(8,128)(2,1)S(1)} %pad_maximum_fusion.8), channel_id=1, source_target_pairs={{0,1},{1,0},{2,3},{3,2},{4,5},{5,4},{6,7},{7,6},{8,24},{9,25},{10,... | collective-permute-start | bytes 405512 | tf_op jit(solution)/shard_map/ppermute | solution.py:80
  13.8 0.3 collective-permute-start.1
  14.1 0.5 collective-permute-done.18
  14.6 1.4 %collective-permute-start.19 = (bf16[16,4224]{1,0:T(8,128)(2,1)S(1)}, bf16[16,4224]{1,0:T(8,128)(2,1)S(1)}, u32[]{:S(2)}, u32[]{:S(2)}) collective-permute-start(bf16[16,4224]{1,0:T(8,128)(2,1)S(1)} %pad_maximum_fusion.9), channel_id=1, source_target_pairs={{0,2},{1,3},{2,0},{3,1},{4,6},{5,7},{6,4},{7,5},{8,10},{9,11},{10,... | collective-permute-start | bytes 405512 | tf_op jit(solution)/shard_map/ppermute | solution.py:80
  16.1 0.8 collective-permute-done.8
  16.8 2.1 %collective-permute-start.9 = (bf16[32,4224]{1,0:T(8,128)(2,1)S(1)}, bf16[32,4224]{1,0:T(8,128)(2,1)S(1)}, u32[]{:S(2)}, u32[]{:S(2)}) collective-permute-start(bf16[32,4224]{1,0:T(8,128)(2,1)S(1)} %pad_maximum_fusion.4), channel_id=1, source_target_pairs={{0,16},{1,17},{2,18},{3,19},{4,20},{5,21},{6,22},{7,23},{8,9},{9,8... | collective-permute-start | bytes 811016 | tf_op jit(solution)/shard_map/ppermute | solution.py:80
  18.9 0.9 %collective-permute-done.1 = bf16[16,4224]{1,0:T(8,128)(2,1)S(1)} collective-permute-done((bf16[16,4224]{1,0:T(8,128)(2,1)S(1)}, bf16[16,4224]{1,0:T(8,128)(2,1)S(1)}, u32[]{:S(2)}, u32[]{:S(2)}) %collective-permute-start.1) | collective-permute-done | bytes 135200 | tf_op jit(solution)/shard_map/ppermute | solution.py:80
  19.9 1.9 %collective-permute-start.2 = (bf16[32,4224]{1,0:T(8,128)(2,1)S(1)}, bf16[32,4224]{1,0:T(8,128)(2,1)S(1)}, u32[]{:S(2)}, u32[]{:S(2)}) collective-permute-start(bf16[32,4224]{1,0:T(8,128)(2,1)S(1)} %pad_maximum_fusion.3), channel_id=1, source_target_pairs={{0,1},{1,0},{2,3},{3,2},{4,5},{5,4},{6,7},{7,6},{8,24},{9,25},{10,... | collective-permute-start | bytes 811016 | tf_op jit(solution)/shard_map/ppermute | solution.py:80
  21.8 1.4 %collective-permute-start.20 = (bf16[32,4224]{1,0:T(8,128)(2,1)S(1)}, bf16[32,4224]{1,0:T(8,128)(2,1)S(1)}, u32[]{:S(2)}, u32[]{:S(2)}) collective-permute-start(bf16[32,4224]{1,0:T(8,128)(2,1)S(1)} %pad_maximum_fusion.5), channel_id=1, source_target_pairs={{0,1},{1,0},{2,3},{3,2},{4,5},{5,4},{6,7},{7,6},{8,24},{9,25},{10,... | collective-permute-start | bytes 811016 | tf_op jit(solution)/shard_map/ppermute | solution.py:80
  23.3 2.9 %collective-permute-done.9 = bf16[32,4224]{1,0:T(8,128)(2,1)S(1)} collective-permute-done((bf16[32,4224]{1,0:T(8,128)(2,1)S(1)}, bf16[32,4224]{1,0:T(8,128)(2,1)S(1)}, u32[]{:S(2)}, u32[]{:S(2)}) %collective-permute-start.9) | collective-permute-done | bytes 270368 | tf_op jit(solution)/shard_map/ppermute | solution.py:80
  26.3 0.8 collective-permute-start.10
  27.1 1.6 %collective-permute-start.3 = (bf16[64,4224]{1,0:T(8,128)(2,1)S(1)}, bf16[64,4224]{1,0:T(8,128)(2,1)S(1)}, u32[]{:S(2)}, u32[]{:S(2)}) collective-permute-start(bf16[64,4224]{1,0:T(8,128)(2,1)S(1)} %pad_maximum_fusion), channel_id=1, source_target_pairs={{0,16},{1,17},{2,18},{3,19},{4,20},{5,21},{6,22},{7,23},{8,9},{9,8... | collective-permute-start | bytes 1622024 | tf_op jit(solution)/shard_map/ppermute | solution.py:80
  28.7 1.9 %collective-permute-done.20 = bf16[32,4224]{1,0:T(8,128)(2,1)S(1)} collective-permute-done((bf16[32,4224]{1,0:T(8,128)(2,1)S(1)}, bf16[32,4224]{1,0:T(8,128)(2,1)S(1)}, u32[]{:S(2)}, u32[]{:S(2)}) %collective-permute-start.20) | collective-permute-done | bytes 270368 | tf_op jit(solution)/shard_map/ppermute | solution.py:80
  30.6 2.4 %collective-permute-start.21 = (bf16[64,4224]{1,0:T(8,128)(2,1)S(1)}, bf16[64,4224]{1,0:T(8,128)(2,1)S(1)}, u32[]{:S(2)}, u32[]{:S(2)}) collective-permute-start(bf16[64,4224]{1,0:T(8,128)(2,1)S(1)} %pad_maximum_fusion.2), channel_id=1, source_target_pairs={{0,16},{1,17},{2,18},{3,19},{4,20},{5,21},{6,22},{7,23},{8,9},{9,8... | collective-permute-start | bytes 1622024 | tf_op jit(solution)/shard_map/ppermute | solution.py:80
  33.0 3.5 %collective-permute-done.3 = bf16[64,4224]{1,0:T(8,128)(2,1)S(1)} collective-permute-done((bf16[64,4224]{1,0:T(8,128)(2,1)S(1)}, bf16[64,4224]{1,0:T(8,128)(2,1)S(1)}, u32[]{:S(2)}, u32[]{:S(2)}) %collective-permute-start.3) | collective-permute-done | bytes 540704 | tf_op jit(solution)/shard_map/ppermute | solution.py:80
  36.6 0.1 collective-permute-start.4
  36.7 0.1 constant_dynamic-update-slice_fusion.5.own
  36.8 0.6 collective-permute-start.11
  37.3 2.0 %collective-permute-done.4.sib = bf16[128,4224]{1,0:T(8,128)(2,1)S(1)} collective-permute-done((bf16[128,4224]{1,0:T(8,128)(2,1)S(1)}, bf16[128,4224]{1,0:T(8,128)(2,1)S(1)}, u32[]{:S(2)}, u32[]{:S(2)}) %collective-permute-start.4) | collective-permute-done | bytes 1081376 | tf_op jit(solution)/shard_map/ppermute | solution.py:80
  39.4 4.1 %serve_rows.3 = (bf16[128,4096]{1,0:T(8,128)(2,1)S(1)}, bf16[128,4096]{1,0:T(8,128)(2,1)S(1)}) custom-call(s32[1]{0:T(128)} %served_expert.1.mine, bf16[128,4224]{1,0:T(8,128)(2,1)S(1)} %constant_dynamic-update-slice_fusion.own, bf16[128,4224]{1,0:T(8,128)(2,1)S(1)} %collective-permute-done.4.sib, bf16[4096,512]{1,0:T(8,128)(2,1)S(1)} %bitcast.37, ...), custom_call_target="tpu_custom_call" | custom-call | flops 3221225472 | bytes 16777216 | tf_op jit(solution)/shard_map/serve_rows/pallas_call | solution.py:207
  43.5 0.2 collective-permute-start.5
  43.7 0.1 constant_dynamic-update-slice_fusion.10.own
  43.8 0.4 collective-permute-start.22
  44.2 4.1 %serve_rows.4 = (bf16[128,4096]{1,0:T(8,128)(2,1)S(1)}, bf16[128,4096]{1,0:T(8,128)(2,1)S(1)}) custom-call(s32[1]{0:T(128)} %served_expert.1.mine, bf16[128,4224]{1,0:T(8,128)(2,1)S(1)} %constant_dynamic-update-slice_fusion.5.own, bf16[128,4224]{1,0:T(8,128)(2,1)S(1)} %collective-permute-done.11.sib, bf16[4096,512]{1,0:T(8,128)(2,1)S(1)} %bitcast.38, ...), custom_call_target="tpu_custom_call" | custom-call | flops 3221225472 | bytes 16777216 | tf_op jit(solution)/shard_map/serve_rows/pallas_call | solution.py:207
  48.4 0.2 collective-permute-start.12
  48.6 0.1 add_convert_fusion.2
  48.7 1.6 %collective-permute-start.6 = (bf16[64,4096]{1,0:T(8,128)(2,1)S(1)}, bf16[64,4096]{1,0:T(8,128)(2,1)S(1)}, u32[]{:S(2)}, u32[]{:S(2)}) collective-permute-start(bf16[64,4096]{1,0:T(8,128)(2,1)S(1)} %add_convert_fusion.2), channel_id=1, source_target_pairs={{0,16},{1,17},{2,18},{3,19},{4,20},{5,21},{6,22},{7,23},{8,9},{9,8... | collective-permute-start | bytes 1572872 | tf_op jit(solution)/shard_map/ppermute | solution.py:80
  50.3 4.1 %serve_rows.5 = (bf16[128,4096]{1,0:T(8,128)(2,1)S(1)}, bf16[128,4096]{1,0:T(8,128)(2,1)S(1)}) custom-call(s32[1]{0:T(128)} %served_expert.1.mine, bf16[128,4224]{1,0:T(8,128)(2,1)S(1)} %constant_dynamic-update-slice_fusion.10.own, bf16[128,4224]{1,0:T(8,128)(2,1)S(1)} %collective-permute-done.22.sib, bf16[4096,512]{1,0:T(8,128)(2,1)S(1)} %bitcast.39, ...), custom_call_target="tpu_custom_call" | custom-call | flops 3221225472 | bytes 16777216 | tf_op jit(solution)/shard_map/serve_rows/pallas_call | solution.py:207
  54.4 0.2 collective-permute-start.23
  54.6 0.1 add_convert_fusion.1
  54.7 1.6 %collective-permute-start.13 = (bf16[64,4096]{1,0:T(8,128)(2,1)S(1)}, bf16[64,4096]{1,0:T(8,128)(2,1)S(1)}, u32[]{:S(2)}, u32[]{:S(2)}) collective-permute-start(bf16[64,4096]{1,0:T(8,128)(2,1)S(1)} %bitcast.56), channel_id=1, source_target_pairs={{0,16},{1,17},{2,18},{3,19},{4,20},{5,21},{6,22},{7,23},{8,9},{9,8... | collective-permute-start | bytes 1572872 | tf_op jit(solution)/shard_map/ppermute | solution.py:80
  56.3 0.1 convert_add_fusion
  56.3 0.8 collective-permute-done.23
  57.1 0.1 add_convert_fusion
  57.3 1.3 %collective-permute-start.24 = (bf16[64,4096]{1,0:T(8,128)(2,1)S(1)}, bf16[64,4096]{1,0:T(8,128)(2,1)S(1)}, u32[]{:S(2)}, u32[]{:S(2)}) collective-permute-start(bf16[64,4096]{1,0:T(8,128)(2,1)S(1)} %add_convert_fusion), channel_id=1, source_target_pairs={{0,16},{1,17},{2,18},{3,19},{4,20},{5,21},{6,22},{7,23},{8,9},{9,8... | collective-permute-start | bytes 1572872 | tf_op jit(solution)/shard_map/ppermute | solution.py:80
  58.6 5.4 %collective-permute-done.13 = bf16[64,4096]{1,0:T(8,128)(2,1)S(1)} collective-permute-done((bf16[64,4096]{1,0:T(8,128)(2,1)S(1)}, bf16[64,4096]{1,0:T(8,128)(2,1)S(1)}, u32[]{:S(2)}, u32[]{:S(2)}) %collective-permute-start.13) | collective-permute-done | bytes 524320 | tf_op jit(solution)/shard_map/ppermute | solution.py:80
  64.0 1.9 %collective-permute-start.16 = (bf16[32,4096]{1,0:T(8,128)(2,1)S(1)}, bf16[32,4096]{1,0:T(8,128)(2,1)S(1)}, u32[]{:S(2)}, u32[]{:S(2)}) collective-permute-start(bf16[32,4096]{1,0:T(8,128)(2,1)S(1)} %fusion), channel_id=1, source_target_pairs={{0,2},{1,3},{2,0},{3,1},{4,6},{5,7},{6,4},{7,5},{8,10},{9,11},{10,... | collective-permute-start | bytes 786440 | tf_op jit(solution)/shard_map/ppermute | solution.py:80
  65.9 0.1 add_convert_fusion.4
  66.0 1.5 %collective-permute-start.14 = (bf16[32,4096]{1,0:T(8,128)(2,1)S(1)}, bf16[32,4096]{1,0:T(8,128)(2,1)S(1)}, u32[]{:S(2)}, u32[]{:S(2)}) collective-permute-start(bf16[32,4096]{1,0:T(8,128)(2,1)S(1)} %add_convert_fusion.4), channel_id=1, source_target_pairs={{0,1},{1,0},{2,3},{3,2},{4,5},{5,4},{6,7},{7,6},{8,24},{9,25},{10,... | collective-permute-start | bytes 786440 | tf_op jit(solution)/shard_map/ppermute | solution.py:80
  67.5 3.7 %collective-permute-done.24 = bf16[64,4096]{1,0:T(8,128)(2,1)S(1)} collective-permute-done((bf16[64,4096]{1,0:T(8,128)(2,1)S(1)}, bf16[64,4096]{1,0:T(8,128)(2,1)S(1)}, u32[]{:S(2)}, u32[]{:S(2)}) %collective-permute-start.24) | collective-permute-done | bytes 524320 | tf_op jit(solution)/shard_map/ppermute | solution.py:80
  71.2 0.1 add_convert_fusion.3
  71.3 1.4 %collective-permute-start.25 = (bf16[32,4096]{1,0:T(8,128)(2,1)S(1)}, bf16[32,4096]{1,0:T(8,128)(2,1)S(1)}, u32[]{:S(2)}, u32[]{:S(2)}) collective-permute-start(bf16[32,4096]{1,0:T(8,128)(2,1)S(1)} %add_convert_fusion.3), channel_id=1, source_target_pairs={{0,1},{1,0},{2,3},{3,2},{4,5},{5,4},{6,7},{7,6},{8,24},{9,25},{10,... | collective-permute-start | bytes 786440 | tf_op jit(solution)/shard_map/ppermute | solution.py:80
  72.7 0.1 fusion.2
  72.8 0.8 collective-permute-start.28
  73.6 0.1 add_convert_fusion.6
  73.6 3.1 %collective-permute-start.15 = (bf16[16,4096]{1,0:T(8,128)(2,1)S(1)}, bf16[16,4096]{1,0:T(8,128)(2,1)S(1)}, u32[]{:S(2)}, u32[]{:S(2)}) collective-permute-start(bf16[16,4096]{1,0:T(8,128)(2,1)S(1)} %add_convert_fusion.6), channel_id=1, source_target_pairs={{0,2},{1,3},{2,0},{3,1},{4,6},{5,7},{6,4},{7,5},{8,10},{9,11},{10,... | collective-permute-start | bytes 393224 | tf_op jit(solution)/shard_map/ppermute | solution.py:80
  76.7 1.0 %collective-permute-done.25 = bf16[32,4096]{1,0:T(8,128)(2,1)S(1)} collective-permute-done((bf16[32,4096]{1,0:T(8,128)(2,1)S(1)}, bf16[32,4096]{1,0:T(8,128)(2,1)S(1)}, u32[]{:S(2)}, u32[]{:S(2)}) %collective-permute-start.25) | collective-permute-done | bytes 262176 | tf_op jit(solution)/shard_map/ppermute | solution.py:80
  77.7 0.1 add_convert_fusion.5
  77.8 3.1 %collective-permute-start.26 = (bf16[16,4096]{1,0:T(8,128)(2,1)S(1)}, bf16[16,4096]{1,0:T(8,128)(2,1)S(1)}, u32[]{:S(2)}, u32[]{:S(2)}) collective-permute-start(bf16[16,4096]{1,0:T(8,128)(2,1)S(1)} %add_convert_fusion.5), channel_id=1, source_target_pairs={{0,2},{1,3},{2,0},{3,1},{4,6},{5,7},{6,4},{7,5},{8,10},{9,11},{10,... | collective-permute-start | bytes 393224 | tf_op jit(solution)/shard_map/ppermute | solution.py:80
  81.0 2.9 %collective-permute-start.29 = (bf16[8,4096]{1,0:T(8,128)(2,1)S(1)}, bf16[8,4096]{1,0:T(8,128)(2,1)S(1)}, u32[]{:S(2)}, u32[]{:S(2)}) collective-permute-start(bf16[8,4096]{1,0:T(8,128)(2,1)S(1)} %fusion.5), channel_id=1, source_target_pairs={{0,4},{1,5},{2,6},{3,7},{4,0},{5,1},{6,2},{7,3},{8,12},{9,13},{10,... | collective-permute-start | bytes 196616 | tf_op jit(solution)/shard_map/ppermute | solution.py:80
  83.9 0.8 collective-permute-start.17
  84.8 3.5 %collective-permute-start.27 = (bf16[8,4096]{1,0:T(8,128)(2,1)S(1)}, bf16[8,4096]{1,0:T(8,128)(2,1)S(1)}, u32[]{:S(2)}, u32[]{:S(2)}) collective-permute-start(bf16[8,4096]{1,0:T(8,128)(2,1)S(1)} %add_convert_fusion.8), channel_id=1, source_target_pairs={{0,4},{1,5},{2,6},{3,7},{4,0},{5,1},{6,2},{7,3},{8,12},{9,13},{10,... | collective-permute-start | bytes 196616 | tf_op jit(solution)/shard_map/ppermute | solution.py:80
  88.3 0.1 fusion.9
  88.3 2.0 %collective-permute-done.17 = bf16[8,4096]{1,0:T(8,128)(2,1)S(1)} collective-permute-done((bf16[8,4096]{1,0:T(8,128)(2,1)S(1)}, bf16[8,4096]{1,0:T(8,128)(2,1)S(1)}, u32[]{:S(2)}, u32[]{:S(2)}) %collective-permute-start.17) | collective-permute-done | bytes 65568 | tf_op jit(solution)/shard_map/ppermute | solution.py:80
  90.3 0.1 add_convert_fusion.9
  90.4 1.3 %collective-permute-done.27 = bf16[8,4096]{1,0:T(8,128)(2,1)S(1)} collective-permute-done((bf16[8,4096]{1,0:T(8,128)(2,1)S(1)}, bf16[8,4096]{1,0:T(8,128)(2,1)S(1)}, u32[]{:S(2)}, u32[]{:S(2)}) %collective-permute-start.27) | collective-permute-done | bytes 65568 | tf_op jit(solution)/shard_map/ppermute | solution.py:80
  91.7 0.1 add_convert_fusion.7
  91.7 0.7 pad_maximum_fusion.6
  (47 shorter events, 0.7 us)
Async XLA Ops:
  1.0 9.1 %collective-permute-start.7 = (bf16[8,4224]{1,0:T(8,128)(2,1)S(1)}, bf16[8,4224]{1,0:T(8,128)(2,1)S(1)}, u32[]{:S(2)}, u32[]{:S(2)}) collective-permute-start(bf16[8,4224]{1,0:T(8,128)(2,1)S(1)} %get-tuple-element.27), channel_id=1, source_target_pairs={{0,4},{1,5},{2,6},{3,7},{4,0},{5,1},{6,2},{7,3},{8,12},{9,13},{10,... | collective-permute-start | bytes 202760 | tf_op jit(solution)/shard_map/ppermute | solution.py:80
  5.1 8.7 %collective-permute-start = (bf16[8,4224]{1,0:T(8,128)(2,1)S(1)}, bf16[8,4224]{1,0:T(8,128)(2,1)S(1)}, u32[]{:S(2)}, u32[]{:S(2)}) collective-permute-start(bf16[8,4224]{1,0:T(8,128)(2,1)S(1)} %get-tuple-element.23), channel_id=1, source_target_pairs={{0,4},{1,5},{2,6},{3,7},{4,0},{5,1},{6,2},{7,3},{8,12},{9,13},{10,... | collective-permute-start | bytes 202760 | tf_op jit(solution)/shard_map/ppermute | solution.py:80
  5.2 9.4 %collective-permute-start.18 = (bf16[8,4224]{1,0:T(8,128)(2,1)S(1)}, bf16[8,4224]{1,0:T(8,128)(2,1)S(1)}, u32[]{:S(2)}, u32[]{:S(2)}) collective-permute-start(bf16[8,4224]{1,0:T(8,128)(2,1)S(1)} %get-tuple-element.34), channel_id=1, source_target_pairs={{0,4},{1,5},{2,6},{3,7},{4,0},{5,1},{6,2},{7,3},{8,12},{9,13},{10,... | collective-permute-start | bytes 202760 | tf_op jit(solution)/shard_map/ppermute | solution.py:80
  8.7 30.6 %copy-start.2 = (bf16[1,512,4096]{2,1,0:T(8,128)(2,1)S(1)}, bf16[1,512,4096]{2,1,0:T(8,128)(2,1)}, u32[]{:S(2)}) copy-start(bf16[1,512,4096]{2,1,0:T(8,128)(2,1)} %param.15) | copy-start | bytes 12582916
  10.2 6.7 %collective-permute-start.8 = (bf16[16,4224]{1,0:T(8,128)(2,1)S(1)}, bf16[16,4224]{1,0:T(8,128)(2,1)S(1)}, u32[]{:S(2)}, u32[]{:S(2)}) collective-permute-start(bf16[16,4224]{1,0:T(8,128)(2,1)S(1)} %pad_maximum_fusion.8), channel_id=1, source_target_pairs={{0,1},{1,0},{2,3},{3,2},{4,5},{5,4},{6,7},{7,6},{8,24},{9,25},{10,... | collective-permute-start | bytes 405512 | tf_op jit(solution)/shard_map/ppermute | solution.py:80
  13.8 6.0 %collective-permute-start.1 = (bf16[16,4224]{1,0:T(8,128)(2,1)S(1)}, bf16[16,4224]{1,0:T(8,128)(2,1)S(1)}, u32[]{:S(2)}, u32[]{:S(2)}) collective-permute-start(bf16[16,4224]{1,0:T(8,128)(2,1)S(1)} %pad_maximum_fusion.7), channel_id=1, source_target_pairs={{0,2},{1,3},{2,0},{3,1},{4,6},{5,7},{6,4},{7,5},{8,10},{9,11},{10,... | collective-permute-start | bytes 405512 | tf_op jit(solution)/shard_map/ppermute | solution.py:80
  14.6 7.2 %collective-permute-start.19 = (bf16[16,4224]{1,0:T(8,128)(2,1)S(1)}, bf16[16,4224]{1,0:T(8,128)(2,1)S(1)}, u32[]{:S(2)}, u32[]{:S(2)}) collective-permute-start(bf16[16,4224]{1,0:T(8,128)(2,1)S(1)} %pad_maximum_fusion.9), channel_id=1, source_target_pairs={{0,2},{1,3},{2,0},{3,1},{4,6},{5,7},{6,4},{7,5},{8,10},{9,11},{10,... | collective-permute-start | bytes 405512 | tf_op jit(solution)/shard_map/ppermute | solution.py:80
  16.8 22.5 %copy-start.1 = (bf16[1,4096,512]{2,1,0:T(8,128)(2,1)S(1)}, bf16[1,4096,512]{2,1,0:T(8,128)(2,1)}, u32[]{:S(2)}) copy-start(bf16[1,4096,512]{2,1,0:T(8,128)(2,1)} %param.14) | copy-start | bytes 12582916
  16.8 9.4 %collective-permute-start.9 = (bf16[32,4224]{1,0:T(8,128)(2,1)S(1)}, bf16[32,4224]{1,0:T(8,128)(2,1)S(1)}, u32[]{:S(2)}, u32[]{:S(2)}) collective-permute-start(bf16[32,4224]{1,0:T(8,128)(2,1)S(1)} %pad_maximum_fusion.4), channel_id=1, source_target_pairs={{0,16},{1,17},{2,18},{3,19},{4,20},{5,21},{6,22},{7,23},{8,9},{9,8... | collective-permute-start | bytes 811016 | tf_op jit(solution)/shard_map/ppermute | solution.py:80
  19.9 7.2 %collective-permute-start.2 = (bf16[32,4224]{1,0:T(8,128)(2,1)S(1)}, bf16[32,4224]{1,0:T(8,128)(2,1)S(1)}, u32[]{:S(2)}, u32[]{:S(2)}) collective-permute-start(bf16[32,4224]{1,0:T(8,128)(2,1)S(1)} %pad_maximum_fusion.3), channel_id=1, source_target_pairs={{0,1},{1,0},{2,3},{3,2},{4,5},{5,4},{6,7},{7,6},{8,24},{9,25},{10,... | collective-permute-start | bytes 811016 | tf_op jit(solution)/shard_map/ppermute | solution.py:80
  21.8 8.7 %collective-permute-start.20 = (bf16[32,4224]{1,0:T(8,128)(2,1)S(1)}, bf16[32,4224]{1,0:T(8,128)(2,1)S(1)}, u32[]{:S(2)}, u32[]{:S(2)}) collective-permute-start(bf16[32,4224]{1,0:T(8,128)(2,1)S(1)} %pad_maximum_fusion.5), channel_id=1, source_target_pairs={{0,1},{1,0},{2,3},{3,2},{4,5},{5,4},{6,7},{7,6},{8,24},{9,25},{10,... | collective-permute-start | bytes 811016 | tf_op jit(solution)/shard_map/ppermute | solution.py:80
  26.3 10.4 %collective-permute-start.10 = (bf16[64,4224]{1,0:T(8,128)(2,1)S(1)}, bf16[64,4224]{1,0:T(8,128)(2,1)S(1)}, u32[]{:S(2)}, u32[]{:S(2)}) collective-permute-start(bf16[64,4224]{1,0:T(8,128)(2,1)S(1)} %pad_maximum_fusion.1), channel_id=1, source_target_pairs={{0,2},{1,3},{2,0},{3,1},{4,6},{5,7},{6,4},{7,5},{8,10},{9,11},{10,... | collective-permute-start | bytes 1622024 | tf_op jit(solution)/shard_map/ppermute | solution.py:80
  27.1 9.4 %collective-permute-start.3 = (bf16[64,4224]{1,0:T(8,128)(2,1)S(1)}, bf16[64,4224]{1,0:T(8,128)(2,1)S(1)}, u32[]{:S(2)}, u32[]{:S(2)}) collective-permute-start(bf16[64,4224]{1,0:T(8,128)(2,1)S(1)} %pad_maximum_fusion), channel_id=1, source_target_pairs={{0,16},{1,17},{2,18},{3,19},{4,20},{5,21},{6,22},{7,23},{8,9},{9,8... | collective-permute-start | bytes 1622024 | tf_op jit(solution)/shard_map/ppermute | solution.py:80
  30.6 8.8 %copy-start = (bf16[1,4096,512]{2,1,0:T(8,128)(2,1)S(1)}, bf16[1,4096,512]{2,1,0:T(8,128)(2,1)}, u32[]{:S(2)}) copy-start(bf16[1,4096,512]{2,1,0:T(8,128)(2,1)} %param.13) | copy-start | bytes 12582916
  30.6 13.1 %collective-permute-start.21 = (bf16[64,4224]{1,0:T(8,128)(2,1)S(1)}, bf16[64,4224]{1,0:T(8,128)(2,1)S(1)}, u32[]{:S(2)}, u32[]{:S(2)}) collective-permute-start(bf16[64,4224]{1,0:T(8,128)(2,1)S(1)} %pad_maximum_fusion.2), channel_id=1, source_target_pairs={{0,16},{1,17},{2,18},{3,19},{4,20},{5,21},{6,22},{7,23},{8,9},{9,8... | collective-permute-start | bytes 1622024 | tf_op jit(solution)/shard_map/ppermute | solution.py:80
  36.6 2.8 %collective-permute-start.4 = (bf16[128,4224]{1,0:T(8,128)(2,1)S(1)}, bf16[128,4224]{1,0:T(8,128)(2,1)S(1)}, u32[]{:S(2)}, u32[]{:S(2)}) collective-permute-start(bf16[128,4224]{1,0:T(8,128)(2,1)S(1)} %constant_dynamic-update-slice_fusion.own), channel_id=1, source_target_pairs={{0,8},{1,9},{2,10},{3,11},{4,12},{5,13},{6,14},{7,15},{8,0},{9,1},... | collective-permute-start | bytes 3244040 | tf_op jit(solution)/shard_map/ppermute | solution.py:80
  36.8 7.5 %collective-permute-start.11 = (bf16[128,4224]{1,0:T(8,128)(2,1)S(1)}, bf16[128,4224]{1,0:T(8,128)(2,1)S(1)}, u32[]{:S(2)}, u32[]{:S(2)}) collective-permute-start(bf16[128,4224]{1,0:T(8,128)(2,1)S(1)} %constant_dynamic-update-slice_fusion.5.own), channel_id=1, source_target_pairs={{0,8},{1,9},{2,10},{3,11},{4,12},{5,13},{6,14},{7,15},{8,0},{9,1},... | collective-permute-start | bytes 3244040 | tf_op jit(solution)/shard_map/ppermute | solution.py:80
  43.5 4.9 %collective-permute-start.5 = (bf16[128,4096]{1,0:T(8,128)(2,1)S(1)}, bf16[128,4096]{1,0:T(8,128)(2,1)S(1)}, u32[]{:S(2)}, u32[]{:S(2)}) collective-permute-start(bf16[128,4096]{1,0:T(8,128)(2,1)S(1)} %get-tuple-element.26), channel_id=1, source_target_pairs={{0,8},{1,9},{2,10},{3,11},{4,12},{5,13},{6,14},{7,15},{8,0},{9,1},... | collective-permute-start | bytes 3145736 | tf_op jit(solution)/shard_map/ppermute | solution.py:80
  43.8 6.5 %collective-permute-start.22 = (bf16[128,4224]{1,0:T(8,128)(2,1)S(1)}, bf16[128,4224]{1,0:T(8,128)(2,1)S(1)}, u32[]{:S(2)}, u32[]{:S(2)}) collective-permute-start(bf16[128,4224]{1,0:T(8,128)(2,1)S(1)} %constant_dynamic-update-slice_fusion.10.own), channel_id=1, source_target_pairs={{0,8},{1,9},{2,10},{3,11},{4,12},{5,13},{6,14},{7,15},{8,0},{9,1},... | collective-permute-start | bytes 3244040 | tf_op jit(solution)/shard_map/ppermute | solution.py:80
  48.4 6.2 %collective-permute-start.12 = (bf16[128,4096]{1,0:T(8,128)(2,1)S(1)}, bf16[128,4096]{1,0:T(8,128)(2,1)S(1)}, u32[]{:S(2)}, u32[]{:S(2)}) collective-permute-start(bf16[128,4096]{1,0:T(8,128)(2,1)S(1)} %get-tuple-element.30), channel_id=1, source_target_pairs={{0,8},{1,9},{2,10},{3,11},{4,12},{5,13},{6,14},{7,15},{8,0},{9,1},... | collective-permute-start | bytes 3145736 | tf_op jit(solution)/shard_map/ppermute | solution.py:80
  48.7 17.2 %collective-permute-start.6 = (bf16[64,4096]{1,0:T(8,128)(2,1)S(1)}, bf16[64,4096]{1,0:T(8,128)(2,1)S(1)}, u32[]{:S(2)}, u32[]{:S(2)}) collective-permute-start(bf16[64,4096]{1,0:T(8,128)(2,1)S(1)} %add_convert_fusion.2), channel_id=1, source_target_pairs={{0,16},{1,17},{2,18},{3,19},{4,20},{5,21},{6,22},{7,23},{8,9},{9,8... | collective-permute-start | bytes 1572872 | tf_op jit(solution)/shard_map/ppermute | solution.py:80
  54.4 2.7 %collective-permute-start.23 = (bf16[128,4096]{1,0:T(8,128)(2,1)S(1)}, bf16[128,4096]{1,0:T(8,128)(2,1)S(1)}, u32[]{:S(2)}, u32[]{:S(2)}) collective-permute-start(bf16[128,4096]{1,0:T(8,128)(2,1)S(1)} %get-tuple-element.39), channel_id=1, source_target_pairs={{0,8},{1,9},{2,10},{3,11},{4,12},{5,13},{6,14},{7,15},{8,0},{9,1},... | collective-permute-start | bytes 3145736 | tf_op jit(solution)/shard_map/ppermute | solution.py:80
  54.7 9.2 %collective-permute-start.13 = (bf16[64,4096]{1,0:T(8,128)(2,1)S(1)}, bf16[64,4096]{1,0:T(8,128)(2,1)S(1)}, u32[]{:S(2)}, u32[]{:S(2)}) collective-permute-start(bf16[64,4096]{1,0:T(8,128)(2,1)S(1)} %bitcast.56), channel_id=1, source_target_pairs={{0,16},{1,17},{2,18},{3,19},{4,20},{5,21},{6,22},{7,23},{8,9},{9,8... | collective-permute-start | bytes 1572872 | tf_op jit(solution)/shard_map/ppermute | solution.py:80
  57.3 13.9 %collective-permute-start.24 = (bf16[64,4096]{1,0:T(8,128)(2,1)S(1)}, bf16[64,4096]{1,0:T(8,128)(2,1)S(1)}, u32[]{:S(2)}, u32[]{:S(2)}) collective-permute-start(bf16[64,4096]{1,0:T(8,128)(2,1)S(1)} %add_convert_fusion), channel_id=1, source_target_pairs={{0,16},{1,17},{2,18},{3,19},{4,20},{5,21},{6,22},{7,23},{8,9},{9,8... | collective-permute-start | bytes 1572872 | tf_op jit(solution)/shard_map/ppermute | solution.py:80
  64.0 8.7 %collective-permute-start.16 = (bf16[32,4096]{1,0:T(8,128)(2,1)S(1)}, bf16[32,4096]{1,0:T(8,128)(2,1)S(1)}, u32[]{:S(2)}, u32[]{:S(2)}) collective-permute-start(bf16[32,4096]{1,0:T(8,128)(2,1)S(1)} %fusion), channel_id=1, source_target_pairs={{0,2},{1,3},{2,0},{3,1},{4,6},{5,7},{6,4},{7,5},{8,10},{9,11},{10,... | collective-permute-start | bytes 786440 | tf_op jit(solution)/shard_map/ppermute | solution.py:80
  66.0 7.6 %collective-permute-start.14 = (bf16[32,4096]{1,0:T(8,128)(2,1)S(1)}, bf16[32,4096]{1,0:T(8,128)(2,1)S(1)}, u32[]{:S(2)}, u32[]{:S(2)}) collective-permute-start(bf16[32,4096]{1,0:T(8,128)(2,1)S(1)} %add_convert_fusion.4), channel_id=1, source_target_pairs={{0,1},{1,0},{2,3},{3,2},{4,5},{5,4},{6,7},{7,6},{8,24},{9,25},{10,... | collective-permute-start | bytes 786440 | tf_op jit(solution)/shard_map/ppermute | solution.py:80
  71.3 6.4 %collective-permute-start.25 = (bf16[32,4096]{1,0:T(8,128)(2,1)S(1)}, bf16[32,4096]{1,0:T(8,128)(2,1)S(1)}, u32[]{:S(2)}, u32[]{:S(2)}) collective-permute-start(bf16[32,4096]{1,0:T(8,128)(2,1)S(1)} %add_convert_fusion.3), channel_id=1, source_target_pairs={{0,1},{1,0},{2,3},{3,2},{4,5},{5,4},{6,7},{7,6},{8,24},{9,25},{10,... | collective-permute-start | bytes 786440 | tf_op jit(solution)/shard_map/ppermute | solution.py:80
  72.8 8.2 %collective-permute-start.28 = (bf16[16,4096]{1,0:T(8,128)(2,1)S(1)}, bf16[16,4096]{1,0:T(8,128)(2,1)S(1)}, u32[]{:S(2)}, u32[]{:S(2)}) collective-permute-start(bf16[16,4096]{1,0:T(8,128)(2,1)S(1)} %fusion.2), channel_id=1, source_target_pairs={{0,1},{1,0},{2,3},{3,2},{4,5},{5,4},{6,7},{7,6},{8,24},{9,25},{10,... | collective-permute-start | bytes 393224 | tf_op jit(solution)/shard_map/ppermute | solution.py:80
  73.6 10.2 %collective-permute-start.15 = (bf16[16,4096]{1,0:T(8,128)(2,1)S(1)}, bf16[16,4096]{1,0:T(8,128)(2,1)S(1)}, u32[]{:S(2)}, u32[]{:S(2)}) collective-permute-start(bf16[16,4096]{1,0:T(8,128)(2,1)S(1)} %add_convert_fusion.6), channel_id=1, source_target_pairs={{0,2},{1,3},{2,0},{3,1},{4,6},{5,7},{6,4},{7,5},{8,10},{9,11},{10,... | collective-permute-start | bytes 393224 | tf_op jit(solution)/shard_map/ppermute | solution.py:80
  77.8 6.9 %collective-permute-start.26 = (bf16[16,4096]{1,0:T(8,128)(2,1)S(1)}, bf16[16,4096]{1,0:T(8,128)(2,1)S(1)}, u32[]{:S(2)}, u32[]{:S(2)}) collective-permute-start(bf16[16,4096]{1,0:T(8,128)(2,1)S(1)} %add_convert_fusion.5), channel_id=1, source_target_pairs={{0,2},{1,3},{2,0},{3,1},{4,6},{5,7},{6,4},{7,5},{8,10},{9,11},{10,... | collective-permute-start | bytes 393224 | tf_op jit(solution)/shard_map/ppermute | solution.py:80
  81.0 7.3 %collective-permute-start.29 = (bf16[8,4096]{1,0:T(8,128)(2,1)S(1)}, bf16[8,4096]{1,0:T(8,128)(2,1)S(1)}, u32[]{:S(2)}, u32[]{:S(2)}) collective-permute-start(bf16[8,4096]{1,0:T(8,128)(2,1)S(1)} %fusion.5), channel_id=1, source_target_pairs={{0,4},{1,5},{2,6},{3,7},{4,0},{5,1},{6,2},{7,3},{8,12},{9,13},{10,... | collective-permute-start | bytes 196616 | tf_op jit(solution)/shard_map/ppermute | solution.py:80
  83.9 6.4 %collective-permute-start.17 = (bf16[8,4096]{1,0:T(8,128)(2,1)S(1)}, bf16[8,4096]{1,0:T(8,128)(2,1)S(1)}, u32[]{:S(2)}, u32[]{:S(2)}) collective-permute-start(bf16[8,4096]{1,0:T(8,128)(2,1)S(1)} %add_convert_fusion.10), channel_id=1, source_target_pairs={{0,4},{1,5},{2,6},{3,7},{4,0},{5,1},{6,2},{7,3},{8,12},{9,13},{10,... | collective-permute-start | bytes 196616 | tf_op jit(solution)/shard_map/ppermute | solution.py:80
  84.8 6.9 %collective-permute-start.27 = (bf16[8,4096]{1,0:T(8,128)(2,1)S(1)}, bf16[8,4096]{1,0:T(8,128)(2,1)S(1)}, u32[]{:S(2)}, u32[]{:S(2)}) collective-permute-start(bf16[8,4096]{1,0:T(8,128)(2,1)S(1)} %add_convert_fusion.8), channel_id=1, source_target_pairs={{0,4},{1,5},{2,6},{3,7},{4,0},{5,1},{6,2},{7,3},{8,12},{9,13},{10,... | collective-permute-start | bytes 196616 | tf_op jit(solution)/shard_map/ppermute | solution.py:80

commit v15 on v14

--- a/solution.py
+++ b/solution.py
@@ -230,7 +230,7 @@
     (held,) = yield (own,)
     for move in moves:
         (got,) = yield (permute(held, move),)
-        if move is moves[0] and beside:
+        if move is moves[2] and beside:
             got = lax.optimization_barrier((got, *beside))[0]
         held = jnp.concatenate([held, got])
     (sib,) = yield (permute(held, to_sibling),)
@@ -275,7 +275,7 @@
     along = [along_line(2**bit) for bit in range(line_bits)][::-1]
     across = [over_first, over_second]
     routes = [along + across, along + across, along[:1] + across + along[1:]]
-    backs = [[3, 2, 1, 0], [3, 2, 1, 0], [2, 3, 1, 0]] if line_bits == 2 else [range(len(along + across))[::-1]]
+    backs = [[3, 2, 1, 0], [3, 2, 1, 0], [2, 1, 3, 0]] if line_bits == 2 else [range(len(along + across))[::-1]]
     step = ROWS_AT_ONCE if tok_rows % ROWS_AT_ONCE == 0 else tok_rows
     owns = packed(tokens, expert_ids, route_weight, step)
     mine = served_expert(slot_of, lax.optimization_barrier((swap_flag, owns[0]))[0])

time: 92.7 us -> 94.6 us (1.020)
  waiting for transfers between devices: 26.8 us -> 32.5 us
  starting transfers between devices: 47.5 us -> 43.7 us
    ppermute x30, waiting for transfers between devices: 26.8 us -> 32.5 us  [permute(): return lax.ppermute(value, AXES, pairs)]
    ppermute x30, starting transfers between devices: 47.5 us -> 43.7 us  [permute(): return lax.ppermute(value, AXES, pairs)]
  transfers between devices with their start and end apart: 30 -> 30, of which waited for: 13 -> 14; matrix products, arithmetic and copies ran while one was open for 2% -> 2% of each run, Pallas kernels for 15% -> 15%
where the time goes in v15:
time: 94.6 us; the launch traced here: 94.4 us
  starting transfers between devices  43.7 us (46%)
  waiting for transfers between devices  32.5 us (34%)
  Pallas kernels  14.8 us (16%)
  other arithmetic  2.11 us (2%)
    ppermute x30, starting transfers between devices, permute(): return lax.ppermute(value, AXES, pairs)  43.7 us
    ppermute x30, waiting for transfers between devices, permute(): return lax.ppermute(value, AXES, pairs)  32.5 us
    pallas_call x3, Pallas kernels, serve_rows(): pl.pallas_call(functools.partial(serve_kernel, top_count), out_shape=(out...  12.4 us
  transfers between devices with their start and end apart: 30, of which 14 were waited for; matrix products, arithmetic and copies ran while one was open for 2% of the time, Pallas kernels for 15%

profile of v15, /device:TPU:0, one launch (start us, length us, event | category | flops | bytes accessed | tf_op | source)
XLA Modules:
  0.0 94.4 jit_solution(14706430886753213546)
XLA Ops:
  0.0 1.0 %pack_rows.1 = (bf16[8,4224]{1,0:T(8,128)(2,1)S(1)}, bf16[8,4224]{1,0:T(8,128)(2,1)S(1)}, bf16[8,4224]{1,0:T(8,128)(2,1)S(1)}) custom-call(bf16[24,4096]{1,0:T(8,128)(2,1)} %tokens_hbm.1, s32[8,24]{1,0:T(8,128)} %bitcast.56, f32[8,24]{1,0:T(8,128)} %bitcast.57), custom_call_target="tpu_custom_call" | custom-call | bytes 393216 | tf_op jit(solution)/shard_map/pack_rows/pallas_call | solution.py:158
  1.0 4.1 %collective-permute-start.7 = (bf16[8,4224]{1,0:T(8,128)(2,1)S(1)}, bf16[8,4224]{1,0:T(8,128)(2,1)S(1)}, u32[]{:S(2)}, u32[]{:S(2)}) collective-permute-start(bf16[8,4224]{1,0:T(8,128)(2,1)S(1)} %get-tuple-element.27), channel_id=1, source_target_pairs={{0,4},{1,5},{2,6},{3,7},{4,0},{5,1},{6,2},{7,3},{8,12},{9,13},{10,... | collective-permute-start | bytes 202760 | tf_op jit(solution)/shard_map/ppermute | solution.py:80
  5.1 0.1 collective-permute-start
  5.2 2.8 %collective-permute-start.18 = (bf16[8,4224]{1,0:T(8,128)(2,1)S(1)}, bf16[8,4224]{1,0:T(8,128)(2,1)S(1)}, u32[]{:S(2)}, u32[]{:S(2)}) collective-permute-start(bf16[8,4224]{1,0:T(8,128)(2,1)S(1)} %get-tuple-element.34), channel_id=1, source_target_pairs={{0,4},{1,5},{2,6},{3,7},{4,0},{5,1},{6,2},{7,3},{8,12},{9,13},{10,... | collective-permute-start | bytes 202760 | tf_op jit(solution)/shard_map/ppermute | solution.py:80
  8.7 0.0 copy-start.2
  8.7 1.4 %served_expert.1.mine = s32[1]{0:T(128)} custom-call(s32[2,16]{1,0:T(2,128)} %bitcast.58, s32[1]{0:T(128)S(6)} %copy.25.flag), custom_call_target="tpu_custom_call" | custom-call | flops 10000000000 | tf_op jit(solution)/shard_map/served_expert/pallas_call | solution.py:111
  10.2 3.7 %collective-permute-start.8 = (bf16[16,4224]{1,0:T(8,128)(2,1)S(1)}, bf16[16,4224]{1,0:T(8,128)(2,1)S(1)}, u32[]{:S(2)}, u32[]{:S(2)}) collective-permute-start(bf16[16,4224]{1,0:T(8,128)(2,1)S(1)} %pad_maximum_fusion.8), channel_id=1, source_target_pairs={{0,1},{1,0},{2,3},{3,2},{4,5},{5,4},{6,7},{7,6},{8,24},{9,25},{10,... | collective-permute-start | bytes 405512 | tf_op jit(solution)/shard_map/ppermute | solution.py:80
  13.8 0.3 collective-permute-start.1
  14.1 0.5 collective-permute-done.18
  14.6 1.4 %collective-permute-start.19 = (bf16[16,4224]{1,0:T(8,128)(2,1)S(1)}, bf16[16,4224]{1,0:T(8,128)(2,1)S(1)}, u32[]{:S(2)}, u32[]{:S(2)}) collective-permute-start(bf16[16,4224]{1,0:T(8,128)(2,1)S(1)} %pad_maximum_fusion.9), channel_id=1, source_target_pairs={{0,2},{1,3},{2,0},{3,1},{4,6},{5,7},{6,4},{7,5},{8,10},{9,11},{10,... | collective-permute-start | bytes 405512 | tf_op jit(solution)/shard_map/ppermute | solution.py:80
  16.0 0.8 collective-permute-done.8
  16.8 2.1 %collective-permute-start.9 = (bf16[32,4224]{1,0:T(8,128)(2,1)S(1)}, bf16[32,4224]{1,0:T(8,128)(2,1)S(1)}, u32[]{:S(2)}, u32[]{:S(2)}) collective-permute-start(bf16[32,4224]{1,0:T(8,128)(2,1)S(1)} %pad_maximum_fusion.4), channel_id=1, source_target_pairs={{0,16},{1,17},{2,18},{3,19},{4,20},{5,21},{6,22},{7,23},{8,9},{9,8... | collective-permute-start | bytes 811016 | tf_op jit(solution)/shard_map/ppermute | solution.py:80
  18.9 0.9 collective-permute-done.1
  19.8 2.0 %collective-permute-start.2 = (bf16[32,4224]{1,0:T(8,128)(2,1)S(1)}, bf16[32,4224]{1,0:T(8,128)(2,1)S(1)}, u32[]{:S(2)}, u32[]{:S(2)}) collective-permute-start(bf16[32,4224]{1,0:T(8,128)(2,1)S(1)} %pad_maximum_fusion.3), channel_id=1, source_target_pairs={{0,1},{1,0},{2,3},{3,2},{4,5},{5,4},{6,7},{7,6},{8,24},{9,25},{10,... | collective-permute-start | bytes 811016 | tf_op jit(solution)/shard_map/ppermute | solution.py:80
  21.9 1.4 %collective-permute-start.20 = (bf16[32,4224]{1,0:T(8,128)(2,1)S(1)}, bf16[32,4224]{1,0:T(8,128)(2,1)S(1)}, u32[]{:S(2)}, u32[]{:S(2)}) collective-permute-start(bf16[32,4224]{1,0:T(8,128)(2,1)S(1)} %pad_maximum_fusion.5), channel_id=1, source_target_pairs={{0,1},{1,0},{2,3},{3,2},{4,5},{5,4},{6,7},{7,6},{8,24},{9,25},{10,... | collective-permute-start | bytes 811016 | tf_op jit(solution)/shard_map/ppermute | solution.py:80
  23.3 2.9 %collective-permute-done.9 = bf16[32,4224]{1,0:T(8,128)(2,1)S(1)} collective-permute-done((bf16[32,4224]{1,0:T(8,128)(2,1)S(1)}, bf16[32,4224]{1,0:T(8,128)(2,1)S(1)}, u32[]{:S(2)}, u32[]{:S(2)}) %collective-permute-start.9) | collective-permute-done | bytes 270368 | tf_op jit(solution)/shard_map/ppermute | solution.py:80
  26.2 0.8 collective-permute-start.10
  27.1 1.6 %collective-permute-start.3 = (bf16[64,4224]{1,0:T(8,128)(2,1)S(1)}, bf16[64,4224]{1,0:T(8,128)(2,1)S(1)}, u32[]{:S(2)}, u32[]{:S(2)}) collective-permute-start(bf16[64,4224]{1,0:T(8,128)(2,1)S(1)} %pad_maximum_fusion), channel_id=1, source_target_pairs={{0,16},{1,17},{2,18},{3,19},{4,20},{5,21},{6,22},{7,23},{8,9},{9,8... | collective-permute-start | bytes 1622024 | tf_op jit(solution)/shard_map/ppermute | solution.py:80
  28.7 1.9 %collective-permute-done.20 = bf16[32,4224]{1,0:T(8,128)(2,1)S(1)} collective-permute-done((bf16[32,4224]{1,0:T(8,128)(2,1)S(1)}, bf16[32,4224]{1,0:T(8,128)(2,1)S(1)}, u32[]{:S(2)}, u32[]{:S(2)}) %collective-permute-start.20) | collective-permute-done | bytes 270368 | tf_op jit(solution)/shard_map/ppermute | solution.py:80
  30.6 2.4 %collective-permute-start.21 = (bf16[64,4224]{1,0:T(8,128)(2,1)S(1)}, bf16[64,4224]{1,0:T(8,128)(2,1)S(1)}, u32[]{:S(2)}, u32[]{:S(2)}) collective-permute-start(bf16[64,4224]{1,0:T(8,128)(2,1)S(1)} %pad_maximum_fusion.2), channel_id=1, source_target_pairs={{0,16},{1,17},{2,18},{3,19},{4,20},{5,21},{6,22},{7,23},{8,9},{9,8... | collective-permute-start | bytes 1622024 | tf_op jit(solution)/shard_map/ppermute | solution.py:80
  33.0 3.5 %collective-permute-done.3 = bf16[64,4224]{1,0:T(8,128)(2,1)S(1)} collective-permute-done((bf16[64,4224]{1,0:T(8,128)(2,1)S(1)}, bf16[64,4224]{1,0:T(8,128)(2,1)S(1)}, u32[]{:S(2)}, u32[]{:S(2)}) %collective-permute-start.3) | collective-permute-done | bytes 540704 | tf_op jit(solution)/shard_map/ppermute | solution.py:80
  36.6 0.1 collective-permute-start.4
  36.7 0.1 constant_dynamic-update-slice_fusion.5.own
  36.7 0.6 collective-permute-start.11
  37.3 2.0 %collective-permute-done.4.sib = bf16[128,4224]{1,0:T(8,128)(2,1)S(1)} collective-permute-done((bf16[128,4224]{1,0:T(8,128)(2,1)S(1)}, bf16[128,4224]{1,0:T(8,128)(2,1)S(1)}, u32[]{:S(2)}, u32[]{:S(2)}) %collective-permute-start.4) | collective-permute-done | bytes 1081376 | tf_op jit(solution)/shard_map/ppermute | solution.py:80
  39.4 4.1 %serve_rows.3 = (bf16[128,4096]{1,0:T(8,128)(2,1)S(1)}, bf16[128,4096]{1,0:T(8,128)(2,1)S(1)}) custom-call(s32[1]{0:T(128)} %served_expert.1.mine, bf16[128,4224]{1,0:T(8,128)(2,1)S(1)} %constant_dynamic-update-slice_fusion.own, bf16[128,4224]{1,0:T(8,128)(2,1)S(1)} %collective-permute-done.4.sib, bf16[4096,512]{1,0:T(8,128)(2,1)S(1)} %bitcast.37, ...), custom_call_target="tpu_custom_call" | custom-call | flops 3221225472 | bytes 16777216 | tf_op jit(solution)/shard_map/serve_rows/pallas_call | solution.py:207
  43.5 0.2 collective-permute-start.5
  43.8 0.4 collective-permute-start.22
  44.2 4.1 %serve_rows.4 = (bf16[128,4096]{1,0:T(8,128)(2,1)S(1)}, bf16[128,4096]{1,0:T(8,128)(2,1)S(1)}) custom-call(s32[1]{0:T(128)} %served_expert.1.mine, bf16[128,4224]{1,0:T(8,128)(2,1)S(1)} %constant_dynamic-update-slice_fusion.5.own, bf16[128,4224]{1,0:T(8,128)(2,1)S(1)} %collective-permute-done.11.sib, bf16[4096,512]{1,0:T(8,128)(2,1)S(1)} %bitcast.38, ...), custom_call_target="tpu_custom_call" | custom-call | flops 3221225472 | bytes 16777216 | tf_op jit(solution)/shard_map/serve_rows/pallas_call | solution.py:207
  48.4 0.2 collective-permute-start.12
  48.6 0.1 add_convert_fusion.2
  48.7 1.6 %collective-permute-start.6 = (bf16[64,4096]{1,0:T(8,128)(2,1)S(1)}, bf16[64,4096]{1,0:T(8,128)(2,1)S(1)}, u32[]{:S(2)}, u32[]{:S(2)}) collective-permute-start(bf16[64,4096]{1,0:T(8,128)(2,1)S(1)} %add_convert_fusion.2), channel_id=1, source_target_pairs={{0,16},{1,17},{2,18},{3,19},{4,20},{5,21},{6,22},{7,23},{8,9},{9,8... | collective-permute-start | bytes 1572872 | tf_op jit(solution)/shard_map/ppermute | solution.py:80
  50.3 4.1 %serve_rows.5 = (bf16[128,4096]{1,0:T(8,128)(2,1)S(1)}, bf16[128,4096]{1,0:T(8,128)(2,1)S(1)}) custom-call(s32[1]{0:T(128)} %served_expert.1.mine, bf16[128,4224]{1,0:T(8,128)(2,1)S(1)} %constant_dynamic-update-slice_fusion.10.own, bf16[128,4224]{1,0:T(8,128)(2,1)S(1)} %collective-permute-done.22.sib, bf16[4096,512]{1,0:T(8,128)(2,1)S(1)} %bitcast.39, ...), custom_call_target="tpu_custom_call" | custom-call | flops 3221225472 | bytes 16777216 | tf_op jit(solution)/shard_map/serve_rows/pallas_call | solution.py:207
  54.4 0.2 collective-permute-start.23
  54.6 0.1 add_convert_fusion.1
  54.7 1.6 %collective-permute-start.13 = (bf16[64,4096]{1,0:T(8,128)(2,1)S(1)}, bf16[64,4096]{1,0:T(8,128)(2,1)S(1)}, u32[]{:S(2)}, u32[]{:S(2)}) collective-permute-start(bf16[64,4096]{1,0:T(8,128)(2,1)S(1)} %bitcast.50), channel_id=1, source_target_pairs={{0,16},{1,17},{2,18},{3,19},{4,20},{5,21},{6,22},{7,23},{8,9},{9,8... | collective-permute-start | bytes 1572872 | tf_op jit(solution)/shard_map/ppermute | solution.py:80
  56.3 0.8 collective-permute-done.23
  57.1 0.1 add_convert_fusion
  57.3 1.3 %collective-permute-start.24 = (bf16[64,4096]{1,0:T(8,128)(2,1)S(1)}, bf16[64,4096]{1,0:T(8,128)(2,1)S(1)}, u32[]{:S(2)}, u32[]{:S(2)}) collective-permute-start(bf16[64,4096]{1,0:T(8,128)(2,1)S(1)} %add_convert_fusion), channel_id=1, source_target_pairs={{0,16},{1,17},{2,18},{3,19},{4,20},{5,21},{6,22},{7,23},{8,9},{9,8... | collective-permute-start | bytes 1572872 | tf_op jit(solution)/shard_map/ppermute | solution.py:80
  58.6 5.4 %collective-permute-done.13 = bf16[64,4096]{1,0:T(8,128)(2,1)S(1)} collective-permute-done((bf16[64,4096]{1,0:T(8,128)(2,1)S(1)}, bf16[64,4096]{1,0:T(8,128)(2,1)S(1)}, u32[]{:S(2)}, u32[]{:S(2)}) %collective-permute-start.13) | collective-permute-done | bytes 524320 | tf_op jit(solution)/shard_map/ppermute | solution.py:80
  64.0 0.1 add_convert_fusion.4
  64.1 1.5 %collective-permute-start.16 = (bf16[32,4096]{1,0:T(8,128)(2,1)S(1)}, bf16[32,4096]{1,0:T(8,128)(2,1)S(1)}, u32[]{:S(2)}, u32[]{:S(2)}) collective-permute-start(bf16[32,4096]{1,0:T(8,128)(2,1)S(1)} %bitcast.55), channel_id=1, source_target_pairs={{0,1},{1,0},{2,3},{3,2},{4,5},{5,4},{6,7},{7,6},{8,24},{9,25},{10,... | collective-permute-start | bytes 786440 | tf_op jit(solution)/shard_map/ppermute | solution.py:80
  65.6 0.1 add_convert_fusion.5
  65.7 0.7 collective-permute-start.14
  66.3 6.5 %collective-permute-done.24 = bf16[64,4096]{1,0:T(8,128)(2,1)S(1)} collective-permute-done((bf16[64,4096]{1,0:T(8,128)(2,1)S(1)}, bf16[64,4096]{1,0:T(8,128)(2,1)S(1)}, u32[]{:S(2)}, u32[]{:S(2)}) %collective-permute-start.24) | collective-permute-done | bytes 524320 | tf_op jit(solution)/shard_map/ppermute | solution.py:80
  72.9 0.1 add_convert_fusion.3
  73.0 1.4 %collective-permute-start.25 = (bf16[32,4096]{1,0:T(8,128)(2,1)S(1)}, bf16[32,4096]{1,0:T(8,128)(2,1)S(1)}, u32[]{:S(2)}, u32[]{:S(2)}) collective-permute-start(bf16[32,4096]{1,0:T(8,128)(2,1)S(1)} %add_convert_fusion.3), channel_id=1, source_target_pairs={{0,1},{1,0},{2,3},{3,2},{4,5},{5,4},{6,7},{7,6},{8,24},{9,25},{10,... | collective-permute-start | bytes 786440 | tf_op jit(solution)/shard_map/ppermute | solution.py:80
  74.4 0.1 fusion
  74.4 1.9 %collective-permute-start.28 = (bf16[16,4096]{1,0:T(8,128)(2,1)S(1)}, bf16[16,4096]{1,0:T(8,128)(2,1)S(1)}, u32[]{:S(2)}, u32[]{:S(2)}) collective-permute-start(bf16[16,4096]{1,0:T(8,128)(2,1)S(1)} %fusion), channel_id=1, source_target_pairs={{0,2},{1,3},{2,0},{3,1},{4,6},{5,7},{6,4},{7,5},{8,10},{9,11},{10,... | collective-permute-start | bytes 393224 | tf_op jit(solution)/shard_map/ppermute | solution.py:80
  76.3 0.1 add_convert_fusion.7
  76.4 0.3 collective-permute-start.15
  76.7 2.7 %collective-permute-done.25 = bf16[32,4096]{1,0:T(8,128)(2,1)S(1)} collective-permute-done((bf16[32,4096]{1,0:T(8,128)(2,1)S(1)}, bf16[32,4096]{1,0:T(8,128)(2,1)S(1)}, u32[]{:S(2)}, u32[]{:S(2)}) %collective-permute-start.25) | collective-permute-done | bytes 262176 | tf_op jit(solution)/shard_map/ppermute | solution.py:80
  79.4 0.1 add_convert_fusion.6
  79.5 1.9 %collective-permute-start.26 = (bf16[16,4096]{1,0:T(8,128)(2,1)S(1)}, bf16[16,4096]{1,0:T(8,128)(2,1)S(1)}, u32[]{:S(2)}, u32[]{:S(2)}) collective-permute-start(bf16[16,4096]{1,0:T(8,128)(2,1)S(1)} %add_convert_fusion.6), channel_id=1, source_target_pairs={{0,2},{1,3},{2,0},{3,1},{4,6},{5,7},{6,4},{7,5},{8,10},{9,11},{10,... | collective-permute-start | bytes 393224 | tf_op jit(solution)/shard_map/ppermute | solution.py:80
  81.4 2.7 %collective-permute-start.29 = (bf16[8,4096]{1,0:T(8,128)(2,1)S(1)}, bf16[8,4096]{1,0:T(8,128)(2,1)S(1)}, u32[]{:S(2)}, u32[]{:S(2)}) collective-permute-start(bf16[8,4096]{1,0:T(8,128)(2,1)S(1)} %fusion.2), channel_id=1, source_target_pairs={{0,4},{1,5},{2,6},{3,7},{4,0},{5,1},{6,2},{7,3},{8,12},{9,13},{10,... | collective-permute-start | bytes 196616 | tf_op jit(solution)/shard_map/ppermute | solution.py:80
  84.2 2.4 %collective-permute-start.17 = (bf16[8,4096]{1,0:T(8,128)(2,1)S(1)}, bf16[8,4096]{1,0:T(8,128)(2,1)S(1)}, u32[]{:S(2)}, u32[]{:S(2)}) collective-permute-start(bf16[8,4096]{1,0:T(8,128)(2,1)S(1)} %add_convert_fusion.11), channel_id=1, source_target_pairs={{0,4},{1,5},{2,6},{3,7},{4,0},{5,1},{6,2},{7,3},{8,12},{9,13},{10,... | collective-permute-start | bytes 196616 | tf_op jit(solution)/shard_map/ppermute | solution.py:80
  86.6 0.4 collective-permute-done.26
  87.0 2.4 %collective-permute-start.27 = (bf16[8,4096]{1,0:T(8,128)(2,1)S(1)}, bf16[8,4096]{1,0:T(8,128)(2,1)S(1)}, u32[]{:S(2)}, u32[]{:S(2)}) collective-permute-start(bf16[8,4096]{1,0:T(8,128)(2,1)S(1)} %add_convert_fusion.9), channel_id=1, source_target_pairs={{0,4},{1,5},{2,6},{3,7},{4,0},{5,1},{6,2},{7,3},{8,12},{9,13},{10,... | collective-permute-start | bytes 196616 | tf_op jit(solution)/shard_map/ppermute | solution.py:80
  89.5 0.1 fusion.5
  89.5 3.4 %collective-permute-done.17 = bf16[8,4096]{1,0:T(8,128)(2,1)S(1)} collective-permute-done((bf16[8,4096]{1,0:T(8,128)(2,1)S(1)}, bf16[8,4096]{1,0:T(8,128)(2,1)S(1)}, u32[]{:S(2)}, u32[]{:S(2)}) %collective-permute-start.17) | collective-permute-done | bytes 65568 | tf_op jit(solution)/shard_map/ppermute | solution.py:80
  93.0 0.1 add_convert_fusion.10
  93.0 0.6 collective-permute-done.27
  93.7 0.1 add_convert_fusion.8
  93.7 0.7 pad_maximum_fusion.6
  (48 shorter events, 0.8 us)
Async XLA Ops:
  1.0 9.1 %collective-permute-start.7 = (bf16[8,4224]{1,0:T(8,128)(2,1)S(1)}, bf16[8,4224]{1,0:T(8,128)(2,1)S(1)}, u32[]{:S(2)}, u32[]{:S(2)}) collective-permute-start(bf16[8,4224]{1,0:T(8,128)(2,1)S(1)} %get-tuple-element.27), channel_id=1, source_target_pairs={{0,4},{1,5},{2,6},{3,7},{4,0},{5,1},{6,2},{7,3},{8,12},{9,13},{10,... | collective-permute-start | bytes 202760 | tf_op jit(solution)/shard_map/ppermute | solution.py:80
  5.1 8.7 %collective-permute-start = (bf16[8,4224]{1,0:T(8,128)(2,1)S(1)}, bf16[8,4224]{1,0:T(8,128)(2,1)S(1)}, u32[]{:S(2)}, u32[]{:S(2)}) collective-permute-start(bf16[8,4224]{1,0:T(8,128)(2,1)S(1)} %get-tuple-element.23), channel_id=1, source_target_pairs={{0,4},{1,5},{2,6},{3,7},{4,0},{5,1},{6,2},{7,3},{8,12},{9,13},{10,... | collective-permute-start | bytes 202760 | tf_op jit(solution)/shard_map/ppermute | solution.py:80
  5.2 9.4 %collective-permute-start.18 = (bf16[8,4224]{1,0:T(8,128)(2,1)S(1)}, bf16[8,4224]{1,0:T(8,128)(2,1)S(1)}, u32[]{:S(2)}, u32[]{:S(2)}) collective-permute-start(bf16[8,4224]{1,0:T(8,128)(2,1)S(1)} %get-tuple-element.34), channel_id=1, source_target_pairs={{0,4},{1,5},{2,6},{3,7},{4,0},{5,1},{6,2},{7,3},{8,12},{9,13},{10,... | collective-permute-start | bytes 202760 | tf_op jit(solution)/shard_map/ppermute | solution.py:80
  8.7 30.6 %copy-start.2 = (bf16[1,512,4096]{2,1,0:T(8,128)(2,1)S(1)}, bf16[1,512,4096]{2,1,0:T(8,128)(2,1)}, u32[]{:S(2)}) copy-start(bf16[1,512,4096]{2,1,0:T(8,128)(2,1)} %param.15) | copy-start | bytes 12582916
  10.2 6.7 %collective-permute-start.8 = (bf16[16,4224]{1,0:T(8,128)(2,1)S(1)}, bf16[16,4224]{1,0:T(8,128)(2,1)S(1)}, u32[]{:S(2)}, u32[]{:S(2)}) collective-permute-start(bf16[16,4224]{1,0:T(8,128)(2,1)S(1)} %pad_maximum_fusion.8), channel_id=1, source_target_pairs={{0,1},{1,0},{2,3},{3,2},{4,5},{5,4},{6,7},{7,6},{8,24},{9,25},{10,... | collective-permute-start | bytes 405512 | tf_op jit(solution)/shard_map/ppermute | solution.py:80
  13.8 6.0 %collective-permute-start.1 = (bf16[16,4224]{1,0:T(8,128)(2,1)S(1)}, bf16[16,4224]{1,0:T(8,128)(2,1)S(1)}, u32[]{:S(2)}, u32[]{:S(2)}) collective-permute-start(bf16[16,4224]{1,0:T(8,128)(2,1)S(1)} %pad_maximum_fusion.7), channel_id=1, source_target_pairs={{0,2},{1,3},{2,0},{3,1},{4,6},{5,7},{6,4},{7,5},{8,10},{9,11},{10,... | collective-permute-start | bytes 405512 | tf_op jit(solution)/shard_map/ppermute | solution.py:80
  14.6 7.2 %collective-permute-start.19 = (bf16[16,4224]{1,0:T(8,128)(2,1)S(1)}, bf16[16,4224]{1,0:T(8,128)(2,1)S(1)}, u32[]{:S(2)}, u32[]{:S(2)}) collective-permute-start(bf16[16,4224]{1,0:T(8,128)(2,1)S(1)} %pad_maximum_fusion.9), channel_id=1, source_target_pairs={{0,2},{1,3},{2,0},{3,1},{4,6},{5,7},{6,4},{7,5},{8,10},{9,11},{10,... | collective-permute-start | bytes 405512 | tf_op jit(solution)/shard_map/ppermute | solution.py:80
  16.8 9.4 %collective-permute-start.9 = (bf16[32,4224]{1,0:T(8,128)(2,1)S(1)}, bf16[32,4224]{1,0:T(8,128)(2,1)S(1)}, u32[]{:S(2)}, u32[]{:S(2)}) collective-permute-start(bf16[32,4224]{1,0:T(8,128)(2,1)S(1)} %pad_maximum_fusion.4), channel_id=1, source_target_pairs={{0,16},{1,17},{2,18},{3,19},{4,20},{5,21},{6,22},{7,23},{8,9},{9,8... | collective-permute-start | bytes 811016 | tf_op jit(solution)/shard_map/ppermute | solution.py:80
  19.8 19.5 %copy-start.1 = (bf16[1,4096,512]{2,1,0:T(8,128)(2,1)S(1)}, bf16[1,4096,512]{2,1,0:T(8,128)(2,1)}, u32[]{:S(2)}) copy-start(bf16[1,4096,512]{2,1,0:T(8,128)(2,1)} %param.14) | copy-start | bytes 12582916
  19.8 7.2 %collective-permute-start.2 = (bf16[32,4224]{1,0:T(8,128)(2,1)S(1)}, bf16[32,4224]{1,0:T(8,128)(2,1)S(1)}, u32[]{:S(2)}, u32[]{:S(2)}) collective-permute-start(bf16[32,4224]{1,0:T(8,128)(2,1)S(1)} %pad_maximum_fusion.3), channel_id=1, source_target_pairs={{0,1},{1,0},{2,3},{3,2},{4,5},{5,4},{6,7},{7,6},{8,24},{9,25},{10,... | collective-permute-start | bytes 811016 | tf_op jit(solution)/shard_map/ppermute | solution.py:80
  21.9 8.7 %collective-permute-start.20 = (bf16[32,4224]{1,0:T(8,128)(2,1)S(1)}, bf16[32,4224]{1,0:T(8,128)(2,1)S(1)}, u32[]{:S(2)}, u32[]{:S(2)}) collective-permute-start(bf16[32,4224]{1,0:T(8,128)(2,1)S(1)} %pad_maximum_fusion.5), channel_id=1, source_target_pairs={{0,1},{1,0},{2,3},{3,2},{4,5},{5,4},{6,7},{7,6},{8,24},{9,25},{10,... | collective-permute-start | bytes 811016 | tf_op jit(solution)/shard_map/ppermute | solution.py:80
  26.2 10.4 %collective-permute-start.10 = (bf16[64,4224]{1,0:T(8,128)(2,1)S(1)}, bf16[64,4224]{1,0:T(8,128)(2,1)S(1)}, u32[]{:S(2)}, u32[]{:S(2)}) collective-permute-start(bf16[64,4224]{1,0:T(8,128)(2,1)S(1)} %pad_maximum_fusion.1), channel_id=1, source_target_pairs={{0,2},{1,3},{2,0},{3,1},{4,6},{5,7},{6,4},{7,5},{8,10},{9,11},{10,... | collective-permute-start | bytes 1622024 | tf_op jit(solution)/shard_map/ppermute | solution.py:80
  27.1 9.4 %collective-permute-start.3 = (bf16[64,4224]{1,0:T(8,128)(2,1)S(1)}, bf16[64,4224]{1,0:T(8,128)(2,1)S(1)}, u32[]{:S(2)}, u32[]{:S(2)}) collective-permute-start(bf16[64,4224]{1,0:T(8,128)(2,1)S(1)} %pad_maximum_fusion), channel_id=1, source_target_pairs={{0,16},{1,17},{2,18},{3,19},{4,20},{5,21},{6,22},{7,23},{8,9},{9,8... | collective-permute-start | bytes 1622024 | tf_op jit(solution)/shard_map/ppermute | solution.py:80
  30.5 8.8 %copy-start = (bf16[1,4096,512]{2,1,0:T(8,128)(2,1)S(1)}, bf16[1,4096,512]{2,1,0:T(8,128)(2,1)}, u32[]{:S(2)}) copy-start(bf16[1,4096,512]{2,1,0:T(8,128)(2,1)} %param.13) | copy-start | bytes 12582916
  30.6 13.1 %collective-permute-start.21 = (bf16[64,4224]{1,0:T(8,128)(2,1)S(1)}, bf16[64,4224]{1,0:T(8,128)(2,1)S(1)}, u32[]{:S(2)}, u32[]{:S(2)}) collective-permute-start(bf16[64,4224]{1,0:T(8,128)(2,1)S(1)} %pad_maximum_fusion.2), channel_id=1, source_target_pairs={{0,16},{1,17},{2,18},{3,19},{4,20},{5,21},{6,22},{7,23},{8,9},{9,8... | collective-permute-start | bytes 1622024 | tf_op jit(solution)/shard_map/ppermute | solution.py:80
  36.6 2.8 %collective-permute-start.4 = (bf16[128,4224]{1,0:T(8,128)(2,1)S(1)}, bf16[128,4224]{1,0:T(8,128)(2,1)S(1)}, u32[]{:S(2)}, u32[]{:S(2)}) collective-permute-start(bf16[128,4224]{1,0:T(8,128)(2,1)S(1)} %constant_dynamic-update-slice_fusion.own), channel_id=1, source_target_pairs={{0,8},{1,9},{2,10},{3,11},{4,12},{5,13},{6,14},{7,15},{8,0},{9,1},... | collective-permute-start | bytes 3244040 | tf_op jit(solution)/shard_map/ppermute | solution.py:80
  36.7 7.5 %collective-permute-start.11 = (bf16[128,4224]{1,0:T(8,128)(2,1)S(1)}, bf16[128,4224]{1,0:T(8,128)(2,1)S(1)}, u32[]{:S(2)}, u32[]{:S(2)}) collective-permute-start(bf16[128,4224]{1,0:T(8,128)(2,1)S(1)} %constant_dynamic-update-slice_fusion.5.own), channel_id=1, source_target_pairs={{0,8},{1,9},{2,10},{3,11},{4,12},{5,13},{6,14},{7,15},{8,0},{9,1},... | collective-permute-start | bytes 3244040 | tf_op jit(solution)/shard_map/ppermute | solution.py:80
  43.5 4.9 %collective-permute-start.5 = (bf16[128,4096]{1,0:T(8,128)(2,1)S(1)}, bf16[128,4096]{1,0:T(8,128)(2,1)S(1)}, u32[]{:S(2)}, u32[]{:S(2)}) collective-permute-start(bf16[128,4096]{1,0:T(8,128)(2,1)S(1)} %get-tuple-element.26), channel_id=1, source_target_pairs={{0,8},{1,9},{2,10},{3,11},{4,12},{5,13},{6,14},{7,15},{8,0},{9,1},... | collective-permute-start | bytes 3145736 | tf_op jit(solution)/shard_map/ppermute | solution.py:80
  43.8 6.5 %collective-permute-start.22 = (bf16[128,4224]{1,0:T(8,128)(2,1)S(1)}, bf16[128,4224]{1,0:T(8,128)(2,1)S(1)}, u32[]{:S(2)}, u32[]{:S(2)}) collective-permute-start(bf16[128,4224]{1,0:T(8,128)(2,1)S(1)} %constant_dynamic-update-slice_fusion.10.own), channel_id=1, source_target_pairs={{0,8},{1,9},{2,10},{3,11},{4,12},{5,13},{6,14},{7,15},{8,0},{9,1},... | collective-permute-start | bytes 3244040 | tf_op jit(solution)/shard_map/ppermute | solution.py:80
  48.4 6.2 %collective-permute-start.12 = (bf16[128,4096]{1,0:T(8,128)(2,1)S(1)}, bf16[128,4096]{1,0:T(8,128)(2,1)S(1)}, u32[]{:S(2)}, u32[]{:S(2)}) collective-permute-start(bf16[128,4096]{1,0:T(8,128)(2,1)S(1)} %get-tuple-element.30), channel_id=1, source_target_pairs={{0,8},{1,9},{2,10},{3,11},{4,12},{5,13},{6,14},{7,15},{8,0},{9,1},... | collective-permute-start | bytes 3145736 | tf_op jit(solution)/shard_map/ppermute | solution.py:80
  48.7 16.8 %collective-permute-start.6 = (bf16[64,4096]{1,0:T(8,128)(2,1)S(1)}, bf16[64,4096]{1,0:T(8,128)(2,1)S(1)}, u32[]{:S(2)}, u32[]{:S(2)}) collective-permute-start(bf16[64,4096]{1,0:T(8,128)(2,1)S(1)} %add_convert_fusion.2), channel_id=1, source_target_pairs={{0,16},{1,17},{2,18},{3,19},{4,20},{5,21},{6,22},{7,23},{8,9},{9,8... | collective-permute-start | bytes 1572872 | tf_op jit(solution)/shard_map/ppermute | solution.py:80
  54.4 2.7 %collective-permute-start.23 = (bf16[128,4096]{1,0:T(8,128)(2,1)S(1)}, bf16[128,4096]{1,0:T(8,128)(2,1)S(1)}, u32[]{:S(2)}, u32[]{:S(2)}) collective-permute-start(bf16[128,4096]{1,0:T(8,128)(2,1)S(1)} %get-tuple-element.39), channel_id=1, source_target_pairs={{0,8},{1,9},{2,10},{3,11},{4,12},{5,13},{6,14},{7,15},{8,0},{9,1},... | collective-permute-start | bytes 3145736 | tf_op jit(solution)/shard_map/ppermute | solution.py:80
  54.7 9.2 %collective-permute-start.13 = (bf16[64,4096]{1,0:T(8,128)(2,1)S(1)}, bf16[64,4096]{1,0:T(8,128)(2,1)S(1)}, u32[]{:S(2)}, u32[]{:S(2)}) collective-permute-start(bf16[64,4096]{1,0:T(8,128)(2,1)S(1)} %bitcast.50), channel_id=1, source_target_pairs={{0,16},{1,17},{2,18},{3,19},{4,20},{5,21},{6,22},{7,23},{8,9},{9,8... | collective-permute-start | bytes 1572872 | tf_op jit(solution)/shard_map/ppermute | solution.py:80
  57.3 15.6 %collective-permute-start.24 = (bf16[64,4096]{1,0:T(8,128)(2,1)S(1)}, bf16[64,4096]{1,0:T(8,128)(2,1)S(1)}, u32[]{:S(2)}, u32[]{:S(2)}) collective-permute-start(bf16[64,4096]{1,0:T(8,128)(2,1)S(1)} %add_convert_fusion), channel_id=1, source_target_pairs={{0,16},{1,17},{2,18},{3,19},{4,20},{5,21},{6,22},{7,23},{8,9},{9,8... | collective-permute-start | bytes 1572872 | tf_op jit(solution)/shard_map/ppermute | solution.py:80
  64.1 10.3 %collective-permute-start.16 = (bf16[32,4096]{1,0:T(8,128)(2,1)S(1)}, bf16[32,4096]{1,0:T(8,128)(2,1)S(1)}, u32[]{:S(2)}, u32[]{:S(2)}) collective-permute-start(bf16[32,4096]{1,0:T(8,128)(2,1)S(1)} %bitcast.55), channel_id=1, source_target_pairs={{0,1},{1,0},{2,3},{3,2},{4,5},{5,4},{6,7},{7,6},{8,24},{9,25},{10,... | collective-permute-start | bytes 786440 | tf_op jit(solution)/shard_map/ppermute | solution.py:80
  65.7 10.6 %collective-permute-start.14 = (bf16[32,4096]{1,0:T(8,128)(2,1)S(1)}, bf16[32,4096]{1,0:T(8,128)(2,1)S(1)}, u32[]{:S(2)}, u32[]{:S(2)}) collective-permute-start(bf16[32,4096]{1,0:T(8,128)(2,1)S(1)} %add_convert_fusion.5), channel_id=1, source_target_pairs={{0,1},{1,0},{2,3},{3,2},{4,5},{5,4},{6,7},{7,6},{8,24},{9,25},{10,... | collective-permute-start | bytes 786440 | tf_op jit(solution)/shard_map/ppermute | solution.py:80
  73.0 6.4 %collective-permute-start.25 = (bf16[32,4096]{1,0:T(8,128)(2,1)S(1)}, bf16[32,4096]{1,0:T(8,128)(2,1)S(1)}, u32[]{:S(2)}, u32[]{:S(2)}) collective-permute-start(bf16[32,4096]{1,0:T(8,128)(2,1)S(1)} %add_convert_fusion.3), channel_id=1, source_target_pairs={{0,1},{1,0},{2,3},{3,2},{4,5},{5,4},{6,7},{7,6},{8,24},{9,25},{10,... | collective-permute-start | bytes 786440 | tf_op jit(solution)/shard_map/ppermute | solution.py:80
  74.4 6.9 %collective-permute-start.28 = (bf16[16,4096]{1,0:T(8,128)(2,1)S(1)}, bf16[16,4096]{1,0:T(8,128)(2,1)S(1)}, u32[]{:S(2)}, u32[]{:S(2)}) collective-permute-start(bf16[16,4096]{1,0:T(8,128)(2,1)S(1)} %fusion), channel_id=1, source_target_pairs={{0,2},{1,3},{2,0},{3,1},{4,6},{5,7},{6,4},{7,5},{8,10},{9,11},{10,... | collective-permute-start | bytes 393224 | tf_op jit(solution)/shard_map/ppermute | solution.py:80
  76.4 7.7 %collective-permute-start.15 = (bf16[16,4096]{1,0:T(8,128)(2,1)S(1)}, bf16[16,4096]{1,0:T(8,128)(2,1)S(1)}, u32[]{:S(2)}, u32[]{:S(2)}) collective-permute-start(bf16[16,4096]{1,0:T(8,128)(2,1)S(1)} %add_convert_fusion.7), channel_id=1, source_target_pairs={{0,2},{1,3},{2,0},{3,1},{4,6},{5,7},{6,4},{7,5},{8,10},{9,11},{10,... | collective-permute-start | bytes 393224 | tf_op jit(solution)/shard_map/ppermute | solution.py:80
  79.5 7.5 %collective-permute-start.26 = (bf16[16,4096]{1,0:T(8,128)(2,1)S(1)}, bf16[16,4096]{1,0:T(8,128)(2,1)S(1)}, u32[]{:S(2)}, u32[]{:S(2)}) collective-permute-start(bf16[16,4096]{1,0:T(8,128)(2,1)S(1)} %add_convert_fusion.6), channel_id=1, source_target_pairs={{0,2},{1,3},{2,0},{3,1},{4,6},{5,7},{6,4},{7,5},{8,10},{9,11},{10,... | collective-permute-start | bytes 393224 | tf_op jit(solution)/shard_map/ppermute | solution.py:80
  81.4 8.1 %collective-permute-start.29 = (bf16[8,4096]{1,0:T(8,128)(2,1)S(1)}, bf16[8,4096]{1,0:T(8,128)(2,1)S(1)}, u32[]{:S(2)}, u32[]{:S(2)}) collective-permute-start(bf16[8,4096]{1,0:T(8,128)(2,1)S(1)} %fusion.2), channel_id=1, source_target_pairs={{0,4},{1,5},{2,6},{3,7},{4,0},{5,1},{6,2},{7,3},{8,12},{9,13},{10,... | collective-permute-start | bytes 196616 | tf_op jit(solution)/shard_map/ppermute | solution.py:80
  84.2 8.8 %collective-permute-start.17 = (bf16[8,4096]{1,0:T(8,128)(2,1)S(1)}, bf16[8,4096]{1,0:T(8,128)(2,1)S(1)}, u32[]{:S(2)}, u32[]{:S(2)}) collective-permute-start(bf16[8,4096]{1,0:T(8,128)(2,1)S(1)} %add_convert_fusion.11), channel_id=1, source_target_pairs={{0,4},{1,5},{2,6},{3,7},{4,0},{5,1},{6,2},{7,3},{8,12},{9,13},{10,... | collective-permute-start | bytes 196616 | tf_op jit(solution)/shard_map/ppermute | solution.py:80
  87.0 6.7 %collective-permute-start.27 = (bf16[8,4096]{1,0:T(8,128)(2,1)S(1)}, bf16[8,4096]{1,0:T(8,128)(2,1)S(1)}, u32[]{:S(2)}, u32[]{:S(2)}) collective-permute-start(bf16[8,4096]{1,0:T(8,128)(2,1)S(1)} %add_convert_fusion.9), channel_id=1, source_target_pairs={{0,4},{1,5},{2,6},{3,7},{4,0},{5,1},{6,2},{7,3},{8,12},{9,13},{10,... | collective-permute-start | bytes 196616 | tf_op jit(solution)/shard_map/ppermute | solution.py:80

commit v16 on v15

--- a/solution.py
+++ b/solution.py
@@ -96,7 +96,7 @@
     return lambda d, e: (d, e ^ (2 * distance))
 
 
-def expert_kernel(slots, flag, mine):
+def expert_kernel(slots, flag, after, mine):
     d = lax.axis_index("dp")
     serving = jnp.where(flag[0] == 1, d ^ 1, d) * lax.axis_size("expert") + lax.axis_index("expert")
     expert = jnp.int32(0)
@@ -106,17 +106,17 @@
     mine[0] = expert
 
 
-def served_expert(slot_of, swap_flag):
+def served_expert(slot_of, swap_flag, after):
     scalars = pl.BlockSpec(memory_space=pltpu.SMEM)
     return pl.pallas_call(
         expert_kernel,
         out_shape=jax.ShapeDtypeStruct((1,), jnp.int32),
-        in_specs=[scalars] * 2,
+        in_specs=[scalars] * 2 + [pl.BlockSpec(memory_space=pl.ANY)],
         out_specs=scalars,
         compiler_params=pltpu.CompilerParams(vmem_limit_bytes=2**20),
         cost_estimate=pl.CostEstimate(flops=10**10, bytes_accessed=0, transcendentals=0),
         name="served_expert",
-    )(*in_hbm(slot_of.T), swap_flag)
+    )(*in_hbm(slot_of.T), swap_flag, after)
 
 
 def pack_kernel(tokens_hbm, ids_hbm, weights_hbm, *outs_and_scratch):
@@ -231,7 +231,8 @@
     for move in moves:
         (got,) = yield (permute(held, move),)
         if move is moves[2] and beside:
-            got = lax.optimization_barrier((got, *beside))[0]
+            got = lax.optimization_barrier((got, beside(before)))[0]
+        before = got
         held = jnp.concatenate([held, got])
     (sib,) = yield (permute(held, to_sibling),)
     out, out_sib = serve(held, sib)
@@ -275,12 +276,20 @@
     along = [along_line(2**bit) for bit in range(line_bits)][::-1]
     across = [over_first, over_second]
     routes = [along + across, along + across, along[:1] + across + along[1:]]
-    backs = [[3, 2, 1, 0], [3, 2, 1, 0], [2, 1, 3, 0]] if line_bits == 2 else [range(len(along + across))[::-1]]
+    backs = [[3, 2, 1, 0], [3, 2, 1, 0], [2, 3, 1, 0]] if line_bits == 2 else [range(len(along + across))[::-1]]
     step = ROWS_AT_ONCE if tok_rows % ROWS_AT_ONCE == 0 else tok_rows
     owns = packed(tokens, expert_ids, route_weight, step)
-    mine = served_expert(slot_of, lax.optimization_barrier((swap_flag, owns[0]))[0])
-    serve = lambda held, sib: serve_rows(held, sib, mine, top_count, w_gate[0], w_up[0], w_down[0])
-    chunks = [chunk_steps(own, routes[i % len(routes)], backs[i % len(backs)], serve, (mine,) if i == 1 else ()) for i, own in enumerate(owns)]
+    found = []
+
+    def find(after):
+        found.append(served_expert(slot_of, swap_flag, after))
+        return found[0]
+
+    serve = lambda held, sib: serve_rows(held, sib, found[0], top_count, w_gate[0], w_up[0], w_down[0])
+    chunks = [
+        chunk_steps(own, routes[i % len(routes)], backs[i % len(backs)], serve, find if i == 0 else None)
+        for i, own in enumerate(owns)
+    ]
     guards = GUARDS if len(chunks) == 3 and line_bits == 2 else []
     return jnp.concatenate(run_steps(chunks, guards))
 

time: 94.6 us -> 93.7 us (level)
  starting transfers between devices: 43.7 us -> 42.4 us
    ppermute x30, starting transfers between devices: 43.7 us -> 42.4 us  [permute(): return lax.ppermute(value, AXES, pairs)]
  transfers between devices with their start and end apart: 30 -> 30, of which waited for: 14 -> 13; matrix products, arithmetic and copies ran while one was open for 2% -> 2% of each run, Pallas kernels for 15% -> 15%
where the time goes in v16:
time: 93.7 us; the launch traced here: 93.5 us
  starting transfers between devices  42.4 us (45%)
  waiting for transfers between devices  33 us (35%)
  Pallas kernels  14.8 us (16%)
  other arithmetic  2.13 us (2%)
    ppermute x30, starting transfers between devices, permute(): return lax.ppermute(value, AXES, pairs)  42.4 us
    ppermute x30, waiting for transfers between devices, permute(): return lax.ppermute(value, AXES, pairs)  33 us
    pallas_call x3, Pallas kernels, serve_rows(): pl.pallas_call(functools.partial(serve_kernel, top_count), out_shape=(out...  12.4 us
  transfers between devices with their start and end apart: 30, of which 13 were waited for; matrix products, arithmetic and copies ran while one was open for 2% of the time, Pallas kernels for 15%

profile of v16, /device:TPU:0, one launch (start us, length us, event | category | flops | bytes accessed | tf_op | source)
XLA Modules:
  0.0 93.5 jit_solution(4738941541703227854)
XLA Ops:
  0.0 1.0 %pack_rows.1 = (bf16[8,4224]{1,0:T(8,128)(2,1)S(1)}, bf16[8,4224]{1,0:T(8,128)(2,1)S(1)}, bf16[8,4224]{1,0:T(8,128)(2,1)S(1)}) custom-call(bf16[24,4096]{1,0:T(8,128)(2,1)} %tokens_hbm.1, s32[8,24]{1,0:T(8,128)} %bitcast.57, f32[8,24]{1,0:T(8,128)} %bitcast.58), custom_call_target="tpu_custom_call" | custom-call | bytes 393216 | tf_op jit(solution)/shard_map/pack_rows/pallas_call | solution.py:158
  1.0 4.1 %collective-permute-start = (bf16[8,4224]{1,0:T(8,128)(2,1)S(1)}, bf16[8,4224]{1,0:T(8,128)(2,1)S(1)}, u32[]{:S(2)}, u32[]{:S(2)}) collective-permute-start(bf16[8,4224]{1,0:T(8,128)(2,1)S(1)} %get-tuple-element.22), channel_id=1, source_target_pairs={{0,4},{1,5},{2,6},{3,7},{4,0},{5,1},{6,2},{7,3},{8,12},{9,13},{10,... | collective-permute-start | bytes 202760 | tf_op jit(solution)/shard_map/ppermute | solution.py:80
  5.1 0.1 collective-permute-start.7
  5.2 2.8 %collective-permute-start.18 = (bf16[8,4224]{1,0:T(8,128)(2,1)S(1)}, bf16[8,4224]{1,0:T(8,128)(2,1)S(1)}, u32[]{:S(2)}, u32[]{:S(2)}) collective-permute-start(bf16[8,4224]{1,0:T(8,128)(2,1)S(1)} %get-tuple-element.33), channel_id=1, source_target_pairs={{0,4},{1,5},{2,6},{3,7},{4,0},{5,1},{6,2},{7,3},{8,12},{9,13},{10,... | collective-permute-start | bytes 202760 | tf_op jit(solution)/shard_map/ppermute | solution.py:80
  8.7 0.2 collective-permute-done
  8.9 3.6 %collective-permute-start.1 = (bf16[16,4224]{1,0:T(8,128)(2,1)S(1)}, bf16[16,4224]{1,0:T(8,128)(2,1)S(1)}, u32[]{:S(2)}, u32[]{:S(2)}) collective-permute-start(bf16[16,4224]{1,0:T(8,128)(2,1)S(1)} %pad_maximum_fusion.7), channel_id=1, source_target_pairs={{0,2},{1,3},{2,0},{3,1},{4,6},{5,7},{6,4},{7,5},{8,10},{9,11},{10,... | collective-permute-start | bytes 405512 | tf_op jit(solution)/shard_map/ppermute | solution.py:80
  12.5 1.2 %collective-permute-done.7 = bf16[8,4224]{1,0:T(8,128)(2,1)S(1)} collective-permute-done((bf16[8,4224]{1,0:T(8,128)(2,1)S(1)}, bf16[8,4224]{1,0:T(8,128)(2,1)S(1)}, u32[]{:S(2)}, u32[]{:S(2)}) %collective-permute-start.7) | collective-permute-done | bytes 67616 | tf_op jit(solution)/shard_map/ppermute | solution.py:80
  13.7 1.6 %collective-permute-start.8 = (bf16[16,4224]{1,0:T(8,128)(2,1)S(1)}, bf16[16,4224]{1,0:T(8,128)(2,1)S(1)}, u32[]{:S(2)}, u32[]{:S(2)}) collective-permute-start(bf16[16,4224]{1,0:T(8,128)(2,1)S(1)} %pad_maximum_fusion.8), channel_id=1, source_target_pairs={{0,1},{1,0},{2,3},{3,2},{4,5},{5,4},{6,7},{7,6},{8,24},{9,25},{10,... | collective-permute-start | bytes 405512 | tf_op jit(solution)/shard_map/ppermute | solution.py:80
  15.3 0.7 collective-permute-start.19
  16.0 2.7 %collective-permute-done.8 = bf16[16,4224]{1,0:T(8,128)(2,1)S(1)} collective-permute-done((bf16[16,4224]{1,0:T(8,128)(2,1)S(1)}, bf16[16,4224]{1,0:T(8,128)(2,1)S(1)}, u32[]{:S(2)}, u32[]{:S(2)}) %collective-permute-start.8) | collective-permute-done | bytes 135200 | tf_op jit(solution)/shard_map/ppermute | solution.py:80
  18.8 1.6 %collective-permute-start.9 = (bf16[32,4224]{1,0:T(8,128)(2,1)S(1)}, bf16[32,4224]{1,0:T(8,128)(2,1)S(1)}, u32[]{:S(2)}, u32[]{:S(2)}) collective-permute-start(bf16[32,4224]{1,0:T(8,128)(2,1)S(1)} %pad_maximum_fusion.4), channel_id=1, source_target_pairs={{0,16},{1,17},{2,18},{3,19},{4,20},{5,21},{6,22},{7,23},{8,9},{9,8... | collective-permute-start | bytes 811016 | tf_op jit(solution)/shard_map/ppermute | solution.py:80
  20.4 1.6 %collective-permute-start.2 = (bf16[32,4224]{1,0:T(8,128)(2,1)S(1)}, bf16[32,4224]{1,0:T(8,128)(2,1)S(1)}, u32[]{:S(2)}, u32[]{:S(2)}) collective-permute-start(bf16[32,4224]{1,0:T(8,128)(2,1)S(1)} %pad_maximum_fusion.3), channel_id=1, source_target_pairs={{0,1},{1,0},{2,3},{3,2},{4,5},{5,4},{6,7},{7,6},{8,24},{9,25},{10,... | collective-permute-start | bytes 811016 | tf_op jit(solution)/shard_map/ppermute | solution.py:80
  22.0 0.6 collective-permute-start.20
  22.6 0.0 copy-start.2
  22.7 1.4 %served_expert.1.mine = s32[1]{0:T(128)} custom-call(s32[2,16]{1,0:T(2,128)} %bitcast.59, s32[1]{0:T(128)S(6)} %copy.21.flag, bf16[16,4224]{1,0:T(8,128)(2,1)S(1)} %collective-permute-done.1.after), custom_call_target="tpu_custom_call" | custom-call | flops 10000000000 | tf_op jit(solution)/shard_map/served_expert/pallas_call | solution.py:111
  24.1 4.2 %collective-permute-done.9 = bf16[32,4224]{1,0:T(8,128)(2,1)S(1)} collective-permute-done((bf16[32,4224]{1,0:T(8,128)(2,1)S(1)}, bf16[32,4224]{1,0:T(8,128)(2,1)S(1)}, u32[]{:S(2)}, u32[]{:S(2)}) %collective-permute-start.9) | collective-permute-done | bytes 270368 | tf_op jit(solution)/shard_map/ppermute | solution.py:80
  28.3 0.2 collective-permute-start.10
  28.5 2.1 %collective-permute-start.3 = (bf16[64,4224]{1,0:T(8,128)(2,1)S(1)}, bf16[64,4224]{1,0:T(8,128)(2,1)S(1)}, u32[]{:S(2)}, u32[]{:S(2)}) collective-permute-start(bf16[64,4224]{1,0:T(8,128)(2,1)S(1)} %pad_maximum_fusion), channel_id=1, source_target_pairs={{0,16},{1,17},{2,18},{3,19},{4,20},{5,21},{6,22},{7,23},{8,9},{9,8... | collective-permute-start | bytes 1622024 | tf_op jit(solution)/shard_map/ppermute | solution.py:80
  30.6 0.2 collective-permute-done.20
  30.9 0.1 collective-permute-start.21
  31.0 7.0 %collective-permute-done.3 = bf16[64,4224]{1,0:T(8,128)(2,1)S(1)} collective-permute-done((bf16[64,4224]{1,0:T(8,128)(2,1)S(1)}, bf16[64,4224]{1,0:T(8,128)(2,1)S(1)}, u32[]{:S(2)}, u32[]{:S(2)}) %collective-permute-start.3) | collective-permute-done | bytes 540704 | tf_op jit(solution)/shard_map/ppermute | solution.py:80
  38.0 0.1 collective-permute-start.4
  38.1 0.1 constant_dynamic-update-slice_fusion.5.own
  38.1 0.6 collective-permute-start.11
  38.7 2.0 %collective-permute-done.4.sib = bf16[128,4224]{1,0:T(8,128)(2,1)S(1)} collective-permute-done((bf16[128,4224]{1,0:T(8,128)(2,1)S(1)}, bf16[128,4224]{1,0:T(8,128)(2,1)S(1)}, u32[]{:S(2)}, u32[]{:S(2)}) %collective-permute-start.4) | collective-permute-done | bytes 1081376 | tf_op jit(solution)/shard_map/ppermute | solution.py:80
  40.8 4.1 %serve_rows.3 = (bf16[128,4096]{1,0:T(8,128)(2,1)S(1)}, bf16[128,4096]{1,0:T(8,128)(2,1)S(1)}) custom-call(s32[1]{0:T(128)} %served_expert.1.mine, bf16[128,4224]{1,0:T(8,128)(2,1)S(1)} %constant_dynamic-update-slice_fusion.own, bf16[128,4224]{1,0:T(8,128)(2,1)S(1)} %collective-permute-done.4.sib, bf16[4096,512]{1,0:T(8,128)(2,1)S(1)} %bitcast.37, ...), custom_call_target="tpu_custom_call" | custom-call | flops 3221225472 | bytes 16777216 | tf_op jit(solution)/shard_map/serve_rows/pallas_call | solution.py:207
  44.9 0.2 collective-permute-start.5
  45.1 0.1 constant_dynamic-update-slice_fusion.10.own
  45.2 0.4 collective-permute-start.22
  45.6 4.1 %serve_rows.4 = (bf16[128,4096]{1,0:T(8,128)(2,1)S(1)}, bf16[128,4096]{1,0:T(8,128)(2,1)S(1)}) custom-call(s32[1]{0:T(128)} %served_expert.1.mine, bf16[128,4224]{1,0:T(8,128)(2,1)S(1)} %constant_dynamic-update-slice_fusion.5.own, bf16[128,4224]{1,0:T(8,128)(2,1)S(1)} %collective-permute-done.11.sib, bf16[4096,512]{1,0:T(8,128)(2,1)S(1)} %bitcast.38, ...), custom_call_target="tpu_custom_call" | custom-call | flops 3221225472 | bytes 16777216 | tf_op jit(solution)/shard_map/serve_rows/pallas_call | solution.py:207
  49.8 0.2 collective-permute-start.12
  50.0 0.1 add_convert_fusion.2
  50.1 2.1 %collective-permute-start.6 = (bf16[64,4096]{1,0:T(8,128)(2,1)S(1)}, bf16[64,4096]{1,0:T(8,128)(2,1)S(1)}, u32[]{:S(2)}, u32[]{:S(2)}) collective-permute-start(bf16[64,4096]{1,0:T(8,128)(2,1)S(1)} %add_convert_fusion.2), channel_id=1, source_target_pairs={{0,16},{1,17},{2,18},{3,19},{4,20},{5,21},{6,22},{7,23},{8,9},{9,8... | collective-permute-start | bytes 1572872 | tf_op jit(solution)/shard_map/ppermute | solution.py:80
  52.2 4.1 %serve_rows.5 = (bf16[128,4096]{1,0:T(8,128)(2,1)S(1)}, bf16[128,4096]{1,0:T(8,128)(2,1)S(1)}) custom-call(s32[1]{0:T(128)} %served_expert.1.mine, bf16[128,4224]{1,0:T(8,128)(2,1)S(1)} %constant_dynamic-update-slice_fusion.10.own, bf16[128,4224]{1,0:T(8,128)(2,1)S(1)} %collective-permute-done.22.sib, bf16[4096,512]{1,0:T(8,128)(2,1)S(1)} %bitcast.39, ...), custom_call_target="tpu_custom_call" | custom-call | flops 3221225472 | bytes 16777216 | tf_op jit(solution)/shard_map/serve_rows/pallas_call | solution.py:207
  56.3 0.3 collective-permute-start.23
  56.6 0.1 add_convert_fusion.1
  56.7 1.6 %collective-permute-start.13 = (bf16[64,4096]{1,0:T(8,128)(2,1)S(1)}, bf16[64,4096]{1,0:T(8,128)(2,1)S(1)}, u32[]{:S(2)}, u32[]{:S(2)}) collective-permute-start(bf16[64,4096]{1,0:T(8,128)(2,1)S(1)} %bitcast.56), channel_id=1, source_target_pairs={{0,16},{1,17},{2,18},{3,19},{4,20},{5,21},{6,22},{7,23},{8,9},{9,8... | collective-permute-start | bytes 1572872 | tf_op jit(solution)/shard_map/ppermute | solution.py:80
  58.3 0.1 convert_add_fusion
  58.3 0.7 collective-permute-done.23
  59.1 0.1 add_convert_fusion
  59.2 1.4 %collective-permute-start.24 = (bf16[64,4096]{1,0:T(8,128)(2,1)S(1)}, bf16[64,4096]{1,0:T(8,128)(2,1)S(1)}, u32[]{:S(2)}, u32[]{:S(2)}) collective-permute-start(bf16[64,4096]{1,0:T(8,128)(2,1)S(1)} %add_convert_fusion), channel_id=1, source_target_pairs={{0,16},{1,17},{2,18},{3,19},{4,20},{5,21},{6,22},{7,23},{8,9},{9,8... | collective-permute-start | bytes 1572872 | tf_op jit(solution)/shard_map/ppermute | solution.py:80
  60.6 5.4 %collective-permute-done.13 = bf16[64,4096]{1,0:T(8,128)(2,1)S(1)} collective-permute-done((bf16[64,4096]{1,0:T(8,128)(2,1)S(1)}, bf16[64,4096]{1,0:T(8,128)(2,1)S(1)}, u32[]{:S(2)}, u32[]{:S(2)}) %collective-permute-start.13) | collective-permute-done | bytes 524320 | tf_op jit(solution)/shard_map/ppermute | solution.py:80
  66.0 1.5 %collective-permute-start.16 = (bf16[32,4096]{1,0:T(8,128)(2,1)S(1)}, bf16[32,4096]{1,0:T(8,128)(2,1)S(1)}, u32[]{:S(2)}, u32[]{:S(2)}) collective-permute-start(bf16[32,4096]{1,0:T(8,128)(2,1)S(1)} %fusion), channel_id=1, source_target_pairs={{0,2},{1,3},{2,0},{3,1},{4,6},{5,7},{6,4},{7,5},{8,10},{9,11},{10,... | collective-permute-start | bytes 786440 | tf_op jit(solution)/shard_map/ppermute | solution.py:80
  67.5 0.1 add_convert_fusion.4
  67.6 1.5 %collective-permute-start.14 = (bf16[32,4096]{1,0:T(8,128)(2,1)S(1)}, bf16[32,4096]{1,0:T(8,128)(2,1)S(1)}, u32[]{:S(2)}, u32[]{:S(2)}) collective-permute-start(bf16[32,4096]{1,0:T(8,128)(2,1)S(1)} %add_convert_fusion.4), channel_id=1, source_target_pairs={{0,1},{1,0},{2,3},{3,2},{4,5},{5,4},{6,7},{7,6},{8,24},{9,25},{10,... | collective-permute-start | bytes 786440 | tf_op jit(solution)/shard_map/ppermute | solution.py:80
  69.1 4.6 %collective-permute-done.24 = bf16[64,4096]{1,0:T(8,128)(2,1)S(1)} collective-permute-done((bf16[64,4096]{1,0:T(8,128)(2,1)S(1)}, bf16[64,4096]{1,0:T(8,128)(2,1)S(1)}, u32[]{:S(2)}, u32[]{:S(2)}) %collective-permute-start.24) | collective-permute-done | bytes 524320 | tf_op jit(solution)/shard_map/ppermute | solution.py:80
  73.7 0.1 add_convert_fusion.3
  73.8 1.3 %collective-permute-start.25 = (bf16[32,4096]{1,0:T(8,128)(2,1)S(1)}, bf16[32,4096]{1,0:T(8,128)(2,1)S(1)}, u32[]{:S(2)}, u32[]{:S(2)}) collective-permute-start(bf16[32,4096]{1,0:T(8,128)(2,1)S(1)} %add_convert_fusion.3), channel_id=1, source_target_pairs={{0,1},{1,0},{2,3},{3,2},{4,5},{5,4},{6,7},{7,6},{8,24},{9,25},{10,... | collective-permute-start | bytes 786440 | tf_op jit(solution)/shard_map/ppermute | solution.py:80
  75.1 0.1 fusion.2
  75.2 0.8 collective-permute-start.28
  76.0 0.1 add_convert_fusion.6
  76.1 2.3 %collective-permute-start.15 = (bf16[16,4096]{1,0:T(8,128)(2,1)S(1)}, bf16[16,4096]{1,0:T(8,128)(2,1)S(1)}, u32[]{:S(2)}, u32[]{:S(2)}) collective-permute-start(bf16[16,4096]{1,0:T(8,128)(2,1)S(1)} %add_convert_fusion.6), channel_id=1, source_target_pairs={{0,2},{1,3},{2,0},{3,1},{4,6},{5,7},{6,4},{7,5},{8,10},{9,11},{10,... | collective-permute-start | bytes 393224 | tf_op jit(solution)/shard_map/ppermute | solution.py:80
  78.3 1.9 %collective-permute-done.25 = bf16[32,4096]{1,0:T(8,128)(2,1)S(1)} collective-permute-done((bf16[32,4096]{1,0:T(8,128)(2,1)S(1)}, bf16[32,4096]{1,0:T(8,128)(2,1)S(1)}, u32[]{:S(2)}, u32[]{:S(2)}) %collective-permute-start.25) | collective-permute-done | bytes 262176 | tf_op jit(solution)/shard_map/ppermute | solution.py:80
  80.2 0.1 add_convert_fusion.5
  80.3 2.3 %collective-permute-start.26 = (bf16[16,4096]{1,0:T(8,128)(2,1)S(1)}, bf16[16,4096]{1,0:T(8,128)(2,1)S(1)}, u32[]{:S(2)}, u32[]{:S(2)}) collective-permute-start(bf16[16,4096]{1,0:T(8,128)(2,1)S(1)} %add_convert_fusion.5), channel_id=1, source_target_pairs={{0,2},{1,3},{2,0},{3,1},{4,6},{5,7},{6,4},{7,5},{8,10},{9,11},{10,... | collective-permute-start | bytes 393224 | tf_op jit(solution)/shard_map/ppermute | solution.py:80
  82.6 2.8 %collective-permute-start.29 = (bf16[8,4096]{1,0:T(8,128)(2,1)S(1)}, bf16[8,4096]{1,0:T(8,128)(2,1)S(1)}, u32[]{:S(2)}, u32[]{:S(2)}) collective-permute-start(bf16[8,4096]{1,0:T(8,128)(2,1)S(1)} %fusion.5), channel_id=1, source_target_pairs={{0,4},{1,5},{2,6},{3,7},{4,0},{5,1},{6,2},{7,3},{8,12},{9,13},{10,... | collective-permute-start | bytes 196616 | tf_op jit(solution)/shard_map/ppermute | solution.py:80
  85.4 0.8 collective-permute-start.17
  86.3 3.5 %collective-permute-start.27 = (bf16[8,4096]{1,0:T(8,128)(2,1)S(1)}, bf16[8,4096]{1,0:T(8,128)(2,1)S(1)}, u32[]{:S(2)}, u32[]{:S(2)}) collective-permute-start(bf16[8,4096]{1,0:T(8,128)(2,1)S(1)} %add_convert_fusion.8), channel_id=1, source_target_pairs={{0,4},{1,5},{2,6},{3,7},{4,0},{5,1},{6,2},{7,3},{8,12},{9,13},{10,... | collective-permute-start | bytes 196616 | tf_op jit(solution)/shard_map/ppermute | solution.py:80
  89.8 0.1 fusion.9
  89.9 1.5 %collective-permute-done.17 = bf16[8,4096]{1,0:T(8,128)(2,1)S(1)} collective-permute-done((bf16[8,4096]{1,0:T(8,128)(2,1)S(1)}, bf16[8,4096]{1,0:T(8,128)(2,1)S(1)}, u32[]{:S(2)}, u32[]{:S(2)}) %collective-permute-start.17) | collective-permute-done | bytes 65568 | tf_op jit(solution)/shard_map/ppermute | solution.py:80
  91.4 0.1 add_convert_fusion.9
  91.4 1.3 %collective-permute-done.27 = bf16[8,4096]{1,0:T(8,128)(2,1)S(1)} collective-permute-done((bf16[8,4096]{1,0:T(8,128)(2,1)S(1)}, bf16[8,4096]{1,0:T(8,128)(2,1)S(1)}, u32[]{:S(2)}, u32[]{:S(2)}) %collective-permute-start.27) | collective-permute-done | bytes 65568 | tf_op jit(solution)/shard_map/ppermute | solution.py:80
  92.8 0.1 add_convert_fusion.7
  92.8 0.7 pad_maximum_fusion.6
  (47 shorter events, 0.7 us)
Async XLA Ops:
  1.0 7.9 %collective-permute-start = (bf16[8,4224]{1,0:T(8,128)(2,1)S(1)}, bf16[8,4224]{1,0:T(8,128)(2,1)S(1)}, u32[]{:S(2)}, u32[]{:S(2)}) collective-permute-start(bf16[8,4224]{1,0:T(8,128)(2,1)S(1)} %get-tuple-element.22), channel_id=1, source_target_pairs={{0,4},{1,5},{2,6},{3,7},{4,0},{5,1},{6,2},{7,3},{8,12},{9,13},{10,... | collective-permute-start | bytes 202760 | tf_op jit(solution)/shard_map/ppermute | solution.py:80
  5.1 8.6 %collective-permute-start.7 = (bf16[8,4224]{1,0:T(8,128)(2,1)S(1)}, bf16[8,4224]{1,0:T(8,128)(2,1)S(1)}, u32[]{:S(2)}, u32[]{:S(2)}) collective-permute-start(bf16[8,4224]{1,0:T(8,128)(2,1)S(1)} %get-tuple-element.26), channel_id=1, source_target_pairs={{0,4},{1,5},{2,6},{3,7},{4,0},{5,1},{6,2},{7,3},{8,12},{9,13},{10,... | collective-permute-start | bytes 202760 | tf_op jit(solution)/shard_map/ppermute | solution.py:80
  5.2 10.1 %collective-permute-start.18 = (bf16[8,4224]{1,0:T(8,128)(2,1)S(1)}, bf16[8,4224]{1,0:T(8,128)(2,1)S(1)}, u32[]{:S(2)}, u32[]{:S(2)}) collective-permute-start(bf16[8,4224]{1,0:T(8,128)(2,1)S(1)} %get-tuple-element.33), channel_id=1, source_target_pairs={{0,4},{1,5},{2,6},{3,7},{4,0},{5,1},{6,2},{7,3},{8,12},{9,13},{10,... | collective-permute-start | bytes 202760 | tf_op jit(solution)/shard_map/ppermute | solution.py:80
  8.9 11.5 %collective-permute-start.1 = (bf16[16,4224]{1,0:T(8,128)(2,1)S(1)}, bf16[16,4224]{1,0:T(8,128)(2,1)S(1)}, u32[]{:S(2)}, u32[]{:S(2)}) collective-permute-start(bf16[16,4224]{1,0:T(8,128)(2,1)S(1)} %pad_maximum_fusion.7), channel_id=1, source_target_pairs={{0,2},{1,3},{2,0},{3,1},{4,6},{5,7},{6,4},{7,5},{8,10},{9,11},{10,... | collective-permute-start | bytes 405512 | tf_op jit(solution)/shard_map/ppermute | solution.py:80
  13.7 5.1 %collective-permute-start.8 = (bf16[16,4224]{1,0:T(8,128)(2,1)S(1)}, bf16[16,4224]{1,0:T(8,128)(2,1)S(1)}, u32[]{:S(2)}, u32[]{:S(2)}) collective-permute-start(bf16[16,4224]{1,0:T(8,128)(2,1)S(1)} %pad_maximum_fusion.8), channel_id=1, source_target_pairs={{0,1},{1,0},{2,3},{3,2},{4,5},{5,4},{6,7},{7,6},{8,24},{9,25},{10,... | collective-permute-start | bytes 405512 | tf_op jit(solution)/shard_map/ppermute | solution.py:80
  15.3 6.7 %collective-permute-start.19 = (bf16[16,4224]{1,0:T(8,128)(2,1)S(1)}, bf16[16,4224]{1,0:T(8,128)(2,1)S(1)}, u32[]{:S(2)}, u32[]{:S(2)}) collective-permute-start(bf16[16,4224]{1,0:T(8,128)(2,1)S(1)} %pad_maximum_fusion.9), channel_id=1, source_target_pairs={{0,2},{1,3},{2,0},{3,1},{4,6},{5,7},{6,4},{7,5},{8,10},{9,11},{10,... | collective-permute-start | bytes 405512 | tf_op jit(solution)/shard_map/ppermute | solution.py:80
  18.8 9.4 %collective-permute-start.9 = (bf16[32,4224]{1,0:T(8,128)(2,1)S(1)}, bf16[32,4224]{1,0:T(8,128)(2,1)S(1)}, u32[]{:S(2)}, u32[]{:S(2)}) collective-permute-start(bf16[32,4224]{1,0:T(8,128)(2,1)S(1)} %pad_maximum_fusion.4), channel_id=1, source_target_pairs={{0,16},{1,17},{2,18},{3,19},{4,20},{5,21},{6,22},{7,23},{8,9},{9,8... | collective-permute-start | bytes 811016 | tf_op jit(solution)/shard_map/ppermute | solution.py:80
  20.4 8.0 %collective-permute-start.2 = (bf16[32,4224]{1,0:T(8,128)(2,1)S(1)}, bf16[32,4224]{1,0:T(8,128)(2,1)S(1)}, u32[]{:S(2)}, u32[]{:S(2)}) collective-permute-start(bf16[32,4224]{1,0:T(8,128)(2,1)S(1)} %pad_maximum_fusion.3), channel_id=1, source_target_pairs={{0,1},{1,0},{2,3},{3,2},{4,5},{5,4},{6,7},{7,6},{8,24},{9,25},{10,... | collective-permute-start | bytes 811016 | tf_op jit(solution)/shard_map/ppermute | solution.py:80
  22.0 8.8 %collective-permute-start.20 = (bf16[32,4224]{1,0:T(8,128)(2,1)S(1)}, bf16[32,4224]{1,0:T(8,128)(2,1)S(1)}, u32[]{:S(2)}, u32[]{:S(2)}) collective-permute-start(bf16[32,4224]{1,0:T(8,128)(2,1)S(1)} %pad_maximum_fusion.5), channel_id=1, source_target_pairs={{0,1},{1,0},{2,3},{3,2},{4,5},{5,4},{6,7},{7,6},{8,24},{9,25},{10,... | collective-permute-start | bytes 811016 | tf_op jit(solution)/shard_map/ppermute | solution.py:80
  22.6 18.1 %copy-start.1 = (bf16[1,4096,512]{2,1,0:T(8,128)(2,1)S(1)}, bf16[1,4096,512]{2,1,0:T(8,128)(2,1)}, u32[]{:S(2)}) copy-start(bf16[1,4096,512]{2,1,0:T(8,128)(2,1)} %param.14) | copy-start | bytes 12582916
  22.6 18.1 %copy-start.2 = (bf16[1,512,4096]{2,1,0:T(8,128)(2,1)S(1)}, bf16[1,512,4096]{2,1,0:T(8,128)(2,1)}, u32[]{:S(2)}) copy-start(bf16[1,512,4096]{2,1,0:T(8,128)(2,1)} %param.15) | copy-start | bytes 12582916
  28.3 9.8 %collective-permute-start.10 = (bf16[64,4224]{1,0:T(8,128)(2,1)S(1)}, bf16[64,4224]{1,0:T(8,128)(2,1)S(1)}, u32[]{:S(2)}, u32[]{:S(2)}) collective-permute-start(bf16[64,4224]{1,0:T(8,128)(2,1)S(1)} %pad_maximum_fusion.1), channel_id=1, source_target_pairs={{0,2},{1,3},{2,0},{3,1},{4,6},{5,7},{6,4},{7,5},{8,10},{9,11},{10,... | collective-permute-start | bytes 1622024 | tf_op jit(solution)/shard_map/ppermute | solution.py:80
  28.5 9.4 %collective-permute-start.3 = (bf16[64,4224]{1,0:T(8,128)(2,1)S(1)}, bf16[64,4224]{1,0:T(8,128)(2,1)S(1)}, u32[]{:S(2)}, u32[]{:S(2)}) collective-permute-start(bf16[64,4224]{1,0:T(8,128)(2,1)S(1)} %pad_maximum_fusion), channel_id=1, source_target_pairs={{0,16},{1,17},{2,18},{3,19},{4,20},{5,21},{6,22},{7,23},{8,9},{9,8... | collective-permute-start | bytes 1622024 | tf_op jit(solution)/shard_map/ppermute | solution.py:80
  30.8 9.9 %copy-start = (bf16[1,4096,512]{2,1,0:T(8,128)(2,1)S(1)}, bf16[1,4096,512]{2,1,0:T(8,128)(2,1)}, u32[]{:S(2)}) copy-start(bf16[1,4096,512]{2,1,0:T(8,128)(2,1)} %param.13) | copy-start | bytes 12582916
  30.9 14.3 %collective-permute-start.21 = (bf16[64,4224]{1,0:T(8,128)(2,1)S(1)}, bf16[64,4224]{1,0:T(8,128)(2,1)S(1)}, u32[]{:S(2)}, u32[]{:S(2)}) collective-permute-start(bf16[64,4224]{1,0:T(8,128)(2,1)S(1)} %pad_maximum_fusion.2), channel_id=1, source_target_pairs={{0,16},{1,17},{2,18},{3,19},{4,20},{5,21},{6,22},{7,23},{8,9},{9,8... | collective-permute-start | bytes 1622024 | tf_op jit(solution)/shard_map/ppermute | solution.py:80
  38.0 2.8 %collective-permute-start.4 = (bf16[128,4224]{1,0:T(8,128)(2,1)S(1)}, bf16[128,4224]{1,0:T(8,128)(2,1)S(1)}, u32[]{:S(2)}, u32[]{:S(2)}) collective-permute-start(bf16[128,4224]{1,0:T(8,128)(2,1)S(1)} %constant_dynamic-update-slice_fusion.own), channel_id=1, source_target_pairs={{0,8},{1,9},{2,10},{3,11},{4,12},{5,13},{6,14},{7,15},{8,0},{9,1},... | collective-permute-start | bytes 3244040 | tf_op jit(solution)/shard_map/ppermute | solution.py:80
  38.1 7.5 %collective-permute-start.11 = (bf16[128,4224]{1,0:T(8,128)(2,1)S(1)}, bf16[128,4224]{1,0:T(8,128)(2,1)S(1)}, u32[]{:S(2)}, u32[]{:S(2)}) collective-permute-start(bf16[128,4224]{1,0:T(8,128)(2,1)S(1)} %constant_dynamic-update-slice_fusion.5.own), channel_id=1, source_target_pairs={{0,8},{1,9},{2,10},{3,11},{4,12},{5,13},{6,14},{7,15},{8,0},{9,1},... | collective-permute-start | bytes 3244040 | tf_op jit(solution)/shard_map/ppermute | solution.py:80
  44.9 4.9 %collective-permute-start.5 = (bf16[128,4096]{1,0:T(8,128)(2,1)S(1)}, bf16[128,4096]{1,0:T(8,128)(2,1)S(1)}, u32[]{:S(2)}, u32[]{:S(2)}) collective-permute-start(bf16[128,4096]{1,0:T(8,128)(2,1)S(1)} %get-tuple-element.25), channel_id=1, source_target_pairs={{0,8},{1,9},{2,10},{3,11},{4,12},{5,13},{6,14},{7,15},{8,0},{9,1},... | collective-permute-start | bytes 3145736 | tf_op jit(solution)/shard_map/ppermute | solution.py:80
  45.2 7.0 %collective-permute-start.22 = (bf16[128,4224]{1,0:T(8,128)(2,1)S(1)}, bf16[128,4224]{1,0:T(8,128)(2,1)S(1)}, u32[]{:S(2)}, u32[]{:S(2)}) collective-permute-start(bf16[128,4224]{1,0:T(8,128)(2,1)S(1)} %constant_dynamic-update-slice_fusion.10.own), channel_id=1, source_target_pairs={{0,8},{1,9},{2,10},{3,11},{4,12},{5,13},{6,14},{7,15},{8,0},{9,1},... | collective-permute-start | bytes 3244040 | tf_op jit(solution)/shard_map/ppermute | solution.py:80
  49.8 6.8 %collective-permute-start.12 = (bf16[128,4096]{1,0:T(8,128)(2,1)S(1)}, bf16[128,4096]{1,0:T(8,128)(2,1)S(1)}, u32[]{:S(2)}, u32[]{:S(2)}) collective-permute-start(bf16[128,4096]{1,0:T(8,128)(2,1)S(1)} %get-tuple-element.29), channel_id=1, source_target_pairs={{0,8},{1,9},{2,10},{3,11},{4,12},{5,13},{6,14},{7,15},{8,0},{9,1},... | collective-permute-start | bytes 3145736 | tf_op jit(solution)/shard_map/ppermute | solution.py:80
  50.1 17.4 %collective-permute-start.6 = (bf16[64,4096]{1,0:T(8,128)(2,1)S(1)}, bf16[64,4096]{1,0:T(8,128)(2,1)S(1)}, u32[]{:S(2)}, u32[]{:S(2)}) collective-permute-start(bf16[64,4096]{1,0:T(8,128)(2,1)S(1)} %add_convert_fusion.2), channel_id=1, source_target_pairs={{0,16},{1,17},{2,18},{3,19},{4,20},{5,21},{6,22},{7,23},{8,9},{9,8... | collective-permute-start | bytes 1572872 | tf_op jit(solution)/shard_map/ppermute | solution.py:80
  56.3 2.7 %collective-permute-start.23 = (bf16[128,4096]{1,0:T(8,128)(2,1)S(1)}, bf16[128,4096]{1,0:T(8,128)(2,1)S(1)}, u32[]{:S(2)}, u32[]{:S(2)}) collective-permute-start(bf16[128,4096]{1,0:T(8,128)(2,1)S(1)} %get-tuple-element.37), channel_id=1, source_target_pairs={{0,8},{1,9},{2,10},{3,11},{4,12},{5,13},{6,14},{7,15},{8,0},{9,1},... | collective-permute-start | bytes 3145736 | tf_op jit(solution)/shard_map/ppermute | solution.py:80
  56.7 9.2 %collective-permute-start.13 = (bf16[64,4096]{1,0:T(8,128)(2,1)S(1)}, bf16[64,4096]{1,0:T(8,128)(2,1)S(1)}, u32[]{:S(2)}, u32[]{:S(2)}) collective-permute-start(bf16[64,4096]{1,0:T(8,128)(2,1)S(1)} %bitcast.56), channel_id=1, source_target_pairs={{0,16},{1,17},{2,18},{3,19},{4,20},{5,21},{6,22},{7,23},{8,9},{9,8... | collective-permute-start | bytes 1572872 | tf_op jit(solution)/shard_map/ppermute | solution.py:80
  59.2 14.5 %collective-permute-start.24 = (bf16[64,4096]{1,0:T(8,128)(2,1)S(1)}, bf16[64,4096]{1,0:T(8,128)(2,1)S(1)}, u32[]{:S(2)}, u32[]{:S(2)}) collective-permute-start(bf16[64,4096]{1,0:T(8,128)(2,1)S(1)} %add_convert_fusion), channel_id=1, source_target_pairs={{0,16},{1,17},{2,18},{3,19},{4,20},{5,21},{6,22},{7,23},{8,9},{9,8... | collective-permute-start | bytes 1572872 | tf_op jit(solution)/shard_map/ppermute | solution.py:80
  66.0 9.1 %collective-permute-start.16 = (bf16[32,4096]{1,0:T(8,128)(2,1)S(1)}, bf16[32,4096]{1,0:T(8,128)(2,1)S(1)}, u32[]{:S(2)}, u32[]{:S(2)}) collective-permute-start(bf16[32,4096]{1,0:T(8,128)(2,1)S(1)} %fusion), channel_id=1, source_target_pairs={{0,2},{1,3},{2,0},{3,1},{4,6},{5,7},{6,4},{7,5},{8,10},{9,11},{10,... | collective-permute-start | bytes 786440 | tf_op jit(solution)/shard_map/ppermute | solution.py:80
  67.6 8.4 %collective-permute-start.14 = (bf16[32,4096]{1,0:T(8,128)(2,1)S(1)}, bf16[32,4096]{1,0:T(8,128)(2,1)S(1)}, u32[]{:S(2)}, u32[]{:S(2)}) collective-permute-start(bf16[32,4096]{1,0:T(8,128)(2,1)S(1)} %add_convert_fusion.4), channel_id=1, source_target_pairs={{0,1},{1,0},{2,3},{3,2},{4,5},{5,4},{6,7},{7,6},{8,24},{9,25},{10,... | collective-permute-start | bytes 786440 | tf_op jit(solution)/shard_map/ppermute | solution.py:80
  73.8 6.4 %collective-permute-start.25 = (bf16[32,4096]{1,0:T(8,128)(2,1)S(1)}, bf16[32,4096]{1,0:T(8,128)(2,1)S(1)}, u32[]{:S(2)}, u32[]{:S(2)}) collective-permute-start(bf16[32,4096]{1,0:T(8,128)(2,1)S(1)} %add_convert_fusion.3), channel_id=1, source_target_pairs={{0,1},{1,0},{2,3},{3,2},{4,5},{5,4},{6,7},{7,6},{8,24},{9,25},{10,... | collective-permute-start | bytes 786440 | tf_op jit(solution)/shard_map/ppermute | solution.py:80
  75.2 7.4 %collective-permute-start.28 = (bf16[16,4096]{1,0:T(8,128)(2,1)S(1)}, bf16[16,4096]{1,0:T(8,128)(2,1)S(1)}, u32[]{:S(2)}, u32[]{:S(2)}) collective-permute-start(bf16[16,4096]{1,0:T(8,128)(2,1)S(1)} %fusion.2), channel_id=1, source_target_pairs={{0,1},{1,0},{2,3},{3,2},{4,5},{5,4},{6,7},{7,6},{8,24},{9,25},{10,... | collective-permute-start | bytes 393224 | tf_op jit(solution)/shard_map/ppermute | solution.py:80
  76.1 9.3 %collective-permute-start.15 = (bf16[16,4096]{1,0:T(8,128)(2,1)S(1)}, bf16[16,4096]{1,0:T(8,128)(2,1)S(1)}, u32[]{:S(2)}, u32[]{:S(2)}) collective-permute-start(bf16[16,4096]{1,0:T(8,128)(2,1)S(1)} %add_convert_fusion.6), channel_id=1, source_target_pairs={{0,2},{1,3},{2,0},{3,1},{4,6},{5,7},{6,4},{7,5},{8,10},{9,11},{10,... | collective-permute-start | bytes 393224 | tf_op jit(solution)/shard_map/ppermute | solution.py:80
  80.3 6.0 %collective-permute-start.26 = (bf16[16,4096]{1,0:T(8,128)(2,1)S(1)}, bf16[16,4096]{1,0:T(8,128)(2,1)S(1)}, u32[]{:S(2)}, u32[]{:S(2)}) collective-permute-start(bf16[16,4096]{1,0:T(8,128)(2,1)S(1)} %add_convert_fusion.5), channel_id=1, source_target_pairs={{0,2},{1,3},{2,0},{3,1},{4,6},{5,7},{6,4},{7,5},{8,10},{9,11},{10,... | collective-permute-start | bytes 393224 | tf_op jit(solution)/shard_map/ppermute | solution.py:80
  82.6 7.2 %collective-permute-start.29 = (bf16[8,4096]{1,0:T(8,128)(2,1)S(1)}, bf16[8,4096]{1,0:T(8,128)(2,1)S(1)}, u32[]{:S(2)}, u32[]{:S(2)}) collective-permute-start(bf16[8,4096]{1,0:T(8,128)(2,1)S(1)} %fusion.5), channel_id=1, source_target_pairs={{0,4},{1,5},{2,6},{3,7},{4,0},{5,1},{6,2},{7,3},{8,12},{9,13},{10,... | collective-permute-start | bytes 196616 | tf_op jit(solution)/shard_map/ppermute | solution.py:80
  85.4 5.9 %collective-permute-start.17 = (bf16[8,4096]{1,0:T(8,128)(2,1)S(1)}, bf16[8,4096]{1,0:T(8,128)(2,1)S(1)}, u32[]{:S(2)}, u32[]{:S(2)}) collective-permute-start(bf16[8,4096]{1,0:T(8,128)(2,1)S(1)} %add_convert_fusion.10), channel_id=1, source_target_pairs={{0,4},{1,5},{2,6},{3,7},{4,0},{5,1},{6,2},{7,3},{8,12},{9,13},{10,... | collective-permute-start | bytes 196616 | tf_op jit(solution)/shard_map/ppermute | solution.py:80
  86.3 6.5 %collective-permute-start.27 = (bf16[8,4096]{1,0:T(8,128)(2,1)S(1)}, bf16[8,4096]{1,0:T(8,128)(2,1)S(1)}, u32[]{:S(2)}, u32[]{:S(2)}) collective-permute-start(bf16[8,4096]{1,0:T(8,128)(2,1)S(1)} %add_convert_fusion.8), channel_id=1, source_target_pairs={{0,4},{1,5},{2,6},{3,7},{4,0},{5,1},{6,2},{7,3},{8,12},{9,13},{10,... | collective-permute-start | bytes 196616 | tf_op jit(solution)/shard_map/ppermute | solution.py:80

commit v17 on v16

--- a/solution.py
+++ b/solution.py
@@ -230,7 +230,7 @@
     (held,) = yield (own,)
     for move in moves:
         (got,) = yield (permute(held, move),)
-        if move is moves[2] and beside:
+        if move is moves[3] and beside:
             got = lax.optimization_barrier((got, beside(before)))[0]
         before = got
         held = jnp.concatenate([held, got])
@@ -287,7 +287,7 @@
 
     serve = lambda held, sib: serve_rows(held, sib, found[0], top_count, w_gate[0], w_up[0], w_down[0])
     chunks = [
-        chunk_steps(own, routes[i % len(routes)], backs[i % len(backs)], serve, find if i == 0 else None)
+        chunk_steps(own, routes[i % len(routes)], backs[i % len(backs)], serve, find if i == 2 else None)
         for i, own in enumerate(owns)
     ]
     guards = GUARDS if len(chunks) == 3 and line_bits == 2 else []

time: 93.7 us -> 92.7 us (0.989)
  waiting for transfers between devices: 33 us -> 25.6 us
  starting transfers between devices: 42.4 us -> 48.8 us
    ppermute x30, waiting for transfers between devices: 33 us -> 25.6 us  [permute(): return lax.ppermute(value, AXES, pairs)]
    ppermute x30, starting transfers between devices: 42.4 us -> 48.8 us  [permute(): return lax.ppermute(value, AXES, pairs)]
  transfers between devices with their start and end apart: 30 -> 30, of which waited for: 13 -> 14; matrix products, arithmetic and copies ran while one was open for 2% -> 2% of each run, Pallas kernels for 15% -> 15%
where the time goes in v17:
time: 92.7 us; the launch traced here: 92.5 us
  starting transfers between devices  48.8 us (53%)
  waiting for transfers between devices  25.6 us (28%)
  Pallas kernels  14.8 us (16%)
  other arithmetic  2.13 us (2%)
    ppermute x30, starting transfers between devices, permute(): return lax.ppermute(value, AXES, pairs)  48.8 us
    ppermute x30, waiting for transfers between devices, permute(): return lax.ppermute(value, AXES, pairs)  25.6 us
    pallas_call x3, Pallas kernels, serve_rows(): pl.pallas_call(functools.partial(serve_kernel, top_count), out_shape=(out...  12.4 us
  transfers between devices with their start and end apart: 30, of which 14 were waited for; matrix products, arithmetic and copies ran while one was open for 2% of the time, Pallas kernels for 15%

profile of v17, /device:TPU:0, one launch (start us, length us, event | category | flops | bytes accessed | tf_op | source)
XLA Modules:
  0.0 92.5 jit_solution(13315014292324591500)
XLA Ops:
  0.0 1.0 %pack_rows.1 = (bf16[8,4224]{1,0:T(8,128)(2,1)S(1)}, bf16[8,4224]{1,0:T(8,128)(2,1)S(1)}, bf16[8,4224]{1,0:T(8,128)(2,1)S(1)}) custom-call(bf16[24,4096]{1,0:T(8,128)(2,1)} %tokens_hbm.1, s32[8,24]{1,0:T(8,128)} %bitcast.57, f32[8,24]{1,0:T(8,128)} %bitcast.58), custom_call_target="tpu_custom_call" | custom-call | bytes 393216 | tf_op jit(solution)/shard_map/pack_rows/pallas_call | solution.py:158
  1.0 4.1 %collective-permute-start = (bf16[8,4224]{1,0:T(8,128)(2,1)S(1)}, bf16[8,4224]{1,0:T(8,128)(2,1)S(1)}, u32[]{:S(2)}, u32[]{:S(2)}) collective-permute-start(bf16[8,4224]{1,0:T(8,128)(2,1)S(1)} %get-tuple-element.22), channel_id=1, source_target_pairs={{0,4},{1,5},{2,6},{3,7},{4,0},{5,1},{6,2},{7,3},{8,12},{9,13},{10,... | collective-permute-start | bytes 202760 | tf_op jit(solution)/shard_map/ppermute | solution.py:80
  5.1 0.1 collective-permute-start.3
  5.2 2.8 %collective-permute-start.18 = (bf16[8,4224]{1,0:T(8,128)(2,1)S(1)}, bf16[8,4224]{1,0:T(8,128)(2,1)S(1)}, u32[]{:S(2)}, u32[]{:S(2)}) collective-permute-start(bf16[8,4224]{1,0:T(8,128)(2,1)S(1)} %get-tuple-element.33), channel_id=1, source_target_pairs={{0,4},{1,5},{2,6},{3,7},{4,0},{5,1},{6,2},{7,3},{8,12},{9,13},{10,... | collective-permute-start | bytes 202760 | tf_op jit(solution)/shard_map/ppermute | solution.py:80
  8.7 0.2 collective-permute-done
  8.9 4.9 %collective-permute-start.1 = (bf16[16,4224]{1,0:T(8,128)(2,1)S(1)}, bf16[16,4224]{1,0:T(8,128)(2,1)S(1)}, u32[]{:S(2)}, u32[]{:S(2)}) collective-permute-start(bf16[16,4224]{1,0:T(8,128)(2,1)S(1)} %pad_maximum_fusion.7), channel_id=1, source_target_pairs={{0,1},{1,0},{2,3},{3,2},{4,5},{5,4},{6,7},{7,6},{8,24},{9,25},{10,... | collective-permute-start | bytes 405512 | tf_op jit(solution)/shard_map/ppermute | solution.py:80
  13.8 0.3 collective-permute-start.4
  14.1 0.5 collective-permute-done.18
  14.6 1.4 %collective-permute-start.19 = (bf16[16,4224]{1,0:T(8,128)(2,1)S(1)}, bf16[16,4224]{1,0:T(8,128)(2,1)S(1)}, u32[]{:S(2)}, u32[]{:S(2)}) collective-permute-start(bf16[16,4224]{1,0:T(8,128)(2,1)S(1)} %pad_maximum_fusion.9), channel_id=1, source_target_pairs={{0,2},{1,3},{2,0},{3,1},{4,6},{5,7},{6,4},{7,5},{8,10},{9,11},{10,... | collective-permute-start | bytes 405512 | tf_op jit(solution)/shard_map/ppermute | solution.py:80
  16.0 0.8 collective-permute-done.1
  16.8 2.1 %collective-permute-start.2 = (bf16[32,4224]{1,0:T(8,128)(2,1)S(1)}, bf16[32,4224]{1,0:T(8,128)(2,1)S(1)}, u32[]{:S(2)}, u32[]{:S(2)}) collective-permute-start(bf16[32,4224]{1,0:T(8,128)(2,1)S(1)} %pad_maximum_fusion.3), channel_id=1, source_target_pairs={{0,16},{1,17},{2,18},{3,19},{4,20},{5,21},{6,22},{7,23},{8,9},{9,8... | collective-permute-start | bytes 811016 | tf_op jit(solution)/shard_map/ppermute | solution.py:80
  18.9 0.9 %collective-permute-done.4 = bf16[16,4224]{1,0:T(8,128)(2,1)S(1)} collective-permute-done((bf16[16,4224]{1,0:T(8,128)(2,1)S(1)}, bf16[16,4224]{1,0:T(8,128)(2,1)S(1)}, u32[]{:S(2)}, u32[]{:S(2)}) %collective-permute-start.4) | collective-permute-done | bytes 135200 | tf_op jit(solution)/shard_map/ppermute | solution.py:80
  19.8 2.0 %collective-permute-start.5 = (bf16[32,4224]{1,0:T(8,128)(2,1)S(1)}, bf16[32,4224]{1,0:T(8,128)(2,1)S(1)}, u32[]{:S(2)}, u32[]{:S(2)}) collective-permute-start(bf16[32,4224]{1,0:T(8,128)(2,1)S(1)} %pad_maximum_fusion.4), channel_id=1, source_target_pairs={{0,1},{1,0},{2,3},{3,2},{4,5},{5,4},{6,7},{7,6},{8,24},{9,25},{10,... | collective-permute-start | bytes 811016 | tf_op jit(solution)/shard_map/ppermute | solution.py:80
  21.9 1.4 %collective-permute-start.20 = (bf16[32,4224]{1,0:T(8,128)(2,1)S(1)}, bf16[32,4224]{1,0:T(8,128)(2,1)S(1)}, u32[]{:S(2)}, u32[]{:S(2)}) collective-permute-start(bf16[32,4224]{1,0:T(8,128)(2,1)S(1)} %pad_maximum_fusion.5), channel_id=1, source_target_pairs={{0,1},{1,0},{2,3},{3,2},{4,5},{5,4},{6,7},{7,6},{8,24},{9,25},{10,... | collective-permute-start | bytes 811016 | tf_op jit(solution)/shard_map/ppermute | solution.py:80
  23.3 2.9 %collective-permute-done.2.after = bf16[32,4224]{1,0:T(8,128)(2,1)S(1)} collective-permute-done((bf16[32,4224]{1,0:T(8,128)(2,1)S(1)}, bf16[32,4224]{1,0:T(8,128)(2,1)S(1)}, u32[]{:S(2)}, u32[]{:S(2)}) %collective-permute-start.2) | collective-permute-done | bytes 270368 | tf_op jit(solution)/shard_map/ppermute | solution.py:80
  26.2 0.8 collective-permute-start.10
  27.1 0.1 pad_maximum_fusion
  27.1 1.6 %collective-permute-start.6 = (bf16[64,4224]{1,0:T(8,128)(2,1)S(1)}, bf16[64,4224]{1,0:T(8,128)(2,1)S(1)}, u32[]{:S(2)}, u32[]{:S(2)}) collective-permute-start(bf16[64,4224]{1,0:T(8,128)(2,1)S(1)} %pad_maximum_fusion), channel_id=1, source_target_pairs={{0,16},{1,17},{2,18},{3,19},{4,20},{5,21},{6,22},{7,23},{8,9},{9,8... | collective-permute-start | bytes 1622024 | tf_op jit(solution)/shard_map/ppermute | solution.py:80
  28.7 1.8 %collective-permute-done.20 = bf16[32,4224]{1,0:T(8,128)(2,1)S(1)} collective-permute-done((bf16[32,4224]{1,0:T(8,128)(2,1)S(1)}, bf16[32,4224]{1,0:T(8,128)(2,1)S(1)}, u32[]{:S(2)}, u32[]{:S(2)}) %collective-permute-start.20) | collective-permute-done | bytes 270368 | tf_op jit(solution)/shard_map/ppermute | solution.py:80
  30.6 2.4 %collective-permute-start.21 = (bf16[64,4224]{1,0:T(8,128)(2,1)S(1)}, bf16[64,4224]{1,0:T(8,128)(2,1)S(1)}, u32[]{:S(2)}, u32[]{:S(2)}) collective-permute-start(bf16[64,4224]{1,0:T(8,128)(2,1)S(1)} %pad_maximum_fusion.2), channel_id=1, source_target_pairs={{0,16},{1,17},{2,18},{3,19},{4,20},{5,21},{6,22},{7,23},{8,9},{9,8... | collective-permute-start | bytes 1622024 | tf_op jit(solution)/shard_map/ppermute | solution.py:80
  33.0 1.4 %served_expert.1.mine = s32[1]{0:T(128)} custom-call(s32[2,16]{1,0:T(2,128)} %bitcast.59, s32[1]{0:T(128)S(6)} %copy.21.flag, bf16[32,4224]{1,0:T(8,128)(2,1)S(1)} %collective-permute-done.2.after), custom_call_target="tpu_custom_call" | custom-call | flops 10000000000 | tf_op jit(solution)/shard_map/served_expert/pallas_call | solution.py:111
  34.4 2.2 %collective-permute-done.6 = bf16[64,4224]{1,0:T(8,128)(2,1)S(1)} collective-permute-done((bf16[64,4224]{1,0:T(8,128)(2,1)S(1)}, bf16[64,4224]{1,0:T(8,128)(2,1)S(1)}, u32[]{:S(2)}, u32[]{:S(2)}) %collective-permute-start.6) | collective-permute-done | bytes 540704 | tf_op jit(solution)/shard_map/ppermute | solution.py:80
  36.6 0.1 collective-permute-start.7
  36.8 0.6 collective-permute-start.11
  37.3 2.0 %collective-permute-done.7.sib = bf16[128,4224]{1,0:T(8,128)(2,1)S(1)} collective-permute-done((bf16[128,4224]{1,0:T(8,128)(2,1)S(1)}, bf16[128,4224]{1,0:T(8,128)(2,1)S(1)}, u32[]{:S(2)}, u32[]{:S(2)}) %collective-permute-start.7) | collective-permute-done | bytes 1081376 | tf_op jit(solution)/shard_map/ppermute | solution.py:80
  39.4 4.1 %serve_rows.3 = (bf16[128,4096]{1,0:T(8,128)(2,1)S(1)}, bf16[128,4096]{1,0:T(8,128)(2,1)S(1)}) custom-call(s32[1]{0:T(128)} %served_expert.1.mine, bf16[128,4224]{1,0:T(8,128)(2,1)S(1)} %constant_dynamic-update-slice_fusion.own, bf16[128,4224]{1,0:T(8,128)(2,1)S(1)} %collective-permute-done.7.sib, bf16[4096,512]{1,0:T(8,128)(2,1)S(1)} %bitcast.37, ...), custom_call_target="tpu_custom_call" | custom-call | flops 3221225472 | bytes 16777216 | tf_op jit(solution)/shard_map/serve_rows/pallas_call | solution.py:207
  43.5 0.2 collective-permute-start.8
  43.7 0.1 constant_dynamic-update-slice_fusion.10.own
  43.8 0.4 collective-permute-start.22
  44.3 4.1 %serve_rows.4 = (bf16[128,4096]{1,0:T(8,128)(2,1)S(1)}, bf16[128,4096]{1,0:T(8,128)(2,1)S(1)}) custom-call(s32[1]{0:T(128)} %served_expert.1.mine, bf16[128,4224]{1,0:T(8,128)(2,1)S(1)} %constant_dynamic-update-slice_fusion.5.own, bf16[128,4224]{1,0:T(8,128)(2,1)S(1)} %collective-permute-done.11.sib, bf16[4096,512]{1,0:T(8,128)(2,1)S(1)} %bitcast.38, ...), custom_call_target="tpu_custom_call" | custom-call | flops 3221225472 | bytes 16777216 | tf_op jit(solution)/shard_map/serve_rows/pallas_call | solution.py:207
  48.4 0.2 collective-permute-start.12
  48.6 0.1 add_convert_fusion.2
  48.7 1.6 %collective-permute-start.9 = (bf16[64,4096]{1,0:T(8,128)(2,1)S(1)}, bf16[64,4096]{1,0:T(8,128)(2,1)S(1)}, u32[]{:S(2)}, u32[]{:S(2)}) collective-permute-start(bf16[64,4096]{1,0:T(8,128)(2,1)S(1)} %add_convert_fusion.2), channel_id=1, source_target_pairs={{0,16},{1,17},{2,18},{3,19},{4,20},{5,21},{6,22},{7,23},{8,9},{9,8... | collective-permute-start | bytes 1572872 | tf_op jit(solution)/shard_map/ppermute | solution.py:80
  50.3 4.1 %serve_rows.5 = (bf16[128,4096]{1,0:T(8,128)(2,1)S(1)}, bf16[128,4096]{1,0:T(8,128)(2,1)S(1)}) custom-call(s32[1]{0:T(128)} %served_expert.1.mine, bf16[128,4224]{1,0:T(8,128)(2,1)S(1)} %constant_dynamic-update-slice_fusion.10.own, bf16[128,4224]{1,0:T(8,128)(2,1)S(1)} %collective-permute-done.22.sib, bf16[4096,512]{1,0:T(8,128)(2,1)S(1)} %bitcast.39, ...), custom_call_target="tpu_custom_call" | custom-call | flops 3221225472 | bytes 16777216 | tf_op jit(solution)/shard_map/serve_rows/pallas_call | solution.py:207
  54.4 0.2 collective-permute-start.23
  54.6 0.1 add_convert_fusion.1
  54.8 1.6 %collective-permute-start.13 = (bf16[64,4096]{1,0:T(8,128)(2,1)S(1)}, bf16[64,4096]{1,0:T(8,128)(2,1)S(1)}, u32[]{:S(2)}, u32[]{:S(2)}) collective-permute-start(bf16[64,4096]{1,0:T(8,128)(2,1)S(1)} %bitcast.56), channel_id=1, source_target_pairs={{0,16},{1,17},{2,18},{3,19},{4,20},{5,21},{6,22},{7,23},{8,9},{9,8... | collective-permute-start | bytes 1572872 | tf_op jit(solution)/shard_map/ppermute | solution.py:80
  56.3 0.1 convert_add_fusion
  56.4 0.8 collective-permute-done.23
  57.2 0.1 add_convert_fusion
  57.3 1.3 %collective-permute-start.24 = (bf16[64,4096]{1,0:T(8,128)(2,1)S(1)}, bf16[64,4096]{1,0:T(8,128)(2,1)S(1)}, u32[]{:S(2)}, u32[]{:S(2)}) collective-permute-start(bf16[64,4096]{1,0:T(8,128)(2,1)S(1)} %add_convert_fusion), channel_id=1, source_target_pairs={{0,16},{1,17},{2,18},{3,19},{4,20},{5,21},{6,22},{7,23},{8,9},{9,8... | collective-permute-start | bytes 1572872 | tf_op jit(solution)/shard_map/ppermute | solution.py:80
  58.6 5.4 %collective-permute-done.13 = bf16[64,4096]{1,0:T(8,128)(2,1)S(1)} collective-permute-done((bf16[64,4096]{1,0:T(8,128)(2,1)S(1)}, bf16[64,4096]{1,0:T(8,128)(2,1)S(1)}, u32[]{:S(2)}, u32[]{:S(2)}) %collective-permute-start.13) | collective-permute-done | bytes 524320 | tf_op jit(solution)/shard_map/ppermute | solution.py:80
  64.0 1.9 %collective-permute-start.16 = (bf16[32,4096]{1,0:T(8,128)(2,1)S(1)}, bf16[32,4096]{1,0:T(8,128)(2,1)S(1)}, u32[]{:S(2)}, u32[]{:S(2)}) collective-permute-start(bf16[32,4096]{1,0:T(8,128)(2,1)S(1)} %fusion), channel_id=1, source_target_pairs={{0,2},{1,3},{2,0},{3,1},{4,6},{5,7},{6,4},{7,5},{8,10},{9,11},{10,... | collective-permute-start | bytes 786440 | tf_op jit(solution)/shard_map/ppermute | solution.py:80
  65.9 0.1 add_convert_fusion.4
  66.0 1.5 %collective-permute-start.14 = (bf16[32,4096]{1,0:T(8,128)(2,1)S(1)}, bf16[32,4096]{1,0:T(8,128)(2,1)S(1)}, u32[]{:S(2)}, u32[]{:S(2)}) collective-permute-start(bf16[32,4096]{1,0:T(8,128)(2,1)S(1)} %add_convert_fusion.4), channel_id=1, source_target_pairs={{0,1},{1,0},{2,3},{3,2},{4,5},{5,4},{6,7},{7,6},{8,24},{9,25},{10,... | collective-permute-start | bytes 786440 | tf_op jit(solution)/shard_map/ppermute | solution.py:80
  67.5 3.7 %collective-permute-done.24 = bf16[64,4096]{1,0:T(8,128)(2,1)S(1)} collective-permute-done((bf16[64,4096]{1,0:T(8,128)(2,1)S(1)}, bf16[64,4096]{1,0:T(8,128)(2,1)S(1)}, u32[]{:S(2)}, u32[]{:S(2)}) %collective-permute-start.24) | collective-permute-done | bytes 524320 | tf_op jit(solution)/shard_map/ppermute | solution.py:80
  71.2 0.1 add_convert_fusion.3
  71.3 1.4 %collective-permute-start.25 = (bf16[32,4096]{1,0:T(8,128)(2,1)S(1)}, bf16[32,4096]{1,0:T(8,128)(2,1)S(1)}, u32[]{:S(2)}, u32[]{:S(2)}) collective-permute-start(bf16[32,4096]{1,0:T(8,128)(2,1)S(1)} %add_convert_fusion.3), channel_id=1, source_target_pairs={{0,1},{1,0},{2,3},{3,2},{4,5},{5,4},{6,7},{7,6},{8,24},{9,25},{10,... | collective-permute-start | bytes 786440 | tf_op jit(solution)/shard_map/ppermute | solution.py:80
  72.7 0.1 fusion.2
  72.8 0.8 collective-permute-start.28
  73.6 0.1 add_convert_fusion.6
  73.7 3.1 %collective-permute-start.15 = (bf16[16,4096]{1,0:T(8,128)(2,1)S(1)}, bf16[16,4096]{1,0:T(8,128)(2,1)S(1)}, u32[]{:S(2)}, u32[]{:S(2)}) collective-permute-start(bf16[16,4096]{1,0:T(8,128)(2,1)S(1)} %add_convert_fusion.6), channel_id=1, source_target_pairs={{0,2},{1,3},{2,0},{3,1},{4,6},{5,7},{6,4},{7,5},{8,10},{9,11},{10,... | collective-permute-start | bytes 393224 | tf_op jit(solution)/shard_map/ppermute | solution.py:80
  76.7 1.0 %collective-permute-done.25 = bf16[32,4096]{1,0:T(8,128)(2,1)S(1)} collective-permute-done((bf16[32,4096]{1,0:T(8,128)(2,1)S(1)}, bf16[32,4096]{1,0:T(8,128)(2,1)S(1)}, u32[]{:S(2)}, u32[]{:S(2)}) %collective-permute-start.25) | collective-permute-done | bytes 262176 | tf_op jit(solution)/shard_map/ppermute | solution.py:80
  77.8 0.1 add_convert_fusion.5
  77.8 3.1 %collective-permute-start.26 = (bf16[16,4096]{1,0:T(8,128)(2,1)S(1)}, bf16[16,4096]{1,0:T(8,128)(2,1)S(1)}, u32[]{:S(2)}, u32[]{:S(2)}) collective-permute-start(bf16[16,4096]{1,0:T(8,128)(2,1)S(1)} %add_convert_fusion.5), channel_id=1, source_target_pairs={{0,2},{1,3},{2,0},{3,1},{4,6},{5,7},{6,4},{7,5},{8,10},{9,11},{10,... | collective-permute-start | bytes 393224 | tf_op jit(solution)/shard_map/ppermute | solution.py:80
  81.0 2.9 %collective-permute-start.29 = (bf16[8,4096]{1,0:T(8,128)(2,1)S(1)}, bf16[8,4096]{1,0:T(8,128)(2,1)S(1)}, u32[]{:S(2)}, u32[]{:S(2)}) collective-permute-start(bf16[8,4096]{1,0:T(8,128)(2,1)S(1)} %fusion.5), channel_id=1, source_target_pairs={{0,4},{1,5},{2,6},{3,7},{4,0},{5,1},{6,2},{7,3},{8,12},{9,13},{10,... | collective-permute-start | bytes 196616 | tf_op jit(solution)/shard_map/ppermute | solution.py:80
  83.9 0.9 collective-permute-start.17
  84.8 3.5 %collective-permute-start.27 = (bf16[8,4096]{1,0:T(8,128)(2,1)S(1)}, bf16[8,4096]{1,0:T(8,128)(2,1)S(1)}, u32[]{:S(2)}, u32[]{:S(2)}) collective-permute-start(bf16[8,4096]{1,0:T(8,128)(2,1)S(1)} %add_convert_fusion.8), channel_id=1, source_target_pairs={{0,4},{1,5},{2,6},{3,7},{4,0},{5,1},{6,2},{7,3},{8,12},{9,13},{10,... | collective-permute-start | bytes 196616 | tf_op jit(solution)/shard_map/ppermute | solution.py:80
  88.3 0.1 fusion.9
  88.4 1.9 %collective-permute-done.17 = bf16[8,4096]{1,0:T(8,128)(2,1)S(1)} collective-permute-done((bf16[8,4096]{1,0:T(8,128)(2,1)S(1)}, bf16[8,4096]{1,0:T(8,128)(2,1)S(1)}, u32[]{:S(2)}, u32[]{:S(2)}) %collective-permute-start.17) | collective-permute-done | bytes 65568 | tf_op jit(solution)/shard_map/ppermute | solution.py:80
  90.3 0.1 add_convert_fusion.9
  90.4 1.3 %collective-permute-done.27 = bf16[8,4096]{1,0:T(8,128)(2,1)S(1)} collective-permute-done((bf16[8,4096]{1,0:T(8,128)(2,1)S(1)}, bf16[8,4096]{1,0:T(8,128)(2,1)S(1)}, u32[]{:S(2)}, u32[]{:S(2)}) %collective-permute-start.27) | collective-permute-done | bytes 65568 | tf_op jit(solution)/shard_map/ppermute | solution.py:80
  91.7 0.1 add_convert_fusion.7
  91.8 0.7 pad_maximum_fusion.6
  (47 shorter events, 0.7 us)
Async XLA Ops:
  1.0 7.9 %collective-permute-start = (bf16[8,4224]{1,0:T(8,128)(2,1)S(1)}, bf16[8,4224]{1,0:T(8,128)(2,1)S(1)}, u32[]{:S(2)}, u32[]{:S(2)}) collective-permute-start(bf16[8,4224]{1,0:T(8,128)(2,1)S(1)} %get-tuple-element.22), channel_id=1, source_target_pairs={{0,4},{1,5},{2,6},{3,7},{4,0},{5,1},{6,2},{7,3},{8,12},{9,13},{10,... | collective-permute-start | bytes 202760 | tf_op jit(solution)/shard_map/ppermute | solution.py:80
  5.1 8.7 %collective-permute-start.3 = (bf16[8,4224]{1,0:T(8,128)(2,1)S(1)}, bf16[8,4224]{1,0:T(8,128)(2,1)S(1)}, u32[]{:S(2)}, u32[]{:S(2)}) collective-permute-start(bf16[8,4224]{1,0:T(8,128)(2,1)S(1)} %get-tuple-element.23), channel_id=1, source_target_pairs={{0,4},{1,5},{2,6},{3,7},{4,0},{5,1},{6,2},{7,3},{8,12},{9,13},{10,... | collective-permute-start | bytes 202760 | tf_op jit(solution)/shard_map/ppermute | solution.py:80
  5.2 9.4 %collective-permute-start.18 = (bf16[8,4224]{1,0:T(8,128)(2,1)S(1)}, bf16[8,4224]{1,0:T(8,128)(2,1)S(1)}, u32[]{:S(2)}, u32[]{:S(2)}) collective-permute-start(bf16[8,4224]{1,0:T(8,128)(2,1)S(1)} %get-tuple-element.33), channel_id=1, source_target_pairs={{0,4},{1,5},{2,6},{3,7},{4,0},{5,1},{6,2},{7,3},{8,12},{9,13},{10,... | collective-permute-start | bytes 202760 | tf_op jit(solution)/shard_map/ppermute | solution.py:80
  8.9 7.9 %collective-permute-start.1 = (bf16[16,4224]{1,0:T(8,128)(2,1)S(1)}, bf16[16,4224]{1,0:T(8,128)(2,1)S(1)}, u32[]{:S(2)}, u32[]{:S(2)}) collective-permute-start(bf16[16,4224]{1,0:T(8,128)(2,1)S(1)} %pad_maximum_fusion.7), channel_id=1, source_target_pairs={{0,1},{1,0},{2,3},{3,2},{4,5},{5,4},{6,7},{7,6},{8,24},{9,25},{10,... | collective-permute-start | bytes 405512 | tf_op jit(solution)/shard_map/ppermute | solution.py:80
  13.8 6.0 %collective-permute-start.4 = (bf16[16,4224]{1,0:T(8,128)(2,1)S(1)}, bf16[16,4224]{1,0:T(8,128)(2,1)S(1)}, u32[]{:S(2)}, u32[]{:S(2)}) collective-permute-start(bf16[16,4224]{1,0:T(8,128)(2,1)S(1)} %pad_maximum_fusion.8), channel_id=1, source_target_pairs={{0,2},{1,3},{2,0},{3,1},{4,6},{5,7},{6,4},{7,5},{8,10},{9,11},{10,... | collective-permute-start | bytes 405512 | tf_op jit(solution)/shard_map/ppermute | solution.py:80
  14.6 7.2 %collective-permute-start.19 = (bf16[16,4224]{1,0:T(8,128)(2,1)S(1)}, bf16[16,4224]{1,0:T(8,128)(2,1)S(1)}, u32[]{:S(2)}, u32[]{:S(2)}) collective-permute-start(bf16[16,4224]{1,0:T(8,128)(2,1)S(1)} %pad_maximum_fusion.9), channel_id=1, source_target_pairs={{0,2},{1,3},{2,0},{3,1},{4,6},{5,7},{6,4},{7,5},{8,10},{9,11},{10,... | collective-permute-start | bytes 405512 | tf_op jit(solution)/shard_map/ppermute | solution.py:80
  16.8 9.4 %collective-permute-start.2 = (bf16[32,4224]{1,0:T(8,128)(2,1)S(1)}, bf16[32,4224]{1,0:T(8,128)(2,1)S(1)}, u32[]{:S(2)}, u32[]{:S(2)}) collective-permute-start(bf16[32,4224]{1,0:T(8,128)(2,1)S(1)} %pad_maximum_fusion.3), channel_id=1, source_target_pairs={{0,16},{1,17},{2,18},{3,19},{4,20},{5,21},{6,22},{7,23},{8,9},{9,8... | collective-permute-start | bytes 811016 | tf_op jit(solution)/shard_map/ppermute | solution.py:80
  19.8 7.2 %collective-permute-start.5 = (bf16[32,4224]{1,0:T(8,128)(2,1)S(1)}, bf16[32,4224]{1,0:T(8,128)(2,1)S(1)}, u32[]{:S(2)}, u32[]{:S(2)}) collective-permute-start(bf16[32,4224]{1,0:T(8,128)(2,1)S(1)} %pad_maximum_fusion.4), channel_id=1, source_target_pairs={{0,1},{1,0},{2,3},{3,2},{4,5},{5,4},{6,7},{7,6},{8,24},{9,25},{10,... | collective-permute-start | bytes 811016 | tf_op jit(solution)/shard_map/ppermute | solution.py:80
  21.9 8.7 %collective-permute-start.20 = (bf16[32,4224]{1,0:T(8,128)(2,1)S(1)}, bf16[32,4224]{1,0:T(8,128)(2,1)S(1)}, u32[]{:S(2)}, u32[]{:S(2)}) collective-permute-start(bf16[32,4224]{1,0:T(8,128)(2,1)S(1)} %pad_maximum_fusion.5), channel_id=1, source_target_pairs={{0,1},{1,0},{2,3},{3,2},{4,5},{5,4},{6,7},{7,6},{8,24},{9,25},{10,... | collective-permute-start | bytes 811016 | tf_op jit(solution)/shard_map/ppermute | solution.py:80
  26.2 10.5 %collective-permute-start.10 = (bf16[64,4224]{1,0:T(8,128)(2,1)S(1)}, bf16[64,4224]{1,0:T(8,128)(2,1)S(1)}, u32[]{:S(2)}, u32[]{:S(2)}) collective-permute-start(bf16[64,4224]{1,0:T(8,128)(2,1)S(1)} %pad_maximum_fusion.1), channel_id=1, source_target_pairs={{0,2},{1,3},{2,0},{3,1},{4,6},{5,7},{6,4},{7,5},{8,10},{9,11},{10,... | collective-permute-start | bytes 1622024 | tf_op jit(solution)/shard_map/ppermute | solution.py:80
  27.1 9.4 %collective-permute-start.6 = (bf16[64,4224]{1,0:T(8,128)(2,1)S(1)}, bf16[64,4224]{1,0:T(8,128)(2,1)S(1)}, u32[]{:S(2)}, u32[]{:S(2)}) collective-permute-start(bf16[64,4224]{1,0:T(8,128)(2,1)S(1)} %pad_maximum_fusion), channel_id=1, source_target_pairs={{0,16},{1,17},{2,18},{3,19},{4,20},{5,21},{6,22},{7,23},{8,9},{9,8... | collective-permute-start | bytes 1622024 | tf_op jit(solution)/shard_map/ppermute | solution.py:80
  30.6 13.2 %collective-permute-start.21 = (bf16[64,4224]{1,0:T(8,128)(2,1)S(1)}, bf16[64,4224]{1,0:T(8,128)(2,1)S(1)}, u32[]{:S(2)}, u32[]{:S(2)}) collective-permute-start(bf16[64,4224]{1,0:T(8,128)(2,1)S(1)} %pad_maximum_fusion.2), channel_id=1, source_target_pairs={{0,16},{1,17},{2,18},{3,19},{4,20},{5,21},{6,22},{7,23},{8,9},{9,8... | collective-permute-start | bytes 1622024 | tf_op jit(solution)/shard_map/ppermute | solution.py:80
  32.9 6.4 %copy-start = (bf16[1,4096,512]{2,1,0:T(8,128)(2,1)S(1)}, bf16[1,4096,512]{2,1,0:T(8,128)(2,1)}, u32[]{:S(2)}) copy-start(bf16[1,4096,512]{2,1,0:T(8,128)(2,1)} %param.13) | copy-start | bytes 12582916
  33.0 6.4 %copy-start.1 = (bf16[1,4096,512]{2,1,0:T(8,128)(2,1)S(1)}, bf16[1,4096,512]{2,1,0:T(8,128)(2,1)}, u32[]{:S(2)}) copy-start(bf16[1,4096,512]{2,1,0:T(8,128)(2,1)} %param.14) | copy-start | bytes 12582916
  33.0 6.4 %copy-start.2 = (bf16[1,512,4096]{2,1,0:T(8,128)(2,1)S(1)}, bf16[1,512,4096]{2,1,0:T(8,128)(2,1)}, u32[]{:S(2)}) copy-start(bf16[1,512,4096]{2,1,0:T(8,128)(2,1)} %param.15) | copy-start | bytes 12582916
  36.6 2.8 %collective-permute-start.7 = (bf16[128,4224]{1,0:T(8,128)(2,1)S(1)}, bf16[128,4224]{1,0:T(8,128)(2,1)S(1)}, u32[]{:S(2)}, u32[]{:S(2)}) collective-permute-start(bf16[128,4224]{1,0:T(8,128)(2,1)S(1)} %constant_dynamic-update-slice_fusion.own), channel_id=1, source_target_pairs={{0,8},{1,9},{2,10},{3,11},{4,12},{5,13},{6,14},{7,15},{8,0},{9,1},... | collective-permute-start | bytes 3244040 | tf_op jit(solution)/shard_map/ppermute | solution.py:80
  36.8 7.5 %collective-permute-start.11 = (bf16[128,4224]{1,0:T(8,128)(2,1)S(1)}, bf16[128,4224]{1,0:T(8,128)(2,1)S(1)}, u32[]{:S(2)}, u32[]{:S(2)}) collective-permute-start(bf16[128,4224]{1,0:T(8,128)(2,1)S(1)} %constant_dynamic-update-slice_fusion.5.own), channel_id=1, source_target_pairs={{0,8},{1,9},{2,10},{3,11},{4,12},{5,13},{6,14},{7,15},{8,0},{9,1},... | collective-permute-start | bytes 3244040 | tf_op jit(solution)/shard_map/ppermute | solution.py:80
  43.5 4.9 %collective-permute-start.8 = (bf16[128,4096]{1,0:T(8,128)(2,1)S(1)}, bf16[128,4096]{1,0:T(8,128)(2,1)S(1)}, u32[]{:S(2)}, u32[]{:S(2)}) collective-permute-start(bf16[128,4096]{1,0:T(8,128)(2,1)S(1)} %get-tuple-element.25), channel_id=1, source_target_pairs={{0,8},{1,9},{2,10},{3,11},{4,12},{5,13},{6,14},{7,15},{8,0},{9,1},... | collective-permute-start | bytes 3145736 | tf_op jit(solution)/shard_map/ppermute | solution.py:80
  43.8 6.5 %collective-permute-start.22 = (bf16[128,4224]{1,0:T(8,128)(2,1)S(1)}, bf16[128,4224]{1,0:T(8,128)(2,1)S(1)}, u32[]{:S(2)}, u32[]{:S(2)}) collective-permute-start(bf16[128,4224]{1,0:T(8,128)(2,1)S(1)} %constant_dynamic-update-slice_fusion.10.own), channel_id=1, source_target_pairs={{0,8},{1,9},{2,10},{3,11},{4,12},{5,13},{6,14},{7,15},{8,0},{9,1},... | collective-permute-start | bytes 3244040 | tf_op jit(solution)/shard_map/ppermute | solution.py:80
  48.4 6.2 %collective-permute-start.12 = (bf16[128,4096]{1,0:T(8,128)(2,1)S(1)}, bf16[128,4096]{1,0:T(8,128)(2,1)S(1)}, u32[]{:S(2)}, u32[]{:S(2)}) collective-permute-start(bf16[128,4096]{1,0:T(8,128)(2,1)S(1)} %get-tuple-element.29), channel_id=1, source_target_pairs={{0,8},{1,9},{2,10},{3,11},{4,12},{5,13},{6,14},{7,15},{8,0},{9,1},... | collective-permute-start | bytes 3145736 | tf_op jit(solution)/shard_map/ppermute | solution.py:80
  48.7 17.2 %collective-permute-start.9 = (bf16[64,4096]{1,0:T(8,128)(2,1)S(1)}, bf16[64,4096]{1,0:T(8,128)(2,1)S(1)}, u32[]{:S(2)}, u32[]{:S(2)}) collective-permute-start(bf16[64,4096]{1,0:T(8,128)(2,1)S(1)} %add_convert_fusion.2), channel_id=1, source_target_pairs={{0,16},{1,17},{2,18},{3,19},{4,20},{5,21},{6,22},{7,23},{8,9},{9,8... | collective-permute-start | bytes 1572872 | tf_op jit(solution)/shard_map/ppermute | solution.py:80
  54.4 2.7 %collective-permute-start.23 = (bf16[128,4096]{1,0:T(8,128)(2,1)S(1)}, bf16[128,4096]{1,0:T(8,128)(2,1)S(1)}, u32[]{:S(2)}, u32[]{:S(2)}) collective-permute-start(bf16[128,4096]{1,0:T(8,128)(2,1)S(1)} %get-tuple-element.37), channel_id=1, source_target_pairs={{0,8},{1,9},{2,10},{3,11},{4,12},{5,13},{6,14},{7,15},{8,0},{9,1},... | collective-permute-start | bytes 3145736 | tf_op jit(solution)/shard_map/ppermute | solution.py:80
  54.8 9.2 %collective-permute-start.13 = (bf16[64,4096]{1,0:T(8,128)(2,1)S(1)}, bf16[64,4096]{1,0:T(8,128)(2,1)S(1)}, u32[]{:S(2)}, u32[]{:S(2)}) collective-permute-start(bf16[64,4096]{1,0:T(8,128)(2,1)S(1)} %bitcast.56), channel_id=1, source_target_pairs={{0,16},{1,17},{2,18},{3,19},{4,20},{5,21},{6,22},{7,23},{8,9},{9,8... | collective-permute-start | bytes 1572872 | tf_op jit(solution)/shard_map/ppermute | solution.py:80
  57.3 13.9 %collective-permute-start.24 = (bf16[64,4096]{1,0:T(8,128)(2,1)S(1)}, bf16[64,4096]{1,0:T(8,128)(2,1)S(1)}, u32[]{:S(2)}, u32[]{:S(2)}) collective-permute-start(bf16[64,4096]{1,0:T(8,128)(2,1)S(1)} %add_convert_fusion), channel_id=1, source_target_pairs={{0,16},{1,17},{2,18},{3,19},{4,20},{5,21},{6,22},{7,23},{8,9},{9,8... | collective-permute-start | bytes 1572872 | tf_op jit(solution)/shard_map/ppermute | solution.py:80
  64.0 8.7 %collective-permute-start.16 = (bf16[32,4096]{1,0:T(8,128)(2,1)S(1)}, bf16[32,4096]{1,0:T(8,128)(2,1)S(1)}, u32[]{:S(2)}, u32[]{:S(2)}) collective-permute-start(bf16[32,4096]{1,0:T(8,128)(2,1)S(1)} %fusion), channel_id=1, source_target_pairs={{0,2},{1,3},{2,0},{3,1},{4,6},{5,7},{6,4},{7,5},{8,10},{9,11},{10,... | collective-permute-start | bytes 786440 | tf_op jit(solution)/shard_map/ppermute | solution.py:80
  66.0 7.6 %collective-permute-start.14 = (bf16[32,4096]{1,0:T(8,128)(2,1)S(1)}, bf16[32,4096]{1,0:T(8,128)(2,1)S(1)}, u32[]{:S(2)}, u32[]{:S(2)}) collective-permute-start(bf16[32,4096]{1,0:T(8,128)(2,1)S(1)} %add_convert_fusion.4), channel_id=1, source_target_pairs={{0,1},{1,0},{2,3},{3,2},{4,5},{5,4},{6,7},{7,6},{8,24},{9,25},{10,... | collective-permute-start | bytes 786440 | tf_op jit(solution)/shard_map/ppermute | solution.py:80
  71.3 6.4 %collective-permute-start.25 = (bf16[32,4096]{1,0:T(8,128)(2,1)S(1)}, bf16[32,4096]{1,0:T(8,128)(2,1)S(1)}, u32[]{:S(2)}, u32[]{:S(2)}) collective-permute-start(bf16[32,4096]{1,0:T(8,128)(2,1)S(1)} %add_convert_fusion.3), channel_id=1, source_target_pairs={{0,1},{1,0},{2,3},{3,2},{4,5},{5,4},{6,7},{7,6},{8,24},{9,25},{10,... | collective-permute-start | bytes 786440 | tf_op jit(solution)/shard_map/ppermute | solution.py:80
  72.8 8.1 %collective-permute-start.28 = (bf16[16,4096]{1,0:T(8,128)(2,1)S(1)}, bf16[16,4096]{1,0:T(8,128)(2,1)S(1)}, u32[]{:S(2)}, u32[]{:S(2)}) collective-permute-start(bf16[16,4096]{1,0:T(8,128)(2,1)S(1)} %fusion.2), channel_id=1, source_target_pairs={{0,1},{1,0},{2,3},{3,2},{4,5},{5,4},{6,7},{7,6},{8,24},{9,25},{10,... | collective-permute-start | bytes 393224 | tf_op jit(solution)/shard_map/ppermute | solution.py:80
  73.7 10.2 %collective-permute-start.15 = (bf16[16,4096]{1,0:T(8,128)(2,1)S(1)}, bf16[16,4096]{1,0:T(8,128)(2,1)S(1)}, u32[]{:S(2)}, u32[]{:S(2)}) collective-permute-start(bf16[16,4096]{1,0:T(8,128)(2,1)S(1)} %add_convert_fusion.6), channel_id=1, source_target_pairs={{0,2},{1,3},{2,0},{3,1},{4,6},{5,7},{6,4},{7,5},{8,10},{9,11},{10,... | collective-permute-start | bytes 393224 | tf_op jit(solution)/shard_map/ppermute | solution.py:80
  77.8 6.9 %collective-permute-start.26 = (bf16[16,4096]{1,0:T(8,128)(2,1)S(1)}, bf16[16,4096]{1,0:T(8,128)(2,1)S(1)}, u32[]{:S(2)}, u32[]{:S(2)}) collective-permute-start(bf16[16,4096]{1,0:T(8,128)(2,1)S(1)} %add_convert_fusion.5), channel_id=1, source_target_pairs={{0,2},{1,3},{2,0},{3,1},{4,6},{5,7},{6,4},{7,5},{8,10},{9,11},{10,... | collective-permute-start | bytes 393224 | tf_op jit(solution)/shard_map/ppermute | solution.py:80
  81.0 7.3 %collective-permute-start.29 = (bf16[8,4096]{1,0:T(8,128)(2,1)S(1)}, bf16[8,4096]{1,0:T(8,128)(2,1)S(1)}, u32[]{:S(2)}, u32[]{:S(2)}) collective-permute-start(bf16[8,4096]{1,0:T(8,128)(2,1)S(1)} %fusion.5), channel_id=1, source_target_pairs={{0,4},{1,5},{2,6},{3,7},{4,0},{5,1},{6,2},{7,3},{8,12},{9,13},{10,... | collective-permute-start | bytes 196616 | tf_op jit(solution)/shard_map/ppermute | solution.py:80
  83.9 6.4 %collective-permute-start.17 = (bf16[8,4096]{1,0:T(8,128)(2,1)S(1)}, bf16[8,4096]{1,0:T(8,128)(2,1)S(1)}, u32[]{:S(2)}, u32[]{:S(2)}) collective-permute-start(bf16[8,4096]{1,0:T(8,128)(2,1)S(1)} %add_convert_fusion.10), channel_id=1, source_target_pairs={{0,4},{1,5},{2,6},{3,7},{4,0},{5,1},{6,2},{7,3},{8,12},{9,13},{10,... | collective-permute-start | bytes 196616 | tf_op jit(solution)/shard_map/ppermute | solution.py:80
  84.8 6.9 %collective-permute-start.27 = (bf16[8,4096]{1,0:T(8,128)(2,1)S(1)}, bf16[8,4096]{1,0:T(8,128)(2,1)S(1)}, u32[]{:S(2)}, u32[]{:S(2)}) collective-permute-start(bf16[8,4096]{1,0:T(8,128)(2,1)S(1)} %add_convert_fusion.8), channel_id=1, source_target_pairs={{0,4},{1,5},{2,6},{3,7},{4,0},{5,1},{6,2},{7,3},{8,12},{9,13},{10,... | collective-permute-start | bytes 196616 | tf_op jit(solution)/shard_map/ppermute | solution.py:80
